TPU v7x, 32 devices: a whole 2x2x4 slice. The times are simulated.
32 devices in a mesh: sweep: 2 (over y), wide: 4 (over z), narrow: 4 (over x, core).
Axes of the slice: x: 2, y: 2, z: 4, core: 2. Of those that a mesh axis runs over, the one named last changes fastest.
Arguments:
- fresh_coefs: bfloat16 [1024, 32, 128], P(('sweep', 'wide', 'narrow')), parts along dimension 0, may hold values from -1.5 to 1.5
- older_coefs: bfloat16 [8, 4, 8, 2, 32, 128], P(('sweep', 'wide'), 'narrow'), parts along dimension 0, may hold values from -1.5 to 1.5
- state: float32 [2, 131072], P(None, ('sweep', 'wide', 'narrow')), parts along dimension 1, may hold values from 0 to 1
- lesion: int32 [131072], P(('sweep', 'wide', 'narrow')), parts along dimension 0, may hold values 0 or 1
- stim_nodes: int32 [128], P('sweep'), parts along dimension 0, may hold values from 0 to 65535
- stim_wave: float32 [64], P('sweep'), parts along dimension 0, may hold values from -12 to 12
- read_blocks: int32 [4, 4, 4, 2], P('wide', 'narrow'), may hold values from -1 to 31, as said below
- tract_slot: int32 [4, 4, 96], P('wide', 'narrow'), may hold values from 0 to 7, as said below
- tract_target: int32 [4, 4, 96], P('wide', 'narrow'), may hold values from 0 to 127, as said below
- tract_delay: int32 [4, 4, 96], P('wide', 'narrow'), may hold values from 32 to 95
- tract_frac: float32 [4, 4, 96], P('wide', 'narrow'), may hold values from 0 to 1
- tract_weights: bfloat16 [4, 4, 96, 128, 128], P('wide', 'narrow'), may hold values from -0.3125 to 0.3125
Outputs:
- new_coefs: bfloat16 [1024, 32, 128], P(('sweep', 'wide', 'narrow')), parts along dimension 0
- final_state: float32 [2, 131072], P(None, ('sweep', 'wide', 'narrow')), parts along dimension 1
There are 2 independent parts, one for each index of `sweep`. A program takes and returns all parts, laid end to end along the dimension named above; an argument that names none is the same for every part. Nothing has to cross between parts.
Inputs may be any that keep to these rules, and one draw needn't show every extreme that they name: `read_blocks`: entry [w, n, o, c] is a block of device (o, n) or -1 for an empty slot; the blocks named for one (w, n, o) are distinct and fill its first slots; some owner fills all 2 slots of every reader. `tract_slot`: each entry names a slot of its own device whose read_blocks entry is not -1. `tract_target`: the tiles of one device (w, n) name, for every narrow index p, exactly 12 distinct targets among p * 32 to (p + 1) * 32 - 1.
All inputs are finite; a program needn't handle non-finite values. No bound on the sum of `lesion` on one device may be relied on, other than what follows from the above.
Results may differ from a plain program's by a relative error of at most 0.003.
Values may be sent and summed in bfloat16 or wider, within the bound.
No kernel may reach another device: no remote copies, remote signals or barrier semaphores. Data moves between devices by JAX's collectives and lax.ppermute only.
A program may use at most 128 MiB of HBM per device.

v0:
```python
import math

import jax
import jax.numpy as jnp
from jax import lax
from jax.sharding import PartitionSpec as P

STEPS = 32
HSEG = 2


excite_rate = 0.1
inhibit_rate = 0.05
excite_excite = 1.5
inhibit_excite = 2.0
excite_inhibit = 2.0
inhibit_inhibit = 0.5
excite_offset = 0.5
inhibit_offset = 0.5
tract_gain = 2.0


def basis_table(coef_count, step_count):
    order = jnp.arange(coef_count, dtype=jnp.float32)[:, None]
    places = jnp.arange(step_count, dtype=jnp.float32)[None, :]
    angles = math.pi * (step_count - places - 0.5) / step_count
    return jnp.cos(order * angles)


def fit_table(coef_count, step_count):
    scales = jnp.where(jnp.arange(coef_count)[:, None] == 0, 1.0, 2.0) / step_count
    return basis_table(coef_count, step_count) * scales


def join_history(older_values, newest_values):
    slot_count = older_values.shape[0]
    earlier = older_values[:, ::-1].reshape(slot_count, HSEG * STEPS, older_values.shape[-1])
    return jnp.concatenate([earlier, newest_values], axis=1)


def delayed_inputs(history, slot_ids, delay_bins, fractions):
    history_length = history.shape[1]

    def one_tile(slot_id, delay_bin, fraction):
        source_rows = jnp.take(history, slot_id, axis=0)
        window = lax.dynamic_slice_in_dim(source_rows, history_length - delay_bin - 1, STEPS + 1, 0)
        return ((1.0 - fraction) * window[1:] + fraction * window[:-1]).astype(jnp.bfloat16)

    return jax.vmap(one_tile)(slot_ids, delay_bins, fractions)


def integrate(state, forcing):

    def advance(current, inflow):
        excite, inhibit = current
        excite_next = excite + excite_rate * (
            -excite
            + jax.nn.sigmoid(
                excite_excite * excite - inhibit_excite * inhibit + inflow - excite_offset
            )
        )
        inhibit_next = inhibit + inhibit_rate * (
            -inhibit
            + jax.nn.sigmoid(excite_inhibit * excite - inhibit_inhibit * inhibit - inhibit_offset)
        )
        return ((excite_next, inhibit_next), excite_next)

    (excite, inhibit), samples = lax.scan(advance, (state[0], state[1]), forcing)
    return (jnp.stack([excite, inhibit]), samples)


def local(
    fresh_coefs,
    older_coefs,
    state,
    lesion,
    stim_nodes,
    stim_wave,
    read_blocks,
    tract_slot,
    tract_target,
    tract_delay,
    tract_frac,
    tract_weights,
):
    wide_count = lax.axis_size("wide")
    narrow_count = lax.axis_size("narrow")
    own_blocks, coef_count, block_rows = fresh_coefs.shape
    capacity = read_blocks.shape[3]
    slot_count = wide_count * capacity
    tile_count = tract_slot.shape[2]
    table = basis_table(coef_count, STEPS).astype(jnp.bfloat16)
    wanted = read_blocks.reshape(wide_count, capacity)
    everything = jnp.einsum(
        "bkn,km->bmn",
        lax.all_gather(fresh_coefs, "wide", axis=0, tiled=True),
        table,
        preferred_element_type=jnp.float32,
    )
    flat = (
        jnp.arange(wide_count, dtype=jnp.int32)[:, None] * own_blocks + jnp.maximum(wanted, 0)
    ).reshape(-1)
    newest = jnp.take(everything, flat, axis=0)
    older = older_coefs.reshape(slot_count, HSEG, coef_count, block_rows)
    older_values = jnp.einsum("shkn,km->shmn", older, table, preferred_element_type=jnp.float32)
    history = join_history(older_values, newest)
    delayed = delayed_inputs(
        history,
        tract_slot.reshape(tile_count),
        tract_delay.reshape(tile_count),
        tract_frac.reshape(tile_count),
    )
    weights = tract_weights.reshape(tile_count, block_rows, block_rows)
    contrib = jnp.einsum("tjs,tqs->tjq", delayed, weights, preferred_element_type=jnp.float32)
    target_count = own_blocks * narrow_count
    onehot = (
        jnp.arange(target_count, dtype=jnp.int32)[:, None]
        == tract_target.reshape(tile_count)[None, :]
    ).astype(jnp.float32)
    partial_sum = jnp.einsum("gt,tjq->gjq", onehot, contrib, precision=lax.Precision.HIGHEST)
    coupling = lax.psum_scatter(
        partial_sum.astype(jnp.bfloat16), "narrow", scatter_dimension=0, tiled=True
    ).astype(jnp.float32)
    node_count = own_blocks * block_rows
    first_node = (lax.axis_index("wide") * narrow_count + lax.axis_index("narrow")) * node_count
    node_ids = first_node + jnp.arange(node_count, dtype=jnp.int32)
    counts = jnp.sum((stim_nodes[:, None] == node_ids[None, :]).astype(jnp.float32), axis=0)
    inflow = coupling.transpose(1, 0, 2).reshape(STEPS, node_count)
    forcing = (
        tract_gain * inflow * (1.0 - lesion.astype(jnp.float32))[None, :]
        + stim_wave[:, None] * counts[None, :]
    )
    final_state, samples = integrate(state, forcing)
    fitted = jnp.dot(fit_table(coef_count, STEPS), samples, precision=lax.Precision.HIGHEST)
    new_coefs = (
        fitted.reshape(coef_count, own_blocks, block_rows).transpose(1, 0, 2).astype(jnp.bfloat16)
    )
    return (new_coefs, final_state)


def solution(mesh):
    in_specs = (
        P(("sweep", "wide", "narrow"), None, None),
        P(("sweep", "wide"), "narrow", None, None, None, None),
        P(None, ("sweep", "wide", "narrow")),
        P(("sweep", "wide", "narrow")),
        P("sweep"),
        P("sweep"),
        P("wide", "narrow", None, None),
        P("wide", "narrow", None),
        P("wide", "narrow", None),
        P("wide", "narrow", None),
        P("wide", "narrow", None),
        P("wide", "narrow", None, None, None),
    )
    out_specs = (P(("sweep", "wide", "narrow"), None, None), P(None, ("sweep", "wide", "narrow")))
    return jax.shard_map(local, mesh=mesh, in_specs=in_specs, out_specs=out_specs, check_vma=False)
```

profile of v0, /device:TPU:0, one launch (start us, length us, event | category | flops | bytes accessed | tf_op | source)
XLA Modules:
  0.0 191.1 jit_solution(4689292501746492347)
XLA Ops:
  8.8 1.2 convolution_bitcast_fusion.1
  11.9 1.2 compare_and_fusion.1
  14.4 25.8 %all-gather.2.cloned.1.call-done = bf16[128,32,128]{2,1,0:T(8,128)(2,1)} async-done(((bf16[32,32,128]{2,1,0:T(8,128)(2,1)}), bf16[128,32,128]{2,1,0:T(8,128)(2,1)}) %all-gather.2.cloned.1.call-update) | async-done | bytes 1048592 | tf_op jit(solution)/shard_map/all_gather | solution.py:96
  40.2 3.1 %convolution_bitcast_fusion = f32[128,32,128]{2,1,0:T(8,128)} fusion(bf16[128,32,128]{2,1,0:T(8,128)(2,1)} %all-gather.2.cloned.1.call-done, f32[32]{0:T(128)S(1)} %subtract_multiply_fusion.1), kind=kOutput, calls=%fused_computation.10 | convolution fusion | flops 33556480 | bytes 3145856 | tf_op jit(solution)/shard_map/bkn,km->bmn/dot_general | solution.py:94
  43.3 2.1 %gather_fusion = f32[8,32,128]{2,1,0:T(8,128)S(1)} fusion(f32[128,32,128]{2,1,0:T(8,128)} %convolution_bitcast_fusion, s32[1024]{0:T(1024)S(1)} %pad_clamp_fusion.1), kind=kCustom, calls=%fused_computation | custom fusion | bytes 262176 | tf_op jit(solution)/shard_map/jit(_take)/gather | solution.py:103
  45.6 1.0 pad_maximum_fusion
  46.6 3.0 %gather_fusion.1 = f32[96,96,128]{2,1,0:T(8,128)} fusion(f32[8,96,128]{2,1,0:T(8,128)S(1)} %pad_maximum_fusion, s32[1024]{0:T(1024)S(1)} %pad_clamp_fusion), kind=kCustom, calls=%fused_computation.1 | custom fusion | bytes 9437568 | tf_op jit(solution)/shard_map/vmap(jit(_take))/gather | solution.py:45
  49.6 2.7 %broadcast_select_fusion = f32[96,96,128]{2,1,0:T(8,128)S(1)} fusion(f32[96,96,128]{2,1,0:T(8,128)} %gather_fusion.1, pred[96]{0:T(512)(128)(4,1)} %compare_and_fusion.1), kind=kLoop, calls=%fused_computation.9 | loop fusion | flops 1179648 | bytes 9437280 | tf_op jit(solution)/shard_map/vmap(jit(_take))/select_n | solution.py:45
  52.3 4.9 %copy.29 = f32[96,96,128]{2,0,1:T(8,128)} copy(f32[96,96,128]{2,1,0:T(8,128)S(1)} %broadcast_select_fusion) | data formatting | bytes 9437184 | tf_op jit(solution)/shard_map/vmap(jit(_take))/select_n | solution.py:45
  57.2 7.7 %gather_fusion.2 = f32[96,33,128]{2,0,1:T(8,128)} fusion(f32[96,96,128]{2,0,1:T(8,128)} %copy.29, s32[96]{0:T(128)S(1)} %or_bitcast_fusion), kind=kCustom, calls=%fused_computation.2 | custom fusion | bytes 3245184 | tf_op jit(solution)/shard_map/vmap()/gather | solution.py:46
  64.8 2.2 %fusion.3 = bf16[96,32,128]{2,0,1:T(8,128)(2,1)S(1)} fusion(f32[96,33,128]{2,0,1:T(8,128)} %gather_fusion.2, f32[96]{0:T(128)S(1)} %bitcast.78, f32[96]{0:T(128)S(1)} %broadcast_subtract_fusion), kind=kLoop, calls=%fused_computation.13 | loop fusion | flops 1572864 | bytes 3932928 | tf_op jit(solution)/shard_map/vmap()/convert_element_type | solution.py:47
  67.1 1.8 fusion
  68.9 3.1 %fusion.6 = bf16[128,32,128]{2,0,1:T(8,128)(2,1)} fusion(f32[96,32,128]{2,1,0:T(8,128)S(1)} %fusion, s32[96]{0:T(128)S(1)} %bitcast.79), kind=kOutput, calls=%fused_computation.17 | convolution fusion | flops 604516352 | bytes 2621824 | tf_op jit(solution)/shard_map/gt,tjq->gjq/dot_general | solution.py:120
  72.4 24.3 %reduce-scatter.2.cloned.1.call-done = bf16[32,32,128]{2,0,1:T(8,128)(2,1)} async-done(((bf16[128,32,128]{2,0,1:T(8,128)(2,1)}), bf16[32,32,128]{2,0,1:T(8,128)(2,1)}) %reduce-scatter.2.cloned.1.call-update) | async-done | bytes 262160 | tf_op jit(solution)/shard_map/reduce_scatter | solution.py:121
  96.7 1.0 reshape.184
  97.7 1.1 fusion.11
  98.8 82.3 %while.17 = (s32[]{:T(128)}, f32[4096]{0:T(1024)S(1)}, f32[4096]{0:T(1024)S(1)}, f32[32,4096]{1,0:T(8,128)}, f32[32,4096]{1,0:T(8,128)}, /*index=5*/s32[]{:T(128)}, s32[]{:T(128)}) while((s32[]{:T(128)}, f32[4096]{0:T(1024)S(1)}, f32[4096]{0:T(1024)S(1)}, f32[32,4096]{1,0:T(8,128)}, f32[32,4096]{1,0:T(8,128)}, /*index=5*/s32[]{:T(128)}, ...), condition=%wide.region_3.4_spmd, body=%wide.region_2.3_spmd.sunk | while | flops 94210 | bytes 147541 | solution.py:68
  98.8 0.9 constant_dynamic-slice_fusion.2
  99.7 1.6 dynamic_update_slice.9
  101.4 0.9 constant_dynamic-slice_fusion.2
  102.3 1.6 dynamic_update_slice.9
  103.9 0.9 constant_dynamic-slice_fusion.2
  104.9 1.6 dynamic_update_slice.9
  107.5 1.6 dynamic_update_slice.9
  110.0 1.6 dynamic_update_slice.9
  112.6 1.6 dynamic_update_slice.9
  115.2 1.6 dynamic_update_slice.9
  116.8 0.9 constant_dynamic-slice_fusion.2
  117.8 1.6 dynamic_update_slice.9
  119.4 0.9 constant_dynamic-slice_fusion.2
  120.3 1.6 dynamic_update_slice.9
  122.9 1.6 dynamic_update_slice.9
  125.5 1.6 dynamic_update_slice.9
  128.1 1.6 dynamic_update_slice.9
  130.7 1.6 dynamic_update_slice.9
  132.3 0.9 constant_dynamic-slice_fusion.2
  133.3 1.6 dynamic_update_slice.9
  134.9 0.9 constant_dynamic-slice_fusion.2
  135.8 1.6 dynamic_update_slice.9
  137.5 0.9 constant_dynamic-slice_fusion.2
  138.4 1.6 dynamic_update_slice.9
  141.0 1.6 dynamic_update_slice.9
  143.6 1.6 dynamic_update_slice.9
  145.2 0.9 constant_dynamic-slice_fusion.2
  146.1 1.6 dynamic_update_slice.9
  148.7 1.6 dynamic_update_slice.9
  150.3 0.9 constant_dynamic-slice_fusion.2
  151.2 1.6 dynamic_update_slice.9
  153.8 1.6 dynamic_update_slice.9
  155.4 0.9 constant_dynamic-slice_fusion.2
  156.4 1.6 dynamic_update_slice.9
  158.9 1.6 dynamic_update_slice.9
  161.5 1.6 dynamic_update_slice.9
  164.1 1.6 dynamic_update_slice.9
  166.6 1.6 dynamic_update_slice.9
  169.2 1.6 dynamic_update_slice.9
  171.8 1.6 dynamic_update_slice.9
  173.4 0.9 constant_dynamic-slice_fusion.2
  174.3 1.6 dynamic_update_slice.9
  176.0 0.9 constant_dynamic-slice_fusion.2
  176.9 1.6 dynamic_update_slice.9
  178.5 0.9 constant_dynamic-slice_fusion.2
  179.5 1.6 dynamic_update_slice.9
  181.1 1.8 fusion.9
  (94 shorter events, 24.1 us)
Async XLA Ops:
  7.2 59.9 %copy-start = (bf16[1,1,96,128,128]{4,3,2,1,0:T(8,128)(2,1)S(1)}, bf16[1,1,96,128,128]{4,3,2,1,0:T(8,128)(2,1)}, u32[]{:S(2)}) copy-start(bf16[1,1,96,128,128]{4,3,2,1,0:T(8,128)(2,1)} %param.25) | copy-start | bytes 9437188
  7.2 33.1 %all-gather.2.cloned.1.call-start = ((), (), s32[]{:S(2)}) async-start(), calls=%async_computation.1 | async-start | bytes 1310720 | tf_op jit(solution)/shard_map/all_gather | solution.py:96
  7.9 88.7 %reduce-scatter.2.cloned.1.call-start = ((), (), s32[]{:S(2)}) async-start(), calls=%async_computation.2 | async-start | bytes 1310720 | tf_op jit(solution)/shard_map/reduce_scatter | solution.py:121
  57.2 7.7 %copy-start.3 = (f32[1,1,96]{2,1,0:T(1,128)S(1)}, f32[1,1,96]{2,1,0:T(1,128)}, u32[]{:S(2)}) copy-start(f32[1,1,96]{2,1,0:T(1,128)} %param.24) | copy-start | bytes 1156
  67.1 1.8 copy-start.6
  68.9 3.2 %copy-start.4 = (s32[64]{0:T(128)S(1)}, s32[64]{0:T(128)}, u32[]{:S(2)}) copy-start(s32[64]{0:T(128)} %param.18) | copy-start | bytes 772
  68.9 3.4 %copy-start.2 = (s32[4096]{0:T(1024)S(1)}, s32[4096]{0:T(1024)}, u32[]{:S(2)}) copy-start(s32[4096]{0:T(1024)} %param.17) | copy-start | bytes 49156
  68.9 3.4 %copy-start.1 = (f32[2,4096]{1,0:T(2,128)S(1)}, f32[2,4096]{1,0:T(2,128)}, u32[]{:S(2)}) copy-start(f32[2,4096]{1,0:T(2,128)} %param.16) | copy-start | bytes 98308
  68.9 28.8 %copy-start.5 = (f32[32]{0:T(128)S(1)}, f32[32]{0:T(128)}, u32[]{:S(2)}) copy-start(f32[32]{0:T(128)} %param.19) | copy-start | bytes 388
Sparse Core Ops, SparseCore 0:
  9.6 30.6 all-gather.1
  72.1 24.4 reduce-scatter.1
where the time goes:
time: 193 us; the launch traced here: 191 us
  local copies, waits for them, and re-layouts  101 us (52%)
  waiting for transfers between devices  50.8 us (26%)
  between operations  14.3 us (7%)
  other arithmetic  14 us (7%)
  matrix products  10.9 us (6%)
    dynamic_update_slice x32, local copies, waits for them, and re-layouts, integrate(): lax.scan(advance, (state[0], state[1]), forcing)  51.7 us
    dynamic_slice x32, local copies, waits for them, and re-layouts, integrate(): lax.scan(advance, (state[0], state[1]), forcing)  29.4 us
    all_gather x1, waiting for transfers between devices, local(): lax.all_gather(fresh_coefs, 'wide', axis=0, tiled=True)  25.8 us
    reduce_scatter x1, waiting for transfers between devices, local(): lax.psum_scatter(partial_sum.astype(jnp.bfloat16), 'narrow', scatter_dime...  24.3 us
    gather x1, local copies, waits for them, and re-layouts, one_tile(): lax.dynamic_slice_in_dim(source_rows, history_length - delay_bin - 1, STE...  7.67 us
    select_n x1, local copies, waits for them, and re-layouts, one_tile(): source_rows = jnp.take(history, slot_id, axis=0)  4.88 us
  transfers between devices with their start and end apart: 2, of which 2 were waited for; matrix products, arithmetic and copies ran while one was open for 3% of the time, Pallas kernels for 0%

commit v1 on v0

v1 whole, which is shorter than its diff:
```python
import functools

import jax
import jax.numpy as jnp
import ml_dtypes
import numpy as np
from jax import lax
from jax.experimental import pallas as pl
from jax.experimental.pallas import tpu as pltpu
from jax.sharding import PartitionSpec as P

STEPS = 32
HSEG = 2
SEGS = HSEG + 1
LENGTH = SEGS * STEPS
GROUP = 4

excite_rate = 0.1
inhibit_rate = 0.05
excite_excite = 1.5
inhibit_excite = 2.0
excite_inhibit = 2.0
inhibit_inhibit = 0.5
excite_offset = 0.5
inhibit_offset = 0.5
tract_gain = 2.0

SMEM = pltpu.SMEM
VMEM = pltpu.VMEM
smem_spec = pl.BlockSpec(memory_space=SMEM)
vmem_spec = pl.BlockSpec(memory_space=VMEM)
any_spec = pl.BlockSpec(memory_space=pl.ANY)


def basis_table(coef_count, step_count):
    order = np.arange(coef_count, dtype=np.float32)[:, None]
    places = np.arange(step_count, dtype=np.float32)[None, :]
    angles = np.float32(np.pi) * (step_count - places - np.float32(0.5)) / np.float32(step_count)
    return np.cos((order * angles).astype(np.float64)).astype(np.float32)


def expand_table(coef_count):
    basis = basis_table(coef_count, STEPS).astype(ml_dtypes.bfloat16)
    table = np.zeros((LENGTH, SEGS * coef_count), ml_dtypes.bfloat16)
    for seg in range(SEGS):
        table[seg * STEPS : (seg + 1) * STEPS, seg * coef_count : (seg + 1) * coef_count] = basis.T
    return table


def fit_tables(coef_count):
    scales = np.where(np.arange(coef_count)[:, None] == 0, 1.0, 2.0) / STEPS
    fit = (basis_table(coef_count, STEPS) * scales).astype(np.float32)
    whole = np.zeros((GROUP * coef_count, GROUP * STEPS), np.float32)
    for g in range(GROUP):
        whole[g * coef_count : (g + 1) * coef_count, g * STEPS : (g + 1) * STEPS] = fit
    high = whole.astype(ml_dtypes.bfloat16)
    low = (whole - high.astype(np.float32)).astype(ml_dtypes.bfloat16)
    return high, low


def pick_kernel(place_ref, own_reads, *refs, capacity, peers):
    asked = (own_reads,) + refs[: peers - 1]
    fresh = refs[peers - 1]
    outs = refs[peers : 2 * peers]
    sems = refs[2 * peers]
    place = place_ref[0]
    copies = []
    for r in range(peers):
        for c in range(capacity):
            block = jnp.maximum(asked[r][c, place], 0)
            copy = pltpu.make_async_copy(fresh.at[block], outs[r].at[c], sems.at[r, c])
            copy.start()
            copies.append(copy)
    for copy in copies:
        copy.wait()


def list_kernel(target_ref, compact_ref, ids_ref, seen, counts, *, peers, own_blocks, peer_targets):
    tile_count = target_ref.shape[1]

    @pl.loop(0, peers * own_blocks)
    def _(g):
        seen[g] = -1

    for p in range(peers):
        counts[p] = 0

    @pl.loop(0, tile_count)
    def _(t):
        target = target_ref[0, t]
        known = seen[target]
        peer = target // own_blocks
        rank = counts[peer]
        number = jnp.where(known < 0, peer * peer_targets + rank, known)
        counts[peer] = rank + jnp.where(known < 0, 1, 0)
        seen[target] = number
        compact_ref[0, t] = number
        ids_ref[0, number] = target - peer * own_blocks


def tract_kernel(
    place_ref, slot_ref, delay_ref, frac_ref, compact_ref, table_ref, older_ref, weights_ref, *refs,
    wide_peers, narrow_peers, capacity, peer_targets, unroll,
):
    news = refs[:wide_peers]
    outs = refs[wide_peers : wide_peers + narrow_peers]
    hist, total = refs[wide_peers + narrow_peers :]
    tile_count = slot_ref.shape[1]
    wide_place = place_ref[0]
    narrow_place = place_ref[1]
    table = table_ref[...]
    for r in range(wide_peers):
        owner = wide_place ^ r
        for c in range(capacity):
            slot = owner * capacity + c
            segments = [older_ref[slot, h] for h in range(HSEG - 1, -1, -1)] + [news[r][c]]
            coefs = jnp.concatenate(segments, axis=0)
            values = jnp.dot(table, coefs, preferred_element_type=jnp.float32)
            hist[pl.ds(pl.multiple_of(slot * LENGTH, 8), LENGTH), :] = values
    total[...] = jnp.zeros_like(total)

    @pl.loop(0, tile_count // unroll)
    def _(step):
        sums = []
        for u in range(unroll):
            t = step * unroll + u
            fraction = frac_ref[0, t]
            start = slot_ref[0, t] * LENGTH + LENGTH - 1 - delay_ref[0, t]
            earlier = hist[pl.ds(start, STEPS), :]
            later = hist[pl.ds(start + 1, STEPS), :]
            delayed = ((1.0 - fraction) * later + fraction * earlier).astype(jnp.bfloat16)
            sums.append(
                lax.dot_general(
                    delayed, weights_ref[t], (((1,), (1,)), ((), ())),
                    preferred_element_type=jnp.float32,
                )
            )
        for u in range(unroll):
            t = step * unroll + u
            rows = pl.ds(pl.multiple_of(compact_ref[0, t] * STEPS, 8), STEPS)
            total[rows, :] += sums[u]

    span = peer_targets * STEPS
    for r in range(narrow_peers):
        first = pl.multiple_of((narrow_place ^ r) * span, 8)
        outs[r][...] = total[pl.ds(first, span), :].astype(jnp.bfloat16)


def window_kernel(
    place_ref, stim_ref, wave_ref, *refs, narrow_peers, own_blocks, peer_targets, coef_count
):
    ids = refs[:narrow_peers]
    sums = refs[narrow_peers : 2 * narrow_peers]
    state_ref, lesion_ref, high_ref, low_ref, coefs_out, state_out = refs[
        2 * narrow_peers : 2 * narrow_peers + 6
    ]
    inflow, samples, rates = refs[2 * narrow_peers + 6 :]
    block_rows = lesion_ref.shape[1]
    narrow_place = place_ref[1]
    first_node = (place_ref[0] * narrow_peers + narrow_place) * (own_blocks * block_rows)

    inflow[...] = jnp.zeros_like(inflow)
    for r in range(narrow_peers):
        for i in range(peer_targets):
            target = ids[r][0, narrow_place * peer_targets + i]
            rows = pl.ds(pl.multiple_of(target * STEPS, 8), STEPS)
            inflow[rows, :] += sums[r][i * STEPS : (i + 1) * STEPS, :].astype(jnp.float32)

    for b in range(own_blocks):
        piece = state_ref[:, b * block_rows : (b + 1) * block_rows]
        rates[0, b : b + 1, :] = piece[0:1, :]
        rates[1, b : b + 1, :] = piece[1:2, :]

    shape = (own_blocks, block_rows)
    nodes = (
        first_node
        + lax.broadcasted_iota(jnp.int32, shape, 0) * block_rows
        + lax.broadcasted_iota(jnp.int32, shape, 1)
    )
    counts = jnp.zeros(shape, jnp.float32)
    for n in range(stim_ref.shape[0]):
        counts = counts + jnp.where(nodes == stim_ref[n], 1.0, 0.0)
    gain = tract_gain * (1.0 - lesion_ref[...].astype(jnp.float32))
    excite = rates[0]
    inhibit = rates[1]
    for j in range(STEPS):
        arriving = inflow[pl.ds(j, own_blocks, stride=STEPS), :]
        forcing = gain * arriving + wave_ref[j] * counts
        excite_drive = excite_excite * excite - inhibit_excite * inhibit + forcing - excite_offset
        inhibit_drive = excite_inhibit * excite - inhibit_inhibit * inhibit - inhibit_offset
        excite, inhibit = (
            excite + excite_rate * (0.5 * jnp.tanh(0.5 * excite_drive) + 0.5 - excite),
            inhibit + inhibit_rate * (0.5 * jnp.tanh(0.5 * inhibit_drive) + 0.5 - inhibit),
        )
        samples[pl.ds(j, own_blocks, stride=STEPS), :] = excite
    rates[0] = excite
    rates[1] = inhibit
    for b in range(own_blocks):
        columns = slice(b * block_rows, (b + 1) * block_rows)
        state_out[0:1, columns] = rates[0, b : b + 1, :]
        state_out[1:2, columns] = rates[1, b : b + 1, :]

    high = high_ref[...]
    low = low_ref[...]
    rows = GROUP * STEPS
    for g in range(own_blocks // GROUP):
        part = samples[g * rows : (g + 1) * rows, :]
        part_high = part.astype(jnp.bfloat16)
        part_low = (part - part_high.astype(jnp.float32)).astype(jnp.bfloat16)
        fitted = (
            jnp.dot(high, part_high, preferred_element_type=jnp.float32)
            + jnp.dot(high, part_low, preferred_element_type=jnp.float32)
            + jnp.dot(low, part_high, preferred_element_type=jnp.float32)
        )
        coefs_out[g * GROUP : (g + 1) * GROUP] = fitted.astype(jnp.bfloat16).reshape(
            GROUP, coef_count, block_rows
        )


def local(
    fresh_coefs,
    older_coefs,
    state,
    lesion,
    stim_nodes,
    stim_wave,
    read_blocks,
    tract_slot,
    tract_target,
    tract_delay,
    tract_frac,
    tract_weights,
):
    wide_peers = lax.axis_size("wide")
    narrow_peers = lax.axis_size("narrow")
    own_blocks, coef_count, block_rows = fresh_coefs.shape
    capacity = read_blocks.shape[3]
    slot_count = wide_peers * capacity
    tile_count = tract_slot.shape[2]
    peer_targets = tile_count // (2 * narrow_peers)
    target_count = narrow_peers * own_blocks

    def swap(x, axis, peers, r):
        return lax.ppermute(x, axis, [(i, i ^ r) for i in range(peers)])

    place = jnp.stack([lax.axis_index("wide"), lax.axis_index("narrow")]).astype(jnp.int32)
    reads = read_blocks.reshape(wide_peers, capacity).T
    asked = [swap(reads, "wide", wide_peers, r) for r in range(1, wide_peers)]

    picked = pl.pallas_call(
        functools.partial(pick_kernel, capacity=capacity, peers=wide_peers),
        out_shape=[
            jax.ShapeDtypeStruct((capacity, coef_count, block_rows), jnp.bfloat16)
        ]
        * wide_peers,
        in_specs=[smem_spec] * (wide_peers + 1) + [any_spec],
        out_specs=[any_spec] * wide_peers,
        scratch_shapes=[pltpu.SemaphoreType.DMA((wide_peers, capacity))],
        name="pick_blocks",
    )(place, reads, *asked, fresh_coefs)

    compact, ids = pl.pallas_call(
        functools.partial(
            list_kernel, peers=narrow_peers, own_blocks=own_blocks, peer_targets=peer_targets
        ),
        out_shape=[
            jax.ShapeDtypeStruct((1, tile_count), jnp.int32),
            jax.ShapeDtypeStruct((1, narrow_peers * peer_targets), jnp.int32),
        ],
        in_specs=[smem_spec],
        out_specs=[smem_spec] * 2,
        scratch_shapes=[SMEM((target_count,), jnp.int32), SMEM((narrow_peers,), jnp.int32)],
        name="list_targets",
    )(tract_target.reshape(1, tile_count))
    ids_by_peer = [ids] + [swap(ids, "narrow", narrow_peers, r) for r in range(1, narrow_peers)]

    news = [picked[0]] + [
        swap(picked[r], "wide", wide_peers, r) for r in range(1, wide_peers)
    ]

    span = peer_targets * STEPS
    shares = pl.pallas_call(
        functools.partial(
            tract_kernel,
            wide_peers=wide_peers,
            narrow_peers=narrow_peers,
            capacity=capacity,
            peer_targets=peer_targets,
            unroll=16,
        ),
        out_shape=[jax.ShapeDtypeStruct((span, block_rows), jnp.bfloat16)] * narrow_peers,
        in_specs=[smem_spec] * 5 + [vmem_spec] * (3 + wide_peers),
        out_specs=[vmem_spec] * narrow_peers,
        scratch_shapes=[
            VMEM((slot_count * LENGTH, block_rows), jnp.float32),
            VMEM((narrow_peers * span, block_rows), jnp.float32),
        ],
        compiler_params=pltpu.CompilerParams(vmem_limit_bytes=24 << 20),
        name="tract_tiles",
    )(
        place,
        tract_slot.reshape(1, tile_count),
        tract_delay.reshape(1, tile_count),
        tract_frac.reshape(1, tile_count),
        compact,
        expand_table(coef_count),
        older_coefs.reshape(slot_count, HSEG, coef_count, block_rows),
        tract_weights.reshape(tile_count, block_rows, block_rows),
        *news,
    )
    sums = [shares[0]] + [
        swap(shares[r], "narrow", narrow_peers, r) for r in range(1, narrow_peers)
    ]

    high, low = fit_tables(coef_count)
    new_coefs, final_state = pl.pallas_call(
        functools.partial(
            window_kernel,
            narrow_peers=narrow_peers,
            own_blocks=own_blocks,
            peer_targets=peer_targets,
            coef_count=coef_count,
        ),
        out_shape=[
            jax.ShapeDtypeStruct(fresh_coefs.shape, jnp.bfloat16),
            jax.ShapeDtypeStruct(state.shape, jnp.float32),
        ],
        in_specs=[smem_spec] * (3 + narrow_peers) + [vmem_spec] * (narrow_peers + 4),
        out_specs=[vmem_spec] * 2,
        scratch_shapes=[
            VMEM((own_blocks * STEPS, block_rows), jnp.float32),
            VMEM((own_blocks * STEPS, block_rows), jnp.float32),
            VMEM((2, own_blocks, block_rows), jnp.float32),
        ],
        compiler_params=pltpu.CompilerParams(vmem_limit_bytes=24 << 20),
        name="window_steps",
    )(
        place,
        stim_nodes,
        stim_wave,
        *ids_by_peer,
        *sums,
        state,
        lesion.reshape(own_blocks, block_rows),
        high,
        low,
    )
    return new_coefs, final_state


def solution(mesh):
    in_specs = (
        P(("sweep", "wide", "narrow"), None, None),
        P(("sweep", "wide"), "narrow", None, None, None, None),
        P(None, ("sweep", "wide", "narrow")),
        P(("sweep", "wide", "narrow")),
        P("sweep"),
        P("sweep"),
        P("wide", "narrow", None, None),
        P("wide", "narrow", None),
        P("wide", "narrow", None),
        P("wide", "narrow", None),
        P("wide", "narrow", None),
        P("wide", "narrow", None, None, None),
    )
    out_specs = (P(("sweep", "wide", "narrow"), None, None), P(None, ("sweep", "wide", "narrow")))
    return jax.shard_map(local, mesh=mesh, in_specs=in_specs, out_specs=out_specs, check_vma=False)
```

time: 193 us -> 45.6 us (0.24)
  local copies, waits for them, and re-layouts: 101 us -> 8.58 us
  waiting for transfers between devices: 50.8 us -> 7.4 us
  starting transfers between devices: 0.08 us -> 14.4 us
  Pallas kernels: 0 us -> 13.5 us
  between operations: 14.3 us -> 0.83 us
  other arithmetic: 14 us -> 0.58 us
  matrix products: 10.9 us -> 0 us
    dynamic_update_slice x32 -> x0, local copies, waits for them, and re-layouts: 51.7 us -> none  [integrate(): lax.scan(advance, (state[0], state[1]), forcing)]
    dynamic_slice x32 -> x0, local copies, waits for them, and re-layouts: 29.4 us -> none  [integrate(): lax.scan(advance, (state[0], state[1]), forcing)]
    all_gather x1 -> x0, waiting for transfers between devices: 25.8 us -> none  [local(): lax.all_gather(fresh_coefs, 'wide', axis=0, tiled=True)]
    reduce_scatter x1 -> x0, waiting for transfers between devices: 24.3 us -> none  [local(): lax.psum_scatter(partial_sum.astype(jnp.bfloat16), 'narrow', scatter_dime...]
    ppermute x0 -> x12, starting transfers between devices: none -> 14.4 us  [swap(): return lax.ppermute(x, axis, [(i, i ^ r) for i in range(peers)])]
    pallas_call x0 -> x4, Pallas kernels: none -> 13.5 us  [the longest x1 3.91 us: local(): pl.pallas_call(functools.partial(pick_kernel, capacity=capacity, peers=wi...]
    gather x3 -> x0, local copies, waits for them, and re-layouts: 12.8 us -> none  [the longest x1 7.67 us: one_tile(): lax.dynamic_slice_in_dim(source_rows, history_length - delay_bin - 1, STE...]
    dot_general x5 -> x0, matrix products: 10.9 us -> none  [the longest x1 3.1 us: local(): jnp.einsum('bkn,km->bmn', lax.all_gather(fresh_coefs, 'wide', axis=0, til...]
  transfers between devices with their start and end apart: 2 -> 12, of which waited for: 2 -> 5; matrix products, arithmetic and copies ran while one was open for 3% -> 1% of each run, Pallas kernels for 0% -> 8%
where the time goes in v1:
time: 45.6 us; the launch traced here: 45.3 us
  starting transfers between devices  14.4 us (32%)
  Pallas kernels  13.5 us (30%)
  local copies, waits for them, and re-layouts  8.58 us (19%)
  waiting for transfers between devices  7.4 us (16%)
  between operations  0.83 us (2%)
  other arithmetic  0.58 us (1%)
    ppermute x12, starting transfers between devices, swap(): return lax.ppermute(x, axis, [(i, i ^ r) for i in range(peers)])  14.4 us
    unnamed x38, local copies, waits for them, and re-layouts  8.58 us
    ppermute x12, waiting for transfers between devices, swap(): return lax.ppermute(x, axis, [(i, i ^ r) for i in range(peers)])  7.4 us
    pallas_call x1, Pallas kernels, local(): pl.pallas_call(functools.partial(pick_kernel, capacity=capacity, peers=wi...  3.91 us
    pallas_call x1, Pallas kernels, local(): pl.pallas_call(functools.partial(list_kernel, peers=narrow_peers, own_blo...  3.46 us
    pallas_call x1, Pallas kernels, local(): pl.pallas_call(functools.partial(tract_kernel, wide_peers=wide_peers, nar...  3.2 us
    pallas_call x1, Pallas kernels, local(): pl.pallas_call(functools.partial(window_kernel, narrow_peers=narrow_peers...  2.92 us
  transfers between devices with their start and end apart: 12, of which 5 were waited for; matrix products, arithmetic and copies ran while one was open for 1% of the time, Pallas kernels for 8%

profile of v1, /device:TPU:0, one launch (start us, length us, event | category | flops | bytes accessed | tf_op | source)
XLA Modules:
  0.0 45.3 jit_solution(17093431091192154365)
XLA Ops:
  0.6 0.0 copy-start.3
  0.6 0.0 copy-start.4
  0.7 0.0 copy-start.13
  0.7 0.0 copy-start.12
  0.7 0.0 copy-start.7
  0.7 0.0 copy-start.2
  0.7 5.1 %collective-permute-start.5 = (s32[2,4]{1,0:T(2,128)}, s32[2,4]{1,0:T(2,128)S(1)}, u32[]{:S(2)}, u32[]{:S(2)}) collective-permute-start(s32[2,4]{1,0:T(2,128)} %bitcast.18), channel_id=1, source_target_pairs={{0,12},{4,8},{8,4},{12,0},{1,13},{5,9},{9,5},{13,1},{2,14},{6,10},... | collective-permute-start | bytes 104 | tf_op jit(solution)/shard_map/ppermute | solution.py:244
  5.8 0.0 collective-permute-start.4
  5.8 0.6 %collective-permute-start.3 = (s32[2,4]{1,0:T(2,128)}, s32[2,4]{1,0:T(2,128)S(1)}, u32[]{:S(2)}, u32[]{:S(2)}) collective-permute-start(s32[2,4]{1,0:T(2,128)} %bitcast.20), channel_id=1, source_target_pairs={{0,4},{4,0},{8,12},{12,8},{1,5},{5,1},{9,13},{13,9},{2,6},{6,2},{1... | collective-permute-start | bytes 104 | tf_op jit(solution)/shard_map/ppermute | solution.py:244
  6.5 0.6 %pad_add_fusion.place_ref = s32[2]{0:T(128)} fusion(s32[1]{0:T(128)} %bitcast.1, s32[1]{0:T(128)} %bitcast), kind=kLoop, calls=%fused_computation | loop fusion | flops 2 | bytes 16 | tf_op jit(solution)/shard_map/stack | solution.py:246
  7.0 0.5 %collective-permute-done.5.refs_2_ = s32[2,4]{1,0:T(2,128)S(1)} collective-permute-done((s32[2,4]{1,0:T(2,128)}, s32[2,4]{1,0:T(2,128)S(1)}, u32[]{:S(2)}, u32[]{:S(2)}) %collective-permute-start.5) | collective-permute-done | bytes 64 | tf_op jit(solution)/shard_map/ppermute | solution.py:244
  7.6 0.0 copy-start.16
  7.6 2.9 %collective-permute-done.4.refs_1_ = s32[2,4]{1,0:T(2,128)S(1)} collective-permute-done((s32[2,4]{1,0:T(2,128)}, s32[2,4]{1,0:T(2,128)S(1)}, u32[]{:S(2)}, u32[]{:S(2)}) %collective-permute-start.4) | collective-permute-done | bytes 64 | tf_op jit(solution)/shard_map/ppermute | solution.py:244
  10.5 0.0 copy-start.17
  10.5 0.0 collective-permute-done.3.refs_0_
  10.5 0.0 copy-done.16
  10.5 0.6 %copy-done.17 = s32[2,4]{1,0:T(2,128)} copy-done((s32[2,4]{1,0:T(2,128)}, s32[2,4]{1,0:T(2,128)S(1)}, u32[]{:S(2)}) %copy-start.17) | copy-done | bytes 56
  11.1 0.6 %copy-done.18 = s32[2,4]{1,0:T(2,128)} copy-done((s32[2,4]{1,0:T(2,128)}, s32[2,4]{1,0:T(2,128)S(1)}, u32[]{:S(2)}) %copy-start.18) | copy-done | bytes 56
  11.6 3.9 %pick_blocks.1 = (bf16[2,32,128]{2,1,0:T(8,128)(2,1)}, bf16[2,32,128]{2,1,0:T(8,128)(2,1)}, bf16[2,32,128]{2,1,0:T(8,128)(2,1)}, bf16[2,32,128]{2,1,0:T(8,128)(2,1)}) custom-call(s32[2]{0:T(128)} %pad_add_fusion.place_ref, s32[2,4]{1,0:T(2,128)} %bitcast.21, s32[2,4]{1,0:T(2,128)} %copy-done.18, s32[2,4]{1,0:T(2,128)} %copy-done.17, s32[2,4]{1,0:T(2,128)} %copy-done.16, ...), custom_call_target="tpu_custom_call" | custom-call | tf_op jit(solution)/shard_map/pick_blocks/pallas_call | solution.py:250
  15.6 0.1 collective-permute-start.6
  15.6 1.5 %collective-permute-start.7 = (bf16[2,32,128]{2,1,0:T(8,128)(2,1)}, bf16[2,32,128]{2,1,0:T(8,128)(2,1)S(1)}, u32[]{:S(2)}, u32[]{:S(2)}) collective-permute-start(bf16[2,32,128]{2,1,0:T(8,128)(2,1)} %get-tuple-element.16), channel_id=1, source_target_pairs={{0,8},{4,12},{8,0},{12,4},{1,9},{5,13},{9,1},{13,5},{2,10},{6,14},... | collective-permute-start | bytes 49160 | tf_op jit(solution)/shard_map/ppermute | solution.py:244
  17.2 2.9 %collective-permute-start.8 = (bf16[2,32,128]{2,1,0:T(8,128)(2,1)}, bf16[2,32,128]{2,1,0:T(8,128)(2,1)S(1)}, u32[]{:S(2)}, u32[]{:S(2)}) collective-permute-start(bf16[2,32,128]{2,1,0:T(8,128)(2,1)} %get-tuple-element.17), channel_id=1, source_target_pairs={{0,12},{4,8},{8,4},{12,0},{1,13},{5,9},{9,5},{13,1},{2,14},{6,10},... | collective-permute-start | bytes 49160 | tf_op jit(solution)/shard_map/ppermute | solution.py:244
  20.0 3.5 %list_targets.1 = (s32[1,96]{1,0:T(1,128)}, s32[1,48]{1,0:T(1,128)}) custom-call(s32[1,96]{1,0:T(1,128)} %bitcast.22), custom_call_target="tpu_custom_call" | custom-call | tf_op jit(solution)/shard_map/list_targets/pallas_call | solution.py:262
  23.5 0.0 copy-start.14
  23.5 0.0 collective-permute-done.6.refs_1_
  23.5 0.0 collective-permute-done.7.refs_2_
  23.5 0.0 collective-permute-done.8.refs_3_
  23.5 0.0 copy-start
  23.5 1.9 %copy-done = bf16[1,1,96,128,128]{4,3,2,1,0:T(8,128)(2,1)S(1)} copy-done((bf16[1,1,96,128,128]{4,3,2,1,0:T(8,128)(2,1)S(1)}, bf16[1,1,96,128,128]{4,3,2,1,0:T(8,128)(2,1)}, u32[]{:S(2)}) %copy-start) | copy-done | bytes 3145752
  25.4 0.0 copy-start.1
  25.4 0.9 %copy-done.1 = bf16[1,1,8,2,32,128]{5,4,3,2,1,0:T(8,128)(2,1)S(1)} copy-done((bf16[1,1,8,2,32,128]{5,4,3,2,1,0:T(8,128)(2,1)S(1)}, bf16[1,1,8,2,32,128]{5,4,3,2,1,0:T(8,128)(2,1)}, u32[]{:S(2)}) %copy-start.1) | copy-done | bytes 131096
  26.3 0.0 copy-start.5
  26.3 0.7 %copy-done.5 = bf16[96,96]{1,0:T(8,128)(2,1)S(1)} copy-done((bf16[96,96]{1,0:T(8,128)(2,1)S(1)}, bf16[96,96]{1,0:T(8,128)(2,1)}, u32[]{:S(2)}) %copy-start.5) | copy-done | bytes 18456
  27.1 0.0 copy-start.6
  27.1 0.7 %copy-done.6 = bf16[2,32,128]{2,1,0:T(8,128)(2,1)S(1)} copy-done((bf16[2,32,128]{2,1,0:T(8,128)(2,1)S(1)}, bf16[2,32,128]{2,1,0:T(8,128)(2,1)}, u32[]{:S(2)}) %copy-start.6) | copy-done | bytes 16408
  27.8 0.0 copy-start.8
  27.8 0.6 %copy-done.8 = s32[2]{0:T(128)S(1)} copy-done((s32[2]{0:T(128)S(1)}, s32[2]{0:T(128)}, u32[]{:S(2)}) %copy-start.8) | copy-done | bytes 32
  28.4 0.0 copy-start.9
  28.4 0.7 %copy-done.9 = s32[1,1,96]{2,1,0:T(1,128)S(1)} copy-done((s32[1,1,96]{2,1,0:T(1,128)S(1)}, s32[1,1,96]{2,1,0:T(1,128)}, u32[]{:S(2)}) %copy-start.9) | copy-done | bytes 408
  29.0 0.0 copy-start.10
  29.0 0.7 %copy-done.10 = s32[1,1,96]{2,1,0:T(1,128)S(1)} copy-done((s32[1,1,96]{2,1,0:T(1,128)S(1)}, s32[1,1,96]{2,1,0:T(1,128)}, u32[]{:S(2)}) %copy-start.10) | copy-done | bytes 408
  29.7 0.7 %copy-done.11 = f32[1,1,96]{2,1,0:T(1,128)S(1)} copy-done((f32[1,1,96]{2,1,0:T(1,128)S(1)}, f32[1,1,96]{2,1,0:T(1,128)}, u32[]{:S(2)}) %copy-start.11) | copy-done | bytes 408
  30.3 0.6 %copy-done.15 = s32[1,96]{1,0:T(1,128)S(1)} copy-done((s32[1,96]{1,0:T(1,128)S(1)}, s32[1,96]{1,0:T(1,128)}, u32[]{:S(2)}) %copy-start.15) | copy-done | bytes 408
  30.9 3.2 %tract_tiles.1 = (bf16[384,128]{1,0:T(8,128)(2,1)S(1)}, bf16[384,128]{1,0:T(8,128)(2,1)S(1)}, bf16[384,128]{1,0:T(8,128)(2,1)S(1)}, bf16[384,128]{1,0:T(8,128)(2,1)S(1)}) custom-call(s32[2]{0:T(128)S(1)} %copy-done.8, s32[1,96]{1,0:T(1,128)S(1)} %bitcast.15, s32[1,96]{1,0:T(1,128)S(1)} %bitcast.16, f32[1,96]{1,0:T(1,128)S(1)} %bitcast.17, ...), custom_call_target="tpu_custom_call" | custom-call | tf_op jit(solution)/shard_map/tract_tiles/pallas_call | solution.py:282
  34.1 0.1 collective-permute-start.9
  34.2 1.6 %collective-permute-start.10 = (bf16[384,128]{1,0:T(8,128)(2,1)S(1)}, bf16[384,128]{1,0:T(8,128)(2,1)S(1)}, u32[]{:S(2)}, u32[]{:S(2)}) collective-permute-start(bf16[384,128]{1,0:T(8,128)(2,1)S(1)} %get-tuple-element.20), channel_id=1, source_target_pairs={{0,2},{1,3},{2,0},{3,1},{4,6},{5,7},{6,4},{7,5},{8,10},{9,11},{10,... | collective-permute-start | bytes 294920 | tf_op jit(solution)/shard_map/ppermute | solution.py:244
  35.8 0.3 collective-permute-start.11
  36.1 0.0 copy-done.14
  36.1 1.4 %collective-permute-start.2 = (s32[1,48]{1,0:T(1,128)S(1)}, s32[1,48]{1,0:T(1,128)S(1)}, u32[]{:S(2)}, u32[]{:S(2)}) collective-permute-start(s32[1,48]{1,0:T(1,128)S(1)} %copy-done.14), channel_id=1, source_target_pairs={{0,3},{1,2},{2,1},{3,0},{4,7},{5,6},{6,5},{7,4},{8,11},{9,10},{10,... | collective-permute-start | bytes 584 | tf_op jit(solution)/shard_map/ppermute | solution.py:244
  37.5 0.5 %collective-permute-start.1 = (s32[1,48]{1,0:T(1,128)S(1)}, s32[1,48]{1,0:T(1,128)S(1)}, u32[]{:S(2)}, u32[]{:S(2)}) collective-permute-start(s32[1,48]{1,0:T(1,128)S(1)} %copy-done.14), channel_id=1, source_target_pairs={{0,2},{1,3},{2,0},{3,1},{4,6},{5,7},{6,4},{7,5},{8,10},{9,11},{10,... | collective-permute-start | bytes 584 | tf_op jit(solution)/shard_map/ppermute | solution.py:244
  38.1 3.1 %collective-permute-done.2.refs_3_ = s32[1,48]{1,0:T(1,128)S(1)} collective-permute-done((s32[1,48]{1,0:T(1,128)S(1)}, s32[1,48]{1,0:T(1,128)S(1)}, u32[]{:S(2)}, u32[]{:S(2)}) %collective-permute-start.2) | collective-permute-done | bytes 224 | tf_op jit(solution)/shard_map/ppermute | solution.py:244
  41.2 0.3 collective-permute-start
  41.4 0.1 collective-permute-done.1.refs_2_
  41.5 0.7 %collective-permute-done.refs_1_ = s32[1,48]{1,0:T(1,128)S(1)} collective-permute-done((s32[1,48]{1,0:T(1,128)S(1)}, s32[1,48]{1,0:T(1,128)S(1)}, u32[]{:S(2)}, u32[]{:S(2)}) %collective-permute-start) | collective-permute-done | bytes 224 | tf_op jit(solution)/shard_map/ppermute | solution.py:244
  42.3 0.0 collective-permute-done.9.refs_5_
  42.3 0.0 collective-permute-done.10.refs_6_
  42.3 0.0 collective-permute-done.11.refs_7_
  42.3 0.0 copy-done.3
  42.3 0.0 copy-done.4
  42.3 0.0 copy-done.13
  42.3 0.0 copy-done.12
  42.3 0.0 copy-done.7
  42.3 0.0 copy-done.2
  42.3 2.9 %window_steps.1 = (bf16[32,32,128]{2,1,0:T(8,128)(2,1)}, f32[2,4096]{1,0:T(2,128)}) custom-call(s32[2]{0:T(128)S(1)} %copy-done.8, s32[64]{0:T(128)S(1)} %copy-done.12, f32[32]{0:T(128)S(1)} %copy-done.13, s32[1,48]{1,0:T(1,128)S(1)} %copy-done.14, s32[1,48]{1,0:T(1,128)S(1)} %collective-permute-done.refs_1_, s32[1,48]{1,0:T(1,128)S(1)} %collective-permute-done.1.refs_2_, ...), custom_call_target="tpu_custom_call" | custom-call | tf_op jit(solution)/shard_map/window_steps/pallas_call | solution.py:316
  (3 shorter events, 0.0 us)
Async XLA Ops:
  0.6 41.7 %copy-start.3 = (bf16[128,128]{1,0:T(8,128)(2,1)S(1)}, bf16[128,128]{1,0:T(8,128)(2,1)}, u32[]{:S(2)}) copy-start(bf16[128,128]{1,0:T(8,128)(2,1)} %constant.15.clone.refs_11_) | copy-start | bytes 98308
  0.6 41.7 %copy-start.4 = (bf16[128,128]{1,0:T(8,128)(2,1)S(1)}, bf16[128,128]{1,0:T(8,128)(2,1)}, u32[]{:S(2)}) copy-start(bf16[128,128]{1,0:T(8,128)(2,1)} %constant.14.clone.refs_10_) | copy-start | bytes 98308
  0.7 41.7 %copy-start.13 = (f32[32]{0:T(128)S(1)}, f32[32]{0:T(128)}, u32[]{:S(2)}) copy-start(f32[32]{0:T(128)} %wave_ref.1) | copy-start | bytes 388
  0.7 41.7 %copy-start.12 = (s32[64]{0:T(128)S(1)}, s32[64]{0:T(128)}, u32[]{:S(2)}) copy-start(s32[64]{0:T(128)} %stim_ref.1) | copy-start | bytes 772
  0.7 41.7 %copy-start.7 = (s32[4096]{0:T(1024)S(1)}, s32[4096]{0:T(1024)}, u32[]{:S(2)}) copy-start(s32[4096]{0:T(1024)} %param.18) | copy-start | bytes 49156
  0.7 41.7 %copy-start.2 = (f32[2,4096]{1,0:T(2,128)S(1)}, f32[2,4096]{1,0:T(2,128)}, u32[]{:S(2)}) copy-start(f32[2,4096]{1,0:T(2,128)} %refs_8_.1) | copy-start | bytes 98308
  0.7 6.9 %collective-permute-start.5 = (s32[2,4]{1,0:T(2,128)}, s32[2,4]{1,0:T(2,128)S(1)}, u32[]{:S(2)}, u32[]{:S(2)}) collective-permute-start(s32[2,4]{1,0:T(2,128)} %bitcast.18), channel_id=1, source_target_pairs={{0,12},{4,8},{8,4},{12,0},{1,13},{5,9},{9,5},{13,1},{2,14},{6,10},... | collective-permute-start | bytes 104 | tf_op jit(solution)/shard_map/ppermute | solution.py:244
  5.8 4.7 %collective-permute-start.4 = (s32[2,4]{1,0:T(2,128)}, s32[2,4]{1,0:T(2,128)S(1)}, u32[]{:S(2)}, u32[]{:S(2)}) collective-permute-start(s32[2,4]{1,0:T(2,128)} %bitcast.19), channel_id=1, source_target_pairs={{0,8},{4,12},{8,0},{12,4},{1,9},{5,13},{9,1},{13,5},{2,10},{6,14},... | collective-permute-start | bytes 104 | tf_op jit(solution)/shard_map/ppermute | solution.py:244
  5.8 4.7 %collective-permute-start.3 = (s32[2,4]{1,0:T(2,128)}, s32[2,4]{1,0:T(2,128)S(1)}, u32[]{:S(2)}, u32[]{:S(2)}) collective-permute-start(s32[2,4]{1,0:T(2,128)} %bitcast.20), channel_id=1, source_target_pairs={{0,4},{4,0},{8,12},{12,8},{1,5},{5,1},{9,13},{13,9},{2,6},{6,2},{1... | collective-permute-start | bytes 104 | tf_op jit(solution)/shard_map/ppermute | solution.py:244
  7.6 2.9 %copy-start.16 = (s32[2,4]{1,0:T(2,128)}, s32[2,4]{1,0:T(2,128)S(1)}, u32[]{:S(2)}) copy-start(s32[2,4]{1,0:T(2,128)S(1)} %collective-permute-done.5.refs_2_) | copy-start | bytes 100
  10.5 0.6 %copy-start.17 = (s32[2,4]{1,0:T(2,128)}, s32[2,4]{1,0:T(2,128)S(1)}, u32[]{:S(2)}) copy-start(s32[2,4]{1,0:T(2,128)S(1)} %collective-permute-done.4.refs_1_) | copy-start | bytes 100
  11.1 0.6 %copy-start.18 = (s32[2,4]{1,0:T(2,128)}, s32[2,4]{1,0:T(2,128)S(1)}, u32[]{:S(2)}) copy-start(s32[2,4]{1,0:T(2,128)S(1)} %collective-permute-done.3.refs_0_) | copy-start | bytes 100
  15.6 7.9 %collective-permute-start.6 = (bf16[2,32,128]{2,1,0:T(8,128)(2,1)}, bf16[2,32,128]{2,1,0:T(8,128)(2,1)S(1)}, u32[]{:S(2)}, u32[]{:S(2)}) collective-permute-start(bf16[2,32,128]{2,1,0:T(8,128)(2,1)} %get-tuple-element.15), channel_id=1, source_target_pairs={{0,4},{4,0},{8,12},{12,8},{1,5},{5,1},{9,13},{13,9},{2,6},{6,2},{1... | collective-permute-start | bytes 49160 | tf_op jit(solution)/shard_map/ppermute | solution.py:244
  15.6 7.9 %collective-permute-start.7 = (bf16[2,32,128]{2,1,0:T(8,128)(2,1)}, bf16[2,32,128]{2,1,0:T(8,128)(2,1)S(1)}, u32[]{:S(2)}, u32[]{:S(2)}) collective-permute-start(bf16[2,32,128]{2,1,0:T(8,128)(2,1)} %get-tuple-element.16), channel_id=1, source_target_pairs={{0,8},{4,12},{8,0},{12,4},{1,9},{5,13},{9,1},{13,5},{2,10},{6,14},... | collective-permute-start | bytes 49160 | tf_op jit(solution)/shard_map/ppermute | solution.py:244
  17.2 6.4 %collective-permute-start.8 = (bf16[2,32,128]{2,1,0:T(8,128)(2,1)}, bf16[2,32,128]{2,1,0:T(8,128)(2,1)S(1)}, u32[]{:S(2)}, u32[]{:S(2)}) collective-permute-start(bf16[2,32,128]{2,1,0:T(8,128)(2,1)} %get-tuple-element.17), channel_id=1, source_target_pairs={{0,12},{4,8},{8,4},{12,0},{1,13},{5,9},{9,5},{13,1},{2,14},{6,10},... | collective-permute-start | bytes 49160 | tf_op jit(solution)/shard_map/ppermute | solution.py:244
  23.5 12.6 %copy-start.14 = (s32[1,48]{1,0:T(1,128)S(1)}, s32[1,48]{1,0:T(1,128)}, u32[]{:S(2)}) copy-start(s32[1,48]{1,0:T(1,128)} %get-tuple-element.12.refs_0_) | copy-start | bytes 580
  23.5 1.9 %copy-start = (bf16[1,1,96,128,128]{4,3,2,1,0:T(8,128)(2,1)S(1)}, bf16[1,1,96,128,128]{4,3,2,1,0:T(8,128)(2,1)}, u32[]{:S(2)}) copy-start(bf16[1,1,96,128,128]{4,3,2,1,0:T(8,128)(2,1)} %param.26) | copy-start | bytes 9437188
  25.4 0.9 %copy-start.1 = (bf16[1,1,8,2,32,128]{5,4,3,2,1,0:T(8,128)(2,1)S(1)}, bf16[1,1,8,2,32,128]{5,4,3,2,1,0:T(8,128)(2,1)}, u32[]{:S(2)}) copy-start(bf16[1,1,8,2,32,128]{5,4,3,2,1,0:T(8,128)(2,1)} %param.16) | copy-start | bytes 393220
  26.3 0.7 %copy-start.5 = (bf16[96,96]{1,0:T(8,128)(2,1)S(1)}, bf16[96,96]{1,0:T(8,128)(2,1)}, u32[]{:S(2)}) copy-start(bf16[96,96]{1,0:T(8,128)(2,1)} %constant.13.clone.table_ref) | copy-start | bytes 55300
  27.1 0.7 %copy-start.6 = (bf16[2,32,128]{2,1,0:T(8,128)(2,1)S(1)}, bf16[2,32,128]{2,1,0:T(8,128)(2,1)}, u32[]{:S(2)}) copy-start(bf16[2,32,128]{2,1,0:T(8,128)(2,1)} %get-tuple-element.14.refs_0_) | copy-start | bytes 49156
  27.8 0.6 %copy-start.8 = (s32[2]{0:T(128)S(1)}, s32[2]{0:T(128)}, u32[]{:S(2)}) copy-start(s32[2]{0:T(128)} %pad_add_fusion.place_ref) | copy-start | bytes 28
  28.4 0.7 %copy-start.9 = (s32[1,1,96]{2,1,0:T(1,128)S(1)}, s32[1,1,96]{2,1,0:T(1,128)}, u32[]{:S(2)}) copy-start(s32[1,1,96]{2,1,0:T(1,128)} %param.22) | copy-start | bytes 1156
  29.0 0.7 %copy-start.10 = (s32[1,1,96]{2,1,0:T(1,128)S(1)}, s32[1,1,96]{2,1,0:T(1,128)}, u32[]{:S(2)}) copy-start(s32[1,1,96]{2,1,0:T(1,128)} %param.24) | copy-start | bytes 1156
  29.7 0.7 %copy-start.11 = (f32[1,1,96]{2,1,0:T(1,128)S(1)}, f32[1,1,96]{2,1,0:T(1,128)}, u32[]{:S(2)}) copy-start(f32[1,1,96]{2,1,0:T(1,128)} %param.25) | copy-start | bytes 1156
  30.3 0.6 %copy-start.15 = (s32[1,96]{1,0:T(1,128)S(1)}, s32[1,96]{1,0:T(1,128)}, u32[]{:S(2)}) copy-start(s32[1,96]{1,0:T(1,128)} %get-tuple-element.13.compact_ref) | copy-start | bytes 1156
  34.1 8.1 %collective-permute-start.9 = (bf16[384,128]{1,0:T(8,128)(2,1)S(1)}, bf16[384,128]{1,0:T(8,128)(2,1)S(1)}, u32[]{:S(2)}, u32[]{:S(2)}) collective-permute-start(bf16[384,128]{1,0:T(8,128)(2,1)S(1)} %get-tuple-element.19), channel_id=1, source_target_pairs={{0,1},{1,0},{2,3},{3,2},{4,5},{5,4},{6,7},{7,6},{8,9},{9,8},{10,11... | collective-permute-start | bytes 294920 | tf_op jit(solution)/shard_map/ppermute | solution.py:244
  34.2 8.1 %collective-permute-start.10 = (bf16[384,128]{1,0:T(8,128)(2,1)S(1)}, bf16[384,128]{1,0:T(8,128)(2,1)S(1)}, u32[]{:S(2)}, u32[]{:S(2)}) collective-permute-start(bf16[384,128]{1,0:T(8,128)(2,1)S(1)} %get-tuple-element.20), channel_id=1, source_target_pairs={{0,2},{1,3},{2,0},{3,1},{4,6},{5,7},{6,4},{7,5},{8,10},{9,11},{10,... | collective-permute-start | bytes 294920 | tf_op jit(solution)/shard_map/ppermute | solution.py:244
  35.8 6.5 %collective-permute-start.11 = (bf16[384,128]{1,0:T(8,128)(2,1)S(1)}, bf16[384,128]{1,0:T(8,128)(2,1)S(1)}, u32[]{:S(2)}, u32[]{:S(2)}) collective-permute-start(bf16[384,128]{1,0:T(8,128)(2,1)S(1)} %get-tuple-element.21), channel_id=1, source_target_pairs={{0,3},{1,2},{2,1},{3,0},{4,7},{5,6},{6,5},{7,4},{8,11},{9,10},{10,... | collective-permute-start | bytes 294920 | tf_op jit(solution)/shard_map/ppermute | solution.py:244
  36.1 5.1 %collective-permute-start.2 = (s32[1,48]{1,0:T(1,128)S(1)}, s32[1,48]{1,0:T(1,128)S(1)}, u32[]{:S(2)}, u32[]{:S(2)}) collective-permute-start(s32[1,48]{1,0:T(1,128)S(1)} %copy-done.14), channel_id=1, source_target_pairs={{0,3},{1,2},{2,1},{3,0},{4,7},{5,6},{6,5},{7,4},{8,11},{9,10},{10,... | collective-permute-start | bytes 584 | tf_op jit(solution)/shard_map/ppermute | solution.py:244
  37.5 4.0 %collective-permute-start.1 = (s32[1,48]{1,0:T(1,128)S(1)}, s32[1,48]{1,0:T(1,128)S(1)}, u32[]{:S(2)}, u32[]{:S(2)}) collective-permute-start(s32[1,48]{1,0:T(1,128)S(1)} %copy-done.14), channel_id=1, source_target_pairs={{0,2},{1,3},{2,0},{3,1},{4,6},{5,7},{6,4},{7,5},{8,10},{9,11},{10,... | collective-permute-start | bytes 584 | tf_op jit(solution)/shard_map/ppermute | solution.py:244
  41.2 1.1 %collective-permute-start = (s32[1,48]{1,0:T(1,128)S(1)}, s32[1,48]{1,0:T(1,128)S(1)}, u32[]{:S(2)}, u32[]{:S(2)}) collective-permute-start(s32[1,48]{1,0:T(1,128)S(1)} %copy-done.14), channel_id=1, source_target_pairs={{0,1},{1,0},{2,3},{3,2},{4,5},{5,4},{6,7},{7,6},{8,9},{9,8},{10,11... | collective-permute-start | bytes 584 | tf_op jit(solution)/shard_map/ppermute | solution.py:244

commit v2 on v1

v2 whole, which is shorter than its diff:
```python
import functools
import math

import jax
import jax.numpy as jnp
import ml_dtypes
import numpy as np
from jax import lax
from jax.experimental import pallas as pl
from jax.experimental.pallas import tpu as pltpu
from jax.sharding import PartitionSpec as P

STEPS = 32
HSEG = 2
SEGS = HSEG + 1
LENGTH = SEGS * STEPS
GROUP = 4
HEAD = 16
UNROLL = 16

excite_rate = 0.1
inhibit_rate = 0.05
excite_excite = 1.5
inhibit_excite = 2.0
excite_inhibit = 2.0
inhibit_inhibit = 0.5
excite_offset = 0.5
inhibit_offset = 0.5
tract_gain = 2.0

SMEM = pltpu.SMEM
VMEM = pltpu.VMEM
smem_spec = pl.BlockSpec(memory_space=SMEM)
vmem_spec = pl.BlockSpec(memory_space=VMEM)
hbm_spec = pl.BlockSpec(memory_space=pltpu.HBM)


def basis_table(coef_count, step_count):
    order = np.arange(coef_count, dtype=np.float32)[:, None]
    places = np.arange(step_count, dtype=np.float32)[None, :]
    angles = np.float32(np.pi) * (step_count - places - np.float32(0.5)) / np.float32(step_count)
    return np.cos((order * angles).astype(np.float64)).astype(np.float32)


def expand_table(coef_count):
    basis = basis_table(coef_count, STEPS).astype(ml_dtypes.bfloat16)
    table = np.zeros((LENGTH, SEGS * coef_count), ml_dtypes.bfloat16)
    for seg in range(SEGS):
        table[seg * STEPS : (seg + 1) * STEPS, seg * coef_count : (seg + 1) * coef_count] = basis.T
    return table


def fit_tables(coef_count):
    scales = np.where(np.arange(coef_count)[:, None] == 0, 1.0, 2.0) / STEPS
    fit = (basis_table(coef_count, STEPS) * scales).astype(np.float32)
    whole = np.zeros((GROUP * coef_count, GROUP * STEPS), np.float32)
    for g in range(GROUP):
        whole[g * coef_count : (g + 1) * coef_count, g * STEPS : (g + 1) * STEPS] = fit
    high = whole.astype(ml_dtypes.bfloat16)
    low = (whole - high.astype(np.float32)).astype(ml_dtypes.bfloat16)
    return high, low


def steps_together(peer_targets):
    return 16 // math.gcd(16, peer_targets)


def lane_tables(peers, peer_targets, own_blocks):
    together = steps_together(peer_targets)
    width = together * peer_targets
    assert together * own_blocks <= 256 and peers * width <= HEAD * 128
    lane = np.arange(HEAD * 128)
    used = lane < peers * width
    within = lane % width
    rank = np.where(used, within % peer_targets, -5)
    offset = within // peer_targets * own_blocks + 1
    place = np.where(used, lane // width, -5)
    return np.stack([rank, offset, place]).astype(np.float32).reshape(3, HEAD, 128)


def pick_kernel(asked_ref, fresh_ref, out_ref, asked, asked_sem, sems, *, capacity, peers):
    asked_copy = pltpu.make_async_copy(asked_ref, asked, asked_sem)
    asked_copy.start()
    asked_copy.wait()
    copies = [
        pltpu.make_async_copy(
            fresh_ref.at[jnp.maximum(asked[reader, c], 0)],
            out_ref.at[reader, c],
            sems.at[reader, c],
        )
        for reader in range(peers)
        for c in range(capacity)
    ]
    for copy in copies:
        copy.start()
    for copy in copies:
        copy.wait()


def list_kernel(
    place_ref, target_ref, lanes_ref, rows_ref, head_ref, *, peers, own_blocks, peer_targets
):
    place = place_ref[1].astype(jnp.float32)
    shape = (own_blocks, 128)
    block = lax.broadcasted_iota(jnp.int32, shape, 0)
    peer = lax.broadcasted_iota(jnp.int32, shape, 1)
    number = peer * own_blocks + block
    present = number == target_ref[0, 0]
    for t in range(1, target_ref.shape[1]):
        present = present | (number == target_ref[0, t])
    below = (
        lax.broadcasted_iota(jnp.int32, (own_blocks, own_blocks), 0)
        > lax.broadcasted_iota(jnp.int32, (own_blocks, own_blocks), 1)
    ).astype(jnp.float32).astype(jnp.bfloat16)
    held = present.astype(jnp.float32)
    rank = jnp.dot(below, held.astype(jnp.bfloat16), preferred_element_type=jnp.float32)
    rows_ref[...] = peer * (peer_targets * STEPS) + rank.astype(jnp.int32)
    rank = jnp.where(present, rank, -1.0)
    block = block.astype(jnp.float32)
    for p in range(peers):
        column = jnp.broadcast_to(rank[:, p : p + 1], shape)
        head_ref[p] = jnp.zeros((HEAD, 128), jnp.float32)
        for h in range(pl.cdiv(peers * steps_together(peer_targets) * peer_targets, 128)):
            match = column == lanes_ref[0, h : h + 1, :]
            ids = jnp.sum(jnp.where(match, block, 0.0), axis=0, keepdims=True)
            mine = lanes_ref[2, h : h + 1, :] == place
            head_ref[p, h : h + 1, :] = jnp.where(mine, ids + lanes_ref[1, h : h + 1, :], 0.0)


def tract_kernel(
    slot_hbm, target_hbm, delay_hbm, frac_hbm, rows_ref, head_ref, table_ref, older_hbm,
    weights_hbm, news_ref, out_ref,
    slot, target, delay, frac, rows, older, weights, hist, total, small_sem, older_sem, sems,
    *, peers, own_blocks, peer_targets,
):
    tile_count = slot_hbm.shape[1]
    slot_count = older.shape[0]
    turns = tile_count // UNROLL
    copies = [
        pltpu.make_async_copy(source, into, small_sem.at[i])
        for i, (source, into) in enumerate(
            [(slot_hbm, slot), (target_hbm, target), (delay_hbm, delay), (frac_hbm, frac),
             (rows_ref, rows)]
        )
    ]
    older_copy = pltpu.make_async_copy(older_hbm, older, older_sem)
    older_copy.start()
    for copy in copies:
        copy.start()

    def weights_copy(turn):
        part = pl.ds(turn * UNROLL, UNROLL)
        return pltpu.make_async_copy(weights_hbm.at[part], weights.at[part], sems.at[turn])

    for turn in range(turns):
        weights_copy(turn).start()
    total[...] = jnp.zeros_like(total)
    older_copy.wait()
    table = table_ref[...]
    for s in range(slot_count):
        segments = [older[s, h] for h in range(HSEG - 1, -1, -1)] + [news_ref[s]]
        values = jnp.dot(
            table, jnp.concatenate(segments, axis=0), preferred_element_type=jnp.float32
        )
        hist[s * LENGTH : (s + 1) * LENGTH, :] = values
    for copy in copies:
        copy.wait()

    @pl.loop(0, turns)
    def _(turn):
        weights_copy(turn).wait()
        sums = []
        for u in range(UNROLL):
            t = turn * UNROLL + u
            fraction = frac[0, t]
            start = slot[0, t] * LENGTH + LENGTH - 1 - delay[0, t]
            earlier = hist[pl.ds(start, STEPS), :]
            later = hist[pl.ds(start + 1, STEPS), :]
            delayed = ((1.0 - fraction) * later + fraction * earlier).astype(jnp.bfloat16)
            sums.append(
                lax.dot_general(
                    delayed, weights[t], (((1,), (1,)), ((), ())),
                    preferred_element_type=jnp.float32,
                )
            )
        for u in range(UNROLL):
            aim = target[0, turn * UNROLL + u]
            first = rows[lax.rem(aim, own_blocks), lax.div(aim, own_blocks)]
            where = pl.ds(first, STEPS, stride=peer_targets)
            total[where, :] += sums[u]

    span = peer_targets * STEPS
    for p in range(peers):
        out_ref[p, :span, :] = total[p * span : (p + 1) * span, :].astype(jnp.bfloat16)
        out_ref[p, span:, :] = head_ref[p].astype(jnp.bfloat16)


def window_kernel(
    place_ref, stim_ref, wave_ref, shares_ref, state_ref, lesion_ref, high_ref, low_ref,
    coefs_out, state_out, samples, rates,
    *, peers, own_blocks, peer_targets, coef_count,
):
    block_rows = lesion_ref.shape[1]
    first_node = (place_ref[0] * peers + place_ref[1]) * (own_blocks * block_rows)
    together = steps_together(peer_targets)
    width = together * peer_targets
    span = peer_targets * STEPS

    head = shares_ref[0, span:, :].astype(jnp.float32)
    for p in range(1, peers):
        head = head + shares_ref[p, span:, :].astype(jnp.float32)
    row = lax.broadcasted_iota(jnp.int32, (together * own_blocks, 128), 0).astype(jnp.float32) + 1.0
    columns = peers * width
    scatter = jnp.concatenate(
        [
            jnp.where(row == head[h : h + 1, :], 1.0, 0.0).astype(jnp.bfloat16)
            for h in range(pl.cdiv(columns, 128))
        ],
        axis=1,
    )[:, :columns]

    for b in range(own_blocks):
        piece = state_ref[:, b * block_rows : (b + 1) * block_rows]
        rates[0, b : b + 1, :] = piece[0:1, :]
        rates[1, b : b + 1, :] = piece[1:2, :]

    shape = (own_blocks, block_rows)
    nodes = (
        first_node
        + lax.broadcasted_iota(jnp.int32, shape, 0) * block_rows
        + lax.broadcasted_iota(jnp.int32, shape, 1)
    )
    counts = jnp.zeros(shape, jnp.float32)
    for n in range(stim_ref.shape[0]):
        counts = counts + jnp.where(nodes == stim_ref[n], 1.0, 0.0)
    gain = tract_gain * (1.0 - lesion_ref[...].astype(jnp.float32))
    excite = rates[0]
    inhibit = rates[1]
    for g in range(STEPS // together):
        arrived = jnp.concatenate(
            [shares_ref[p, g * width : (g + 1) * width, :] for p in range(peers)], axis=0
        )
        inflow = jnp.dot(scatter, arrived, preferred_element_type=jnp.float32)
        for jj in range(together):
            j = g * together + jj
            forcing = gain * inflow[jj * own_blocks : (jj + 1) * own_blocks] + wave_ref[j] * counts
            excite_drive = (
                excite_excite * excite - inhibit_excite * inhibit + forcing - excite_offset
            )
            inhibit_drive = excite_inhibit * excite - inhibit_inhibit * inhibit - inhibit_offset
            excite, inhibit = (
                excite + excite_rate * (0.5 * jnp.tanh(0.5 * excite_drive) + 0.5 - excite),
                inhibit + inhibit_rate * (0.5 * jnp.tanh(0.5 * inhibit_drive) + 0.5 - inhibit),
            )
            samples[pl.ds(j, own_blocks, stride=STEPS), :] = excite
    rates[0] = excite
    rates[1] = inhibit
    for b in range(own_blocks):
        where = slice(b * block_rows, (b + 1) * block_rows)
        state_out[0:1, where] = rates[0, b : b + 1, :]
        state_out[1:2, where] = rates[1, b : b + 1, :]

    high = high_ref[...]
    low = low_ref[...]
    rows = GROUP * STEPS
    for g in range(own_blocks // GROUP):
        part = samples[g * rows : (g + 1) * rows, :]
        part_high = part.astype(jnp.bfloat16)
        part_low = (part - part_high.astype(jnp.float32)).astype(jnp.bfloat16)
        fitted = (
            jnp.dot(high, part_high, preferred_element_type=jnp.float32)
            + jnp.dot(high, part_low, preferred_element_type=jnp.float32)
            + jnp.dot(low, part_high, preferred_element_type=jnp.float32)
        )
        coefs_out[g * GROUP : (g + 1) * GROUP] = fitted.astype(jnp.bfloat16).reshape(
            GROUP, coef_count, block_rows
        )


def local(
    fresh_coefs,
    older_coefs,
    state,
    lesion,
    stim_nodes,
    stim_wave,
    read_blocks,
    tract_slot,
    tract_target,
    tract_delay,
    tract_frac,
    tract_weights,
):
    wide_peers = lax.axis_size("wide")
    peers = lax.axis_size("narrow")
    own_blocks, coef_count, block_rows = fresh_coefs.shape
    capacity = read_blocks.shape[3]
    slot_count = wide_peers * capacity
    tile_count = tract_slot.shape[2]
    peer_targets = tile_count // (2 * peers)
    share_rows = peer_targets * STEPS + HEAD

    place = jnp.stack([lax.axis_index("wide"), lax.axis_index("narrow")]).astype(jnp.int32)
    asked = lax.all_to_all(
        read_blocks.reshape(wide_peers, capacity), "wide", 0, 0, tiled=True
    )
    picked = pl.pallas_call(
        functools.partial(pick_kernel, capacity=capacity, peers=wide_peers),
        out_shape=jax.ShapeDtypeStruct(
            (wide_peers, capacity, coef_count, block_rows), jnp.bfloat16
        ),
        in_specs=[hbm_spec] * 2,
        out_specs=hbm_spec,
        scratch_shapes=[
            SMEM((wide_peers, capacity), jnp.int32),
            pltpu.SemaphoreType.DMA,
            pltpu.SemaphoreType.DMA((wide_peers, capacity)),
        ],
        compiler_params=pltpu.CompilerParams(vmem_limit_bytes=60 << 20),
        name="pick_blocks",
    )(asked, fresh_coefs)
    news = lax.all_to_all(picked, "wide", 0, 0, tiled=True)

    targets = tract_target.reshape(1, tile_count)
    rows, heads = pl.pallas_call(
        functools.partial(
            list_kernel, peers=peers, own_blocks=own_blocks, peer_targets=peer_targets
        ),
        out_shape=[
            jax.ShapeDtypeStruct((own_blocks, 128), jnp.int32),
            jax.ShapeDtypeStruct((peers, HEAD, 128), jnp.float32),
        ],
        in_specs=[smem_spec] * 2 + [vmem_spec],
        out_specs=[vmem_spec] * 2,
        compiler_params=pltpu.CompilerParams(vmem_limit_bytes=60 << 20),
        name="list_targets",
    )(place, targets, lane_tables(peers, peer_targets, own_blocks))

    shares = pl.pallas_call(
        functools.partial(
            tract_kernel, peers=peers, own_blocks=own_blocks, peer_targets=peer_targets
        ),
        out_shape=jax.ShapeDtypeStruct((peers, share_rows, block_rows), jnp.bfloat16),
        in_specs=[hbm_spec] * 5 + [vmem_spec] * 2 + [hbm_spec] * 2 + [vmem_spec],
        out_specs=vmem_spec,
        scratch_shapes=[
            SMEM((1, tile_count), jnp.int32),
            SMEM((1, tile_count), jnp.int32),
            SMEM((1, tile_count), jnp.int32),
            SMEM((1, tile_count), jnp.float32),
            SMEM((own_blocks, 128), jnp.int32),
            VMEM((slot_count, HSEG, coef_count, block_rows), jnp.bfloat16),
            VMEM((tile_count, block_rows, block_rows), jnp.bfloat16),
            VMEM((slot_count * LENGTH, block_rows), jnp.float32),
            VMEM((peers * peer_targets * STEPS, block_rows), jnp.float32),
            pltpu.SemaphoreType.DMA((5,)),
            pltpu.SemaphoreType.DMA,
            pltpu.SemaphoreType.DMA((tile_count // UNROLL,)),
        ],
        compiler_params=pltpu.CompilerParams(vmem_limit_bytes=60 << 20),
        name="tract_tiles",
    )(
        tract_slot.reshape(1, tile_count),
        targets,
        tract_delay.reshape(1, tile_count),
        tract_frac.reshape(1, tile_count),
        rows,
        heads,
        expand_table(coef_count),
        older_coefs.reshape(slot_count, HSEG, coef_count, block_rows),
        tract_weights.reshape(tile_count, block_rows, block_rows),
        news.reshape(slot_count, coef_count, block_rows),
    )
    arrived = lax.all_to_all(shares, "narrow", 0, 0, tiled=True)

    high, low = fit_tables(coef_count)
    new_coefs, final_state = pl.pallas_call(
        functools.partial(
            window_kernel,
            peers=peers,
            own_blocks=own_blocks,
            peer_targets=peer_targets,
            coef_count=coef_count,
        ),
        out_shape=[
            jax.ShapeDtypeStruct(fresh_coefs.shape, jnp.bfloat16),
            jax.ShapeDtypeStruct(state.shape, jnp.float32),
        ],
        in_specs=[smem_spec] * 3 + [vmem_spec] * 5,
        out_specs=[vmem_spec] * 2,
        scratch_shapes=[
            VMEM((own_blocks * STEPS, block_rows), jnp.float32),
            VMEM((2, own_blocks, block_rows), jnp.float32),
        ],
        compiler_params=pltpu.CompilerParams(vmem_limit_bytes=16 << 20),
        name="window_steps",
    )(
        place,
        stim_nodes,
        stim_wave,
        arrived,
        state,
        lesion.reshape(own_blocks, block_rows),
        high,
        low,
    )
    return new_coefs, final_state


def solution(mesh):
    in_specs = (
        P(("sweep", "wide", "narrow"), None, None),
        P(("sweep", "wide"), "narrow", None, None, None, None),
        P(None, ("sweep", "wide", "narrow")),
        P(("sweep", "wide", "narrow")),
        P("sweep"),
        P("sweep"),
        P("wide", "narrow", None, None),
        P("wide", "narrow", None),
        P("wide", "narrow", None),
        P("wide", "narrow", None),
        P("wide", "narrow", None),
        P("wide", "narrow", None, None, None),
    )
    out_specs = (P(("sweep", "wide", "narrow"), None, None), P(None, ("sweep", "wide", "narrow")))
    return jax.shard_map(local, mesh=mesh, in_specs=in_specs, out_specs=out_specs, check_vma=False)
```

time: 45.6 us -> 48.3 us (1.059)
  blocking collectives: 0 us -> 11.1 us
  local copies, waits for them, and re-layouts: 8.58 us -> 2.61 us
  starting transfers between devices: 14.4 us -> 9.61 us
  waiting for transfers between devices: 7.4 us -> 8.79 us
  Pallas kernels: 13.5 us -> 14.3 us
    ppermute x12 -> x0, starting transfers between devices: 14.4 us -> none  [swap(): return lax.ppermute(x, axis, [(i, i ^ r) for i in range(peers)])]
    all_to_all x0 -> x1, blocking collectives: none -> 11.1 us  [local(): arrived = lax.all_to_all(shares, 'narrow', 0, 0, tiled=True)]
    all_to_all x0 -> x2, starting transfers between devices: none -> 9.61 us  [the longest x1 6.32 us: local(): lax.all_to_all(read_blocks.reshape(wide_peers, capacity), 'wide', 0, 0, t...]
    all_to_all x0 -> x2, waiting for transfers between devices: none -> 8.79 us  [the longest x1 5.47 us: local(): lax.all_to_all(read_blocks.reshape(wide_peers, capacity), 'wide', 0, 0, t...]
    ppermute x12 -> x0, waiting for transfers between devices: 7.4 us -> none  [swap(): return lax.ppermute(x, axis, [(i, i ^ r) for i in range(peers)])]
    unnamed x38 -> x18, local copies, waits for them, and re-layouts: 8.58 us -> 1.24 us
    all_to_all x0 -> x1, local copies, waits for them, and re-layouts: none -> 1.37 us  [local(): lax.all_to_all(read_blocks.reshape(wide_peers, capacity), 'wide', 0, 0, t...]
    pallas_call x3, Pallas kernels: 9.58 us -> 10.5 us  [the longest x1 6.1 us: local(): pl.pallas_call(functools.partial(tract_kernel, peers=peers, own_blocks=ow...]
  transfers between devices with their start and end apart: 12 -> 2, of which waited for: 5 -> 2; matrix products, arithmetic and copies ran while one was open for 1% -> 1% of each run, Pallas kernels for 8% -> 4%
where the time goes in v2:
time: 48.3 us; the launch traced here: 47.8 us
  Pallas kernels  14.3 us (30%)
  blocking collectives  11.1 us (23%)
  starting transfers between devices  9.61 us (20%)
  waiting for transfers between devices  8.79 us (18%)
  local copies, waits for them, and re-layouts  2.61 us (5%)
  between operations  0.74 us (2%)
  other arithmetic  0.6 us (1%)
    all_to_all x1, blocking collectives, local(): arrived = lax.all_to_all(shares, 'narrow', 0, 0, tiled=True)  11.1 us
    all_to_all x1, starting transfers between devices, local(): lax.all_to_all(read_blocks.reshape(wide_peers, capacity), 'wide', 0, 0, t...  6.32 us
    pallas_call x1, Pallas kernels, local(): pl.pallas_call(functools.partial(tract_kernel, peers=peers, own_blocks=ow...  6.1 us
    all_to_all x1, waiting for transfers between devices, local(): lax.all_to_all(read_blocks.reshape(wide_peers, capacity), 'wide', 0, 0, t...  5.47 us
    pallas_call x1, Pallas kernels, local(): pl.pallas_call(functools.partial(pick_kernel, capacity=capacity, peers=wi...  3.86 us
    all_to_all x1, waiting for transfers between devices, local(): news = lax.all_to_all(picked, 'wide', 0, 0, tiled=True)  3.32 us
    all_to_all x1, starting transfers between devices, local(): news = lax.all_to_all(picked, 'wide', 0, 0, tiled=True)  3.3 us
    pallas_call x1, Pallas kernels, local(): pl.pallas_call(functools.partial(window_kernel, peers=peers, own_blocks=o...  2.6 us
  transfers between devices with their start and end apart: 2, of which 2 were waited for; matrix products, arithmetic and copies ran while one was open for 1% of the time, Pallas kernels for 4%

profile of v2, /device:TPU:0, one launch (start us, length us, event | category | flops | bytes accessed | tf_op | source)
XLA Modules:
  0.0 47.8 jit_solution(15937506565514192179)
XLA Ops:
  0.6 0.0 copy-start.1
  0.6 0.0 copy-start.2
  0.7 0.0 copy-start.6
  0.7 0.0 copy-start.5
  0.7 0.0 copy-start.3
  0.7 0.0 copy-start
  0.7 1.4 %copy.19 = s32[4,1,2]{2,1,0:T(1,128)} copy(s32[4,1,2]{0,2,1:T(2,128)} %bitcast.19) | data formatting | bytes 64 | tf_op jit(solution)/shard_map/all_to_all | solution.py:304
  2.1 6.3 %all-to-all-start = ((s32[4,1,2]{2,1,0:T(1,128)}), s32[4,1,2]{2,1,0:T(1,128)S(1)}, u32[]{:S(2)}, u32[]{:S(2)}) async-start(s32[4,1,2]{2,1,0:T(1,128)} %copy.19), calls=%async_computation | async-start | bytes 4096 | tf_op jit(solution)/shard_map/all_to_all | solution.py:304
  8.4 5.5 %all-to-all-done = s32[4,1,2]{2,1,0:T(1,128)S(1)} async-done(((s32[4,1,2]{2,1,0:T(1,128)}), s32[4,1,2]{2,1,0:T(1,128)S(1)}, u32[]{:S(2)}, u32[]{:S(2)}) %all-to-all-start) | async-done | bytes 64 | tf_op jit(solution)/shard_map/all_to_all | solution.py:304
  13.9 0.0 copy-start.8
  13.9 0.6 %copy-done.8 = s32[4,1,2]{2,1,0:T(1,128)} copy-done((s32[4,1,2]{2,1,0:T(1,128)}, s32[4,1,2]{2,1,0:T(1,128)S(1)}, u32[]{:S(2)}) %copy-start.8) | copy-done | bytes 56
  14.4 3.9 %pick_blocks.1 = bf16[4,2,32,128]{3,2,1,0:T(8,128)(2,1)} custom-call(s32[4,2]{1,0:T(4,128)} %bitcast.16, bf16[32,32,128]{2,1,0:T(8,128)(2,1)} %fresh_ref.1), custom_call_target="tpu_custom_call" | custom-call | tf_op jit(solution)/shard_map/pick_blocks/pallas_call | solution.py:307
  18.3 3.3 %all-to-all-start.1 = ((bf16[4,2,32,128]{3,2,1,0:T(8,128)(2,1)}), bf16[4,2,32,128]{3,2,1,0:T(8,128)(2,1)S(1)}, u32[]{:S(2)}, u32[]{:S(2)}) async-start(bf16[4,2,32,128]{3,2,1,0:T(8,128)(2,1)} %pick_blocks.1), calls=%async_computation.1 | async-start | bytes 131072 | tf_op jit(solution)/shard_map/all_to_all | solution.py:322
  21.6 0.6 %pad_add_fusion.place_ref = s32[2]{0:T(128)} fusion(s32[1]{0:T(128)} %bitcast.1, s32[1]{0:T(128)} %bitcast), kind=kLoop, calls=%fused_computation | loop fusion | flops 2 | bytes 16 | tf_op jit(solution)/shard_map/stack | solution.py:303
  22.2 0.0 copy-start.4
  22.2 1.8 %list_targets.1 = (s32[32,128]{1,0:T(8,128)}, f32[4,16,128]{2,1,0:T(8,128)}) custom-call(s32[2]{0:T(128)} %pad_add_fusion.place_ref, s32[1,96]{1,0:T(1,128)} %bitcast.17, f32[3,16,128]{2,1,0:T(8,128)} %constant.15.clone.lanes_ref), custom_call_target="tpu_custom_call" | custom-call | tf_op jit(solution)/shard_map/list_targets/pallas_call | solution.py:325
  24.0 3.3 %all-to-all-done.1 = bf16[4,2,32,128]{3,2,1,0:T(8,128)(2,1)S(1)} async-done(((bf16[4,2,32,128]{3,2,1,0:T(8,128)(2,1)}), bf16[4,2,32,128]{3,2,1,0:T(8,128)(2,1)S(1)}, u32[]{:S(2)}, u32[]{:S(2)}) %all-to-all-start.1) | async-done | bytes 65568 | tf_op jit(solution)/shard_map/all_to_all | solution.py:322
  27.3 0.0 copy-start.7
  27.3 0.6 %copy-done.7 = bf16[4,2,32,128]{3,2,1,0:T(8,128)(2,1)} copy-done((bf16[4,2,32,128]{3,2,1,0:T(8,128)(2,1)}, bf16[4,2,32,128]{3,2,1,0:T(8,128)(2,1)S(1)}, u32[]{:S(2)}) %copy-start.7) | copy-done | bytes 65560
  27.9 6.1 %tract_tiles.1 = bf16[4,400,128]{2,1,0:T(8,128)(2,1)} custom-call(s32[1,96]{1,0:T(1,128)} %bitcast.20, s32[1,96]{1,0:T(1,128)} %bitcast.18, s32[1,96]{1,0:T(1,128)} %bitcast.21, f32[1,96]{1,0:T(1,128)} %bitcast.22, s32[32,128]{1,0:T(8,128)} %get-tuple-element.4.rows_ref, f32[4,16,128]{2,1,0:T(8,128)} %get-tuple-element.5.head_ref, ...), custom_call_target="tpu_custom_call" | custom-call | tf_op jit(solution)/shard_map/tract_tiles/pallas_call | solution.py:339
  34.1 11.1 %all_to_all.21.shares_ref = bf16[4,400,128]{2,1,0:T(8,128)(2,1)S(1)} all-to-all(bf16[4,400,128]{2,1,0:T(8,128)(2,1)} %tract_tiles.1), channel_id=1, replica_groups=mesh['sweep'=2,'wide'=4,'narrow'=4] {'narrow'}, dimensions={0} | all-to-all | bytes 819200 | tf_op jit(solution)/shard_map/all_to_all | solution.py:374
  45.1 0.0 copy-done.1
  45.1 0.0 copy-done.2
  45.1 0.0 copy-done.6
  45.1 0.0 copy-done.5
  45.1 0.0 copy-done.3
  45.1 0.0 copy-done
  45.1 0.0 copy-done.4
  45.2 2.6 %window_steps.1 = (bf16[32,32,128]{2,1,0:T(8,128)(2,1)}, f32[2,4096]{1,0:T(2,128)}) custom-call(s32[2]{0:T(128)S(1)} %copy-done.4, s32[64]{0:T(128)S(1)} %copy-done.5, f32[32]{0:T(128)S(1)} %copy-done.6, bf16[4,400,128]{2,1,0:T(8,128)(2,1)S(1)} %all_to_all.21.shares_ref, f32[2,4096]{1,0:T(2,128)S(1)} %copy-done, s32[32,128]{1,0:T(8,128)S(1)} %bitcast.12, ...), custom_call_target="tpu_custom_call" | custom-call | tf_op jit(solution)/shard_map/window_steps/pallas_call | solution.py:377
Async XLA Ops:
  0.6 44.5 %copy-start.1 = (bf16[128,128]{1,0:T(8,128)(2,1)S(1)}, bf16[128,128]{1,0:T(8,128)(2,1)}, u32[]{:S(2)}) copy-start(bf16[128,128]{1,0:T(8,128)(2,1)} %constant.18.clone.low_ref) | copy-start | bytes 98308
  0.6 44.5 %copy-start.2 = (bf16[128,128]{1,0:T(8,128)(2,1)S(1)}, bf16[128,128]{1,0:T(8,128)(2,1)}, u32[]{:S(2)}) copy-start(bf16[128,128]{1,0:T(8,128)(2,1)} %constant.17.clone.high_ref) | copy-start | bytes 98308
  0.7 44.5 %copy-start.6 = (f32[32]{0:T(128)S(1)}, f32[32]{0:T(128)}, u32[]{:S(2)}) copy-start(f32[32]{0:T(128)} %wave_ref.1) | copy-start | bytes 388
  0.7 44.5 %copy-start.5 = (s32[64]{0:T(128)S(1)}, s32[64]{0:T(128)}, u32[]{:S(2)}) copy-start(s32[64]{0:T(128)} %stim_ref.1) | copy-start | bytes 772
  0.7 44.5 %copy-start.3 = (s32[4096]{0:T(1024)S(1)}, s32[4096]{0:T(1024)}, u32[]{:S(2)}) copy-start(s32[4096]{0:T(1024)} %param.19) | copy-start | bytes 49156
  0.7 44.5 %copy-start = (f32[2,4096]{1,0:T(2,128)S(1)}, f32[2,4096]{1,0:T(2,128)}, u32[]{:S(2)}) copy-start(f32[2,4096]{1,0:T(2,128)} %state_ref.1) | copy-start | bytes 98308
  2.1 11.8 %all-to-all-start = ((s32[4,1,2]{2,1,0:T(1,128)}), s32[4,1,2]{2,1,0:T(1,128)S(1)}, u32[]{:S(2)}, u32[]{:S(2)}) async-start(s32[4,1,2]{2,1,0:T(1,128)} %copy.19), calls=%async_computation | async-start | bytes 4096 | tf_op jit(solution)/shard_map/all_to_all | solution.py:304
  13.9 0.6 %copy-start.8 = (s32[4,1,2]{2,1,0:T(1,128)}, s32[4,1,2]{2,1,0:T(1,128)S(1)}, u32[]{:S(2)}) copy-start(s32[4,1,2]{2,1,0:T(1,128)S(1)} %all-to-all-done) | copy-start | bytes 100
  18.3 9.0 %all-to-all-start.1 = ((bf16[4,2,32,128]{3,2,1,0:T(8,128)(2,1)}), bf16[4,2,32,128]{3,2,1,0:T(8,128)(2,1)S(1)}, u32[]{:S(2)}, u32[]{:S(2)}) async-start(bf16[4,2,32,128]{3,2,1,0:T(8,128)(2,1)} %pick_blocks.1), calls=%async_computation.1 | async-start | bytes 131072 | tf_op jit(solution)/shard_map/all_to_all | solution.py:322
  22.2 22.9 %copy-start.4 = (s32[2]{0:T(128)S(1)}, s32[2]{0:T(128)}, u32[]{:S(2)}) copy-start(s32[2]{0:T(128)} %pad_add_fusion.place_ref) | copy-start | bytes 28
  27.3 0.6 %copy-start.7 = (bf16[4,2,32,128]{3,2,1,0:T(8,128)(2,1)}, bf16[4,2,32,128]{3,2,1,0:T(8,128)(2,1)S(1)}, u32[]{:S(2)}) copy-start(bf16[4,2,32,128]{3,2,1,0:T(8,128)(2,1)S(1)} %all-to-all-done.1) | copy-start | bytes 196612

commit v3 on v2

v3 whole, which is shorter than its diff:
```python
import functools
import math

import jax
import jax.numpy as jnp
import ml_dtypes
import numpy as np
from jax import lax
from jax.experimental import pallas as pl
from jax.experimental.pallas import tpu as pltpu
from jax.sharding import PartitionSpec as P

STEPS = 32
HSEG = 2
SEGS = HSEG + 1
LENGTH = SEGS * STEPS
GROUP = 4
HEAD = 16
UNROLL = 16

excite_rate = 0.1
inhibit_rate = 0.05
excite_excite = 1.5
inhibit_excite = 2.0
excite_inhibit = 2.0
inhibit_inhibit = 0.5
excite_offset = 0.5
inhibit_offset = 0.5
tract_gain = 2.0

SMEM = pltpu.SMEM
VMEM = pltpu.VMEM
vmem_spec = pl.BlockSpec(memory_space=VMEM)
hbm_spec = pl.BlockSpec(memory_space=pltpu.HBM)


def basis_table(coef_count, step_count):
    order = np.arange(coef_count, dtype=np.float32)[:, None]
    places = np.arange(step_count, dtype=np.float32)[None, :]
    angles = np.float32(np.pi) * (step_count - places - np.float32(0.5)) / np.float32(step_count)
    return np.cos((order * angles).astype(np.float64)).astype(np.float32)


def expand_table(coef_count):
    basis = basis_table(coef_count, STEPS).astype(ml_dtypes.bfloat16)
    table = np.zeros((LENGTH, SEGS * coef_count), ml_dtypes.bfloat16)
    for seg in range(SEGS):
        table[seg * STEPS : (seg + 1) * STEPS, seg * coef_count : (seg + 1) * coef_count] = basis.T
    return table


def fit_tables(coef_count):
    scales = np.where(np.arange(coef_count)[:, None] == 0, 1.0, 2.0) / STEPS
    fit = (basis_table(coef_count, STEPS) * scales).astype(np.float32)
    whole = np.zeros((GROUP * coef_count, GROUP * STEPS), np.float32)
    for g in range(GROUP):
        whole[g * coef_count : (g + 1) * coef_count, g * STEPS : (g + 1) * STEPS] = fit
    high = whole.astype(ml_dtypes.bfloat16)
    low = (whole - high.astype(np.float32)).astype(ml_dtypes.bfloat16)
    return high, low


def steps_together(peer_targets):
    return 16 // math.gcd(16, peer_targets)


def lane_tables(peers, peer_targets, own_blocks):
    together = steps_together(peer_targets)
    width = together * peer_targets
    assert together * own_blocks <= 256 and peers * width <= HEAD * 128
    lane = np.arange(HEAD * 128)
    used = lane < peers * width
    within = lane % width
    rank = np.where(used, within % peer_targets, -5)
    offset = within // peer_targets * own_blocks + 1
    place = np.where(used, lane // width, -5)
    return np.stack([rank, offset, place]).astype(np.float32).reshape(3, HEAD, 128)


def ready_kernel(
    fresh_ref, state_ref, lesion_ref, stim_ref, wave_ref, fresh_out, ready_out, sem,
    *, peers, own_blocks,
):
    copy = pltpu.make_async_copy(fresh_ref, fresh_out, sem)
    copy.start()
    block_rows = lesion_ref.shape[1]
    place = lax.axis_index("wide") * peers + lax.axis_index("narrow")
    for b in range(own_blocks):
        piece = state_ref[:, b * block_rows : (b + 1) * block_rows]
        ready_out[b : b + 1, :] = piece[0:1, :]
        ready_out[own_blocks + b : own_blocks + b + 1, :] = piece[1:2, :]
    ready_out[2 * own_blocks : 3 * own_blocks, :] = tract_gain * (
        1.0 - lesion_ref[...].astype(jnp.float32)
    )
    stim_count = stim_ref.shape[1]
    nodes = stim_ref[...] - place * (own_blocks * block_rows)
    blocks = lax.shift_right_arithmetic(nodes, block_rows.bit_length() - 1)
    offsets = nodes & (block_rows - 1)
    in_block = lax.broadcasted_iota(jnp.int32, (own_blocks, stim_count), 0) == blocks
    at_offset = lax.broadcasted_iota(jnp.int32, (block_rows, stim_count), 0) == offsets
    ready_out[3 * own_blocks : 4 * own_blocks, :] = lax.dot_general(
        in_block.astype(jnp.float32).astype(jnp.bfloat16),
        at_offset.astype(jnp.float32).astype(jnp.bfloat16),
        (((1,), (1,)), ((), ())),
        preferred_element_type=jnp.float32,
    )
    shape = (STEPS, STEPS)
    diagonal = lax.broadcasted_iota(jnp.int32, shape, 0) == lax.broadcasted_iota(jnp.int32, shape, 1)
    column = jnp.sum(jnp.where(diagonal, wave_ref[...], 0.0), axis=1, keepdims=True)
    ready_out[4 * own_blocks :, :] = jnp.broadcast_to(column, (STEPS, block_rows))
    copy.wait()


def pick_kernel(*refs, capacity, peers):
    tables = refs[: peers - 1]
    fresh = refs[peers - 1]
    outs = refs[peers : 2 * peers - 1]
    asked, sems = refs[2 * peers - 1 :]
    place = lax.axis_index("wide")
    copies = [pltpu.make_async_copy(tables[r], asked.at[r], sems.at[r]) for r in range(peers - 1)]
    for copy in copies:
        copy.start()
    for r in range(peers - 1):
        copies[r].wait()
        for c in range(capacity):
            outs[r][c] = fresh[jnp.maximum(asked[r, c, place], 0)]


def tiles_kernel(
    reads_ref, slot_ref, target_ref, delay_ref, lanes_ref, table_ref, older_ref, fresh_ref,
    weights_ref, weights_out, hist_out, tiles_out, head_out, reads, reads_sem, weights_sem,
    *, peers, own_blocks, peer_targets, capacity,
):
    copy = pltpu.make_async_copy(weights_ref, weights_out, weights_sem)
    copy.start()
    reads_copy = pltpu.make_async_copy(reads_ref, reads, reads_sem)
    reads_copy.start()
    tile_count = target_ref.shape[1]
    target_count = peers * own_blocks
    span = peer_targets * STEPS
    place = lax.axis_index("narrow")

    numbers = lax.broadcasted_iota(jnp.int32, (target_count, tile_count), 0)
    hits = (numbers == target_ref[...]).astype(jnp.float32)
    held = jnp.dot(
        hits.astype(jnp.bfloat16), jnp.ones((tile_count, 128), jnp.bfloat16),
        preferred_element_type=jnp.float32,
    )
    held = jnp.minimum(held, 1.0)
    shape = (own_blocks, own_blocks)
    below = (
        lax.broadcasted_iota(jnp.int32, shape, 0) > lax.broadcasted_iota(jnp.int32, shape, 1)
    ).astype(jnp.float32).astype(jnp.bfloat16)
    block = lax.broadcasted_iota(jnp.int32, (own_blocks, 128), 0).astype(jnp.float32)
    first = jnp.zeros((1, tile_count), jnp.float32)
    for p in range(peers):
        part = slice(p * own_blocks, (p + 1) * own_blocks)
        rank = jnp.dot(below, held[part].astype(jnp.bfloat16), preferred_element_type=jnp.float32)
        first = first + jnp.sum(
            hits[part] * (rank[:, :tile_count] + float(p * span)), axis=0, keepdims=True
        )
        rank = jnp.where(held[part] > 0.5, rank, -1.0)
        source = (place ^ p).astype(jnp.float32)
        head_out[p] = jnp.zeros((HEAD, 128), jnp.bfloat16)
        rows = []
        for h in range(pl.cdiv(peers * steps_together(peer_targets) * peer_targets, 128)):
            match = rank == lanes_ref[0, h : h + 1, :]
            ids = jnp.sum(jnp.where(match, block, 0.0), axis=0, keepdims=True)
            mine = lanes_ref[2, h : h + 1, :] == source
            rows.append(jnp.where(mine, ids + lanes_ref[1, h : h + 1, :], 0.0))
        rows.append(jnp.zeros((HEAD - len(rows), 128), jnp.float32))
        head_out[p] = jnp.concatenate(rows, axis=0).astype(jnp.bfloat16)
    tiles_out[0:1, :tile_count] = slot_ref[...] * LENGTH + (LENGTH - 1) - delay_ref[...]
    tiles_out[1:2, :tile_count] = first.astype(jnp.int32)

    table = table_ref[...]
    coef_count = older_ref.shape[2]
    earlier = HSEG * STEPS
    for s in range(older_ref.shape[0]):
        segments = [older_ref[s, h] for h in range(HSEG - 1, -1, -1)]
        hist_out[s * LENGTH : s * LENGTH + earlier, :] = jnp.dot(
            table[:earlier, : HSEG * coef_count], jnp.concatenate(segments, axis=0),
            preferred_element_type=jnp.float32,
        )
    reads_copy.wait()
    owner = lax.axis_index("wide")
    for c in range(capacity):
        rows = pl.ds(pl.multiple_of((owner * capacity + c) * LENGTH + earlier, 8), STEPS)
        hist_out[rows, :] = jnp.dot(
            table[:STEPS, :coef_count], fresh_ref[jnp.maximum(reads[c, owner], 0)],
            preferred_element_type=jnp.float32,
        )
    copy.wait()


def tract_kernel(
    tiles_ref, frac_ref, table_ref, hist_ref, weights, head_ref, *refs,
    wide_peers, peers, capacity, peer_targets,
):
    news = refs[: wide_peers - 1]
    outs = refs[wide_peers - 1 : wide_peers - 1 + peers]
    tiles, frac, hist, total, sems = refs[wide_peers - 1 + peers :]
    tile_count = frac_ref.shape[1]
    owner = lax.axis_index("wide")
    place = lax.axis_index("narrow")
    copies = [
        pltpu.make_async_copy(tiles_ref, tiles, sems.at[0]),
        pltpu.make_async_copy(frac_ref, frac, sems.at[1]),
    ]
    for copy in copies:
        copy.start()
    total[...] = jnp.zeros_like(total)
    hist[...] = hist_ref[...]
    coef_count = news[0].shape[1]
    table = table_ref[:STEPS, :coef_count]
    for r in range(1, wide_peers):
        for c in range(capacity):
            slot = (owner ^ r) * capacity + c
            rows = pl.ds(pl.multiple_of(slot * LENGTH + HSEG * STEPS, 8), STEPS)
            hist[rows, :] = jnp.dot(table, news[r - 1][c], preferred_element_type=jnp.float32)
    for copy in copies:
        copy.wait()

    @pl.loop(0, tile_count // UNROLL)
    def _(turn):
        sums = []
        for u in range(UNROLL):
            t = turn * UNROLL + u
            fraction = frac[0, t]
            start = tiles[0, t]
            earlier = hist[pl.ds(start, STEPS), :]
            later = hist[pl.ds(start + 1, STEPS), :]
            delayed = ((1.0 - fraction) * later + fraction * earlier).astype(jnp.bfloat16)
            sums.append(
                lax.dot_general(
                    delayed, weights[t], (((1,), (1,)), ((), ())),
                    preferred_element_type=jnp.float32,
                )
            )
        for u in range(UNROLL):
            where = pl.ds(tiles[1, turn * UNROLL + u], STEPS, stride=peer_targets)
            total[where, :] += sums[u]

    span = peer_targets * STEPS
    for r in range(peers):
        first = pl.multiple_of((place ^ r) * span, 8)
        outs[r][:span, :] = total[pl.ds(first, span), :].astype(jnp.bfloat16)
        outs[r][span:, :] = head_ref[place ^ r]


def window_kernel(*refs, peers, own_blocks, peer_targets, coef_count):
    shares = refs[:peers]
    ready_ref, high_ref, low_ref, coefs_out, state_out, samples, rates = refs[peers:]
    block_rows = ready_ref.shape[1]
    together = steps_together(peer_targets)
    width = together * peer_targets
    span = peer_targets * STEPS

    head = shares[0][span:, :].astype(jnp.float32)
    for r in range(1, peers):
        head = head + shares[r][span:, :].astype(jnp.float32)
    row = lax.broadcasted_iota(jnp.int32, (together * own_blocks, 128), 0).astype(jnp.float32) + 1.0
    columns = peers * width
    scatter = jnp.concatenate(
        [
            jnp.where(row == head[h : h + 1, :], 1.0, 0.0).astype(jnp.bfloat16)
            for h in range(pl.cdiv(columns, 128))
        ],
        axis=1,
    )[:, :columns]

    excite, inhibit, gain, counts = [
        ready_ref[i * own_blocks : (i + 1) * own_blocks, :] for i in range(4)
    ]
    for g in range(STEPS // together):
        arrived = jnp.concatenate(
            [shares[r][g * width : (g + 1) * width, :] for r in range(peers)], axis=0
        )
        inflow = jnp.dot(scatter, arrived, preferred_element_type=jnp.float32)
        for jj in range(together):
            j = g * together + jj
            wave = ready_ref[4 * own_blocks + j : 4 * own_blocks + j + 1, :]
            forcing = gain * inflow[jj * own_blocks : (jj + 1) * own_blocks] + wave * counts
            excite_drive = (
                excite_excite * excite - inhibit_excite * inhibit + forcing - excite_offset
            )
            inhibit_drive = excite_inhibit * excite - inhibit_inhibit * inhibit - inhibit_offset
            excite, inhibit = (
                excite + excite_rate * (0.5 * jnp.tanh(0.5 * excite_drive) + 0.5 - excite),
                inhibit + inhibit_rate * (0.5 * jnp.tanh(0.5 * inhibit_drive) + 0.5 - inhibit),
            )
            samples[pl.ds(j, own_blocks, stride=STEPS), :] = excite
    rates[0] = excite
    rates[1] = inhibit
    for b in range(own_blocks):
        where = slice(b * block_rows, (b + 1) * block_rows)
        state_out[0:1, where] = rates[0, b : b + 1, :]
        state_out[1:2, where] = rates[1, b : b + 1, :]

    high = high_ref[...]
    low = low_ref[...]
    rows = GROUP * STEPS
    for g in range(own_blocks // GROUP):
        part = samples[g * rows : (g + 1) * rows, :]
        part_high = part.astype(jnp.bfloat16)
        part_low = (part - part_high.astype(jnp.float32)).astype(jnp.bfloat16)
        fitted = (
            jnp.dot(high, part_high, preferred_element_type=jnp.float32)
            + jnp.dot(high, part_low, preferred_element_type=jnp.float32)
            + jnp.dot(low, part_high, preferred_element_type=jnp.float32)
        )
        coefs_out[g * GROUP : (g + 1) * GROUP] = fitted.astype(jnp.bfloat16).reshape(
            GROUP, coef_count, block_rows
        )


def far(x):
    return pltpu.with_memory_space_constraint(x, pltpu.HBM)


def params():
    return pltpu.CompilerParams(vmem_limit_bytes=20 << 20)


def local(
    fresh_coefs,
    older_coefs,
    state,
    lesion,
    stim_nodes,
    stim_wave,
    read_blocks,
    tract_slot,
    tract_target,
    tract_delay,
    tract_frac,
    tract_weights,
):
    wide_peers = lax.axis_size("wide")
    peers = lax.axis_size("narrow")
    own_blocks, coef_count, block_rows = fresh_coefs.shape
    capacity = read_blocks.shape[3]
    slot_count = wide_peers * capacity
    tile_count = tract_slot.shape[2]
    peer_targets = tile_count // (2 * peers)
    share_rows = peer_targets * STEPS + HEAD

    def swap(x, axis, r):
        return lax.ppermute(x, axis, [(i, i ^ r) for i in range(lax.axis_size(axis))])

    reads = read_blocks.reshape(wide_peers, capacity).T
    asked = [swap(reads, "wide", r) for r in range(1, wide_peers)]

    fresh, ready = pl.pallas_call(
        functools.partial(ready_kernel, peers=peers, own_blocks=own_blocks),
        out_shape=[
            pltpu.VMEM(fresh_coefs.shape, jnp.bfloat16),
            pltpu.VMEM((4 * own_blocks + STEPS, block_rows), jnp.float32),
        ],
        in_specs=[hbm_spec] + [vmem_spec] * 4,
        out_specs=[vmem_spec] * 2,
        scratch_shapes=[pltpu.SemaphoreType.DMA],
        compiler_params=params(),
        name="ready",
    )(
        far(fresh_coefs),
        far(state),
        far(lesion.reshape(own_blocks, block_rows)),
        far(stim_nodes.reshape(1, -1)),
        far(stim_wave.reshape(1, -1)),
    )

    picked = pl.pallas_call(
        functools.partial(pick_kernel, capacity=capacity, peers=wide_peers),
        out_shape=[pltpu.VMEM((capacity, coef_count, block_rows), jnp.bfloat16)]
        * (wide_peers - 1),
        in_specs=[vmem_spec] * wide_peers,
        out_specs=[vmem_spec] * (wide_peers - 1),
        scratch_shapes=[
            SMEM((wide_peers - 1, capacity, wide_peers), jnp.int32),
            pltpu.SemaphoreType.DMA((wide_peers - 1,)),
        ],
        compiler_params=params(),
        name="pick_blocks",
    )(*asked, fresh)
    news = [swap(picked[r - 1], "wide", r) for r in range(1, wide_peers)]

    table = expand_table(coef_count)
    weights, hist, tiles, heads = pl.pallas_call(
        functools.partial(
            tiles_kernel,
            peers=peers, own_blocks=own_blocks, peer_targets=peer_targets, capacity=capacity,
        ),
        out_shape=[
            pltpu.VMEM((tile_count, block_rows, block_rows), jnp.bfloat16),
            pltpu.VMEM((slot_count * LENGTH, block_rows), jnp.float32),
            pltpu.VMEM((8, 128), jnp.int32),
            pltpu.VMEM((peers, HEAD, 128), jnp.bfloat16),
        ],
        in_specs=[hbm_spec] + [vmem_spec] * 7 + [hbm_spec],
        out_specs=[vmem_spec] * 4,
        scratch_shapes=[
            SMEM((capacity, wide_peers), jnp.int32),
            pltpu.SemaphoreType.DMA,
            pltpu.SemaphoreType.DMA,
        ],
        compiler_params=params(),
        name="tile_tables",
    )(
        far(reads),
        far(tract_slot.reshape(1, tile_count)),
        far(tract_target.reshape(1, tile_count)),
        far(tract_delay.reshape(1, tile_count)),
        far(jnp.asarray(lane_tables(peers, peer_targets, own_blocks))),
        far(jnp.asarray(table)),
        far(older_coefs.reshape(slot_count, HSEG, coef_count, block_rows)),
        fresh,
        far(tract_weights.reshape(tile_count, block_rows, block_rows)),
    )

    shares = pl.pallas_call(
        functools.partial(
            tract_kernel,
            wide_peers=wide_peers, peers=peers, capacity=capacity, peer_targets=peer_targets,
        ),
        out_shape=[pltpu.VMEM((share_rows, block_rows), jnp.bfloat16)] * peers,
        in_specs=[vmem_spec, hbm_spec] + [vmem_spec] * (3 + wide_peers),
        out_specs=[vmem_spec] * peers,
        scratch_shapes=[
            SMEM((8, 128), jnp.int32),
            SMEM((1, tile_count), jnp.float32),
            VMEM((slot_count * LENGTH, block_rows), jnp.float32),
            VMEM((peers * peer_targets * STEPS, block_rows), jnp.float32),
            pltpu.SemaphoreType.DMA((2,)),
        ],
        compiler_params=params(),
        name="tract_tiles",
    )(
        tiles,
        far(tract_frac.reshape(1, tile_count)),
        far(jnp.asarray(table)),
        hist,
        weights,
        heads,
        *news,
    )
    arrived = [shares[0]] + [swap(shares[r], "narrow", r) for r in range(1, peers)]

    high, low = fit_tables(coef_count)
    new_coefs, final_state = pl.pallas_call(
        functools.partial(
            window_kernel,
            peers=peers, own_blocks=own_blocks, peer_targets=peer_targets, coef_count=coef_count,
        ),
        out_shape=[
            jax.ShapeDtypeStruct(fresh_coefs.shape, jnp.bfloat16),
            jax.ShapeDtypeStruct(state.shape, jnp.float32),
        ],
        in_specs=[vmem_spec] * (peers + 3),
        out_specs=[vmem_spec] * 2,
        scratch_shapes=[
            VMEM((own_blocks * STEPS, block_rows), jnp.float32),
            VMEM((2, own_blocks, block_rows), jnp.float32),
        ],
        compiler_params=params(),
        name="window_steps",
    )(*arrived, ready, high, low)
    return new_coefs, final_state


def solution(mesh):
    in_specs = (
        P(("sweep", "wide", "narrow"), None, None),
        P(("sweep", "wide"), "narrow", None, None, None, None),
        P(None, ("sweep", "wide", "narrow")),
        P(("sweep", "wide", "narrow")),
        P("sweep"),
        P("sweep"),
        P("wide", "narrow", None, None),
        P("wide", "narrow", None),
        P("wide", "narrow", None),
        P("wide", "narrow", None),
        P("wide", "narrow", None),
        P("wide", "narrow", None, None, None),
    )
    out_specs = (P(("sweep", "wide", "narrow"), None, None), P(None, ("sweep", "wide", "narrow")))
    return jax.shard_map(local, mesh=mesh, in_specs=in_specs, out_specs=out_specs, check_vma=False)
```

time: 48.3 us -> 32.3 us (0.67)
  blocking collectives: 11.1 us -> 0 us
  Pallas kernels: 14.3 us -> 11.4 us
  local copies, waits for them, and re-layouts: 2.61 us -> 0.01 us
  starting transfers between devices: 9.61 us -> 12.1 us
  waiting for transfers between devices: 8.79 us -> 7.75 us
  other arithmetic: 0.6 us -> 0 us
    ppermute x0 -> x9, starting transfers between devices: none -> 12.1 us  [swap(): lax.ppermute(x, axis, [(i, i ^ r) for i in range(lax.axis_size(axis))])]
    all_to_all x1 -> x0, blocking collectives: 11.1 us -> none  [local(): arrived = lax.all_to_all(shares, 'narrow', 0, 0, tiled=True)]
    all_to_all x2 -> x0, starting transfers between devices: 9.61 us -> none  [the longest x1 6.32 us: local(): lax.all_to_all(read_blocks.reshape(wide_peers, capacity), 'wide', 0, 0, t...]
    all_to_all x2 -> x0, waiting for transfers between devices: 8.79 us -> none  [the longest x1 5.47 us: local(): lax.all_to_all(read_blocks.reshape(wide_peers, capacity), 'wide', 0, 0, t...]
    ppermute x0 -> x9, waiting for transfers between devices: none -> 7.75 us  [swap(): lax.ppermute(x, axis, [(i, i ^ r) for i in range(lax.axis_size(axis))])]
    pallas_call x1, Pallas kernels: 3.86 us -> 0.62 us  [local(): pl.pallas_call(functools.partial(pick_kernel, capacity=capacity, peers=wi...]
    all_to_all x1 -> x0, local copies, waits for them, and re-layouts: 1.37 us -> none  [local(): lax.all_to_all(read_blocks.reshape(wide_peers, capacity), 'wide', 0, 0, t...]
    unnamed x18 -> x4, local copies, waits for them, and re-layouts: 1.24 us -> 0.01 us
  transfers between devices with their start and end apart: 2 -> 9, of which waited for: 2 -> 4; matrix products, arithmetic and copies ran while one was open for 1% -> 0% of each run, Pallas kernels for 4% -> 15%
where the time goes in v3:
time: 32.3 us; the launch traced here: 32 us
  starting transfers between devices  12.1 us (37%)
  Pallas kernels  11.4 us (35%)
  waiting for transfers between devices  7.75 us (24%)
  between operations  0.71 us (2%)
    ppermute x9, starting transfers between devices, swap(): lax.ppermute(x, axis, [(i, i ^ r) for i in range(lax.axis_size(axis))])  12.1 us
    ppermute x9, waiting for transfers between devices, swap(): lax.ppermute(x, axis, [(i, i ^ r) for i in range(lax.axis_size(axis))])  7.75 us
    pallas_call x1, Pallas kernels, local(): pl.pallas_call(functools.partial(tract_kernel, wide_peers=wide_peers, pee...  3.99 us
    pallas_call x1, Pallas kernels, local(): pl.pallas_call(functools.partial(tiles_kernel, peers=peers, own_blocks=ow...  2.91 us
    pallas_call x1, Pallas kernels, local(): pl.pallas_call(functools.partial(window_kernel, peers=peers, own_blocks=o...  2.1 us
    pallas_call x1, Pallas kernels, local(): pl.pallas_call(functools.partial(ready_kernel, peers=peers, own_blocks=ow...  1.76 us
  transfers between devices with their start and end apart: 9, of which 4 were waited for; matrix products, arithmetic and copies ran while one was open for 0% of the time, Pallas kernels for 15%

profile of v3, /device:TPU:0, one launch (start us, length us, event | category | flops | bytes accessed | tf_op | source)
XLA Modules:
  0.0 32.0 jit_solution(14852164900479289971)
XLA Ops:
  0.6 5.1 %collective-permute-start.2 = (s32[2,4]{1,0:T(2,128)}, s32[2,4]{1,0:T(2,128)S(1)}, u32[]{:S(2)}, u32[]{:S(2)}) collective-permute-start(s32[2,4]{1,0:T(2,128)} %bitcast.15), channel_id=1, source_target_pairs={{0,12},{4,8},{8,4},{12,0},{1,13},{5,9},{9,5},{13,1},{2,14},{6,10},... | collective-permute-start | bytes 104 | tf_op jit(solution)/shard_map/ppermute | solution.py:349
  5.7 0.0 collective-permute-start.1
  5.7 0.6 %collective-permute-start = (s32[2,4]{1,0:T(2,128)}, s32[2,4]{1,0:T(2,128)S(1)}, u32[]{:S(2)}, u32[]{:S(2)}) collective-permute-start(s32[2,4]{1,0:T(2,128)} %bitcast.17), channel_id=1, source_target_pairs={{0,4},{4,0},{8,12},{12,8},{1,5},{5,1},{9,13},{13,9},{2,6},{6,2},{1... | collective-permute-start | bytes 104 | tf_op jit(solution)/shard_map/ppermute | solution.py:349
  6.4 1.8 %ready.1 = (bf16[32,32,128]{2,1,0:T(8,128)(2,1)S(1)}, f32[160,128]{1,0:T(8,128)S(1)}) custom-call(bf16[32,32,128]{2,1,0:T(8,128)(2,1)} %fresh_ref.1, f32[2,4096]{1,0:T(2,128)} %state_ref.1, s32[32,128]{1,0:T(8,128)} %bitcast.14, s32[1,64]{1,0:T(1,128)} %bitcast.19, f32[1,32]{1,0:T(1,128)} %bitcast.20), custom_call_target="tpu_custom_call" | custom-call | tf_op jit(solution)/shard_map/ready/pallas_call | solution.py:354
  8.2 0.0 collective-permute-done.2.refs_2_
  8.2 2.3 %collective-permute-done.1.refs_1_ = s32[2,4]{1,0:T(2,128)S(1)} collective-permute-done((s32[2,4]{1,0:T(2,128)}, s32[2,4]{1,0:T(2,128)S(1)}, u32[]{:S(2)}, u32[]{:S(2)}) %collective-permute-start.1) | collective-permute-done | bytes 64 | tf_op jit(solution)/shard_map/ppermute | solution.py:349
  10.4 0.0 collective-permute-done.refs_0_
  10.4 0.6 %pick_blocks.1 = (bf16[2,32,128]{2,1,0:T(8,128)(2,1)S(1)}, bf16[2,32,128]{2,1,0:T(8,128)(2,1)S(1)}, bf16[2,32,128]{2,1,0:T(8,128)(2,1)S(1)}) custom-call(s32[2,4]{1,0:T(2,128)S(1)} %collective-permute-done.refs_0_, s32[2,4]{1,0:T(2,128)S(1)} %collective-permute-done.1.refs_1_, s32[2,4]{1,0:T(2,128)S(1)} %collective-permute-done.2.refs_2_, ...), custom_call_target="tpu_custom_call" | custom-call | tf_op jit(solution)/shard_map/pick_blocks/pallas_call | solution.py:373
  11.1 0.1 collective-permute-start.3
  11.1 2.1 %collective-permute-start.4 = (bf16[2,32,128]{2,1,0:T(8,128)(2,1)S(1)}, bf16[2,32,128]{2,1,0:T(8,128)(2,1)S(1)}, u32[]{:S(2)}, u32[]{:S(2)}) collective-permute-start(bf16[2,32,128]{2,1,0:T(8,128)(2,1)S(1)} %get-tuple-element.21), channel_id=1, source_target_pairs={{0,8},{4,12},{8,0},{12,4},{1,9},{5,13},{9,1},{13,5},{2,10},{6,14},... | collective-permute-start | bytes 49160 | tf_op jit(solution)/shard_map/ppermute | solution.py:349
  13.2 2.3 %collective-permute-start.5 = (bf16[2,32,128]{2,1,0:T(8,128)(2,1)S(1)}, bf16[2,32,128]{2,1,0:T(8,128)(2,1)S(1)}, u32[]{:S(2)}, u32[]{:S(2)}) collective-permute-start(bf16[2,32,128]{2,1,0:T(8,128)(2,1)S(1)} %get-tuple-element.22), channel_id=1, source_target_pairs={{0,12},{4,8},{8,4},{12,0},{1,13},{5,9},{9,5},{13,1},{2,14},{6,10},... | collective-permute-start | bytes 49160 | tf_op jit(solution)/shard_map/ppermute | solution.py:349
  15.5 0.0 copy-start
  15.5 0.0 copy-start.1
  15.5 2.9 %tile_tables.1 = (bf16[96,128,128]{2,1,0:T(8,128)(2,1)S(1)}, f32[768,128]{1,0:T(8,128)S(1)}, s32[8,128]{1,0:T(8,128)S(1)}, bf16[4,16,128]{2,1,0:T(8,128)(2,1)S(1)}) custom-call(s32[2,4]{1,0:T(2,128)} %bitcast.18, s32[1,96]{1,0:T(1,128)} %bitcast.21, s32[1,96]{1,0:T(1,128)} %bitcast.22, s32[1,96]{1,0:T(1,128)} %bitcast.23, ...), custom_call_target="tpu_custom_call" | custom-call | tf_op jit(solution)/shard_map/tile_tables/pallas_call | solution.py:389
  18.4 0.0 collective-permute-done.3.refs_0_
  18.4 0.0 collective-permute-done.4.refs_1_
  18.4 0.3 collective-permute-done.5.refs_2_
  18.8 4.0 %tract_tiles.1 = (bf16[400,128]{1,0:T(8,128)(2,1)S(1)}, bf16[400,128]{1,0:T(8,128)(2,1)S(1)}, bf16[400,128]{1,0:T(8,128)(2,1)S(1)}, bf16[400,128]{1,0:T(8,128)(2,1)S(1)}) custom-call(s32[8,128]{1,0:T(8,128)S(1)} %get-tuple-element.16.tiles_ref, f32[1,96]{1,0:T(1,128)} %bitcast.24, bf16[96,96]{1,0:T(8,128)(2,1)} %constant.9.clone.table_ref, ...), custom_call_target="tpu_custom_call" | custom-call | tf_op jit(solution)/shard_map/tract_tiles/pallas_call | solution.py:421
  22.8 0.1 collective-permute-start.6
  22.8 1.5 %collective-permute-start.7 = (bf16[400,128]{1,0:T(8,128)(2,1)S(1)}, bf16[400,128]{1,0:T(8,128)(2,1)S(1)}, u32[]{:S(2)}, u32[]{:S(2)}) collective-permute-start(bf16[400,128]{1,0:T(8,128)(2,1)S(1)} %get-tuple-element.25), channel_id=1, source_target_pairs={{0,2},{1,3},{2,0},{3,1},{4,6},{5,7},{6,4},{7,5},{8,10},{9,11},{10,... | collective-permute-start | bytes 307208 | tf_op jit(solution)/shard_map/ppermute | solution.py:349
  24.4 0.3 collective-permute-start.8
  24.7 0.0 collective-permute-done.6.refs_1_
  24.7 3.9 %collective-permute-done.7.refs_2_ = bf16[400,128]{1,0:T(8,128)(2,1)S(1)} collective-permute-done((bf16[400,128]{1,0:T(8,128)(2,1)S(1)}, bf16[400,128]{1,0:T(8,128)(2,1)S(1)}, u32[]{:S(2)}, u32[]{:S(2)}) %collective-permute-start.7) | collective-permute-done | bytes 102432 | tf_op jit(solution)/shard_map/ppermute | solution.py:349
  28.6 1.3 %collective-permute-done.8.refs_3_ = bf16[400,128]{1,0:T(8,128)(2,1)S(1)} collective-permute-done((bf16[400,128]{1,0:T(8,128)(2,1)S(1)}, bf16[400,128]{1,0:T(8,128)(2,1)S(1)}, u32[]{:S(2)}, u32[]{:S(2)}) %collective-permute-start.8) | collective-permute-done | bytes 102432 | tf_op jit(solution)/shard_map/ppermute | solution.py:349
  29.9 0.0 copy-done
  29.9 0.0 copy-done.1
  29.9 2.1 %window_steps.1 = (bf16[32,32,128]{2,1,0:T(8,128)(2,1)}, f32[2,4096]{1,0:T(2,128)}) custom-call(bf16[400,128]{1,0:T(8,128)(2,1)S(1)} %get-tuple-element.23.refs_0_, bf16[400,128]{1,0:T(8,128)(2,1)S(1)} %collective-permute-done.6.refs_1_, bf16[400,128]{1,0:T(8,128)(2,1)S(1)} %collective-permute-done.7.refs_2_, ...), custom_call_target="tpu_custom_call" | custom-call | tf_op jit(solution)/shard_map/window_steps/pallas_call | solution.py:450
Async XLA Ops:
  0.6 7.5 %collective-permute-start.2 = (s32[2,4]{1,0:T(2,128)}, s32[2,4]{1,0:T(2,128)S(1)}, u32[]{:S(2)}, u32[]{:S(2)}) collective-permute-start(s32[2,4]{1,0:T(2,128)} %bitcast.15), channel_id=1, source_target_pairs={{0,12},{4,8},{8,4},{12,0},{1,13},{5,9},{9,5},{13,1},{2,14},{6,10},... | collective-permute-start | bytes 104 | tf_op jit(solution)/shard_map/ppermute | solution.py:349
  5.7 4.7 %collective-permute-start.1 = (s32[2,4]{1,0:T(2,128)}, s32[2,4]{1,0:T(2,128)S(1)}, u32[]{:S(2)}, u32[]{:S(2)}) collective-permute-start(s32[2,4]{1,0:T(2,128)} %bitcast.16), channel_id=1, source_target_pairs={{0,8},{4,12},{8,0},{12,4},{1,9},{5,13},{9,1},{13,5},{2,10},{6,14},... | collective-permute-start | bytes 104 | tf_op jit(solution)/shard_map/ppermute | solution.py:349
  5.7 4.7 %collective-permute-start = (s32[2,4]{1,0:T(2,128)}, s32[2,4]{1,0:T(2,128)S(1)}, u32[]{:S(2)}, u32[]{:S(2)}) collective-permute-start(s32[2,4]{1,0:T(2,128)} %bitcast.17), channel_id=1, source_target_pairs={{0,4},{4,0},{8,12},{12,8},{1,5},{5,1},{9,13},{13,9},{2,6},{6,2},{1... | collective-permute-start | bytes 104 | tf_op jit(solution)/shard_map/ppermute | solution.py:349
  11.1 7.4 %collective-permute-start.3 = (bf16[2,32,128]{2,1,0:T(8,128)(2,1)S(1)}, bf16[2,32,128]{2,1,0:T(8,128)(2,1)S(1)}, u32[]{:S(2)}, u32[]{:S(2)}) collective-permute-start(bf16[2,32,128]{2,1,0:T(8,128)(2,1)S(1)} %get-tuple-element.20), channel_id=1, source_target_pairs={{0,4},{4,0},{8,12},{12,8},{1,5},{5,1},{9,13},{13,9},{2,6},{6,2},{1... | collective-permute-start | bytes 49160 | tf_op jit(solution)/shard_map/ppermute | solution.py:349
  11.1 7.3 %collective-permute-start.4 = (bf16[2,32,128]{2,1,0:T(8,128)(2,1)S(1)}, bf16[2,32,128]{2,1,0:T(8,128)(2,1)S(1)}, u32[]{:S(2)}, u32[]{:S(2)}) collective-permute-start(bf16[2,32,128]{2,1,0:T(8,128)(2,1)S(1)} %get-tuple-element.21), channel_id=1, source_target_pairs={{0,8},{4,12},{8,0},{12,4},{1,9},{5,13},{9,1},{13,5},{2,10},{6,14},... | collective-permute-start | bytes 49160 | tf_op jit(solution)/shard_map/ppermute | solution.py:349
  13.2 5.5 %collective-permute-start.5 = (bf16[2,32,128]{2,1,0:T(8,128)(2,1)S(1)}, bf16[2,32,128]{2,1,0:T(8,128)(2,1)S(1)}, u32[]{:S(2)}, u32[]{:S(2)}) collective-permute-start(bf16[2,32,128]{2,1,0:T(8,128)(2,1)S(1)} %get-tuple-element.22), channel_id=1, source_target_pairs={{0,12},{4,8},{8,4},{12,0},{1,13},{5,9},{9,5},{13,1},{2,14},{6,10},... | collective-permute-start | bytes 49160 | tf_op jit(solution)/shard_map/ppermute | solution.py:349
  15.5 14.4 %copy-start = (bf16[128,128]{1,0:T(8,128)(2,1)S(1)}, bf16[128,128]{1,0:T(8,128)(2,1)}, u32[]{:S(2)}) copy-start(bf16[128,128]{1,0:T(8,128)(2,1)} %constant.11.clone.refs_6_) | copy-start | bytes 98308
  15.5 14.4 %copy-start.1 = (bf16[128,128]{1,0:T(8,128)(2,1)S(1)}, bf16[128,128]{1,0:T(8,128)(2,1)}, u32[]{:S(2)}) copy-start(bf16[128,128]{1,0:T(8,128)(2,1)} %constant.10.clone.refs_5_) | copy-start | bytes 98308
  22.8 1.9 %collective-permute-start.6 = (bf16[400,128]{1,0:T(8,128)(2,1)S(1)}, bf16[400,128]{1,0:T(8,128)(2,1)S(1)}, u32[]{:S(2)}, u32[]{:S(2)}) collective-permute-start(bf16[400,128]{1,0:T(8,128)(2,1)S(1)} %get-tuple-element.24), channel_id=1, source_target_pairs={{0,1},{1,0},{2,3},{3,2},{4,5},{5,4},{6,7},{7,6},{8,9},{9,8},{10,11... | collective-permute-start | bytes 307208 | tf_op jit(solution)/shard_map/ppermute | solution.py:349
  22.8 5.7 %collective-permute-start.7 = (bf16[400,128]{1,0:T(8,128)(2,1)S(1)}, bf16[400,128]{1,0:T(8,128)(2,1)S(1)}, u32[]{:S(2)}, u32[]{:S(2)}) collective-permute-start(bf16[400,128]{1,0:T(8,128)(2,1)S(1)} %get-tuple-element.25), channel_id=1, source_target_pairs={{0,2},{1,3},{2,0},{3,1},{4,6},{5,7},{6,4},{7,5},{8,10},{9,11},{10,... | collective-permute-start | bytes 307208 | tf_op jit(solution)/shard_map/ppermute | solution.py:349
  24.4 5.5 %collective-permute-start.8 = (bf16[400,128]{1,0:T(8,128)(2,1)S(1)}, bf16[400,128]{1,0:T(8,128)(2,1)S(1)}, u32[]{:S(2)}, u32[]{:S(2)}) collective-permute-start(bf16[400,128]{1,0:T(8,128)(2,1)S(1)} %get-tuple-element.26), channel_id=1, source_target_pairs={{0,3},{1,2},{2,1},{3,0},{4,7},{5,6},{6,5},{7,4},{8,11},{9,10},{10,... | collective-permute-start | bytes 307208 | tf_op jit(solution)/shard_map/ppermute | solution.py:349

commit v4 on v3

v4 whole, which is shorter than its diff:
```python
import functools
import math

import jax
import jax.numpy as jnp
import ml_dtypes
import numpy as np
from jax import lax
from jax.experimental import pallas as pl
from jax.experimental.pallas import tpu as pltpu
from jax.sharding import PartitionSpec as P

STEPS = 32
HSEG = 2
SEGS = HSEG + 1
LENGTH = SEGS * STEPS
GROUP = 4
HEAD = 16
UNROLL = 8

excite_rate = 0.1
inhibit_rate = 0.05
excite_excite = 1.5
inhibit_excite = 2.0
excite_inhibit = 2.0
inhibit_inhibit = 0.5
excite_offset = 0.5
inhibit_offset = 0.5
tract_gain = 2.0

SMEM = pltpu.SMEM
VMEM = pltpu.VMEM
vmem_spec = pl.BlockSpec(memory_space=VMEM)
hbm_spec = pl.BlockSpec(memory_space=pltpu.HBM)


def basis_table(coef_count, step_count):
    order = np.arange(coef_count, dtype=np.float32)[:, None]
    places = np.arange(step_count, dtype=np.float32)[None, :]
    angles = np.float32(np.pi) * (step_count - places - np.float32(0.5)) / np.float32(step_count)
    return np.cos((order * angles).astype(np.float64)).astype(np.float32)


def expand_table(coef_count):
    basis = basis_table(coef_count, STEPS).astype(ml_dtypes.bfloat16)
    table = np.zeros((LENGTH, SEGS * coef_count), ml_dtypes.bfloat16)
    for seg in range(SEGS):
        table[seg * STEPS : (seg + 1) * STEPS, seg * coef_count : (seg + 1) * coef_count] = basis.T
    return table


def fit_tables(coef_count):
    scales = np.where(np.arange(coef_count)[:, None] == 0, 1.0, 2.0) / STEPS
    fit = (basis_table(coef_count, STEPS) * scales).astype(np.float32)
    whole = np.zeros((GROUP * coef_count, GROUP * STEPS), np.float32)
    for g in range(GROUP):
        whole[g * coef_count : (g + 1) * coef_count, g * STEPS : (g + 1) * STEPS] = fit
    high = whole.astype(ml_dtypes.bfloat16)
    low = (whole - high.astype(np.float32)).astype(ml_dtypes.bfloat16)
    return high, low


TOGETHER = 8


def lane_tables(peers, peer_targets, own_blocks):
    width = TOGETHER * peer_targets
    assert TOGETHER * own_blocks <= 256 and peers * width <= HEAD * 128
    lane = np.arange(HEAD * 128)
    used = lane < peers * width
    within = lane % width
    rank = np.where(used, within // TOGETHER, -5)
    offset = within % TOGETHER * own_blocks + 1
    place = np.where(used, lane // width, -5)
    return np.stack([rank, offset, place]).astype(np.float32).reshape(3, HEAD, 128)


def prepare_kernel(
    weights_hbm, fresh_hbm, reads_hbm, state_hbm, lesion_hbm, stim_hbm, wave_hbm, slot_hbm,
    target_hbm, delay_hbm, frac_hbm, lanes_hbm, table_hbm, older_hbm,
    weights_out, fresh_out, ready_out, hist_out, tiles_out, fracs_out, head_out,
    reads, state, lesion, stim, wave, slot, target, delay, frac, lanes, table, older, sems,
    *, peers, own_blocks, peer_targets, capacity,
):
    pairs = [
        (fresh_hbm, fresh_out), (reads_hbm, reads), (target_hbm, target), (slot_hbm, slot),
        (delay_hbm, delay), (frac_hbm, frac), (lanes_hbm, lanes), (table_hbm, table),
        (older_hbm, older), (state_hbm, state), (lesion_hbm, lesion), (stim_hbm, stim),
        (wave_hbm, wave), (weights_hbm, weights_out),
    ]
    copies = [
        pltpu.make_async_copy(source, into, sems.at[i]) for i, (source, into) in enumerate(pairs)
    ]
    for copy in copies:
        copy.start()
    for copy in copies[2:7]:
        copy.wait()
    place = lax.axis_index("narrow")
    owner = lax.axis_index("wide")
    tile_count = target.shape[1]
    target_count = peers * own_blocks

    numbers = lax.broadcasted_iota(jnp.int32, (target_count, tile_count), 0)
    hits = jnp.where(numbers == target[...], 1.0, 0.0)
    held = jnp.dot(
        hits.astype(jnp.bfloat16), jnp.ones((tile_count, 128), jnp.bfloat16),
        preferred_element_type=jnp.float32,
    )
    held = jnp.minimum(held, 1.0)
    shape = (own_blocks, own_blocks)
    below = jnp.where(
        lax.broadcasted_iota(jnp.int32, shape, 0) > lax.broadcasted_iota(jnp.int32, shape, 1),
        1.0, 0.0,
    ).astype(jnp.bfloat16)
    block = lax.broadcasted_iota(jnp.int32, (own_blocks, 128), 0).astype(jnp.float32)
    ranks = jnp.zeros((1, tile_count), jnp.float32)
    head_rows = pl.cdiv(peers * TOGETHER * peer_targets, 128)
    for p in range(peers):
        part = slice(p * own_blocks, (p + 1) * own_blocks)
        rank = jnp.dot(below, held[part].astype(jnp.bfloat16), preferred_element_type=jnp.float32)
        ranks = ranks + jnp.sum(hits[part] * rank[:, :tile_count], axis=0, keepdims=True)
        rank = jnp.where(held[part] > 0.5, rank, -1.0)
        source = (place ^ p).astype(jnp.float32)
        rows = []
        for h in range(head_rows):
            match = rank == lanes[0, h : h + 1, :]
            ids = jnp.sum(jnp.where(match, block, 0.0), axis=0, keepdims=True)
            mine = lanes[2, h : h + 1, :] == source
            rows.append(jnp.where(mine, ids + lanes[1, h : h + 1, :], 0.0))
        rows.append(jnp.zeros((HEAD - head_rows, 128), jnp.float32))
        head_out[p] = jnp.concatenate(rows, axis=0).astype(jnp.bfloat16)

    across = jnp.zeros((1, tile_count), jnp.int32)
    for p in range(1, peers):
        across = across + jnp.where(target[...] >= p * own_blocks, 1, 0)
    key_row = ((peers - 1) - (across ^ place)).astype(jnp.float32)
    shape = (tile_count, tile_count)
    down = lax.broadcasted_iota(jnp.int32, shape, 0)
    along = lax.broadcasted_iota(jnp.int32, shape, 1)
    key = jnp.sum(jnp.where(down == along, key_row, 0.0), axis=1, keepdims=True)
    ahead = (key_row < key) | ((key_row == key) & (along < down))
    position = jnp.sum(jnp.where(ahead, 1.0, 0.0), axis=1, keepdims=True)
    lane = lax.broadcasted_iota(jnp.int32, (tile_count, 128), 1).astype(jnp.float32)
    chosen = jnp.where(position == lane, 1.0, 0.0)
    starts = (slot[...] * LENGTH + (LENGTH - 1) - delay[...]).astype(jnp.float32)
    index = lax.broadcasted_iota(jnp.int32, (1, tile_count), 1).astype(jnp.float32)
    facts = jnp.concatenate(
        [index, starts, (key_row * peer_targets + ranks) * TOGETHER, frac[...], jnp.zeros((4, tile_count), jnp.float32)],
        axis=0,
    )
    ordered = jnp.dot(
        facts, chosen, precision=lax.Precision.HIGHEST, preferred_element_type=jnp.float32
    )
    fracs_out[...] = ordered
    tiles_out[...] = (ordered + 0.5).astype(jnp.int32)
    tiles_out[3:4, :] = jnp.sum(
        jnp.where(key < lane, 1.0, 0.0), axis=0, keepdims=True
    ).astype(jnp.int32)

    for copy in copies[7:9]:
        copy.wait()
    coef_count = older.shape[2]
    earlier = HSEG * STEPS
    for s in range(older.shape[0]):
        segments = [older[s, h] for h in range(HSEG - 1, -1, -1)]
        hist_out[s * LENGTH : s * LENGTH + earlier, :] = jnp.dot(
            table[:earlier, : HSEG * coef_count], jnp.concatenate(segments, axis=0),
            preferred_element_type=jnp.float32,
        )
        hist_out[s * LENGTH + earlier : (s + 1) * LENGTH, :] = jnp.zeros(
            (STEPS, hist_out.shape[1]), jnp.float32
        )
    for copy in copies[:2]:
        copy.wait()
    for c in range(capacity):
        rows = pl.ds(pl.multiple_of((owner * capacity + c) * LENGTH + earlier, 8), STEPS)
        hist_out[rows, :] = jnp.dot(
            table[:STEPS, :coef_count], fresh_out[jnp.maximum(reads[c, owner], 0)],
            preferred_element_type=jnp.float32,
        )

    for copy in copies[9:13]:
        copy.wait()
    block_rows = lesion.shape[1]
    for b in range(own_blocks):
        piece = state[:, b * block_rows : (b + 1) * block_rows]
        ready_out[b : b + 1, :] = piece[0:1, :]
        ready_out[own_blocks + b : own_blocks + b + 1, :] = piece[1:2, :]
    ready_out[2 * own_blocks : 3 * own_blocks, :] = tract_gain * (
        1.0 - lesion[...].astype(jnp.float32)
    )
    stim_count = stim.shape[1]
    nodes = stim[...] - (owner * peers + place) * (own_blocks * block_rows)
    blocks = lax.shift_right_arithmetic(nodes, block_rows.bit_length() - 1)
    offsets = nodes & (block_rows - 1)
    in_block = lax.broadcasted_iota(jnp.int32, (own_blocks, stim_count), 0) == blocks
    at_offset = lax.broadcasted_iota(jnp.int32, (block_rows, stim_count), 0) == offsets
    ready_out[3 * own_blocks : 4 * own_blocks, :] = lax.dot_general(
        jnp.where(in_block, 1.0, 0.0).astype(jnp.bfloat16),
        jnp.where(at_offset, 1.0, 0.0).astype(jnp.bfloat16),
        (((1,), (1,)), ((), ())),
        preferred_element_type=jnp.float32,
    )
    shape = (STEPS, STEPS)
    diagonal = lax.broadcasted_iota(jnp.int32, shape, 0) == lax.broadcasted_iota(jnp.int32, shape, 1)
    column = jnp.sum(jnp.where(diagonal, wave[...], 0.0), axis=1, keepdims=True)
    ready_out[4 * own_blocks :, :] = jnp.broadcast_to(column, (STEPS, block_rows))
    copies[13].wait()


def pick_kernel(*refs, capacity, peers):
    tables = refs[: peers - 1]
    fresh = refs[peers - 1]
    outs = refs[peers : 2 * peers - 1]
    asked, sems = refs[2 * peers - 1 :]
    place = lax.axis_index("wide")
    copies = [pltpu.make_async_copy(tables[r], asked.at[r], sems.at[r]) for r in range(peers - 1)]
    for copy in copies:
        copy.start()
    for r in range(peers - 1):
        copies[r].wait()
        for c in range(capacity):
            outs[r][c] = fresh[jnp.maximum(asked[r, c, place], 0)]


def tract_kernel(
    tiles_ref, fracs_ref, table_ref, head_ref, weights, hist_ref, *refs,
    parts, wide_peers, peers, capacity, peer_targets,
):
    place = lax.axis_index("narrow")
    owner = lax.axis_index("wide")
    tiles, fracs, total, sems = refs[-4:]
    if parts[0] == 0:
        news = refs[: wide_peers - 1]
        outs = refs[wide_peers - 1 : -5]
        hist = refs[-5]
        hist[...] = hist_ref[...]
    else:
        news = []
        outs = refs[:-4]
        hist = hist_ref
    copies = [
        pltpu.make_async_copy(tiles_ref, tiles, sems.at[0]),
        pltpu.make_async_copy(fracs_ref, fracs, sems.at[1]),
    ]
    for copy in copies:
        copy.start()
    total[...] = jnp.zeros_like(total)
    for i, block in enumerate(news):
        table = table_ref[:STEPS, : block.shape[1]]
        for c in range(capacity):
            slot = (owner ^ (wide_peers - 1 - i)) * capacity + c
            rows = pl.ds(pl.multiple_of(slot * LENGTH + HSEG * STEPS, 8), STEPS)
            hist[rows, :] = jnp.dot(table, block[c], preferred_element_type=jnp.float32)
    for copy in copies:
        copy.wait()
    begin = tiles[3, parts[0]]
    end = tiles[3, parts[-1] + 1]
    spare = len(parts) * peer_targets * TOGETHER
    pitch = spare + TOGETHER

    @pl.loop(0, lax.div(end - begin + (UNROLL - 1), UNROLL))
    def _(turn):
        sums = []
        for u in range(UNROLL):
            t = begin + turn * UNROLL + u
            fraction = fracs[3, t]
            start = tiles[1, t]
            earlier = hist[pl.ds(start, STEPS), :]
            later = hist[pl.ds(start + 1, STEPS), :]
            delayed = ((1.0 - fraction) * later + fraction * earlier).astype(jnp.bfloat16)
            sums.append(
                lax.dot_general(
                    delayed, weights[tiles[0, t]], (((1,), (1,)), ((), ())),
                    preferred_element_type=jnp.float32,
                )
            )
        for u in range(UNROLL):
            t = begin + turn * UNROLL + u
            first = jnp.where(t < end, tiles[2, t] - parts[0] * peer_targets * TOGETHER, spare)
            for g in range(STEPS // TOGETHER):
                rows = pl.ds(pl.multiple_of(g * pitch + first, 8), TOGETHER)
                total[rows, :] += sums[u][g * TOGETHER : (g + 1) * TOGETHER]

    span = peer_targets * TOGETHER
    for i, part in enumerate(parts):
        for g in range(STEPS // TOGETHER):
            first = g * pitch + i * span
            outs[i][g * span : (g + 1) * span, :] = total[first : first + span, :].astype(
                jnp.bfloat16
            )
        outs[i][peer_targets * STEPS :, :] = head_ref[place ^ (peers - 1 - part)]


def window_kernel(*refs, peers, own_blocks, peer_targets, coef_count):
    shares = refs[:peers][::-1]
    ready_ref, high_ref, low_ref, coefs_out, state_out, samples, rates = refs[peers:]
    block_rows = ready_ref.shape[1]
    width = TOGETHER * peer_targets
    span = peer_targets * STEPS

    head = shares[0][span:, :].astype(jnp.float32)
    for r in range(1, peers):
        head = head + shares[r][span:, :].astype(jnp.float32)
    row = lax.broadcasted_iota(jnp.int32, (TOGETHER * own_blocks, 128), 0).astype(jnp.float32) + 1.0
    columns = peers * width
    scatter = jnp.concatenate(
        [
            jnp.where(row == head[h : h + 1, :], 1.0, 0.0).astype(jnp.bfloat16)
            for h in range(pl.cdiv(columns, 128))
        ],
        axis=1,
    )[:, :columns]

    excite, inhibit, gain, counts = [
        ready_ref[i * own_blocks : (i + 1) * own_blocks, :] for i in range(4)
    ]
    for pair in range(0, STEPS // TOGETHER, 2):
        arrived = jnp.concatenate(
            [
                jnp.concatenate(
                    [shares[r][g * width : (g + 1) * width, :] for r in range(peers)], axis=0
                )
                for g in (pair, pair + 1)
            ],
            axis=1,
        )
        inflow = jnp.dot(scatter, arrived, preferred_element_type=jnp.float32)
        for jj in range(2 * TOGETHER):
            j = pair * TOGETHER + jj
            wave = ready_ref[4 * own_blocks + j : 4 * own_blocks + j + 1, :]
            first = jj % TOGETHER * own_blocks
            left = jj // TOGETHER * block_rows
            forcing = (
                gain * inflow[first : first + own_blocks, left : left + block_rows] + wave * counts
            )
            excite_drive = (
                excite_excite * excite - inhibit_excite * inhibit + forcing - excite_offset
            )
            inhibit_drive = excite_inhibit * excite - inhibit_inhibit * inhibit - inhibit_offset
            excite, inhibit = (
                excite + excite_rate * (0.5 * jnp.tanh(0.5 * excite_drive) + 0.5 - excite),
                inhibit + inhibit_rate * (0.5 * jnp.tanh(0.5 * inhibit_drive) + 0.5 - inhibit),
            )
            samples[pl.ds(j, own_blocks, stride=STEPS), :] = excite
    rates[0] = excite
    rates[1] = inhibit
    for b in range(own_blocks):
        where = slice(b * block_rows, (b + 1) * block_rows)
        state_out[0:1, where] = rates[0, b : b + 1, :]
        state_out[1:2, where] = rates[1, b : b + 1, :]

    high = high_ref[...]
    low = low_ref[...]
    rows = GROUP * STEPS
    for g in range(own_blocks // GROUP):
        part = samples[g * rows : (g + 1) * rows, :]
        part_high = part.astype(jnp.bfloat16)
        part_low = (part - part_high.astype(jnp.float32)).astype(jnp.bfloat16)
        fitted = (
            jnp.dot(high, part_high, preferred_element_type=jnp.float32)
            + jnp.dot(high, part_low, preferred_element_type=jnp.float32)
            + jnp.dot(low, part_high, preferred_element_type=jnp.float32)
        )
        coefs_out[g * GROUP : (g + 1) * GROUP] = fitted.astype(jnp.bfloat16).reshape(
            GROUP, coef_count, block_rows
        )


def far(x):
    return pltpu.with_memory_space_constraint(x, pltpu.HBM)


def params():
    return pltpu.CompilerParams(vmem_limit_bytes=20 << 20)


def local(
    fresh_coefs,
    older_coefs,
    state,
    lesion,
    stim_nodes,
    stim_wave,
    read_blocks,
    tract_slot,
    tract_target,
    tract_delay,
    tract_frac,
    tract_weights,
):
    wide_peers = lax.axis_size("wide")
    peers = lax.axis_size("narrow")
    own_blocks, coef_count, block_rows = fresh_coefs.shape
    capacity = read_blocks.shape[3]
    slot_count = wide_peers * capacity
    tile_count = tract_slot.shape[2]
    peer_targets = tile_count // (2 * peers)
    share_rows = peer_targets * STEPS + HEAD

    def swap(x, axis, r):
        return lax.ppermute(x, axis, [(i, i ^ r) for i in range(lax.axis_size(axis))])

    reads = read_blocks.reshape(wide_peers, capacity).T
    asked = [swap(reads, "wide", r) for r in range(1, wide_peers)]

    vmem_inputs = [
        VMEM(state.shape, jnp.float32),
        VMEM((own_blocks, block_rows), jnp.int32),
        VMEM((1, stim_nodes.shape[0]), jnp.int32),
        VMEM((1, STEPS), jnp.float32),
        VMEM((1, tile_count), jnp.int32),
        VMEM((1, tile_count), jnp.int32),
        VMEM((1, tile_count), jnp.int32),
        VMEM((1, tile_count), jnp.float32),
        VMEM((3, HEAD, 128), jnp.float32),
        VMEM((LENGTH, SEGS * coef_count), jnp.bfloat16),
        VMEM((slot_count, HSEG, coef_count, block_rows), jnp.bfloat16),
    ]
    table = far(jnp.asarray(expand_table(coef_count)))
    weights, fresh, ready, hist, tiles, fracs, heads = pl.pallas_call(
        functools.partial(
            prepare_kernel,
            peers=peers, own_blocks=own_blocks, peer_targets=peer_targets, capacity=capacity,
        ),
        out_shape=[
            pltpu.VMEM((tile_count, block_rows, block_rows), jnp.bfloat16),
            pltpu.VMEM(fresh_coefs.shape, jnp.bfloat16),
            pltpu.VMEM((4 * own_blocks + STEPS, block_rows), jnp.float32),
            pltpu.VMEM((slot_count * LENGTH, block_rows), jnp.float32),
            pltpu.VMEM((8, 128), jnp.int32),
            pltpu.VMEM((8, 128), jnp.float32),
            pltpu.VMEM((peers, HEAD, 128), jnp.bfloat16),
        ],
        in_specs=[hbm_spec] * 14,
        out_specs=[vmem_spec] * 7,
        scratch_shapes=[
            SMEM((capacity, wide_peers), jnp.int32),
            *vmem_inputs,
            pltpu.SemaphoreType.DMA((14,)),
        ],
        compiler_params=params(),
        name="prepare",
    )(
        far(tract_weights.reshape(tile_count, block_rows, block_rows)),
        far(fresh_coefs),
        far(reads),
        far(state),
        far(lesion.reshape(own_blocks, block_rows)),
        far(stim_nodes.reshape(1, -1)),
        far(stim_wave.reshape(1, -1)),
        far(tract_slot.reshape(1, tile_count)),
        far(tract_target.reshape(1, tile_count)),
        far(tract_delay.reshape(1, tile_count)),
        far(tract_frac.reshape(1, tile_count)),
        far(jnp.asarray(lane_tables(peers, peer_targets, own_blocks))),
        table,
        far(older_coefs.reshape(slot_count, HSEG, coef_count, block_rows)),
    )

    picked = pl.pallas_call(
        functools.partial(pick_kernel, capacity=capacity, peers=wide_peers),
        out_shape=[pltpu.VMEM((capacity, coef_count, block_rows), jnp.bfloat16)]
        * (wide_peers - 1),
        in_specs=[vmem_spec] * wide_peers,
        out_specs=[vmem_spec] * (wide_peers - 1),
        scratch_shapes=[
            SMEM((wide_peers - 1, capacity, wide_peers), jnp.int32),
            pltpu.SemaphoreType.DMA((wide_peers - 1,)),
        ],
        compiler_params=params(),
        name="pick_blocks",
    )(*asked, fresh)
    news = [swap(picked[r - 1], "wide", r) for r in range(wide_peers - 1, 0, -1)]

    shares = [None] * peers
    half = (peers + 1) // 2
    for parts in (range(half), range(half, peers)):
        blocks = news if parts[0] == 0 else []
        result = pl.pallas_call(
            functools.partial(
                tract_kernel,
                parts=parts, wide_peers=wide_peers, peers=peers, capacity=capacity,
                peer_targets=peer_targets,
            ),
            out_shape=[pltpu.VMEM((share_rows, block_rows), jnp.bfloat16)] * len(parts)
            + ([pltpu.VMEM(hist.shape, jnp.float32)] if parts[0] == 0 else []),
            in_specs=[vmem_spec] * (6 + len(blocks)),
            out_specs=[vmem_spec] * (len(parts) + (parts[0] == 0)),
            scratch_shapes=[
                SMEM((8, 128), jnp.int32),
                SMEM((8, 128), jnp.float32),
                VMEM(((len(parts) * peer_targets + 1) * STEPS, block_rows), jnp.float32),
                pltpu.SemaphoreType.DMA((2,)),
            ],
            compiler_params=params(),
            name=f"tract_tiles_{parts[0]}",
        )(tiles, fracs, table, heads, weights, hist, *blocks)
        if parts[0] == 0:
            hist = result[-1]
        for i, part in enumerate(parts):
            shares[peers - 1 - part] = result[i]
    arrived = [shares[0]] + [swap(shares[r], "narrow", r) for r in range(1, peers)]

    high, low = fit_tables(coef_count)
    new_coefs, final_state = pl.pallas_call(
        functools.partial(
            window_kernel,
            peers=peers, own_blocks=own_blocks, peer_targets=peer_targets, coef_count=coef_count,
        ),
        out_shape=[
            jax.ShapeDtypeStruct(fresh_coefs.shape, jnp.bfloat16),
            jax.ShapeDtypeStruct(state.shape, jnp.float32),
        ],
        in_specs=[vmem_spec] * (peers + 3),
        out_specs=[vmem_spec] * 2,
        scratch_shapes=[
            VMEM((own_blocks * STEPS, block_rows), jnp.float32),
            VMEM((2, own_blocks, block_rows), jnp.float32),
        ],
        compiler_params=params(),
        name="window_steps",
    )(*arrived[::-1], ready, high, low)
    return new_coefs, final_state


def solution(mesh):
    in_specs = (
        P(("sweep", "wide", "narrow"), None, None),
        P(("sweep", "wide"), "narrow", None, None, None, None),
        P(None, ("sweep", "wide", "narrow")),
        P(("sweep", "wide", "narrow")),
        P("sweep"),
        P("sweep"),
        P("wide", "narrow", None, None),
        P("wide", "narrow", None),
        P("wide", "narrow", None),
        P("wide", "narrow", None),
        P("wide", "narrow", None),
        P("wide", "narrow", None, None, None),
    )
    out_specs = (P(("sweep", "wide", "narrow"), None, None), P(None, ("sweep", "wide", "narrow")))
    return jax.shard_map(local, mesh=mesh, in_specs=in_specs, out_specs=out_specs, check_vma=False)
```

time: 32.3 us -> 34.1 us (1.056)
  waiting for transfers between devices: 7.75 us -> 9.69 us
    ppermute x9, waiting for transfers between devices: 7.75 us -> 9.69 us  [swap(): lax.ppermute(x, axis, [(i, i ^ r) for i in range(lax.axis_size(axis))])]
  transfers between devices with their start and end apart: 9 -> 9, of which waited for: 4 -> 5; matrix products, arithmetic and copies ran while one was open for 0% -> 0% of each run, Pallas kernels for 15% -> 7%
where the time goes in v4:
time: 34.1 us; the launch traced here: 33.8 us
  starting transfers between devices  12.1 us (35%)
  Pallas kernels  11.3 us (33%)
  waiting for transfers between devices  9.69 us (28%)
  between operations  0.69 us (2%)
    ppermute x9, starting transfers between devices, swap(): lax.ppermute(x, axis, [(i, i ^ r) for i in range(lax.axis_size(axis))])  12.1 us
    ppermute x9, waiting for transfers between devices, swap(): lax.ppermute(x, axis, [(i, i ^ r) for i in range(lax.axis_size(axis))])  9.69 us
    pallas_call x2, Pallas kernels, local(): pl.pallas_call(functools.partial(tract_kernel, parts=parts, wide_peers=wi...  6.27 us
    pallas_call x1, Pallas kernels, local(): pl.pallas_call(functools.partial(prepare_kernel, peers=peers, own_blocks=...  2.3 us
    pallas_call x1, Pallas kernels, local(): pl.pallas_call(functools.partial(window_kernel, peers=peers, own_blocks=o...  2.14 us
  transfers between devices with their start and end apart: 9, of which 5 were waited for; matrix products, arithmetic and copies ran while one was open for 0% of the time, Pallas kernels for 7%

profile of v4, /device:TPU:0, one launch (start us, length us, event | category | flops | bytes accessed | tf_op | source)
XLA Modules:
  0.0 33.8 jit_solution(15392085415767939848)
XLA Ops:
  0.6 5.1 %collective-permute-start.2 = (s32[2,4]{1,0:T(2,128)}, s32[2,4]{1,0:T(2,128)S(1)}, u32[]{:S(2)}, u32[]{:S(2)}) collective-permute-start(s32[2,4]{1,0:T(2,128)} %bitcast.15), channel_id=1, source_target_pairs={{0,12},{4,8},{8,4},{12,0},{1,13},{5,9},{9,5},{13,1},{2,14},{6,10},... | collective-permute-start | bytes 104 | tf_op jit(solution)/shard_map/ppermute | solution.py:402
  5.7 0.0 collective-permute-start.1
  5.8 0.6 %collective-permute-start = (s32[2,4]{1,0:T(2,128)}, s32[2,4]{1,0:T(2,128)S(1)}, u32[]{:S(2)}, u32[]{:S(2)}) collective-permute-start(s32[2,4]{1,0:T(2,128)} %bitcast.17), channel_id=1, source_target_pairs={{0,4},{4,0},{8,12},{12,8},{1,5},{5,1},{9,13},{13,9},{2,6},{6,2},{1... | collective-permute-start | bytes 104 | tf_op jit(solution)/shard_map/ppermute | solution.py:402
  6.4 2.3 %prepare.1 = (bf16[96,128,128]{2,1,0:T(8,128)(2,1)S(1)}, bf16[32,32,128]{2,1,0:T(8,128)(2,1)S(1)}, f32[160,128]{1,0:T(8,128)S(1)}, f32[768,128]{1,0:T(8,128)S(1)...) custom-call(bf16[96,128,128]{2,1,0:T(8,128)(2,1)} %bitcast.12, ...), custom_call_target="tpu_custom_call" | custom-call | tf_op jit(solution)/shard_map/prepare/pallas_call | solution.py:421
  8.7 0.0 collective-permute-done.2.refs_2_
  8.7 1.7 %collective-permute-done.1.refs_1_ = s32[2,4]{1,0:T(2,128)S(1)} collective-permute-done((s32[2,4]{1,0:T(2,128)}, s32[2,4]{1,0:T(2,128)S(1)}, u32[]{:S(2)}, u32[]{:S(2)}) %collective-permute-start.1) | collective-permute-done | bytes 64 | tf_op jit(solution)/shard_map/ppermute | solution.py:402
  10.4 0.0 collective-permute-done.refs_0_
  10.4 0.6 %pick_blocks.1 = (bf16[2,32,128]{2,1,0:T(8,128)(2,1)S(1)}, bf16[2,32,128]{2,1,0:T(8,128)(2,1)S(1)}, bf16[2,32,128]{2,1,0:T(8,128)(2,1)S(1)}) custom-call(s32[2,4]{1,0:T(2,128)S(1)} %collective-permute-done.refs_0_, s32[2,4]{1,0:T(2,128)S(1)} %collective-permute-done.1.refs_1_, s32[2,4]{1,0:T(2,128)S(1)} %collective-permute-done.2.refs_2_, ...), custom_call_target="tpu_custom_call" | custom-call | tf_op jit(solution)/shard_map/pick_blocks/pallas_call | solution.py:461
  11.1 2.1 %collective-permute-start.3 = (bf16[2,32,128]{2,1,0:T(8,128)(2,1)S(1)}, bf16[2,32,128]{2,1,0:T(8,128)(2,1)S(1)}, u32[]{:S(2)}, u32[]{:S(2)}) collective-permute-start(bf16[2,32,128]{2,1,0:T(8,128)(2,1)S(1)} %get-tuple-element.23), channel_id=1, source_target_pairs={{0,12},{4,8},{8,4},{12,0},{1,13},{5,9},{9,5},{13,1},{2,14},{6,10},... | collective-permute-start | bytes 49160 | tf_op jit(solution)/shard_map/ppermute | solution.py:402
  13.2 0.1 collective-permute-start.4
  13.2 2.3 %collective-permute-start.5 = (bf16[2,32,128]{2,1,0:T(8,128)(2,1)S(1)}, bf16[2,32,128]{2,1,0:T(8,128)(2,1)S(1)}, u32[]{:S(2)}, u32[]{:S(2)}) collective-permute-start(bf16[2,32,128]{2,1,0:T(8,128)(2,1)S(1)} %get-tuple-element.25), channel_id=1, source_target_pairs={{0,4},{4,0},{8,12},{12,8},{1,5},{5,1},{9,13},{13,9},{2,6},{6,2},{1... | collective-permute-start | bytes 49160 | tf_op jit(solution)/shard_map/ppermute | solution.py:402
  15.5 1.2 %collective-permute-done.3.refs_0_ = bf16[2,32,128]{2,1,0:T(8,128)(2,1)S(1)} collective-permute-done((bf16[2,32,128]{2,1,0:T(8,128)(2,1)S(1)}, bf16[2,32,128]{2,1,0:T(8,128)(2,1)S(1)}, u32[]{:S(2)}, u32[]{:S(2)}) %collective-permute-start.3) | collective-permute-done | bytes 16416 | tf_op jit(solution)/shard_map/ppermute | solution.py:402
  16.8 1.2 %collective-permute-done.4.refs_1_ = bf16[2,32,128]{2,1,0:T(8,128)(2,1)S(1)} collective-permute-done((bf16[2,32,128]{2,1,0:T(8,128)(2,1)S(1)}, bf16[2,32,128]{2,1,0:T(8,128)(2,1)S(1)}, u32[]{:S(2)}, u32[]{:S(2)}) %collective-permute-start.4) | collective-permute-done | bytes 16416 | tf_op jit(solution)/shard_map/ppermute | solution.py:402
  18.0 0.0 collective-permute-done.5.refs_2_
  18.0 0.0 copy-start
  18.0 0.0 copy-start.1
  18.0 3.0 %tract_tiles_0.1 = (bf16[400,128]{1,0:T(8,128)(2,1)S(1)}, bf16[400,128]{1,0:T(8,128)(2,1)S(1)}, f32[768,128]{1,0:T(8,128)S(1)}) custom-call(s32[8,128]{1,0:T(8,128)S(1)} %get-tuple-element.17.tiles_ref, f32[8,128]{1,0:T(8,128)S(1)} %get-tuple-element.18.fracs_ref, bf16[96,96]{1,0:T(8,128)(2,1)} %constant.8.clone.table_hbm.table_ref, ...), custom_call_target="tpu_custom_call" | custom-call | tf_op jit(solution)/shard_map/tract_tiles_0/pallas_call | solution.py:480
  21.0 3.3 %tract_tiles_2.1 = (bf16[400,128]{1,0:T(8,128)(2,1)S(1)}, bf16[400,128]{1,0:T(8,128)(2,1)S(1)}) custom-call(s32[8,128]{1,0:T(8,128)S(1)} %get-tuple-element.17.tiles_ref, f32[8,128]{1,0:T(8,128)S(1)} %get-tuple-element.18.fracs_ref, bf16[96,96]{1,0:T(8,128)(2,1)} %constant.8.clone.table_hbm.table_ref, bf16[4,16,128]{2,1,0:T(8,128)(2,1)S(1)} %get-tuple-element.19.head_ref, ...), custom_call_target="tpu_custom_call" | custom-call | tf_op jit(solution)/shard_map/tract_tiles_2/pallas_call | solution.py:480
  24.3 0.1 collective-permute-start.6
  24.3 1.6 %collective-permute-start.7 = (bf16[400,128]{1,0:T(8,128)(2,1)S(1)}, bf16[400,128]{1,0:T(8,128)(2,1)S(1)}, u32[]{:S(2)}, u32[]{:S(2)}) collective-permute-start(bf16[400,128]{1,0:T(8,128)(2,1)S(1)} %get-tuple-element.27), channel_id=1, source_target_pairs={{0,2},{1,3},{2,0},{3,1},{4,6},{5,7},{6,4},{7,5},{8,10},{9,11},{10,... | collective-permute-start | bytes 307208 | tf_op jit(solution)/shard_map/ppermute | solution.py:402
  25.9 0.3 collective-permute-start.8
  26.2 3.3 %collective-permute-done.6.refs_0_ = bf16[400,128]{1,0:T(8,128)(2,1)S(1)} collective-permute-done((bf16[400,128]{1,0:T(8,128)(2,1)S(1)}, bf16[400,128]{1,0:T(8,128)(2,1)S(1)}, u32[]{:S(2)}, u32[]{:S(2)}) %collective-permute-start.6) | collective-permute-done | bytes 102432 | tf_op jit(solution)/shard_map/ppermute | solution.py:402
  29.5 2.2 %collective-permute-done.7.refs_1_ = bf16[400,128]{1,0:T(8,128)(2,1)S(1)} collective-permute-done((bf16[400,128]{1,0:T(8,128)(2,1)S(1)}, bf16[400,128]{1,0:T(8,128)(2,1)S(1)}, u32[]{:S(2)}, u32[]{:S(2)}) %collective-permute-start.7) | collective-permute-done | bytes 102432 | tf_op jit(solution)/shard_map/ppermute | solution.py:402
  31.7 0.0 collective-permute-done.8.refs_2_
  31.7 0.0 copy-done
  31.7 0.0 copy-done.1
  31.7 2.1 %window_steps.1 = (bf16[32,32,128]{2,1,0:T(8,128)(2,1)}, f32[2,4096]{1,0:T(2,128)}) custom-call(bf16[400,128]{1,0:T(8,128)(2,1)S(1)} %collective-permute-done.6.refs_0_, bf16[400,128]{1,0:T(8,128)(2,1)S(1)} %collective-permute-done.7.refs_1_, bf16[400,128]{1,0:T(8,128)(2,1)S(1)} %collective-permute-done.8.refs_2_, ...), custom_call_target="tpu_custom_call" | custom-call | tf_op jit(solution)/shard_map/window_steps/pallas_call | solution.py:506
Async XLA Ops:
  0.6 8.1 %collective-permute-start.2 = (s32[2,4]{1,0:T(2,128)}, s32[2,4]{1,0:T(2,128)S(1)}, u32[]{:S(2)}, u32[]{:S(2)}) collective-permute-start(s32[2,4]{1,0:T(2,128)} %bitcast.15), channel_id=1, source_target_pairs={{0,12},{4,8},{8,4},{12,0},{1,13},{5,9},{9,5},{13,1},{2,14},{6,10},... | collective-permute-start | bytes 104 | tf_op jit(solution)/shard_map/ppermute | solution.py:402
  5.7 4.7 %collective-permute-start.1 = (s32[2,4]{1,0:T(2,128)}, s32[2,4]{1,0:T(2,128)S(1)}, u32[]{:S(2)}, u32[]{:S(2)}) collective-permute-start(s32[2,4]{1,0:T(2,128)} %bitcast.16), channel_id=1, source_target_pairs={{0,8},{4,12},{8,0},{12,4},{1,9},{5,13},{9,1},{13,5},{2,10},{6,14},... | collective-permute-start | bytes 104 | tf_op jit(solution)/shard_map/ppermute | solution.py:402
  5.8 4.7 %collective-permute-start = (s32[2,4]{1,0:T(2,128)}, s32[2,4]{1,0:T(2,128)S(1)}, u32[]{:S(2)}, u32[]{:S(2)}) collective-permute-start(s32[2,4]{1,0:T(2,128)} %bitcast.17), channel_id=1, source_target_pairs={{0,4},{4,0},{8,12},{12,8},{1,5},{5,1},{9,13},{13,9},{2,6},{6,2},{1... | collective-permute-start | bytes 104 | tf_op jit(solution)/shard_map/ppermute | solution.py:402
  11.1 5.7 %collective-permute-start.3 = (bf16[2,32,128]{2,1,0:T(8,128)(2,1)S(1)}, bf16[2,32,128]{2,1,0:T(8,128)(2,1)S(1)}, u32[]{:S(2)}, u32[]{:S(2)}) collective-permute-start(bf16[2,32,128]{2,1,0:T(8,128)(2,1)S(1)} %get-tuple-element.23), channel_id=1, source_target_pairs={{0,12},{4,8},{8,4},{12,0},{1,13},{5,9},{9,5},{13,1},{2,14},{6,10},... | collective-permute-start | bytes 49160 | tf_op jit(solution)/shard_map/ppermute | solution.py:402
  13.2 4.8 %collective-permute-start.4 = (bf16[2,32,128]{2,1,0:T(8,128)(2,1)S(1)}, bf16[2,32,128]{2,1,0:T(8,128)(2,1)S(1)}, u32[]{:S(2)}, u32[]{:S(2)}) collective-permute-start(bf16[2,32,128]{2,1,0:T(8,128)(2,1)S(1)} %get-tuple-element.24), channel_id=1, source_target_pairs={{0,8},{4,12},{8,0},{12,4},{1,9},{5,13},{9,1},{13,5},{2,10},{6,14},... | collective-permute-start | bytes 49160 | tf_op jit(solution)/shard_map/ppermute | solution.py:402
  13.2 4.7 %collective-permute-start.5 = (bf16[2,32,128]{2,1,0:T(8,128)(2,1)S(1)}, bf16[2,32,128]{2,1,0:T(8,128)(2,1)S(1)}, u32[]{:S(2)}, u32[]{:S(2)}) collective-permute-start(bf16[2,32,128]{2,1,0:T(8,128)(2,1)S(1)} %get-tuple-element.25), channel_id=1, source_target_pairs={{0,4},{4,0},{8,12},{12,8},{1,5},{5,1},{9,13},{13,9},{2,6},{6,2},{1... | collective-permute-start | bytes 49160 | tf_op jit(solution)/shard_map/ppermute | solution.py:402
  18.0 13.7 %copy-start = (bf16[128,128]{1,0:T(8,128)(2,1)S(1)}, bf16[128,128]{1,0:T(8,128)(2,1)}, u32[]{:S(2)}) copy-start(bf16[128,128]{1,0:T(8,128)(2,1)} %constant.11.clone.refs_6_) | copy-start | bytes 98308
  18.0 13.7 %copy-start.1 = (bf16[128,128]{1,0:T(8,128)(2,1)S(1)}, bf16[128,128]{1,0:T(8,128)(2,1)}, u32[]{:S(2)}) copy-start(bf16[128,128]{1,0:T(8,128)(2,1)} %constant.10.clone.refs_5_) | copy-start | bytes 98308
  24.3 5.2 %collective-permute-start.6 = (bf16[400,128]{1,0:T(8,128)(2,1)S(1)}, bf16[400,128]{1,0:T(8,128)(2,1)S(1)}, u32[]{:S(2)}, u32[]{:S(2)}) collective-permute-start(bf16[400,128]{1,0:T(8,128)(2,1)S(1)} %get-tuple-element.26), channel_id=1, source_target_pairs={{0,3},{1,2},{2,1},{3,0},{4,7},{5,6},{6,5},{7,4},{8,11},{9,10},{10,... | collective-permute-start | bytes 307208 | tf_op jit(solution)/shard_map/ppermute | solution.py:402
  24.3 7.4 %collective-permute-start.7 = (bf16[400,128]{1,0:T(8,128)(2,1)S(1)}, bf16[400,128]{1,0:T(8,128)(2,1)S(1)}, u32[]{:S(2)}, u32[]{:S(2)}) collective-permute-start(bf16[400,128]{1,0:T(8,128)(2,1)S(1)} %get-tuple-element.27), channel_id=1, source_target_pairs={{0,2},{1,3},{2,0},{3,1},{4,6},{5,7},{6,4},{7,5},{8,10},{9,11},{10,... | collective-permute-start | bytes 307208 | tf_op jit(solution)/shard_map/ppermute | solution.py:402
  25.9 5.8 %collective-permute-start.8 = (bf16[400,128]{1,0:T(8,128)(2,1)S(1)}, bf16[400,128]{1,0:T(8,128)(2,1)S(1)}, u32[]{:S(2)}, u32[]{:S(2)}) collective-permute-start(bf16[400,128]{1,0:T(8,128)(2,1)S(1)} %get-tuple-element.29), channel_id=1, source_target_pairs={{0,1},{1,0},{2,3},{3,2},{4,5},{5,4},{6,7},{7,6},{8,9},{9,8},{10,11... | collective-permute-start | bytes 307208 | tf_op jit(solution)/shard_map/ppermute | solution.py:402

commit v5 on v4

--- a/solution.py
+++ b/solution.py
@@ -16,7 +16,7 @@
 LENGTH = SEGS * STEPS
 GROUP = 4
 HEAD = 16
-UNROLL = 8
+UNROLL = 16
 
 excite_rate = 0.1
 inhibit_rate = 0.05
@@ -75,18 +75,24 @@
     return np.stack([rank, offset, place]).astype(np.float32).reshape(3, HEAD, 128)
 
 
+def fresh_kernel(fresh_hbm, fresh_out, sem):
+    copy = pltpu.make_async_copy(fresh_hbm, fresh_out, sem)
+    copy.start()
+    copy.wait()
+
+
 def prepare_kernel(
-    weights_hbm, fresh_hbm, reads_hbm, state_hbm, lesion_hbm, stim_hbm, wave_hbm, slot_hbm,
+    fresh_ref, weights_hbm, reads_hbm, state_hbm, lesion_hbm, stim_hbm, wave_hbm, slot_hbm,
     target_hbm, delay_hbm, frac_hbm, lanes_hbm, table_hbm, older_hbm,
-    weights_out, fresh_out, ready_out, hist_out, tiles_out, fracs_out, head_out,
+    weights_out, ready_out, hist_out, tiles_out, fracs_out, head_out,
     reads, state, lesion, stim, wave, slot, target, delay, frac, lanes, table, older, sems,
     *, peers, own_blocks, peer_targets, capacity,
 ):
     pairs = [
-        (fresh_hbm, fresh_out), (reads_hbm, reads), (target_hbm, target), (slot_hbm, slot),
+        (weights_hbm, weights_out), (reads_hbm, reads), (target_hbm, target), (slot_hbm, slot),
         (delay_hbm, delay), (frac_hbm, frac), (lanes_hbm, lanes), (table_hbm, table),
         (older_hbm, older), (state_hbm, state), (lesion_hbm, lesion), (stim_hbm, stim),
-        (wave_hbm, wave), (weights_hbm, weights_out),
+        (wave_hbm, wave),
     ]
     copies = [
         pltpu.make_async_copy(source, into, sems.at[i]) for i, (source, into) in enumerate(pairs)
@@ -170,12 +176,11 @@
         hist_out[s * LENGTH + earlier : (s + 1) * LENGTH, :] = jnp.zeros(
             (STEPS, hist_out.shape[1]), jnp.float32
         )
-    for copy in copies[:2]:
-        copy.wait()
+    copies[1].wait()
     for c in range(capacity):
         rows = pl.ds(pl.multiple_of((owner * capacity + c) * LENGTH + earlier, 8), STEPS)
         hist_out[rows, :] = jnp.dot(
-            table[:STEPS, :coef_count], fresh_out[jnp.maximum(reads[c, owner], 0)],
+            table[:STEPS, :coef_count], fresh_ref[jnp.maximum(reads[c, owner], 0)],
             preferred_element_type=jnp.float32,
         )
 
@@ -205,39 +210,48 @@
     diagonal = lax.broadcasted_iota(jnp.int32, shape, 0) == lax.broadcasted_iota(jnp.int32, shape, 1)
     column = jnp.sum(jnp.where(diagonal, wave[...], 0.0), axis=1, keepdims=True)
     ready_out[4 * own_blocks :, :] = jnp.broadcast_to(column, (STEPS, block_rows))
-    copies[13].wait()
-
-
-def pick_kernel(*refs, capacity, peers):
+    copies[0].wait()
+
+
+def pick_kernel(*refs, capacity, peers, plan):
     tables = refs[: peers - 1]
     fresh = refs[peers - 1]
-    outs = refs[peers : 2 * peers - 1]
-    asked, sems = refs[2 * peers - 1 :]
+    outs = refs[peers : peers + len(plan)]
+    asked, sems = refs[peers + len(plan) :]
     place = lax.axis_index("wide")
     copies = [pltpu.make_async_copy(tables[r], asked.at[r], sems.at[r]) for r in range(peers - 1)]
     for copy in copies:
         copy.start()
-    for r in range(peers - 1):
-        copies[r].wait()
-        for c in range(capacity):
-            outs[r][c] = fresh[jnp.maximum(asked[r, c, place], 0)]
+    for copy in copies:
+        copy.wait()
+    for out, distances in zip(outs, plan):
+        for i, distance in enumerate(distances):
+            for c in range(capacity):
+                block = jnp.maximum(asked[distance - 1, c, place], 0)
+                out[i * capacity + c] = fresh[block]
+
+
+def forward_kernel(*refs, capacity, sources, plan):
+    for out, places in zip(refs[sources + 1 :], plan):
+        for i, (source, place) in enumerate(places):
+            out[i * capacity : (i + 1) * capacity] = refs[source][
+                place * capacity : (place + 1) * capacity
+            ]
 
 
 def tract_kernel(
     tiles_ref, fracs_ref, table_ref, head_ref, weights, hist_ref, *refs,
-    parts, wide_peers, peers, capacity, peer_targets,
+    parts, plan, peers, capacity, peer_targets,
 ):
     place = lax.axis_index("narrow")
     owner = lax.axis_index("wide")
     tiles, fracs, total, sems = refs[-4:]
     if parts[0] == 0:
-        news = refs[: wide_peers - 1]
-        outs = refs[wide_peers - 1 : -5]
+        outs = refs[-5 - len(parts) : -5]
         hist = refs[-5]
         hist[...] = hist_ref[...]
     else:
-        news = []
-        outs = refs[:-4]
+        outs = refs[-4 - len(parts) : -4]
         hist = hist_ref
     copies = [
         pltpu.make_async_copy(tiles_ref, tiles, sems.at[0]),
@@ -246,12 +260,15 @@
     for copy in copies:
         copy.start()
     total[...] = jnp.zeros_like(total)
-    for i, block in enumerate(news):
+    for source, first, distance in plan:
+        block = refs[source]
         table = table_ref[:STEPS, : block.shape[1]]
         for c in range(capacity):
-            slot = (owner ^ (wide_peers - 1 - i)) * capacity + c
+            slot = (owner ^ distance) * capacity + c
             rows = pl.ds(pl.multiple_of(slot * LENGTH + HSEG * STEPS, 8), STEPS)
-            hist[rows, :] = jnp.dot(table, block[c], preferred_element_type=jnp.float32)
+            hist[rows, :] = jnp.dot(
+                table, block[first * capacity + c], preferred_element_type=jnp.float32
+            )
     for copy in copies:
         copy.wait()
     begin = tiles[3, parts[0]]
@@ -402,7 +419,20 @@
         return lax.ppermute(x, axis, [(i, i ^ r) for i in range(lax.axis_size(axis))])
 
     reads = read_blocks.reshape(wide_peers, capacity).T
-    asked = [swap(reads, "wide", r) for r in range(1, wide_peers)]
+    bits = [1 << i for i in reversed(range(wide_peers.bit_length() - 1))]
+    known = {0: reads}
+    for bit in bits:
+        known |= {distance ^ bit: swap(known[distance], "wide", bit) for distance in list(known)}
+
+    fresh = pl.pallas_call(
+        fresh_kernel,
+        out_shape=pltpu.VMEM(fresh_coefs.shape, jnp.bfloat16),
+        in_specs=[hbm_spec],
+        out_specs=vmem_spec,
+        scratch_shapes=[pltpu.SemaphoreType.DMA],
+        compiler_params=params(),
+        name="fresh_near",
+    )(far(fresh_coefs))
 
     vmem_inputs = [
         VMEM(state.shape, jnp.float32),
@@ -418,32 +448,31 @@
         VMEM((slot_count, HSEG, coef_count, block_rows), jnp.bfloat16),
     ]
     table = far(jnp.asarray(expand_table(coef_count)))
-    weights, fresh, ready, hist, tiles, fracs, heads = pl.pallas_call(
+    weights, ready, hist, tiles, fracs, heads = pl.pallas_call(
         functools.partial(
             prepare_kernel,
             peers=peers, own_blocks=own_blocks, peer_targets=peer_targets, capacity=capacity,
         ),
         out_shape=[
             pltpu.VMEM((tile_count, block_rows, block_rows), jnp.bfloat16),
-            pltpu.VMEM(fresh_coefs.shape, jnp.bfloat16),
             pltpu.VMEM((4 * own_blocks + STEPS, block_rows), jnp.float32),
             pltpu.VMEM((slot_count * LENGTH, block_rows), jnp.float32),
             pltpu.VMEM((8, 128), jnp.int32),
             pltpu.VMEM((8, 128), jnp.float32),
             pltpu.VMEM((peers, HEAD, 128), jnp.bfloat16),
         ],
-        in_specs=[hbm_spec] * 14,
-        out_specs=[vmem_spec] * 7,
+        in_specs=[vmem_spec] + [hbm_spec] * 13,
+        out_specs=[vmem_spec] * 6,
         scratch_shapes=[
             SMEM((capacity, wide_peers), jnp.int32),
             *vmem_inputs,
-            pltpu.SemaphoreType.DMA((14,)),
+            pltpu.SemaphoreType.DMA((13,)),
         ],
         compiler_params=params(),
         name="prepare",
     )(
+        fresh,
         far(tract_weights.reshape(tile_count, block_rows, block_rows)),
-        far(fresh_coefs),
         far(reads),
         far(state),
         far(lesion.reshape(own_blocks, block_rows)),
@@ -458,35 +487,65 @@
         far(older_coefs.reshape(slot_count, HSEG, coef_count, block_rows)),
     )
 
-    picked = pl.pallas_call(
-        functools.partial(pick_kernel, capacity=capacity, peers=wide_peers),
-        out_shape=[pltpu.VMEM((capacity, coef_count, block_rows), jnp.bfloat16)]
-        * (wide_peers - 1),
+    def stacked(count):
+        return pltpu.VMEM((count * capacity, coef_count, block_rows), jnp.bfloat16)
+
+    bit = bits[0]
+    sent = [(0, d) for d in range(1, wide_peers) if d & bit]
+    left = [(0, d) for d in range(1, wide_peers) if not d & bit]
+    plan = [[d for _, d in items] for items in (sent, left) if items]
+    payload, *rest = pl.pallas_call(
+        functools.partial(pick_kernel, capacity=capacity, peers=wide_peers, plan=plan),
+        out_shape=[stacked(len(items)) for items in plan],
         in_specs=[vmem_spec] * wide_peers,
-        out_specs=[vmem_spec] * (wide_peers - 1),
+        out_specs=[vmem_spec] * len(plan),
         scratch_shapes=[
             SMEM((wide_peers - 1, capacity, wide_peers), jnp.int32),
             pltpu.SemaphoreType.DMA((wide_peers - 1,)),
         ],
         compiler_params=params(),
         name="pick_blocks",
-    )(*asked, fresh)
-    news = [swap(picked[r - 1], "wide", r) for r in range(wide_peers - 1, 0, -1)]
+    )(*[known[d] for d in range(1, wide_peers)], fresh)
+    news = [swap(payload, "wide", bit)]
+    came = [(source ^ bit, d ^ bit) for source, d in sent]
+    news_plan = [(0, i, source) for i, (source, d) in enumerate(came) if d == 0]
+    for bit in bits[1:]:
+        here = [(item, (0, i)) for i, item in enumerate(left)]
+        here += [(item, (len(rest), i)) for i, item in enumerate(came) if item[1]]
+        going = [x for x in here if x[0][1] & bit]
+        staying = [x for x in here if not x[0][1] & bit]
+        plan = [[place for _, place in items] for items in (going, staying) if items]
+        payload, *rest = pl.pallas_call(
+            functools.partial(
+                forward_kernel, capacity=capacity, sources=len(rest) + 1, plan=plan
+            ),
+            out_shape=[stacked(len(places)) for places in plan],
+            in_specs=[vmem_spec] * (len(rest) + 2),
+            out_specs=[vmem_spec] * len(plan),
+            compiler_params=params(),
+            name=f"pass_on_{bit}",
+        )(*rest, news[-1], tiles)
+        news.append(swap(payload, "wide", bit))
+        came = [(source ^ bit, d ^ bit) for (source, d), _ in going]
+        left = [item for item, _ in staying]
+        news_plan += [(len(news) - 1, i, source) for i, (source, d) in enumerate(came) if d == 0]
 
     shares = [None] * peers
     half = (peers + 1) // 2
+    arrived = [None] * peers
     for parts in (range(half), range(half, peers)):
-        blocks = news if parts[0] == 0 else []
+        far_call = parts[0] == 0
+        others = news if far_call else [arrived[peers - 1]]
         result = pl.pallas_call(
             functools.partial(
                 tract_kernel,
-                parts=parts, wide_peers=wide_peers, peers=peers, capacity=capacity,
-                peer_targets=peer_targets,
+                parts=parts, plan=news_plan if far_call else [], peers=peers,
+                capacity=capacity, peer_targets=peer_targets,
             ),
             out_shape=[pltpu.VMEM((share_rows, block_rows), jnp.bfloat16)] * len(parts)
-            + ([pltpu.VMEM(hist.shape, jnp.float32)] if parts[0] == 0 else []),
-            in_specs=[vmem_spec] * (6 + len(blocks)),
-            out_specs=[vmem_spec] * (len(parts) + (parts[0] == 0)),
+            + ([pltpu.VMEM(hist.shape, jnp.float32)] if far_call else []),
+            in_specs=[vmem_spec] * (6 + len(others)),
+            out_specs=[vmem_spec] * (len(parts) + far_call),
             scratch_shapes=[
                 SMEM((8, 128), jnp.int32),
                 SMEM((8, 128), jnp.float32),
@@ -494,13 +553,13 @@
                 pltpu.SemaphoreType.DMA((2,)),
             ],
             compiler_params=params(),
-            name=f"tract_tiles_{parts[0]}",
-        )(tiles, fracs, table, heads, weights, hist, *blocks)
-        if parts[0] == 0:
+            name="far_tiles" if far_call else "near_tiles",
+        )(tiles, fracs, table, heads, weights, hist, *others)
+        if far_call:
             hist = result[-1]
-        for i, part in enumerate(parts):
-            shares[peers - 1 - part] = result[i]
-    arrived = [shares[0]] + [swap(shares[r], "narrow", r) for r in range(1, peers)]
+        for part, share in zip(parts, result):
+            r = peers - 1 - part
+            arrived[r] = swap(share, "narrow", r) if r else share
 
     high, low = fit_tables(coef_count)
     new_coefs, final_state = pl.pallas_call(

time: 34.1 us -> 35.2 us (1.032)
  Pallas kernels: 11.3 us -> 12.2 us
    pallas_call x1, Pallas kernels: 2.3 us -> 2.85 us  [local(): pl.pallas_call(functools.partial(prepare_kernel, peers=peers, own_blocks=...]
    pallas_call x2 -> x4, Pallas kernels: 6.27 us -> 6.65 us  [the longest x2 5.69 us: local(): pl.pallas_call(functools.partial(tract_kernel, parts=parts, plan=news_pla...]
    ppermute x9 -> x8, starting transfers between devices: 12.1 us -> 12.4 us  [swap(): lax.ppermute(x, axis, [(i, i ^ r) for i in range(lax.axis_size(axis))])]
    ppermute x9 -> x8, waiting for transfers between devices: 9.69 us -> 9.6 us  [swap(): lax.ppermute(x, axis, [(i, i ^ r) for i in range(lax.axis_size(axis))])]
  transfers between devices with their start and end apart: 9 -> 8, of which waited for: 5 -> 5; matrix products, arithmetic and copies ran while one was open for 0% -> 0% of each run, Pallas kernels for 7% -> 20%
where the time goes in v5:
time: 35.2 us; the launch traced here: 34.9 us
  starting transfers between devices  12.4 us (35%)
  Pallas kernels  12.2 us (35%)
  waiting for transfers between devices  9.6 us (27%)
  between operations  0.71 us (2%)
    ppermute x8, starting transfers between devices, swap(): lax.ppermute(x, axis, [(i, i ^ r) for i in range(lax.axis_size(axis))])  12.4 us
    ppermute x8, waiting for transfers between devices, swap(): lax.ppermute(x, axis, [(i, i ^ r) for i in range(lax.axis_size(axis))])  9.6 us
    pallas_call x2, Pallas kernels, local(): pl.pallas_call(functools.partial(tract_kernel, parts=parts, plan=news_pla...  5.69 us
    pallas_call x1, Pallas kernels, local(): pl.pallas_call(functools.partial(prepare_kernel, peers=peers, own_blocks=...  2.85 us
    pallas_call x1, Pallas kernels, local(): pl.pallas_call(functools.partial(window_kernel, peers=peers, own_blocks=o...  2.13 us
    pallas_call x1, Pallas kernels, local(): pl.pallas_call(fresh_kernel, out_shape=pltpu.VMEM(fresh_coefs.shape, jnp....  0.96 us
  transfers between devices with their start and end apart: 8, of which 5 were waited for; matrix products, arithmetic and copies ran while one was open for 0% of the time, Pallas kernels for 20%

profile of v5, /device:TPU:0, one launch (start us, length us, event | category | flops | bytes accessed | tf_op | source)
XLA Modules:
  0.0 34.9 jit_solution(8102703027693045930)
XLA Ops:
  0.6 4.1 %collective-permute-start.1 = (s32[2,4]{1,0:T(2,128)}, s32[2,4]{1,0:T(2,128)S(1)}, u32[]{:S(2)}, u32[]{:S(2)}) collective-permute-start(s32[2,4]{1,0:T(2,128)} %bitcast.15), channel_id=1, source_target_pairs={{0,8},{4,12},{8,0},{12,4},{1,9},{5,13},{9,1},{13,5},{2,10},{6,14},... | collective-permute-start | bytes 104 | tf_op jit(solution)/shard_map/ppermute | solution.py:419
  4.7 1.6 %collective-permute-start = (s32[2,4]{1,0:T(2,128)}, s32[2,4]{1,0:T(2,128)S(1)}, u32[]{:S(2)}, u32[]{:S(2)}) collective-permute-start(s32[2,4]{1,0:T(2,128)} %bitcast.16), channel_id=1, source_target_pairs={{0,4},{4,0},{8,12},{12,8},{1,5},{5,1},{9,13},{13,9},{2,6},{6,2},{1... | collective-permute-start | bytes 104 | tf_op jit(solution)/shard_map/ppermute | solution.py:419
  6.3 1.0 %fresh_near.1.fresh_ref.refs_3_ = bf16[32,32,128]{2,1,0:T(8,128)(2,1)S(1)} custom-call(bf16[32,32,128]{2,1,0:T(8,128)(2,1)} %fresh_hbm.1), custom_call_target="tpu_custom_call" | custom-call | tf_op jit(solution)/shard_map/fresh_near/pallas_call | solution.py:427
  7.3 0.0 collective-permute-done.1.refs_1_
  7.3 1.1 %collective-permute-start.2 = (s32[2,4]{1,0:T(2,128)S(1)}, s32[2,4]{1,0:T(2,128)S(1)}, u32[]{:S(2)}, u32[]{:S(2)}) collective-permute-start(s32[2,4]{1,0:T(2,128)S(1)} %collective-permute-done.1.refs_1_), channel_id=1, source_target_pairs={{0,4},{4,0},{8,12},{12,8},{1,5},{5,1},{9,13},{13,9},{2,6},{6,2},{1... | collective-permute-start | bytes 104 | tf_op jit(solution)/shard_map/ppermute | solution.py:419
  8.4 0.1 collective-permute-done.refs_0_
  8.5 2.4 %collective-permute-done.2.refs_2_ = s32[2,4]{1,0:T(2,128)S(1)} collective-permute-done((s32[2,4]{1,0:T(2,128)S(1)}, s32[2,4]{1,0:T(2,128)S(1)}, u32[]{:S(2)}, u32[]{:S(2)}) %collective-permute-start.2) | collective-permute-done | bytes 64 | tf_op jit(solution)/shard_map/ppermute | solution.py:419
  10.9 0.6 %pick_blocks.1 = (bf16[4,32,128]{2,1,0:T(8,128)(2,1)S(1)}, bf16[2,32,128]{2,1,0:T(8,128)(2,1)S(1)}) custom-call(s32[2,4]{1,0:T(2,128)S(1)} %collective-permute-done.refs_0_, s32[2,4]{1,0:T(2,128)S(1)} %collective-permute-done.1.refs_1_, s32[2,4]{1,0:T(2,128)S(1)} %collective-permute-done.2.refs_2_, bf16[32,32,128]{2,1,0:T(8,128)(2,1)S(1)} %fresh_near.1.fresh_ref.refs_3_), custom_call_target="tpu_custom_call" | custom-call | tf_op jit(solution)/shard_map/pick_blocks/pallas_call | solution.py:497
  11.5 2.1 %collective-permute-start.3 = (bf16[4,32,128]{2,1,0:T(8,128)(2,1)S(1)}, bf16[4,32,128]{2,1,0:T(8,128)(2,1)S(1)}, u32[]{:S(2)}, u32[]{:S(2)}) collective-permute-start(bf16[4,32,128]{2,1,0:T(8,128)(2,1)S(1)} %get-tuple-element.20), channel_id=1, source_target_pairs={{0,8},{4,12},{8,0},{12,4},{1,9},{5,13},{9,1},{13,5},{2,10},{6,14},... | collective-permute-start | bytes 98312 | tf_op jit(solution)/shard_map/ppermute | solution.py:419
  13.7 2.9 %prepare.1 = (bf16[96,128,128]{2,1,0:T(8,128)(2,1)S(1)}, f32[160,128]{1,0:T(8,128)S(1)}, f32[768,128]{1,0:T(8,128)S(1)}, s32[8,128]{1,0:T(8,128)S(1)}, f32[8,128...) custom-call(bf16[32,32,128]{2,1,0:T(8,128)(2,1)S(1)} %fresh_near.1.fresh_ref.refs_3_, bf16[96,128,128]{2,1,0:T(8,128)(2,1)} %bitcast.12, ...), custom_call_target="tpu_custom_call" | custom-call | tf_op jit(solution)/shard_map/prepare/pallas_call | solution.py:451
  16.5 0.0 collective-permute-done.3.refs_1_.refs_0_
  16.5 1.6 %collective-permute-start.4 = (bf16[4,32,128]{2,1,0:T(8,128)(2,1)S(1)}, bf16[4,32,128]{2,1,0:T(8,128)(2,1)S(1)}, u32[]{:S(2)}, u32[]{:S(2)}) collective-permute-start(bf16[4,32,128]{2,1,0:T(8,128)(2,1)S(1)} %pass_on_1.1), channel_id=1, source_target_pairs={{0,4},{4,0},{8,12},{12,8},{1,5},{5,1},{9,13},{13,9},{2,6},{6,2},{1... | collective-permute-start | bytes 98312 | tf_op jit(solution)/shard_map/ppermute | solution.py:419
  18.2 2.3 %collective-permute-done.4.refs_1_ = bf16[4,32,128]{2,1,0:T(8,128)(2,1)S(1)} collective-permute-done((bf16[4,32,128]{2,1,0:T(8,128)(2,1)S(1)}, bf16[4,32,128]{2,1,0:T(8,128)(2,1)S(1)}, u32[]{:S(2)}, u32[]{:S(2)}) %collective-permute-start.4) | collective-permute-done | bytes 32800 | tf_op jit(solution)/shard_map/ppermute | solution.py:419
  20.5 0.0 copy-start
  20.5 0.0 copy-start.1
  20.5 2.6 %far_tiles.1 = (bf16[400,128]{1,0:T(8,128)(2,1)S(1)}, bf16[400,128]{1,0:T(8,128)(2,1)S(1)}, f32[768,128]{1,0:T(8,128)S(1)}) custom-call(s32[8,128]{1,0:T(8,128)S(1)} %get-tuple-element.15.refs_2_.tiles_ref, f32[8,128]{1,0:T(8,128)S(1)} %get-tuple-element.16.fracs_ref, bf16[96,96]{1,0:T(8,128)(2,1)} %constant.8.clone.table_hbm.table_ref, ...), custom_call_target="tpu_custom_call" | custom-call | tf_op jit(solution)/shard_map/far_tiles/pallas_call | solution.py:539
  23.2 0.1 collective-permute-start.5
  23.3 1.6 %collective-permute-start.6 = (bf16[400,128]{1,0:T(8,128)(2,1)S(1)}, bf16[400,128]{1,0:T(8,128)(2,1)S(1)}, u32[]{:S(2)}, u32[]{:S(2)}) collective-permute-start(bf16[400,128]{1,0:T(8,128)(2,1)S(1)} %get-tuple-element.23), channel_id=1, source_target_pairs={{0,2},{1,3},{2,0},{3,1},{4,6},{5,7},{6,4},{7,5},{8,10},{9,11},{10,... | collective-permute-start | bytes 307208 | tf_op jit(solution)/shard_map/ppermute | solution.py:419
  24.8 3.5 %collective-permute-done.5.refs_0_ = bf16[400,128]{1,0:T(8,128)(2,1)S(1)} collective-permute-done((bf16[400,128]{1,0:T(8,128)(2,1)S(1)}, bf16[400,128]{1,0:T(8,128)(2,1)S(1)}, u32[]{:S(2)}, u32[]{:S(2)}) %collective-permute-start.5) | collective-permute-done | bytes 102432 | tf_op jit(solution)/shard_map/ppermute | solution.py:419
  28.4 3.0 %near_tiles.1 = (bf16[400,128]{1,0:T(8,128)(2,1)S(1)}, bf16[400,128]{1,0:T(8,128)(2,1)S(1)}) custom-call(s32[8,128]{1,0:T(8,128)S(1)} %get-tuple-element.15.refs_2_.tiles_ref, f32[8,128]{1,0:T(8,128)S(1)} %get-tuple-element.16.fracs_ref, bf16[96,96]{1,0:T(8,128)(2,1)} %constant.8.clone.table_hbm.table_ref, ...), custom_call_target="tpu_custom_call" | custom-call | tf_op jit(solution)/shard_map/near_tiles/pallas_call | solution.py:539
  31.4 0.2 collective-permute-start.7
  31.6 0.0 collective-permute-done.6.refs_1_
  31.6 1.2 %collective-permute-done.7.refs_2_ = bf16[400,128]{1,0:T(8,128)(2,1)S(1)} collective-permute-done((bf16[400,128]{1,0:T(8,128)(2,1)S(1)}, bf16[400,128]{1,0:T(8,128)(2,1)S(1)}, u32[]{:S(2)}, u32[]{:S(2)}) %collective-permute-start.7) | collective-permute-done | bytes 102432 | tf_op jit(solution)/shard_map/ppermute | solution.py:419
  32.8 0.0 copy-done
  32.8 0.0 copy-done.1
  32.8 2.1 %window_steps.1 = (bf16[32,32,128]{2,1,0:T(8,128)(2,1)}, f32[2,4096]{1,0:T(2,128)}) custom-call(bf16[400,128]{1,0:T(8,128)(2,1)S(1)} %collective-permute-done.5.refs_0_, bf16[400,128]{1,0:T(8,128)(2,1)S(1)} %collective-permute-done.6.refs_1_, bf16[400,128]{1,0:T(8,128)(2,1)S(1)} %collective-permute-done.7.refs_2_, ...), custom_call_target="tpu_custom_call" | custom-call | tf_op jit(solution)/shard_map/window_steps/pallas_call | solution.py:565
  (1 shorter events, 0.0 us)
Async XLA Ops:
  0.6 6.6 %collective-permute-start.1 = (s32[2,4]{1,0:T(2,128)}, s32[2,4]{1,0:T(2,128)S(1)}, u32[]{:S(2)}, u32[]{:S(2)}) collective-permute-start(s32[2,4]{1,0:T(2,128)} %bitcast.15), channel_id=1, source_target_pairs={{0,8},{4,12},{8,0},{12,4},{1,9},{5,13},{9,1},{13,5},{2,10},{6,14},... | collective-permute-start | bytes 104 | tf_op jit(solution)/shard_map/ppermute | solution.py:419
  4.7 3.8 %collective-permute-start = (s32[2,4]{1,0:T(2,128)}, s32[2,4]{1,0:T(2,128)S(1)}, u32[]{:S(2)}, u32[]{:S(2)}) collective-permute-start(s32[2,4]{1,0:T(2,128)} %bitcast.16), channel_id=1, source_target_pairs={{0,4},{4,0},{8,12},{12,8},{1,5},{5,1},{9,13},{13,9},{2,6},{6,2},{1... | collective-permute-start | bytes 104 | tf_op jit(solution)/shard_map/ppermute | solution.py:419
  7.3 3.6 %collective-permute-start.2 = (s32[2,4]{1,0:T(2,128)S(1)}, s32[2,4]{1,0:T(2,128)S(1)}, u32[]{:S(2)}, u32[]{:S(2)}) collective-permute-start(s32[2,4]{1,0:T(2,128)S(1)} %collective-permute-done.1.refs_1_), channel_id=1, source_target_pairs={{0,4},{4,0},{8,12},{12,8},{1,5},{5,1},{9,13},{13,9},{2,6},{6,2},{1... | collective-permute-start | bytes 104 | tf_op jit(solution)/shard_map/ppermute | solution.py:419
  11.5 5.0 %collective-permute-start.3 = (bf16[4,32,128]{2,1,0:T(8,128)(2,1)S(1)}, bf16[4,32,128]{2,1,0:T(8,128)(2,1)S(1)}, u32[]{:S(2)}, u32[]{:S(2)}) collective-permute-start(bf16[4,32,128]{2,1,0:T(8,128)(2,1)S(1)} %get-tuple-element.20), channel_id=1, source_target_pairs={{0,8},{4,12},{8,0},{12,4},{1,9},{5,13},{9,1},{13,5},{2,10},{6,14},... | collective-permute-start | bytes 98312 | tf_op jit(solution)/shard_map/ppermute | solution.py:419
  16.5 4.0 %collective-permute-start.4 = (bf16[4,32,128]{2,1,0:T(8,128)(2,1)S(1)}, bf16[4,32,128]{2,1,0:T(8,128)(2,1)S(1)}, u32[]{:S(2)}, u32[]{:S(2)}) collective-permute-start(bf16[4,32,128]{2,1,0:T(8,128)(2,1)S(1)} %pass_on_1.1), channel_id=1, source_target_pairs={{0,4},{4,0},{8,12},{12,8},{1,5},{5,1},{9,13},{13,9},{2,6},{6,2},{1... | collective-permute-start | bytes 98312 | tf_op jit(solution)/shard_map/ppermute | solution.py:419
  20.5 12.3 %copy-start = (bf16[128,128]{1,0:T(8,128)(2,1)S(1)}, bf16[128,128]{1,0:T(8,128)(2,1)}, u32[]{:S(2)}) copy-start(bf16[128,128]{1,0:T(8,128)(2,1)} %constant.11.clone.refs_6_) | copy-start | bytes 98308
  20.5 12.3 %copy-start.1 = (bf16[128,128]{1,0:T(8,128)(2,1)S(1)}, bf16[128,128]{1,0:T(8,128)(2,1)}, u32[]{:S(2)}) copy-start(bf16[128,128]{1,0:T(8,128)(2,1)} %constant.10.clone.refs_5_) | copy-start | bytes 98308
  23.2 5.2 %collective-permute-start.5 = (bf16[400,128]{1,0:T(8,128)(2,1)S(1)}, bf16[400,128]{1,0:T(8,128)(2,1)S(1)}, u32[]{:S(2)}, u32[]{:S(2)}) collective-permute-start(bf16[400,128]{1,0:T(8,128)(2,1)S(1)} %get-tuple-element.22), channel_id=1, source_target_pairs={{0,3},{1,2},{2,1},{3,0},{4,7},{5,6},{6,5},{7,4},{8,11},{9,10},{10,... | collective-permute-start | bytes 307208 | tf_op jit(solution)/shard_map/ppermute | solution.py:419
  23.3 8.3 %collective-permute-start.6 = (bf16[400,128]{1,0:T(8,128)(2,1)S(1)}, bf16[400,128]{1,0:T(8,128)(2,1)S(1)}, u32[]{:S(2)}, u32[]{:S(2)}) collective-permute-start(bf16[400,128]{1,0:T(8,128)(2,1)S(1)} %get-tuple-element.23), channel_id=1, source_target_pairs={{0,2},{1,3},{2,0},{3,1},{4,6},{5,7},{6,4},{7,5},{8,10},{9,11},{10,... | collective-permute-start | bytes 307208 | tf_op jit(solution)/shard_map/ppermute | solution.py:419
  31.4 1.4 %collective-permute-start.7 = (bf16[400,128]{1,0:T(8,128)(2,1)S(1)}, bf16[400,128]{1,0:T(8,128)(2,1)S(1)}, u32[]{:S(2)}, u32[]{:S(2)}) collective-permute-start(bf16[400,128]{1,0:T(8,128)(2,1)S(1)} %get-tuple-element.25), channel_id=1, source_target_pairs={{0,1},{1,0},{2,3},{3,2},{4,5},{5,4},{6,7},{7,6},{8,9},{9,8},{10,11... | collective-permute-start | bytes 307208 | tf_op jit(solution)/shard_map/ppermute | solution.py:419

commit v6 on v4

--- a/solution.py
+++ b/solution.py
@@ -16,7 +16,7 @@
 LENGTH = SEGS * STEPS
 GROUP = 4
 HEAD = 16
-UNROLL = 8
+UNROLL = 16
 
 excite_rate = 0.1
 inhibit_rate = 0.05
@@ -76,24 +76,23 @@
 
 
 def prepare_kernel(
-    weights_hbm, fresh_hbm, reads_hbm, state_hbm, lesion_hbm, stim_hbm, wave_hbm, slot_hbm,
-    target_hbm, delay_hbm, frac_hbm, lanes_hbm, table_hbm, older_hbm,
-    weights_out, fresh_out, ready_out, hist_out, tiles_out, fracs_out, head_out,
-    reads, state, lesion, stim, wave, slot, target, delay, frac, lanes, table, older, sems,
+    fresh_hbm, reads_hbm, state_hbm, lesion_hbm, stim_hbm, wave_hbm, slot_hbm, target_hbm,
+    delay_hbm, lanes_hbm, table_hbm, older_hbm,
+    fresh_out, ready_out, hist_out, tiles_out, head_out,
+    reads, state, lesion, stim, wave, slot, target, delay, lanes, table, older, sems,
     *, peers, own_blocks, peer_targets, capacity,
 ):
     pairs = [
         (fresh_hbm, fresh_out), (reads_hbm, reads), (target_hbm, target), (slot_hbm, slot),
-        (delay_hbm, delay), (frac_hbm, frac), (lanes_hbm, lanes), (table_hbm, table),
-        (older_hbm, older), (state_hbm, state), (lesion_hbm, lesion), (stim_hbm, stim),
-        (wave_hbm, wave), (weights_hbm, weights_out),
+        (delay_hbm, delay), (lanes_hbm, lanes), (table_hbm, table), (older_hbm, older),
+        (state_hbm, state), (lesion_hbm, lesion), (stim_hbm, stim), (wave_hbm, wave),
     ]
     copies = [
         pltpu.make_async_copy(source, into, sems.at[i]) for i, (source, into) in enumerate(pairs)
     ]
     for copy in copies:
         copy.start()
-    for copy in copies[2:7]:
+    for copy in copies[2:6]:
         copy.wait()
     place = lax.axis_index("narrow")
     owner = lax.axis_index("wide")
@@ -133,31 +132,10 @@
     across = jnp.zeros((1, tile_count), jnp.int32)
     for p in range(1, peers):
         across = across + jnp.where(target[...] >= p * own_blocks, 1, 0)
-    key_row = ((peers - 1) - (across ^ place)).astype(jnp.float32)
-    shape = (tile_count, tile_count)
-    down = lax.broadcasted_iota(jnp.int32, shape, 0)
-    along = lax.broadcasted_iota(jnp.int32, shape, 1)
-    key = jnp.sum(jnp.where(down == along, key_row, 0.0), axis=1, keepdims=True)
-    ahead = (key_row < key) | ((key_row == key) & (along < down))
-    position = jnp.sum(jnp.where(ahead, 1.0, 0.0), axis=1, keepdims=True)
-    lane = lax.broadcasted_iota(jnp.int32, (tile_count, 128), 1).astype(jnp.float32)
-    chosen = jnp.where(position == lane, 1.0, 0.0)
-    starts = (slot[...] * LENGTH + (LENGTH - 1) - delay[...]).astype(jnp.float32)
-    index = lax.broadcasted_iota(jnp.int32, (1, tile_count), 1).astype(jnp.float32)
-    facts = jnp.concatenate(
-        [index, starts, (key_row * peer_targets + ranks) * TOGETHER, frac[...], jnp.zeros((4, tile_count), jnp.float32)],
-        axis=0,
-    )
-    ordered = jnp.dot(
-        facts, chosen, precision=lax.Precision.HIGHEST, preferred_element_type=jnp.float32
-    )
-    fracs_out[...] = ordered
-    tiles_out[...] = (ordered + 0.5).astype(jnp.int32)
-    tiles_out[3:4, :] = jnp.sum(
-        jnp.where(key < lane, 1.0, 0.0), axis=0, keepdims=True
-    ).astype(jnp.int32)
-
-    for copy in copies[7:9]:
+    tiles_out[0:1, :tile_count] = slot[...] * LENGTH + (LENGTH - 1) - delay[...]
+    tiles_out[1:2, :tile_count] = (across * peer_targets + ranks.astype(jnp.int32)) * TOGETHER
+
+    for copy in copies[6:8]:
         copy.wait()
     coef_count = older.shape[2]
     earlier = HSEG * STEPS
@@ -179,7 +157,7 @@
             preferred_element_type=jnp.float32,
         )
 
-    for copy in copies[9:13]:
+    for copy in copies[8:12]:
         copy.wait()
     block_rows = lesion.shape[1]
     for b in range(own_blocks):
@@ -205,7 +183,12 @@
     diagonal = lax.broadcasted_iota(jnp.int32, shape, 0) == lax.broadcasted_iota(jnp.int32, shape, 1)
     column = jnp.sum(jnp.where(diagonal, wave[...], 0.0), axis=1, keepdims=True)
     ready_out[4 * own_blocks :, :] = jnp.broadcast_to(column, (STEPS, block_rows))
-    copies[13].wait()
+
+
+def weights_kernel(weights_hbm, weights_out, sem):
+    copy = pltpu.make_async_copy(weights_hbm, weights_out, sem)
+    copy.start()
+    copy.wait()
 
 
 def pick_kernel(*refs, capacity, peers):
@@ -224,28 +207,22 @@
 
 
 def tract_kernel(
-    tiles_ref, fracs_ref, table_ref, head_ref, weights, hist_ref, *refs,
-    parts, wide_peers, peers, capacity, peer_targets,
+    frac_hbm, tiles_ref, table_ref, head_ref, weights, hist_ref, *refs,
+    wide_peers, peers, capacity, peer_targets,
 ):
+    news = refs[: wide_peers - 1]
+    outs = refs[wide_peers - 1 : wide_peers - 1 + peers]
+    tiles, frac, hist, total, sems = refs[wide_peers - 1 + peers :]
     place = lax.axis_index("narrow")
     owner = lax.axis_index("wide")
-    tiles, fracs, total, sems = refs[-4:]
-    if parts[0] == 0:
-        news = refs[: wide_peers - 1]
-        outs = refs[wide_peers - 1 : -5]
-        hist = refs[-5]
-        hist[...] = hist_ref[...]
-    else:
-        news = []
-        outs = refs[:-4]
-        hist = hist_ref
     copies = [
         pltpu.make_async_copy(tiles_ref, tiles, sems.at[0]),
-        pltpu.make_async_copy(fracs_ref, fracs, sems.at[1]),
+        pltpu.make_async_copy(frac_hbm, frac, sems.at[1]),
     ]
     for copy in copies:
         copy.start()
     total[...] = jnp.zeros_like(total)
+    hist[...] = hist_ref[...]
     for i, block in enumerate(news):
         table = table_ref[:STEPS, : block.shape[1]]
         for c in range(capacity):
@@ -254,46 +231,40 @@
             hist[rows, :] = jnp.dot(table, block[c], preferred_element_type=jnp.float32)
     for copy in copies:
         copy.wait()
-    begin = tiles[3, parts[0]]
-    end = tiles[3, parts[-1] + 1]
-    spare = len(parts) * peer_targets * TOGETHER
-    pitch = spare + TOGETHER
-
-    @pl.loop(0, lax.div(end - begin + (UNROLL - 1), UNROLL))
-    def _(turn):
+
+    span = peer_targets * TOGETHER
+    pitch = peers * span
+    for turn in range(0, frac.shape[1], UNROLL):
         sums = []
-        for u in range(UNROLL):
-            t = begin + turn * UNROLL + u
-            fraction = fracs[3, t]
-            start = tiles[1, t]
+        for t in range(turn, turn + UNROLL):
+            fraction = frac[0, t]
+            start = tiles[0, t]
             earlier = hist[pl.ds(start, STEPS), :]
             later = hist[pl.ds(start + 1, STEPS), :]
             delayed = ((1.0 - fraction) * later + fraction * earlier).astype(jnp.bfloat16)
             sums.append(
                 lax.dot_general(
-                    delayed, weights[tiles[0, t]], (((1,), (1,)), ((), ())),
+                    delayed, weights[t], (((1,), (1,)), ((), ())),
                     preferred_element_type=jnp.float32,
                 )
             )
-        for u in range(UNROLL):
-            t = begin + turn * UNROLL + u
-            first = jnp.where(t < end, tiles[2, t] - parts[0] * peer_targets * TOGETHER, spare)
+        for t in range(turn, turn + UNROLL):
+            first = tiles[1, t]
             for g in range(STEPS // TOGETHER):
-                rows = pl.ds(pl.multiple_of(g * pitch + first, 8), TOGETHER)
-                total[rows, :] += sums[u][g * TOGETHER : (g + 1) * TOGETHER]
-
-    span = peer_targets * TOGETHER
-    for i, part in enumerate(parts):
+                rows = pl.ds(pl.multiple_of(first + g * pitch, 8), TOGETHER)
+                total[rows, :] += sums[t - turn][g * TOGETHER : (g + 1) * TOGETHER]
+
+    for r in range(peers):
         for g in range(STEPS // TOGETHER):
-            first = g * pitch + i * span
-            outs[i][g * span : (g + 1) * span, :] = total[first : first + span, :].astype(
+            first = pl.multiple_of(g * pitch + (place ^ r) * span, 8)
+            outs[r][g * span : (g + 1) * span, :] = total[pl.ds(first, span), :].astype(
                 jnp.bfloat16
             )
-        outs[i][peer_targets * STEPS :, :] = head_ref[place ^ (peers - 1 - part)]
+        outs[r][peer_targets * STEPS :, :] = head_ref[place ^ r]
 
 
 def window_kernel(*refs, peers, own_blocks, peer_targets, coef_count):
-    shares = refs[:peers][::-1]
+    shares = dict(zip([*range(2, peers), 1, 0], refs))
     ready_ref, high_ref, low_ref, coefs_out, state_out, samples, rates = refs[peers:]
     block_rows = ready_ref.shape[1]
     width = TOGETHER * peer_targets
@@ -412,37 +383,33 @@
         VMEM((1, tile_count), jnp.int32),
         VMEM((1, tile_count), jnp.int32),
         VMEM((1, tile_count), jnp.int32),
-        VMEM((1, tile_count), jnp.float32),
         VMEM((3, HEAD, 128), jnp.float32),
         VMEM((LENGTH, SEGS * coef_count), jnp.bfloat16),
         VMEM((slot_count, HSEG, coef_count, block_rows), jnp.bfloat16),
     ]
     table = far(jnp.asarray(expand_table(coef_count)))
-    weights, fresh, ready, hist, tiles, fracs, heads = pl.pallas_call(
+    fresh, ready, hist, tiles, heads = pl.pallas_call(
         functools.partial(
             prepare_kernel,
             peers=peers, own_blocks=own_blocks, peer_targets=peer_targets, capacity=capacity,
         ),
         out_shape=[
-            pltpu.VMEM((tile_count, block_rows, block_rows), jnp.bfloat16),
             pltpu.VMEM(fresh_coefs.shape, jnp.bfloat16),
             pltpu.VMEM((4 * own_blocks + STEPS, block_rows), jnp.float32),
             pltpu.VMEM((slot_count * LENGTH, block_rows), jnp.float32),
             pltpu.VMEM((8, 128), jnp.int32),
-            pltpu.VMEM((8, 128), jnp.float32),
             pltpu.VMEM((peers, HEAD, 128), jnp.bfloat16),
         ],
-        in_specs=[hbm_spec] * 14,
-        out_specs=[vmem_spec] * 7,
+        in_specs=[hbm_spec] * 12,
+        out_specs=[vmem_spec] * 5,
         scratch_shapes=[
             SMEM((capacity, wide_peers), jnp.int32),
             *vmem_inputs,
-            pltpu.SemaphoreType.DMA((14,)),
+            pltpu.SemaphoreType.DMA((12,)),
         ],
         compiler_params=params(),
         name="prepare",
     )(
-        far(tract_weights.reshape(tile_count, block_rows, block_rows)),
         far(fresh_coefs),
         far(reads),
         far(state),
@@ -452,7 +419,6 @@
         far(tract_slot.reshape(1, tile_count)),
         far(tract_target.reshape(1, tile_count)),
         far(tract_delay.reshape(1, tile_count)),
-        far(tract_frac.reshape(1, tile_count)),
         far(jnp.asarray(lane_tables(peers, peer_targets, own_blocks))),
         table,
         far(older_coefs.reshape(slot_count, HSEG, coef_count, block_rows)),
@@ -473,34 +439,37 @@
     )(*asked, fresh)
     news = [swap(picked[r - 1], "wide", r) for r in range(wide_peers - 1, 0, -1)]
 
-    shares = [None] * peers
-    half = (peers + 1) // 2
-    for parts in (range(half), range(half, peers)):
-        blocks = news if parts[0] == 0 else []
-        result = pl.pallas_call(
-            functools.partial(
-                tract_kernel,
-                parts=parts, wide_peers=wide_peers, peers=peers, capacity=capacity,
-                peer_targets=peer_targets,
-            ),
-            out_shape=[pltpu.VMEM((share_rows, block_rows), jnp.bfloat16)] * len(parts)
-            + ([pltpu.VMEM(hist.shape, jnp.float32)] if parts[0] == 0 else []),
-            in_specs=[vmem_spec] * (6 + len(blocks)),
-            out_specs=[vmem_spec] * (len(parts) + (parts[0] == 0)),
-            scratch_shapes=[
-                SMEM((8, 128), jnp.int32),
-                SMEM((8, 128), jnp.float32),
-                VMEM(((len(parts) * peer_targets + 1) * STEPS, block_rows), jnp.float32),
-                pltpu.SemaphoreType.DMA((2,)),
-            ],
-            compiler_params=params(),
-            name=f"tract_tiles_{parts[0]}",
-        )(tiles, fracs, table, heads, weights, hist, *blocks)
-        if parts[0] == 0:
-            hist = result[-1]
-        for i, part in enumerate(parts):
-            shares[peers - 1 - part] = result[i]
-    arrived = [shares[0]] + [swap(shares[r], "narrow", r) for r in range(1, peers)]
+    weights_shape = pltpu.VMEM((tile_count, block_rows, block_rows), jnp.bfloat16)
+    weights = pl.pallas_call(
+        weights_kernel,
+        out_shape=weights_shape,
+        in_specs=[hbm_spec],
+        out_specs=vmem_spec,
+        scratch_shapes=[pltpu.SemaphoreType.DMA],
+        compiler_params=params(),
+        name="weights_near",
+    )(far(tract_weights.reshape(tile_count, block_rows, block_rows)))
+
+    shares = pl.pallas_call(
+        functools.partial(
+            tract_kernel,
+            wide_peers=wide_peers, peers=peers, capacity=capacity, peer_targets=peer_targets,
+        ),
+        out_shape=[pltpu.VMEM((share_rows, block_rows), jnp.bfloat16)] * peers,
+        in_specs=[hbm_spec] + [vmem_spec] * (4 + wide_peers),
+        out_specs=[vmem_spec] * peers,
+        scratch_shapes=[
+            SMEM((8, 128), jnp.int32),
+            SMEM((1, tile_count), jnp.float32),
+            VMEM((slot_count * LENGTH, block_rows), jnp.float32),
+            VMEM((peers * peer_targets * STEPS, block_rows), jnp.float32),
+            pltpu.SemaphoreType.DMA((2,)),
+        ],
+        compiler_params=params(),
+        name="tract_tiles",
+    )(far(tract_frac.reshape(1, tile_count)), tiles, table, heads, weights, hist, *news)
+    order = [*range(2, peers), 1, 0]
+    arrived = [swap(shares[r], "narrow", r) if r else shares[r] for r in order]
 
     high, low = fit_tables(coef_count)
     new_coefs, final_state = pl.pallas_call(
@@ -520,7 +489,7 @@
         ],
         compiler_params=params(),
         name="window_steps",
-    )(*arrived[::-1], ready, high, low)
+    )(*arrived, ready, high, low)
     return new_coefs, final_state
 
 

time: 34.1 us -> 30 us (0.88)
  waiting for transfers between devices: 9.69 us -> 6.78 us
  Pallas kernels: 11.3 us -> 9.79 us
    ppermute x9, waiting for transfers between devices: 9.69 us -> 6.78 us  [swap(): lax.ppermute(x, axis, [(i, i ^ r) for i in range(lax.axis_size(axis))])]
    pallas_call x2, Pallas kernels: 6.27 us -> 5.27 us  [the longest x1 3.37 us: local(): pl.pallas_call(functools.partial(tract_kernel, wide_peers=wide_peers, pee...]
    pallas_call x1, Pallas kernels: 2.3 us -> 1.77 us  [local(): pl.pallas_call(functools.partial(prepare_kernel, peers=peers, own_blocks=...]
  transfers between devices with their start and end apart: 9 -> 9, of which waited for: 5 -> 3; matrix products, arithmetic and copies ran while one was open for 0% -> 0% of each run, Pallas kernels for 7% -> 12%
where the time goes in v6:
time: 30 us; the launch traced here: 29.7 us
  starting transfers between devices  12.4 us (41%)
  Pallas kernels  9.79 us (33%)
  waiting for transfers between devices  6.78 us (23%)
  between operations  0.72 us (2%)
    ppermute x9, starting transfers between devices, swap(): lax.ppermute(x, axis, [(i, i ^ r) for i in range(lax.axis_size(axis))])  12.4 us
    ppermute x9, waiting for transfers between devices, swap(): lax.ppermute(x, axis, [(i, i ^ r) for i in range(lax.axis_size(axis))])  6.78 us
    pallas_call x1, Pallas kernels, local(): pl.pallas_call(functools.partial(tract_kernel, wide_peers=wide_peers, pee...  3.37 us
    pallas_call x1, Pallas kernels, local(): pl.pallas_call(functools.partial(window_kernel, peers=peers, own_blocks=o...  2.14 us
    pallas_call x1, Pallas kernels, local(): pl.pallas_call(weights_kernel, out_shape=weights_shape, in_specs=[hbm_spe...  1.9 us
    pallas_call x1, Pallas kernels, local(): pl.pallas_call(functools.partial(prepare_kernel, peers=peers, own_blocks=...  1.77 us
    pallas_call x1, Pallas kernels, local(): pl.pallas_call(functools.partial(pick_kernel, capacity=capacity, peers=wi...  0.62 us
  transfers between devices with their start and end apart: 9, of which 3 were waited for; matrix products, arithmetic and copies ran while one was open for 0% of the time, Pallas kernels for 12%

profile of v6, /device:TPU:0, one launch (start us, length us, event | category | flops | bytes accessed | tf_op | source)
XLA Modules:
  0.0 29.7 jit_solution(11664324977044126137)
XLA Ops:
  0.6 5.1 %collective-permute-start.2 = (s32[2,4]{1,0:T(2,128)}, s32[2,4]{1,0:T(2,128)S(1)}, u32[]{:S(2)}, u32[]{:S(2)}) collective-permute-start(s32[2,4]{1,0:T(2,128)} %bitcast.15), channel_id=1, source_target_pairs={{0,12},{4,8},{8,4},{12,0},{1,13},{5,9},{9,5},{13,1},{2,14},{6,10},... | collective-permute-start | bytes 104 | tf_op jit(solution)/shard_map/ppermute | solution.py:373
  5.7 0.0 collective-permute-start.1
  5.8 0.6 %collective-permute-start = (s32[2,4]{1,0:T(2,128)}, s32[2,4]{1,0:T(2,128)S(1)}, u32[]{:S(2)}, u32[]{:S(2)}) collective-permute-start(s32[2,4]{1,0:T(2,128)} %bitcast.17), channel_id=1, source_target_pairs={{0,4},{4,0},{8,12},{12,8},{1,5},{5,1},{9,13},{13,9},{2,6},{6,2},{1... | collective-permute-start | bytes 104 | tf_op jit(solution)/shard_map/ppermute | solution.py:373
  6.4 1.8 %prepare.1 = (bf16[32,32,128]{2,1,0:T(8,128)(2,1)S(1)}, f32[160,128]{1,0:T(8,128)S(1)}, f32[768,128]{1,0:T(8,128)S(1)}, s32[8,128]{1,0:T(8,128)S(1)}, bf16[4,16,128]{2,1,0:T(8,128)(2,1)S(1)}) custom-call(bf16[32,32,128]{2,1,0:T(8,128)(2,1)} %fresh_hbm.1, s32[2,4]{1,0:T(2,128)} %bitcast.18, f32[2,4096]{1,0:T(2,128)} %state_hbm.1, s32[32,128]{1,0:T(8,128)} %bitcast.14, ...), custom_call_target="tpu_custom_call" | custom-call | tf_op jit(solution)/shard_map/prepare/pallas_call | solution.py:391
  8.2 0.0 collective-permute-done.2.refs_2_
  8.2 2.3 %collective-permute-done.1.refs_1_ = s32[2,4]{1,0:T(2,128)S(1)} collective-permute-done((s32[2,4]{1,0:T(2,128)}, s32[2,4]{1,0:T(2,128)S(1)}, u32[]{:S(2)}, u32[]{:S(2)}) %collective-permute-start.1) | collective-permute-done | bytes 64 | tf_op jit(solution)/shard_map/ppermute | solution.py:373
  10.4 0.0 collective-permute-done.refs_0_
  10.4 0.6 %pick_blocks.1 = (bf16[2,32,128]{2,1,0:T(8,128)(2,1)S(1)}, bf16[2,32,128]{2,1,0:T(8,128)(2,1)S(1)}, bf16[2,32,128]{2,1,0:T(8,128)(2,1)S(1)}) custom-call(s32[2,4]{1,0:T(2,128)S(1)} %collective-permute-done.refs_0_, s32[2,4]{1,0:T(2,128)S(1)} %collective-permute-done.1.refs_1_, s32[2,4]{1,0:T(2,128)S(1)} %collective-permute-done.2.refs_2_, ...), custom_call_target="tpu_custom_call" | custom-call | tf_op jit(solution)/shard_map/pick_blocks/pallas_call | solution.py:427
  11.1 1.6 %collective-permute-start.3 = (bf16[2,32,128]{2,1,0:T(8,128)(2,1)S(1)}, bf16[2,32,128]{2,1,0:T(8,128)(2,1)S(1)}, u32[]{:S(2)}, u32[]{:S(2)}) collective-permute-start(bf16[2,32,128]{2,1,0:T(8,128)(2,1)S(1)} %get-tuple-element.18), channel_id=1, source_target_pairs={{0,12},{4,8},{8,4},{12,0},{1,13},{5,9},{9,5},{13,1},{2,14},{6,10},... | collective-permute-start | bytes 49160 | tf_op jit(solution)/shard_map/ppermute | solution.py:373
  12.6 0.6 %collective-permute-start.4 = (bf16[2,32,128]{2,1,0:T(8,128)(2,1)S(1)}, bf16[2,32,128]{2,1,0:T(8,128)(2,1)S(1)}, u32[]{:S(2)}, u32[]{:S(2)}) collective-permute-start(bf16[2,32,128]{2,1,0:T(8,128)(2,1)S(1)} %get-tuple-element.19), channel_id=1, source_target_pairs={{0,8},{4,12},{8,0},{12,4},{1,9},{5,13},{9,1},{13,5},{2,10},{6,14},... | collective-permute-start | bytes 49160 | tf_op jit(solution)/shard_map/ppermute | solution.py:373
  13.2 2.3 %collective-permute-start.5 = (bf16[2,32,128]{2,1,0:T(8,128)(2,1)S(1)}, bf16[2,32,128]{2,1,0:T(8,128)(2,1)S(1)}, u32[]{:S(2)}, u32[]{:S(2)}) collective-permute-start(bf16[2,32,128]{2,1,0:T(8,128)(2,1)S(1)} %get-tuple-element.20), channel_id=1, source_target_pairs={{0,4},{4,0},{8,12},{12,8},{1,5},{5,1},{9,13},{13,9},{2,6},{6,2},{1... | collective-permute-start | bytes 49160 | tf_op jit(solution)/shard_map/ppermute | solution.py:373
  15.5 1.9 %weights_near.1.weights = bf16[96,128,128]{2,1,0:T(8,128)(2,1)S(1)} custom-call(bf16[96,128,128]{2,1,0:T(8,128)(2,1)} %bitcast.12), custom_call_target="tpu_custom_call" | custom-call | tf_op jit(solution)/shard_map/weights_near/pallas_call | solution.py:443
  17.4 0.0 copy-start
  17.4 0.0 copy-start.1
  17.4 0.0 collective-permute-done.3.refs_0_
  17.5 0.0 collective-permute-done.4.refs_1_
  17.5 0.0 collective-permute-done.5.refs_2_
  17.5 3.4 %tract_tiles.1 = (bf16[400,128]{1,0:T(8,128)(2,1)S(1)}, bf16[400,128]{1,0:T(8,128)(2,1)S(1)}, bf16[400,128]{1,0:T(8,128)(2,1)S(1)}, bf16[400,128]{1,0:T(8,128)(2,1)S(1)}) custom-call(f32[1,96]{1,0:T(1,128)} %bitcast.24, s32[8,128]{1,0:T(8,128)S(1)} %get-tuple-element.14.tiles_ref, bf16[96,96]{1,0:T(8,128)(2,1)} %constant.8.clone.table_hbm.table_ref, ...), custom_call_target="tpu_custom_call" | custom-call | tf_op jit(solution)/shard_map/tract_tiles/pallas_call | solution.py:453
  20.9 1.6 %collective-permute-start.6 = (bf16[400,128]{1,0:T(8,128)(2,1)S(1)}, bf16[400,128]{1,0:T(8,128)(2,1)S(1)}, u32[]{:S(2)}, u32[]{:S(2)}) collective-permute-start(bf16[400,128]{1,0:T(8,128)(2,1)S(1)} %get-tuple-element.21), channel_id=1, source_target_pairs={{0,2},{1,3},{2,0},{3,1},{4,6},{5,7},{6,4},{7,5},{8,10},{9,11},{10,... | collective-permute-start | bytes 307208 | tf_op jit(solution)/shard_map/ppermute | solution.py:373
  22.4 0.0 collective-permute-start.7
  22.4 0.7 %collective-permute-start.8 = (bf16[400,128]{1,0:T(8,128)(2,1)S(1)}, bf16[400,128]{1,0:T(8,128)(2,1)S(1)}, u32[]{:S(2)}, u32[]{:S(2)}) collective-permute-start(bf16[400,128]{1,0:T(8,128)(2,1)S(1)} %get-tuple-element.23), channel_id=1, source_target_pairs={{0,1},{1,0},{2,3},{3,2},{4,5},{5,4},{6,7},{7,6},{8,9},{9,8},{10,11... | collective-permute-start | bytes 307208 | tf_op jit(solution)/shard_map/ppermute | solution.py:373
  23.1 2.7 %collective-permute-done.6.refs_0_ = bf16[400,128]{1,0:T(8,128)(2,1)S(1)} collective-permute-done((bf16[400,128]{1,0:T(8,128)(2,1)S(1)}, bf16[400,128]{1,0:T(8,128)(2,1)S(1)}, u32[]{:S(2)}, u32[]{:S(2)}) %collective-permute-start.6) | collective-permute-done | bytes 102432 | tf_op jit(solution)/shard_map/ppermute | solution.py:373
  25.8 1.8 %collective-permute-done.7.refs_1_ = bf16[400,128]{1,0:T(8,128)(2,1)S(1)} collective-permute-done((bf16[400,128]{1,0:T(8,128)(2,1)S(1)}, bf16[400,128]{1,0:T(8,128)(2,1)S(1)}, u32[]{:S(2)}, u32[]{:S(2)}) %collective-permute-start.7) | collective-permute-done | bytes 102432 | tf_op jit(solution)/shard_map/ppermute | solution.py:373
  27.6 0.0 collective-permute-done.8.refs_2_
  27.6 0.0 copy-done
  27.6 0.0 copy-done.1
  27.6 2.1 %window_steps.1 = (bf16[32,32,128]{2,1,0:T(8,128)(2,1)}, f32[2,4096]{1,0:T(2,128)}) custom-call(bf16[400,128]{1,0:T(8,128)(2,1)S(1)} %collective-permute-done.6.refs_0_, bf16[400,128]{1,0:T(8,128)(2,1)S(1)} %collective-permute-done.7.refs_1_, bf16[400,128]{1,0:T(8,128)(2,1)S(1)} %collective-permute-done.8.refs_2_, ...), custom_call_target="tpu_custom_call" | custom-call | tf_op jit(solution)/shard_map/window_steps/pallas_call | solution.py:475
Async XLA Ops:
  0.6 7.5 %collective-permute-start.2 = (s32[2,4]{1,0:T(2,128)}, s32[2,4]{1,0:T(2,128)S(1)}, u32[]{:S(2)}, u32[]{:S(2)}) collective-permute-start(s32[2,4]{1,0:T(2,128)} %bitcast.15), channel_id=1, source_target_pairs={{0,12},{4,8},{8,4},{12,0},{1,13},{5,9},{9,5},{13,1},{2,14},{6,10},... | collective-permute-start | bytes 104 | tf_op jit(solution)/shard_map/ppermute | solution.py:373
  5.7 4.7 %collective-permute-start.1 = (s32[2,4]{1,0:T(2,128)}, s32[2,4]{1,0:T(2,128)S(1)}, u32[]{:S(2)}, u32[]{:S(2)}) collective-permute-start(s32[2,4]{1,0:T(2,128)} %bitcast.16), channel_id=1, source_target_pairs={{0,8},{4,12},{8,0},{12,4},{1,9},{5,13},{9,1},{13,5},{2,10},{6,14},... | collective-permute-start | bytes 104 | tf_op jit(solution)/shard_map/ppermute | solution.py:373
  5.8 4.7 %collective-permute-start = (s32[2,4]{1,0:T(2,128)}, s32[2,4]{1,0:T(2,128)S(1)}, u32[]{:S(2)}, u32[]{:S(2)}) collective-permute-start(s32[2,4]{1,0:T(2,128)} %bitcast.17), channel_id=1, source_target_pairs={{0,4},{4,0},{8,12},{12,8},{1,5},{5,1},{9,13},{13,9},{2,6},{6,2},{1... | collective-permute-start | bytes 104 | tf_op jit(solution)/shard_map/ppermute | solution.py:373
  11.1 6.4 %collective-permute-start.3 = (bf16[2,32,128]{2,1,0:T(8,128)(2,1)S(1)}, bf16[2,32,128]{2,1,0:T(8,128)(2,1)S(1)}, u32[]{:S(2)}, u32[]{:S(2)}) collective-permute-start(bf16[2,32,128]{2,1,0:T(8,128)(2,1)S(1)} %get-tuple-element.18), channel_id=1, source_target_pairs={{0,12},{4,8},{8,4},{12,0},{1,13},{5,9},{9,5},{13,1},{2,14},{6,10},... | collective-permute-start | bytes 49160 | tf_op jit(solution)/shard_map/ppermute | solution.py:373
  12.6 4.8 %collective-permute-start.4 = (bf16[2,32,128]{2,1,0:T(8,128)(2,1)S(1)}, bf16[2,32,128]{2,1,0:T(8,128)(2,1)S(1)}, u32[]{:S(2)}, u32[]{:S(2)}) collective-permute-start(bf16[2,32,128]{2,1,0:T(8,128)(2,1)S(1)} %get-tuple-element.19), channel_id=1, source_target_pairs={{0,8},{4,12},{8,0},{12,4},{1,9},{5,13},{9,1},{13,5},{2,10},{6,14},... | collective-permute-start | bytes 49160 | tf_op jit(solution)/shard_map/ppermute | solution.py:373
  13.2 4.2 %collective-permute-start.5 = (bf16[2,32,128]{2,1,0:T(8,128)(2,1)S(1)}, bf16[2,32,128]{2,1,0:T(8,128)(2,1)S(1)}, u32[]{:S(2)}, u32[]{:S(2)}) collective-permute-start(bf16[2,32,128]{2,1,0:T(8,128)(2,1)S(1)} %get-tuple-element.20), channel_id=1, source_target_pairs={{0,4},{4,0},{8,12},{12,8},{1,5},{5,1},{9,13},{13,9},{2,6},{6,2},{1... | collective-permute-start | bytes 49160 | tf_op jit(solution)/shard_map/ppermute | solution.py:373
  17.4 10.2 %copy-start = (bf16[128,128]{1,0:T(8,128)(2,1)S(1)}, bf16[128,128]{1,0:T(8,128)(2,1)}, u32[]{:S(2)}) copy-start(bf16[128,128]{1,0:T(8,128)(2,1)} %constant.11.clone.refs_6_) | copy-start | bytes 98308
  17.4 10.1 %copy-start.1 = (bf16[128,128]{1,0:T(8,128)(2,1)S(1)}, bf16[128,128]{1,0:T(8,128)(2,1)}, u32[]{:S(2)}) copy-start(bf16[128,128]{1,0:T(8,128)(2,1)} %constant.10.clone.refs_5_) | copy-start | bytes 98308
  20.9 4.9 %collective-permute-start.6 = (bf16[400,128]{1,0:T(8,128)(2,1)S(1)}, bf16[400,128]{1,0:T(8,128)(2,1)S(1)}, u32[]{:S(2)}, u32[]{:S(2)}) collective-permute-start(bf16[400,128]{1,0:T(8,128)(2,1)S(1)} %get-tuple-element.21), channel_id=1, source_target_pairs={{0,2},{1,3},{2,0},{3,1},{4,6},{5,7},{6,4},{7,5},{8,10},{9,11},{10,... | collective-permute-start | bytes 307208 | tf_op jit(solution)/shard_map/ppermute | solution.py:373
  22.4 5.2 %collective-permute-start.7 = (bf16[400,128]{1,0:T(8,128)(2,1)S(1)}, bf16[400,128]{1,0:T(8,128)(2,1)S(1)}, u32[]{:S(2)}, u32[]{:S(2)}) collective-permute-start(bf16[400,128]{1,0:T(8,128)(2,1)S(1)} %get-tuple-element.22), channel_id=1, source_target_pairs={{0,3},{1,2},{2,1},{3,0},{4,7},{5,6},{6,5},{7,4},{8,11},{9,10},{10,... | collective-permute-start | bytes 307208 | tf_op jit(solution)/shard_map/ppermute | solution.py:373
  22.4 5.2 %collective-permute-start.8 = (bf16[400,128]{1,0:T(8,128)(2,1)S(1)}, bf16[400,128]{1,0:T(8,128)(2,1)S(1)}, u32[]{:S(2)}, u32[]{:S(2)}) collective-permute-start(bf16[400,128]{1,0:T(8,128)(2,1)S(1)} %get-tuple-element.23), channel_id=1, source_target_pairs={{0,1},{1,0},{2,3},{3,2},{4,5},{5,4},{6,7},{7,6},{8,9},{9,8},{10,11... | collective-permute-start | bytes 307208 | tf_op jit(solution)/shard_map/ppermute | solution.py:373

commit v7 on v6

--- a/solution.py
+++ b/solution.py
@@ -16,7 +16,8 @@
 LENGTH = SEGS * STEPS
 GROUP = 4
 HEAD = 16
-UNROLL = 16
+CHUNKS = 8
+UNROLL = 4
 
 excite_rate = 0.1
 inhibit_rate = 0.05
@@ -76,23 +77,31 @@
 
 
 def prepare_kernel(
-    fresh_hbm, reads_hbm, state_hbm, lesion_hbm, stim_hbm, wave_hbm, slot_hbm, target_hbm,
-    delay_hbm, lanes_hbm, table_hbm, older_hbm,
-    fresh_out, ready_out, hist_out, tiles_out, head_out,
+    fresh_ref, reads_hbm, state_hbm, lesion_hbm, stim_hbm, wave_hbm, slot_hbm, target_hbm,
+    delay_hbm, lanes_hbm, table_hbm, older_hbm, weights_hbm,
+    weights_out, ready_out, hist_out, tiles_out, head_out,
     reads, state, lesion, stim, wave, slot, target, delay, lanes, table, older, sems,
     *, peers, own_blocks, peer_targets, capacity,
 ):
     pairs = [
-        (fresh_hbm, fresh_out), (reads_hbm, reads), (target_hbm, target), (slot_hbm, slot),
+        (reads_hbm, reads), (target_hbm, target), (slot_hbm, slot),
         (delay_hbm, delay), (lanes_hbm, lanes), (table_hbm, table), (older_hbm, older),
         (state_hbm, state), (lesion_hbm, lesion), (stim_hbm, stim), (wave_hbm, wave),
     ]
     copies = [
         pltpu.make_async_copy(source, into, sems.at[i]) for i, (source, into) in enumerate(pairs)
     ]
+    part = weights_hbm.shape[0] // CHUNKS
+    for i in range(CHUNKS):
+        rows = pl.ds(i * part, part)
+        copies.append(
+            pltpu.make_async_copy(
+                weights_hbm.at[rows], weights_out.at[rows], sems.at[len(pairs) + i]
+            )
+        )
     for copy in copies:
         copy.start()
-    for copy in copies[2:6]:
+    for copy in copies[1:5]:
         copy.wait()
     place = lax.axis_index("narrow")
     owner = lax.axis_index("wide")
@@ -135,7 +144,7 @@
     tiles_out[0:1, :tile_count] = slot[...] * LENGTH + (LENGTH - 1) - delay[...]
     tiles_out[1:2, :tile_count] = (across * peer_targets + ranks.astype(jnp.int32)) * TOGETHER
 
-    for copy in copies[6:8]:
+    for copy in copies[5:7]:
         copy.wait()
     coef_count = older.shape[2]
     earlier = HSEG * STEPS
@@ -148,16 +157,15 @@
         hist_out[s * LENGTH + earlier : (s + 1) * LENGTH, :] = jnp.zeros(
             (STEPS, hist_out.shape[1]), jnp.float32
         )
-    for copy in copies[:2]:
-        copy.wait()
+    copies[0].wait()
     for c in range(capacity):
         rows = pl.ds(pl.multiple_of((owner * capacity + c) * LENGTH + earlier, 8), STEPS)
         hist_out[rows, :] = jnp.dot(
-            table[:STEPS, :coef_count], fresh_out[jnp.maximum(reads[c, owner], 0)],
+            table[:STEPS, :coef_count], fresh_ref[jnp.maximum(reads[c, owner], 0)],
             preferred_element_type=jnp.float32,
         )
 
-    for copy in copies[8:12]:
+    for copy in copies[7:11]:
         copy.wait()
     block_rows = lesion.shape[1]
     for b in range(own_blocks):
@@ -183,15 +191,17 @@
     diagonal = lax.broadcasted_iota(jnp.int32, shape, 0) == lax.broadcasted_iota(jnp.int32, shape, 1)
     column = jnp.sum(jnp.where(diagonal, wave[...], 0.0), axis=1, keepdims=True)
     ready_out[4 * own_blocks :, :] = jnp.broadcast_to(column, (STEPS, block_rows))
-
-
-def weights_kernel(weights_hbm, weights_out, sem):
-    copy = pltpu.make_async_copy(weights_hbm, weights_out, sem)
+    for copy in copies[11:]:
+        copy.wait()
+
+
+def fresh_kernel(fresh_hbm, fresh_out, sem):
+    copy = pltpu.make_async_copy(fresh_hbm, fresh_out, sem)
     copy.start()
     copy.wait()
 
 
-def pick_kernel(*refs, capacity, peers):
+def pick_kernel(*refs, capacity, peers, ways):
     tables = refs[: peers - 1]
     fresh = refs[peers - 1]
     outs = refs[peers : 2 * peers - 1]
@@ -200,10 +210,10 @@
     copies = [pltpu.make_async_copy(tables[r], asked.at[r], sems.at[r]) for r in range(peers - 1)]
     for copy in copies:
         copy.start()
-    for r in range(peers - 1):
-        copies[r].wait()
+    for i, r in enumerate(ways):
+        copies[i].wait()
         for c in range(capacity):
-            outs[r][c] = fresh[jnp.maximum(asked[r, c, place], 0)]
+            outs[r - 1][c] = fresh[jnp.maximum(asked[i, c, place], 0)]
 
 
 def tract_kernel(
@@ -265,7 +275,9 @@
 
 def window_kernel(*refs, peers, own_blocks, peer_targets, coef_count):
     shares = dict(zip([*range(2, peers), 1, 0], refs))
-    ready_ref, high_ref, low_ref, coefs_out, state_out, samples, rates = refs[peers:]
+    (
+        ready_ref, high_ref, low_ref, coefs_hbm, state_hbm, samples, rates, coefs, state, sems,
+    ) = refs[peers:]
     block_rows = ready_ref.shape[1]
     width = TOGETHER * peer_targets
     span = peer_targets * STEPS
@@ -286,6 +298,10 @@
     excite, inhibit, gain, counts = [
         ready_ref[i * own_blocks : (i + 1) * own_blocks, :] for i in range(4)
     ]
+    a = excite_excite / 2
+    gain = 0.5 * gain
+    counts = 0.5 * counts
+    carried = a * excite
     for pair in range(0, STEPS // TOGETHER, 2):
         arrived = jnp.concatenate(
             [
@@ -302,40 +318,54 @@
             wave = ready_ref[4 * own_blocks + j : 4 * own_blocks + j + 1, :]
             first = jj % TOGETHER * own_blocks
             left = jj // TOGETHER * block_rows
-            forcing = (
-                gain * inflow[first : first + own_blocks, left : left + block_rows] + wave * counts
-            )
-            excite_drive = (
-                excite_excite * excite - inhibit_excite * inhibit + forcing - excite_offset
-            )
-            inhibit_drive = excite_inhibit * excite - inhibit_inhibit * inhibit - inhibit_offset
-            excite, inhibit = (
-                excite + excite_rate * (0.5 * jnp.tanh(0.5 * excite_drive) + 0.5 - excite),
-                inhibit + inhibit_rate * (0.5 * jnp.tanh(0.5 * inhibit_drive) + 0.5 - inhibit),
-            )
-            samples[pl.ds(j, own_blocks, stride=STEPS), :] = excite
-    rates[0] = excite
+            half_forcing = gain * inflow[
+                first : first + own_blocks, left : left + block_rows
+            ] + (wave * counts - excite_offset / 2)
+            inhibit_drive = (inhibit_inhibit / 2) * inhibit + inhibit_offset / 2
+            excite_turn = jnp.tanh(carried + (half_forcing - (inhibit_excite / 2) * inhibit))
+            inhibit_turn = jnp.tanh((excite_inhibit / 2 / a) * carried - inhibit_drive)
+            carried = ((1 - excite_rate) * carried + a * excite_rate / 2) + (
+                a * excite_rate / 2
+            ) * excite_turn
+            inhibit = ((1 - inhibit_rate) * inhibit + inhibit_rate / 2) + (
+                inhibit_rate / 2
+            ) * inhibit_turn
+            samples[pl.ds(j, own_blocks, stride=STEPS), :] = carried * (1 / a)
+    rates[0] = carried * (1 / a)
     rates[1] = inhibit
     for b in range(own_blocks):
         where = slice(b * block_rows, (b + 1) * block_rows)
-        state_out[0:1, where] = rates[0, b : b + 1, :]
-        state_out[1:2, where] = rates[1, b : b + 1, :]
+        state[0:1, where] = rates[0, b : b + 1, :]
+        state[1:2, where] = rates[1, b : b + 1, :]
+    copies = [pltpu.make_async_copy(state, state_hbm, sems.at[0])]
+    copies[0].start()
 
     high = high_ref[...]
     low = low_ref[...]
     rows = GROUP * STEPS
-    for g in range(own_blocks // GROUP):
-        part = samples[g * rows : (g + 1) * rows, :]
+    for g in range(0, own_blocks // GROUP, 2):
+        part = jnp.concatenate(
+            [samples[g * rows : (g + 1) * rows, :], samples[(g + 1) * rows : (g + 2) * rows, :]],
+            axis=1,
+        )
         part_high = part.astype(jnp.bfloat16)
         part_low = (part - part_high.astype(jnp.float32)).astype(jnp.bfloat16)
         fitted = (
             jnp.dot(high, part_high, preferred_element_type=jnp.float32)
             + jnp.dot(high, part_low, preferred_element_type=jnp.float32)
             + jnp.dot(low, part_high, preferred_element_type=jnp.float32)
-        )
-        coefs_out[g * GROUP : (g + 1) * GROUP] = fitted.astype(jnp.bfloat16).reshape(
-            GROUP, coef_count, block_rows
-        )
+        ).astype(jnp.bfloat16)
+        for i in range(2):
+            coefs[(g + i) * GROUP : (g + i + 1) * GROUP] = fitted[
+                :, i * block_rows : (i + 1) * block_rows
+            ].reshape(GROUP, coef_count, block_rows)
+        where = pl.ds(g * GROUP, 2 * GROUP)
+        copies.append(
+            pltpu.make_async_copy(coefs.at[where], coefs_hbm.at[where], sems.at[1 + g // 2])
+        )
+        copies[-1].start()
+    for copy in copies:
+        copy.wait()
 
 
 def far(x):
@@ -373,7 +403,8 @@
         return lax.ppermute(x, axis, [(i, i ^ r) for i in range(lax.axis_size(axis))])
 
     reads = read_blocks.reshape(wide_peers, capacity).T
-    asked = [swap(reads, "wide", r) for r in range(1, wide_peers)]
+    ways = [1, *range(wide_peers - 1, 1, -1)]
+    asked = [swap(reads, "wide", r) for r in ways]
 
     vmem_inputs = [
         VMEM(state.shape, jnp.float32),
@@ -388,29 +419,38 @@
         VMEM((slot_count, HSEG, coef_count, block_rows), jnp.bfloat16),
     ]
     table = far(jnp.asarray(expand_table(coef_count)))
-    fresh, ready, hist, tiles, heads = pl.pallas_call(
+    fresh = pl.pallas_call(
+        fresh_kernel,
+        out_shape=pltpu.VMEM(fresh_coefs.shape, jnp.bfloat16),
+        in_specs=[hbm_spec],
+        out_specs=vmem_spec,
+        scratch_shapes=[pltpu.SemaphoreType.DMA],
+        compiler_params=params(),
+        name="fresh_near",
+    )(far(fresh_coefs))
+    weights, ready, hist, tiles, heads = pl.pallas_call(
         functools.partial(
             prepare_kernel,
             peers=peers, own_blocks=own_blocks, peer_targets=peer_targets, capacity=capacity,
         ),
         out_shape=[
-            pltpu.VMEM(fresh_coefs.shape, jnp.bfloat16),
+            pltpu.VMEM((tile_count, block_rows, block_rows), jnp.bfloat16),
             pltpu.VMEM((4 * own_blocks + STEPS, block_rows), jnp.float32),
             pltpu.VMEM((slot_count * LENGTH, block_rows), jnp.float32),
             pltpu.VMEM((8, 128), jnp.int32),
             pltpu.VMEM((peers, HEAD, 128), jnp.bfloat16),
         ],
-        in_specs=[hbm_spec] * 12,
+        in_specs=[vmem_spec] + [hbm_spec] * 12,
         out_specs=[vmem_spec] * 5,
         scratch_shapes=[
             SMEM((capacity, wide_peers), jnp.int32),
             *vmem_inputs,
-            pltpu.SemaphoreType.DMA((12,)),
+            pltpu.SemaphoreType.DMA((11 + CHUNKS,)),
         ],
         compiler_params=params(),
         name="prepare",
     )(
-        far(fresh_coefs),
+        fresh,
         far(reads),
         far(state),
         far(lesion.reshape(own_blocks, block_rows)),
@@ -422,10 +462,11 @@
         far(jnp.asarray(lane_tables(peers, peer_targets, own_blocks))),
         table,
         far(older_coefs.reshape(slot_count, HSEG, coef_count, block_rows)),
+        far(tract_weights.reshape(tile_count, block_rows, block_rows)),
     )
 
     picked = pl.pallas_call(
-        functools.partial(pick_kernel, capacity=capacity, peers=wide_peers),
+        functools.partial(pick_kernel, capacity=capacity, peers=wide_peers, ways=ways),
         out_shape=[pltpu.VMEM((capacity, coef_count, block_rows), jnp.bfloat16)]
         * (wide_peers - 1),
         in_specs=[vmem_spec] * wide_peers,
@@ -438,17 +479,6 @@
         name="pick_blocks",
     )(*asked, fresh)
     news = [swap(picked[r - 1], "wide", r) for r in range(wide_peers - 1, 0, -1)]
-
-    weights_shape = pltpu.VMEM((tile_count, block_rows, block_rows), jnp.bfloat16)
-    weights = pl.pallas_call(
-        weights_kernel,
-        out_shape=weights_shape,
-        in_specs=[hbm_spec],
-        out_specs=vmem_spec,
-        scratch_shapes=[pltpu.SemaphoreType.DMA],
-        compiler_params=params(),
-        name="weights_near",
-    )(far(tract_weights.reshape(tile_count, block_rows, block_rows)))
 
     shares = pl.pallas_call(
         functools.partial(
@@ -482,10 +512,13 @@
             jax.ShapeDtypeStruct(state.shape, jnp.float32),
         ],
         in_specs=[vmem_spec] * (peers + 3),
-        out_specs=[vmem_spec] * 2,
+        out_specs=[hbm_spec] * 2,
         scratch_shapes=[
             VMEM((own_blocks * STEPS, block_rows), jnp.float32),
             VMEM((2, own_blocks, block_rows), jnp.float32),
+            VMEM(fresh_coefs.shape, jnp.bfloat16),
+            VMEM(state.shape, jnp.float32),
+            pltpu.SemaphoreType.DMA((1 + own_blocks // GROUP // 2,)),
         ],
         compiler_params=params(),
         name="window_steps",

time: 30 us -> 30 us (level)
  waiting for transfers between devices: 6.78 us -> 7.63 us
  Pallas kernels: 9.79 us -> 9.13 us
    pallas_call x1, Pallas kernels: 1.9 us -> 0.96 us  [local(): pl.pallas_call(fresh_kernel, out_shape=pltpu.VMEM(fresh_coefs.shape, jnp....]
    ppermute x9, waiting for transfers between devices: 6.78 us -> 7.63 us  [swap(): lax.ppermute(x, axis, [(i, i ^ r) for i in range(lax.axis_size(axis))])]
    pallas_call x1, Pallas kernels: 1.77 us -> 2.17 us  [local(): pl.pallas_call(functools.partial(prepare_kernel, peers=peers, own_blocks=...]
  transfers between devices with their start and end apart: 9 -> 9, of which waited for: 3 -> 4; matrix products, arithmetic and copies ran while one was open for 0% -> 0% of each run, Pallas kernels for 12% -> 11%
where the time goes in v7:
time: 30 us; the launch traced here: 29.8 us
  starting transfers between devices  12.3 us (41%)
  Pallas kernels  9.13 us (30%)
  waiting for transfers between devices  7.63 us (25%)
  between operations  0.69 us (2%)
    ppermute x9, starting transfers between devices, swap(): lax.ppermute(x, axis, [(i, i ^ r) for i in range(lax.axis_size(axis))])  12.3 us
    ppermute x9, waiting for transfers between devices, swap(): lax.ppermute(x, axis, [(i, i ^ r) for i in range(lax.axis_size(axis))])  7.63 us
    pallas_call x1, Pallas kernels, local(): pl.pallas_call(functools.partial(tract_kernel, wide_peers=wide_peers, pee...  3.36 us
    pallas_call x1, Pallas kernels, local(): pl.pallas_call(functools.partial(prepare_kernel, peers=peers, own_blocks=...  2.17 us
    pallas_call x1, Pallas kernels, local(): pl.pallas_call(functools.partial(window_kernel, peers=peers, own_blocks=o...  2.02 us
    pallas_call x1, Pallas kernels, local(): pl.pallas_call(fresh_kernel, out_shape=pltpu.VMEM(fresh_coefs.shape, jnp....  0.96 us
    pallas_call x1, Pallas kernels, local(): pl.pallas_call(functools.partial(pick_kernel, capacity=capacity, peers=wi...  0.62 us
  transfers between devices with their start and end apart: 9, of which 4 were waited for; matrix products, arithmetic and copies ran while one was open for 0% of the time, Pallas kernels for 11%

profile of v7, /device:TPU:0, one launch (start us, length us, event | category | flops | bytes accessed | tf_op | source)
XLA Modules:
  0.0 29.8 jit_solution(325616985374164620)
XLA Ops:
  0.6 4.1 %collective-permute-start.2 = (s32[2,4]{1,0:T(2,128)}, s32[2,4]{1,0:T(2,128)S(1)}, u32[]{:S(2)}, u32[]{:S(2)}) collective-permute-start(s32[2,4]{1,0:T(2,128)} %bitcast.15), channel_id=1, source_target_pairs={{0,8},{4,12},{8,0},{12,4},{1,9},{5,13},{9,1},{13,5},{2,10},{6,14},... | collective-permute-start | bytes 104 | tf_op jit(solution)/shard_map/ppermute | solution.py:403
  4.7 1.3 %collective-permute-start.1 = (s32[2,4]{1,0:T(2,128)}, s32[2,4]{1,0:T(2,128)S(1)}, u32[]{:S(2)}, u32[]{:S(2)}) collective-permute-start(s32[2,4]{1,0:T(2,128)} %bitcast.16), channel_id=1, source_target_pairs={{0,12},{4,8},{8,4},{12,0},{1,13},{5,9},{9,5},{13,1},{2,14},{6,10},... | collective-permute-start | bytes 104 | tf_op jit(solution)/shard_map/ppermute | solution.py:403
  6.1 0.2 collective-permute-start
  6.3 1.0 %fresh_near.1.fresh_ref.refs_3_ = bf16[32,32,128]{2,1,0:T(8,128)(2,1)S(1)} custom-call(bf16[32,32,128]{2,1,0:T(8,128)(2,1)} %fresh_hbm.1), custom_call_target="tpu_custom_call" | custom-call | tf_op jit(solution)/shard_map/fresh_near/pallas_call | solution.py:422
  7.3 0.0 collective-permute-done.2.refs_2_
  7.3 3.0 %collective-permute-done.1.refs_1_ = s32[2,4]{1,0:T(2,128)S(1)} collective-permute-done((s32[2,4]{1,0:T(2,128)}, s32[2,4]{1,0:T(2,128)S(1)}, u32[]{:S(2)}, u32[]{:S(2)}) %collective-permute-start.1) | collective-permute-done | bytes 64 | tf_op jit(solution)/shard_map/ppermute | solution.py:403
  10.3 0.0 collective-permute-done.refs_0_
  10.3 0.6 %pick_blocks.1 = (bf16[2,32,128]{2,1,0:T(8,128)(2,1)S(1)}, bf16[2,32,128]{2,1,0:T(8,128)(2,1)S(1)}, bf16[2,32,128]{2,1,0:T(8,128)(2,1)S(1)}) custom-call(s32[2,4]{1,0:T(2,128)S(1)} %collective-permute-done.refs_0_, s32[2,4]{1,0:T(2,128)S(1)} %collective-permute-done.1.refs_1_, s32[2,4]{1,0:T(2,128)S(1)} %collective-permute-done.2.refs_2_, ...), custom_call_target="tpu_custom_call" | custom-call | tf_op jit(solution)/shard_map/pick_blocks/pallas_call | solution.py:468
  10.9 2.1 %collective-permute-start.3 = (bf16[2,32,128]{2,1,0:T(8,128)(2,1)S(1)}, bf16[2,32,128]{2,1,0:T(8,128)(2,1)S(1)}, u32[]{:S(2)}, u32[]{:S(2)}) collective-permute-start(bf16[2,32,128]{2,1,0:T(8,128)(2,1)S(1)} %get-tuple-element.18), channel_id=1, source_target_pairs={{0,12},{4,8},{8,4},{12,0},{1,13},{5,9},{9,5},{13,1},{2,14},{6,10},... | collective-permute-start | bytes 49160 | tf_op jit(solution)/shard_map/ppermute | solution.py:403
  13.0 0.0 collective-permute-start.4
  13.0 2.4 %collective-permute-start.5 = (bf16[2,32,128]{2,1,0:T(8,128)(2,1)S(1)}, bf16[2,32,128]{2,1,0:T(8,128)(2,1)S(1)}, u32[]{:S(2)}, u32[]{:S(2)}) collective-permute-start(bf16[2,32,128]{2,1,0:T(8,128)(2,1)S(1)} %get-tuple-element.20), channel_id=1, source_target_pairs={{0,4},{4,0},{8,12},{12,8},{1,5},{5,1},{9,13},{13,9},{2,6},{6,2},{1... | collective-permute-start | bytes 49160 | tf_op jit(solution)/shard_map/ppermute | solution.py:403
  15.4 0.0 copy-start
  15.4 0.0 copy-start.1
  15.4 2.2 %prepare.1 = (bf16[96,128,128]{2,1,0:T(8,128)(2,1)S(1)}, f32[160,128]{1,0:T(8,128)S(1)}, f32[768,128]{1,0:T(8,128)S(1)}, s32[8,128]{1,0:T(8,128)S(1)}, bf16[4,16,128]{2,1,0:T(8,128)(2,1)S(1)}) custom-call(bf16[32,32,128]{2,1,0:T(8,128)(2,1)S(1)} %fresh_near.1.fresh_ref.refs_3_, s32[2,4]{1,0:T(2,128)} %bitcast.18, f32[2,4096]{1,0:T(2,128)} %state_hbm.1, ...), custom_call_target="tpu_custom_call" | custom-call | tf_op jit(solution)/shard_map/prepare/pallas_call | solution.py:431
  17.6 0.0 collective-permute-done.3.refs_0_
  17.6 0.1 collective-permute-done.4.refs_1_
  17.7 0.0 collective-permute-done.5.refs_2_
  17.7 3.4 %tract_tiles.1 = (bf16[400,128]{1,0:T(8,128)(2,1)S(1)}, bf16[400,128]{1,0:T(8,128)(2,1)S(1)}, bf16[400,128]{1,0:T(8,128)(2,1)S(1)}, bf16[400,128]{1,0:T(8,128)(2,1)S(1)}) custom-call(f32[1,96]{1,0:T(1,128)} %bitcast.24, s32[8,128]{1,0:T(8,128)S(1)} %get-tuple-element.14.tiles_ref, bf16[96,96]{1,0:T(8,128)(2,1)} %constant.8.clone.table_hbm.table_ref, ...), custom_call_target="tpu_custom_call" | custom-call | tf_op jit(solution)/shard_map/tract_tiles/pallas_call | solution.py:483
  21.0 1.6 %collective-permute-start.6 = (bf16[400,128]{1,0:T(8,128)(2,1)S(1)}, bf16[400,128]{1,0:T(8,128)(2,1)S(1)}, u32[]{:S(2)}, u32[]{:S(2)}) collective-permute-start(bf16[400,128]{1,0:T(8,128)(2,1)S(1)} %get-tuple-element.21), channel_id=1, source_target_pairs={{0,2},{1,3},{2,0},{3,1},{4,6},{5,7},{6,4},{7,5},{8,10},{9,11},{10,... | collective-permute-start | bytes 307208 | tf_op jit(solution)/shard_map/ppermute | solution.py:403
  22.6 0.0 collective-permute-start.7
  22.6 0.6 %collective-permute-start.8 = (bf16[400,128]{1,0:T(8,128)(2,1)S(1)}, bf16[400,128]{1,0:T(8,128)(2,1)S(1)}, u32[]{:S(2)}, u32[]{:S(2)}) collective-permute-start(bf16[400,128]{1,0:T(8,128)(2,1)S(1)} %get-tuple-element.23), channel_id=1, source_target_pairs={{0,1},{1,0},{2,3},{3,2},{4,5},{5,4},{6,7},{7,6},{8,9},{9,8},{10,11... | collective-permute-start | bytes 307208 | tf_op jit(solution)/shard_map/ppermute | solution.py:403
  23.2 2.7 %collective-permute-done.6.refs_0_ = bf16[400,128]{1,0:T(8,128)(2,1)S(1)} collective-permute-done((bf16[400,128]{1,0:T(8,128)(2,1)S(1)}, bf16[400,128]{1,0:T(8,128)(2,1)S(1)}, u32[]{:S(2)}, u32[]{:S(2)}) %collective-permute-start.6) | collective-permute-done | bytes 102432 | tf_op jit(solution)/shard_map/ppermute | solution.py:403
  25.9 1.8 %collective-permute-done.7.refs_1_ = bf16[400,128]{1,0:T(8,128)(2,1)S(1)} collective-permute-done((bf16[400,128]{1,0:T(8,128)(2,1)S(1)}, bf16[400,128]{1,0:T(8,128)(2,1)S(1)}, u32[]{:S(2)}, u32[]{:S(2)}) %collective-permute-start.7) | collective-permute-done | bytes 102432 | tf_op jit(solution)/shard_map/ppermute | solution.py:403
  27.8 0.0 collective-permute-done.8.refs_2_
  27.8 0.0 copy-done
  27.8 0.0 copy-done.1
  27.8 2.0 %window_steps.1 = (bf16[32,32,128]{2,1,0:T(8,128)(2,1)}, f32[2,4096]{1,0:T(2,128)}) custom-call(bf16[400,128]{1,0:T(8,128)(2,1)S(1)} %collective-permute-done.6.refs_0_, bf16[400,128]{1,0:T(8,128)(2,1)S(1)} %collective-permute-done.7.refs_1_, bf16[400,128]{1,0:T(8,128)(2,1)S(1)} %collective-permute-done.8.refs_2_, ...), custom_call_target="tpu_custom_call" | custom-call | tf_op jit(solution)/shard_map/window_steps/pallas_call | solution.py:505
Async XLA Ops:
  0.6 6.7 %collective-permute-start.2 = (s32[2,4]{1,0:T(2,128)}, s32[2,4]{1,0:T(2,128)S(1)}, u32[]{:S(2)}, u32[]{:S(2)}) collective-permute-start(s32[2,4]{1,0:T(2,128)} %bitcast.15), channel_id=1, source_target_pairs={{0,8},{4,12},{8,0},{12,4},{1,9},{5,13},{9,1},{13,5},{2,10},{6,14},... | collective-permute-start | bytes 104 | tf_op jit(solution)/shard_map/ppermute | solution.py:403
  4.7 5.6 %collective-permute-start.1 = (s32[2,4]{1,0:T(2,128)}, s32[2,4]{1,0:T(2,128)S(1)}, u32[]{:S(2)}, u32[]{:S(2)}) collective-permute-start(s32[2,4]{1,0:T(2,128)} %bitcast.16), channel_id=1, source_target_pairs={{0,12},{4,8},{8,4},{12,0},{1,13},{5,9},{9,5},{13,1},{2,14},{6,10},... | collective-permute-start | bytes 104 | tf_op jit(solution)/shard_map/ppermute | solution.py:403
  6.1 4.2 %collective-permute-start = (s32[2,4]{1,0:T(2,128)}, s32[2,4]{1,0:T(2,128)S(1)}, u32[]{:S(2)}, u32[]{:S(2)}) collective-permute-start(s32[2,4]{1,0:T(2,128)} %bitcast.17), channel_id=1, source_target_pairs={{0,4},{4,0},{8,12},{12,8},{1,5},{5,1},{9,13},{13,9},{2,6},{6,2},{1... | collective-permute-start | bytes 104 | tf_op jit(solution)/shard_map/ppermute | solution.py:403
  10.9 6.6 %collective-permute-start.3 = (bf16[2,32,128]{2,1,0:T(8,128)(2,1)S(1)}, bf16[2,32,128]{2,1,0:T(8,128)(2,1)S(1)}, u32[]{:S(2)}, u32[]{:S(2)}) collective-permute-start(bf16[2,32,128]{2,1,0:T(8,128)(2,1)S(1)} %get-tuple-element.18), channel_id=1, source_target_pairs={{0,12},{4,8},{8,4},{12,0},{1,13},{5,9},{9,5},{13,1},{2,14},{6,10},... | collective-permute-start | bytes 49160 | tf_op jit(solution)/shard_map/ppermute | solution.py:403
  13.0 4.6 %collective-permute-start.4 = (bf16[2,32,128]{2,1,0:T(8,128)(2,1)S(1)}, bf16[2,32,128]{2,1,0:T(8,128)(2,1)S(1)}, u32[]{:S(2)}, u32[]{:S(2)}) collective-permute-start(bf16[2,32,128]{2,1,0:T(8,128)(2,1)S(1)} %get-tuple-element.19), channel_id=1, source_target_pairs={{0,8},{4,12},{8,0},{12,4},{1,9},{5,13},{9,1},{13,5},{2,10},{6,14},... | collective-permute-start | bytes 49160 | tf_op jit(solution)/shard_map/ppermute | solution.py:403
  13.0 4.6 %collective-permute-start.5 = (bf16[2,32,128]{2,1,0:T(8,128)(2,1)S(1)}, bf16[2,32,128]{2,1,0:T(8,128)(2,1)S(1)}, u32[]{:S(2)}, u32[]{:S(2)}) collective-permute-start(bf16[2,32,128]{2,1,0:T(8,128)(2,1)S(1)} %get-tuple-element.20), channel_id=1, source_target_pairs={{0,4},{4,0},{8,12},{12,8},{1,5},{5,1},{9,13},{13,9},{2,6},{6,2},{1... | collective-permute-start | bytes 49160 | tf_op jit(solution)/shard_map/ppermute | solution.py:403
  15.4 12.4 %copy-start = (bf16[128,128]{1,0:T(8,128)(2,1)S(1)}, bf16[128,128]{1,0:T(8,128)(2,1)}, u32[]{:S(2)}) copy-start(bf16[128,128]{1,0:T(8,128)(2,1)} %constant.11.clone.refs_6_) | copy-start | bytes 98308
  15.4 12.4 %copy-start.1 = (bf16[128,128]{1,0:T(8,128)(2,1)S(1)}, bf16[128,128]{1,0:T(8,128)(2,1)}, u32[]{:S(2)}) copy-start(bf16[128,128]{1,0:T(8,128)(2,1)} %constant.10.clone.refs_5_) | copy-start | bytes 98308
  21.0 4.9 %collective-permute-start.6 = (bf16[400,128]{1,0:T(8,128)(2,1)S(1)}, bf16[400,128]{1,0:T(8,128)(2,1)S(1)}, u32[]{:S(2)}, u32[]{:S(2)}) collective-permute-start(bf16[400,128]{1,0:T(8,128)(2,1)S(1)} %get-tuple-element.21), channel_id=1, source_target_pairs={{0,2},{1,3},{2,0},{3,1},{4,6},{5,7},{6,4},{7,5},{8,10},{9,11},{10,... | collective-permute-start | bytes 307208 | tf_op jit(solution)/shard_map/ppermute | solution.py:403
  22.6 5.2 %collective-permute-start.7 = (bf16[400,128]{1,0:T(8,128)(2,1)S(1)}, bf16[400,128]{1,0:T(8,128)(2,1)S(1)}, u32[]{:S(2)}, u32[]{:S(2)}) collective-permute-start(bf16[400,128]{1,0:T(8,128)(2,1)S(1)} %get-tuple-element.22), channel_id=1, source_target_pairs={{0,3},{1,2},{2,1},{3,0},{4,7},{5,6},{6,5},{7,4},{8,11},{9,10},{10,... | collective-permute-start | bytes 307208 | tf_op jit(solution)/shard_map/ppermute | solution.py:403
  22.6 5.2 %collective-permute-start.8 = (bf16[400,128]{1,0:T(8,128)(2,1)S(1)}, bf16[400,128]{1,0:T(8,128)(2,1)S(1)}, u32[]{:S(2)}, u32[]{:S(2)}) collective-permute-start(bf16[400,128]{1,0:T(8,128)(2,1)S(1)} %get-tuple-element.23), channel_id=1, source_target_pairs={{0,1},{1,0},{2,3},{3,2},{4,5},{5,4},{6,7},{7,6},{8,9},{9,8},{10,11... | collective-permute-start | bytes 307208 | tf_op jit(solution)/shard_map/ppermute | solution.py:403

commit v8 on v7

--- a/solution.py
+++ b/solution.py
@@ -16,6 +16,7 @@
 LENGTH = SEGS * STEPS
 GROUP = 4
 HEAD = 16
+PITCH = STEPS + 1
 CHUNKS = 8
 UNROLL = 4
 
@@ -78,8 +79,8 @@
 
 def prepare_kernel(
     fresh_ref, reads_hbm, state_hbm, lesion_hbm, stim_hbm, wave_hbm, slot_hbm, target_hbm,
-    delay_hbm, lanes_hbm, table_hbm, older_hbm, weights_hbm,
-    weights_out, ready_out, hist_out, tiles_out, head_out,
+    delay_hbm, lanes_hbm, table_hbm, older_hbm, frac_hbm, weights_hbm,
+    weights_out, ready_out, hist_out, tiles_out, fracs_out, head_out,
     reads, state, lesion, stim, wave, slot, target, delay, lanes, table, older, sems,
     *, peers, own_blocks, peer_targets, capacity,
 ):
@@ -87,6 +88,7 @@
         (reads_hbm, reads), (target_hbm, target), (slot_hbm, slot),
         (delay_hbm, delay), (lanes_hbm, lanes), (table_hbm, table), (older_hbm, older),
         (state_hbm, state), (lesion_hbm, lesion), (stim_hbm, stim), (wave_hbm, wave),
+        (frac_hbm, fracs_out),
     ]
     copies = [
         pltpu.make_async_copy(source, into, sems.at[i]) for i, (source, into) in enumerate(pairs)
@@ -217,7 +219,7 @@
 
 
 def tract_kernel(
-    frac_hbm, tiles_ref, table_ref, head_ref, weights, hist_ref, *refs,
+    fracs_ref, tiles_ref, table_ref, head_ref, weights, hist_ref, *refs,
     wide_peers, peers, capacity, peer_targets,
 ):
     news = refs[: wide_peers - 1]
@@ -227,7 +229,7 @@
     owner = lax.axis_index("wide")
     copies = [
         pltpu.make_async_copy(tiles_ref, tiles, sems.at[0]),
-        pltpu.make_async_copy(frac_hbm, frac, sems.at[1]),
+        pltpu.make_async_copy(fracs_ref, frac, sems.at[1]),
     ]
     for copy in copies:
         copy.start()
@@ -244,20 +246,26 @@
 
     span = peer_targets * TOGETHER
     pitch = peers * span
-    for turn in range(0, frac.shape[1], UNROLL):
+    block_rows = weights.shape[2]
+    for turn in range(0, weights.shape[0], UNROLL):
         sums = []
-        for t in range(turn, turn + UNROLL):
-            fraction = frac[0, t]
-            start = tiles[0, t]
-            earlier = hist[pl.ds(start, STEPS), :]
-            later = hist[pl.ds(start + 1, STEPS), :]
-            delayed = ((1.0 - fraction) * later + fraction * earlier).astype(jnp.bfloat16)
-            sums.append(
-                lax.dot_general(
-                    delayed, weights[t], (((1,), (1,)), ((), ())),
-                    preferred_element_type=jnp.float32,
+        for t in range(turn, turn + UNROLL, 2):
+            both = []
+            for u in (t, t + 1):
+                fraction = frac[0, u]
+                start = tiles[0, u]
+                earlier = hist[pl.ds(start, STEPS), :]
+                later = hist[pl.ds(start + 1, STEPS), :]
+                both.append(
+                    ((1.0 - fraction) * later + fraction * earlier).astype(jnp.bfloat16)
                 )
+            product = lax.dot_general(
+                jnp.concatenate(both, axis=0),
+                weights[t : t + 2].reshape(2 * block_rows, block_rows),
+                (((1,), (1,)), ((), ())),
+                preferred_element_type=jnp.float32,
             )
+            sums += [product[:STEPS, :block_rows], product[STEPS:, block_rows:]]
         for t in range(turn, turn + UNROLL):
             first = tiles[1, t]
             for g in range(STEPS // TOGETHER):
@@ -330,7 +338,7 @@
             inhibit = ((1 - inhibit_rate) * inhibit + inhibit_rate / 2) + (
                 inhibit_rate / 2
             ) * inhibit_turn
-            samples[pl.ds(j, own_blocks, stride=STEPS), :] = carried * (1 / a)
+            samples[pl.ds(j, own_blocks, stride=PITCH), :] = carried * (1 / a)
     rates[0] = carried * (1 / a)
     rates[1] = inhibit
     for b in range(own_blocks):
@@ -342,10 +350,18 @@
 
     high = high_ref[...]
     low = low_ref[...]
-    rows = GROUP * STEPS
     for g in range(0, own_blocks // GROUP, 2):
         part = jnp.concatenate(
-            [samples[g * rows : (g + 1) * rows, :], samples[(g + 1) * rows : (g + 2) * rows, :]],
+            [
+                jnp.concatenate(
+                    [
+                        samples[b * PITCH : b * PITCH + STEPS, :]
+                        for b in range((g + i) * GROUP, (g + i + 1) * GROUP)
+                    ],
+                    axis=0,
+                )
+                for i in range(2)
+            ],
             axis=1,
         )
         part_high = part.astype(jnp.bfloat16)
@@ -428,7 +444,7 @@
         compiler_params=params(),
         name="fresh_near",
     )(far(fresh_coefs))
-    weights, ready, hist, tiles, heads = pl.pallas_call(
+    weights, ready, hist, tiles, fracs, heads = pl.pallas_call(
         functools.partial(
             prepare_kernel,
             peers=peers, own_blocks=own_blocks, peer_targets=peer_targets, capacity=capacity,
@@ -438,14 +454,15 @@
             pltpu.VMEM((4 * own_blocks + STEPS, block_rows), jnp.float32),
             pltpu.VMEM((slot_count * LENGTH, block_rows), jnp.float32),
             pltpu.VMEM((8, 128), jnp.int32),
+            pltpu.VMEM((1, tile_count), jnp.float32),
             pltpu.VMEM((peers, HEAD, 128), jnp.bfloat16),
         ],
-        in_specs=[vmem_spec] + [hbm_spec] * 12,
-        out_specs=[vmem_spec] * 5,
+        in_specs=[vmem_spec] + [hbm_spec] * 13,
+        out_specs=[vmem_spec] * 6,
         scratch_shapes=[
             SMEM((capacity, wide_peers), jnp.int32),
             *vmem_inputs,
-            pltpu.SemaphoreType.DMA((11 + CHUNKS,)),
+            pltpu.SemaphoreType.DMA((12 + CHUNKS,)),
         ],
         compiler_params=params(),
         name="prepare",
@@ -462,6 +479,7 @@
         far(jnp.asarray(lane_tables(peers, peer_targets, own_blocks))),
         table,
         far(older_coefs.reshape(slot_count, HSEG, coef_count, block_rows)),
+        far(tract_frac.reshape(1, tile_count)),
         far(tract_weights.reshape(tile_count, block_rows, block_rows)),
     )
 
@@ -486,7 +504,7 @@
             wide_peers=wide_peers, peers=peers, capacity=capacity, peer_targets=peer_targets,
         ),
         out_shape=[pltpu.VMEM((share_rows, block_rows), jnp.bfloat16)] * peers,
-        in_specs=[hbm_spec] + [vmem_spec] * (4 + wide_peers),
+        in_specs=[vmem_spec] * (5 + wide_peers),
         out_specs=[vmem_spec] * peers,
         scratch_shapes=[
             SMEM((8, 128), jnp.int32),
@@ -497,7 +515,7 @@
         ],
         compiler_params=params(),
         name="tract_tiles",
-    )(far(tract_frac.reshape(1, tile_count)), tiles, table, heads, weights, hist, *news)
+    )(fracs, tiles, table, heads, weights, hist, *news)
     order = [*range(2, peers), 1, 0]
     arrived = [swap(shares[r], "narrow", r) if r else shares[r] for r in order]
 
@@ -514,7 +532,7 @@
         in_specs=[vmem_spec] * (peers + 3),
         out_specs=[hbm_spec] * 2,
         scratch_shapes=[
-            VMEM((own_blocks * STEPS, block_rows), jnp.float32),
+            VMEM((own_blocks * PITCH, block_rows), jnp.float32),
             VMEM((2, own_blocks, block_rows), jnp.float32),
             VMEM(fresh_coefs.shape, jnp.bfloat16),
             VMEM(state.shape, jnp.float32),

time: 30 us -> 29.1 us (0.970)
  Pallas kernels: 9.13 us -> 8.21 us
    pallas_call x1, Pallas kernels: 3.36 us -> 2.76 us  [local(): pl.pallas_call(functools.partial(tract_kernel, wide_peers=wide_peers, pee...]
    pallas_call x1, Pallas kernels: 2.02 us -> 1.69 us  [local(): pl.pallas_call(functools.partial(window_kernel, peers=peers, own_blocks=o...]
where the time goes in v8:
time: 29.1 us; the launch traced here: 28.9 us
  starting transfers between devices  12.3 us (42%)
  Pallas kernels  8.21 us (28%)
  waiting for transfers between devices  7.62 us (26%)
  between operations  0.69 us (2%)
    ppermute x9, starting transfers between devices, swap(): lax.ppermute(x, axis, [(i, i ^ r) for i in range(lax.axis_size(axis))])  12.3 us
    ppermute x9, waiting for transfers between devices, swap(): lax.ppermute(x, axis, [(i, i ^ r) for i in range(lax.axis_size(axis))])  7.62 us
    pallas_call x1, Pallas kernels, local(): pl.pallas_call(functools.partial(tract_kernel, wide_peers=wide_peers, pee...  2.76 us
    pallas_call x1, Pallas kernels, local(): pl.pallas_call(functools.partial(prepare_kernel, peers=peers, own_blocks=...  2.19 us
    pallas_call x1, Pallas kernels, local(): pl.pallas_call(functools.partial(window_kernel, peers=peers, own_blocks=o...  1.69 us
    pallas_call x1, Pallas kernels, local(): pl.pallas_call(fresh_kernel, out_shape=pltpu.VMEM(fresh_coefs.shape, jnp....  0.96 us
    pallas_call x1, Pallas kernels, local(): pl.pallas_call(functools.partial(pick_kernel, capacity=capacity, peers=wi...  0.62 us
  transfers between devices with their start and end apart: 9, of which 4 were waited for; matrix products, arithmetic and copies ran while one was open for 0% of the time, Pallas kernels for 11%

profile of v8, /device:TPU:0, one launch (start us, length us, event | category | flops | bytes accessed | tf_op | source)
XLA Modules:
  0.0 28.9 jit_solution(3165330882288302488)
XLA Ops:
  0.6 4.1 %collective-permute-start.2 = (s32[2,4]{1,0:T(2,128)}, s32[2,4]{1,0:T(2,128)S(1)}, u32[]{:S(2)}, u32[]{:S(2)}) collective-permute-start(s32[2,4]{1,0:T(2,128)} %bitcast.15), channel_id=1, source_target_pairs={{0,8},{4,12},{8,0},{12,4},{1,9},{5,13},{9,1},{13,5},{2,10},{6,14},... | collective-permute-start | bytes 104 | tf_op jit(solution)/shard_map/ppermute | solution.py:419
  4.7 1.3 %collective-permute-start.1 = (s32[2,4]{1,0:T(2,128)}, s32[2,4]{1,0:T(2,128)S(1)}, u32[]{:S(2)}, u32[]{:S(2)}) collective-permute-start(s32[2,4]{1,0:T(2,128)} %bitcast.16), channel_id=1, source_target_pairs={{0,12},{4,8},{8,4},{12,0},{1,13},{5,9},{9,5},{13,1},{2,14},{6,10},... | collective-permute-start | bytes 104 | tf_op jit(solution)/shard_map/ppermute | solution.py:419
  6.1 0.2 collective-permute-start
  6.3 1.0 %fresh_near.1.fresh_ref.refs_3_ = bf16[32,32,128]{2,1,0:T(8,128)(2,1)S(1)} custom-call(bf16[32,32,128]{2,1,0:T(8,128)(2,1)} %fresh_hbm.1), custom_call_target="tpu_custom_call" | custom-call | tf_op jit(solution)/shard_map/fresh_near/pallas_call | solution.py:438
  7.3 0.0 collective-permute-done.2.refs_2_
  7.3 3.0 %collective-permute-done.1.refs_1_ = s32[2,4]{1,0:T(2,128)S(1)} collective-permute-done((s32[2,4]{1,0:T(2,128)}, s32[2,4]{1,0:T(2,128)S(1)}, u32[]{:S(2)}, u32[]{:S(2)}) %collective-permute-start.1) | collective-permute-done | bytes 64 | tf_op jit(solution)/shard_map/ppermute | solution.py:419
  10.3 0.0 collective-permute-done.refs_0_
  10.3 0.6 %pick_blocks.1 = (bf16[2,32,128]{2,1,0:T(8,128)(2,1)S(1)}, bf16[2,32,128]{2,1,0:T(8,128)(2,1)S(1)}, bf16[2,32,128]{2,1,0:T(8,128)(2,1)S(1)}) custom-call(s32[2,4]{1,0:T(2,128)S(1)} %collective-permute-done.refs_0_, s32[2,4]{1,0:T(2,128)S(1)} %collective-permute-done.1.refs_1_, s32[2,4]{1,0:T(2,128)S(1)} %collective-permute-done.2.refs_2_, ...), custom_call_target="tpu_custom_call" | custom-call | tf_op jit(solution)/shard_map/pick_blocks/pallas_call | solution.py:486
  10.9 2.1 %collective-permute-start.3 = (bf16[2,32,128]{2,1,0:T(8,128)(2,1)S(1)}, bf16[2,32,128]{2,1,0:T(8,128)(2,1)S(1)}, u32[]{:S(2)}, u32[]{:S(2)}) collective-permute-start(bf16[2,32,128]{2,1,0:T(8,128)(2,1)S(1)} %get-tuple-element.20), channel_id=1, source_target_pairs={{0,12},{4,8},{8,4},{12,0},{1,13},{5,9},{9,5},{13,1},{2,14},{6,10},... | collective-permute-start | bytes 49160 | tf_op jit(solution)/shard_map/ppermute | solution.py:419
  13.0 0.0 collective-permute-start.4
  13.0 2.4 %collective-permute-start.5 = (bf16[2,32,128]{2,1,0:T(8,128)(2,1)S(1)}, bf16[2,32,128]{2,1,0:T(8,128)(2,1)S(1)}, u32[]{:S(2)}, u32[]{:S(2)}) collective-permute-start(bf16[2,32,128]{2,1,0:T(8,128)(2,1)S(1)} %get-tuple-element.22), channel_id=1, source_target_pairs={{0,4},{4,0},{8,12},{12,8},{1,5},{5,1},{9,13},{13,9},{2,6},{6,2},{1... | collective-permute-start | bytes 49160 | tf_op jit(solution)/shard_map/ppermute | solution.py:419
  15.4 0.0 copy-start
  15.4 0.0 copy-start.1
  15.4 2.2 %prepare.1 = (bf16[96,128,128]{2,1,0:T(8,128)(2,1)S(1)}, f32[160,128]{1,0:T(8,128)S(1)}, f32[768,128]{1,0:T(8,128)S(1)}, s32[8,128]{1,0:T(8,128)S(1)}, f32[1,96]...) custom-call(bf16[32,32,128]{2,1,0:T(8,128)(2,1)S(1)} %fresh_near.1.fresh_ref.refs_3_, s32[2,4]{1,0:T(2,128)} %bitcast.18, ...), custom_call_target="tpu_custom_call" | custom-call | tf_op jit(solution)/shard_map/prepare/pallas_call | solution.py:447
  17.6 0.0 collective-permute-done.3.refs_0_
  17.6 0.1 collective-permute-done.4.refs_1_
  17.7 0.0 collective-permute-done.5.refs_2_
  17.7 2.8 %tract_tiles.1 = (bf16[400,128]{1,0:T(8,128)(2,1)S(1)}, bf16[400,128]{1,0:T(8,128)(2,1)S(1)}, bf16[400,128]{1,0:T(8,128)(2,1)S(1)}, bf16[400,128]{1,0:T(8,128)(2,1)S(1)}) custom-call(f32[1,96]{1,0:T(1,128)S(1)} %get-tuple-element.15.fracs_ref, s32[8,128]{1,0:T(8,128)S(1)} %get-tuple-element.16.tiles_ref, bf16[96,96]{1,0:T(8,128)(2,1)} %constant.8.clone.table_hbm.table_ref, ...), custom_call_target="tpu_custom_call" | custom-call | tf_op jit(solution)/shard_map/tract_tiles/pallas_call | solution.py:501
  20.4 1.6 %collective-permute-start.6 = (bf16[400,128]{1,0:T(8,128)(2,1)S(1)}, bf16[400,128]{1,0:T(8,128)(2,1)S(1)}, u32[]{:S(2)}, u32[]{:S(2)}) collective-permute-start(bf16[400,128]{1,0:T(8,128)(2,1)S(1)} %get-tuple-element.23), channel_id=1, source_target_pairs={{0,2},{1,3},{2,0},{3,1},{4,6},{5,7},{6,4},{7,5},{8,10},{9,11},{10,... | collective-permute-start | bytes 307208 | tf_op jit(solution)/shard_map/ppermute | solution.py:419
  22.0 0.0 collective-permute-start.7
  22.0 0.6 %collective-permute-start.8 = (bf16[400,128]{1,0:T(8,128)(2,1)S(1)}, bf16[400,128]{1,0:T(8,128)(2,1)S(1)}, u32[]{:S(2)}, u32[]{:S(2)}) collective-permute-start(bf16[400,128]{1,0:T(8,128)(2,1)S(1)} %get-tuple-element.25), channel_id=1, source_target_pairs={{0,1},{1,0},{2,3},{3,2},{4,5},{5,4},{6,7},{7,6},{8,9},{9,8},{10,11... | collective-permute-start | bytes 307208 | tf_op jit(solution)/shard_map/ppermute | solution.py:419
  22.6 2.7 %collective-permute-done.6.refs_0_ = bf16[400,128]{1,0:T(8,128)(2,1)S(1)} collective-permute-done((bf16[400,128]{1,0:T(8,128)(2,1)S(1)}, bf16[400,128]{1,0:T(8,128)(2,1)S(1)}, u32[]{:S(2)}, u32[]{:S(2)}) %collective-permute-start.6) | collective-permute-done | bytes 102432 | tf_op jit(solution)/shard_map/ppermute | solution.py:419
  25.3 1.8 %collective-permute-done.7.refs_1_ = bf16[400,128]{1,0:T(8,128)(2,1)S(1)} collective-permute-done((bf16[400,128]{1,0:T(8,128)(2,1)S(1)}, bf16[400,128]{1,0:T(8,128)(2,1)S(1)}, u32[]{:S(2)}, u32[]{:S(2)}) %collective-permute-start.7) | collective-permute-done | bytes 102432 | tf_op jit(solution)/shard_map/ppermute | solution.py:419
  27.2 0.0 collective-permute-done.8.refs_2_
  27.2 0.0 copy-done
  27.2 0.0 copy-done.1
  27.2 1.7 %window_steps.1 = (bf16[32,32,128]{2,1,0:T(8,128)(2,1)}, f32[2,4096]{1,0:T(2,128)}) custom-call(bf16[400,128]{1,0:T(8,128)(2,1)S(1)} %collective-permute-done.6.refs_0_, bf16[400,128]{1,0:T(8,128)(2,1)S(1)} %collective-permute-done.7.refs_1_, bf16[400,128]{1,0:T(8,128)(2,1)S(1)} %collective-permute-done.8.refs_2_, ...), custom_call_target="tpu_custom_call" | custom-call | tf_op jit(solution)/shard_map/window_steps/pallas_call | solution.py:523
Async XLA Ops:
  0.6 6.7 %collective-permute-start.2 = (s32[2,4]{1,0:T(2,128)}, s32[2,4]{1,0:T(2,128)S(1)}, u32[]{:S(2)}, u32[]{:S(2)}) collective-permute-start(s32[2,4]{1,0:T(2,128)} %bitcast.15), channel_id=1, source_target_pairs={{0,8},{4,12},{8,0},{12,4},{1,9},{5,13},{9,1},{13,5},{2,10},{6,14},... | collective-permute-start | bytes 104 | tf_op jit(solution)/shard_map/ppermute | solution.py:419
  4.7 5.6 %collective-permute-start.1 = (s32[2,4]{1,0:T(2,128)}, s32[2,4]{1,0:T(2,128)S(1)}, u32[]{:S(2)}, u32[]{:S(2)}) collective-permute-start(s32[2,4]{1,0:T(2,128)} %bitcast.16), channel_id=1, source_target_pairs={{0,12},{4,8},{8,4},{12,0},{1,13},{5,9},{9,5},{13,1},{2,14},{6,10},... | collective-permute-start | bytes 104 | tf_op jit(solution)/shard_map/ppermute | solution.py:419
  6.1 4.2 %collective-permute-start = (s32[2,4]{1,0:T(2,128)}, s32[2,4]{1,0:T(2,128)S(1)}, u32[]{:S(2)}, u32[]{:S(2)}) collective-permute-start(s32[2,4]{1,0:T(2,128)} %bitcast.17), channel_id=1, source_target_pairs={{0,4},{4,0},{8,12},{12,8},{1,5},{5,1},{9,13},{13,9},{2,6},{6,2},{1... | collective-permute-start | bytes 104 | tf_op jit(solution)/shard_map/ppermute | solution.py:419
  10.9 6.7 %collective-permute-start.3 = (bf16[2,32,128]{2,1,0:T(8,128)(2,1)S(1)}, bf16[2,32,128]{2,1,0:T(8,128)(2,1)S(1)}, u32[]{:S(2)}, u32[]{:S(2)}) collective-permute-start(bf16[2,32,128]{2,1,0:T(8,128)(2,1)S(1)} %get-tuple-element.20), channel_id=1, source_target_pairs={{0,12},{4,8},{8,4},{12,0},{1,13},{5,9},{9,5},{13,1},{2,14},{6,10},... | collective-permute-start | bytes 49160 | tf_op jit(solution)/shard_map/ppermute | solution.py:419
  13.0 4.6 %collective-permute-start.4 = (bf16[2,32,128]{2,1,0:T(8,128)(2,1)S(1)}, bf16[2,32,128]{2,1,0:T(8,128)(2,1)S(1)}, u32[]{:S(2)}, u32[]{:S(2)}) collective-permute-start(bf16[2,32,128]{2,1,0:T(8,128)(2,1)S(1)} %get-tuple-element.21), channel_id=1, source_target_pairs={{0,8},{4,12},{8,0},{12,4},{1,9},{5,13},{9,1},{13,5},{2,10},{6,14},... | collective-permute-start | bytes 49160 | tf_op jit(solution)/shard_map/ppermute | solution.py:419
  13.0 4.6 %collective-permute-start.5 = (bf16[2,32,128]{2,1,0:T(8,128)(2,1)S(1)}, bf16[2,32,128]{2,1,0:T(8,128)(2,1)S(1)}, u32[]{:S(2)}, u32[]{:S(2)}) collective-permute-start(bf16[2,32,128]{2,1,0:T(8,128)(2,1)S(1)} %get-tuple-element.22), channel_id=1, source_target_pairs={{0,4},{4,0},{8,12},{12,8},{1,5},{5,1},{9,13},{13,9},{2,6},{6,2},{1... | collective-permute-start | bytes 49160 | tf_op jit(solution)/shard_map/ppermute | solution.py:419
  15.4 11.8 %copy-start = (bf16[128,128]{1,0:T(8,128)(2,1)S(1)}, bf16[128,128]{1,0:T(8,128)(2,1)}, u32[]{:S(2)}) copy-start(bf16[128,128]{1,0:T(8,128)(2,1)} %constant.11.clone.refs_6_) | copy-start | bytes 98308
  15.4 11.8 %copy-start.1 = (bf16[128,128]{1,0:T(8,128)(2,1)S(1)}, bf16[128,128]{1,0:T(8,128)(2,1)}, u32[]{:S(2)}) copy-start(bf16[128,128]{1,0:T(8,128)(2,1)} %constant.10.clone.refs_5_) | copy-start | bytes 98308
  20.4 4.9 %collective-permute-start.6 = (bf16[400,128]{1,0:T(8,128)(2,1)S(1)}, bf16[400,128]{1,0:T(8,128)(2,1)S(1)}, u32[]{:S(2)}, u32[]{:S(2)}) collective-permute-start(bf16[400,128]{1,0:T(8,128)(2,1)S(1)} %get-tuple-element.23), channel_id=1, source_target_pairs={{0,2},{1,3},{2,0},{3,1},{4,6},{5,7},{6,4},{7,5},{8,10},{9,11},{10,... | collective-permute-start | bytes 307208 | tf_op jit(solution)/shard_map/ppermute | solution.py:419
  22.0 5.2 %collective-permute-start.7 = (bf16[400,128]{1,0:T(8,128)(2,1)S(1)}, bf16[400,128]{1,0:T(8,128)(2,1)S(1)}, u32[]{:S(2)}, u32[]{:S(2)}) collective-permute-start(bf16[400,128]{1,0:T(8,128)(2,1)S(1)} %get-tuple-element.24), channel_id=1, source_target_pairs={{0,3},{1,2},{2,1},{3,0},{4,7},{5,6},{6,5},{7,4},{8,11},{9,10},{10,... | collective-permute-start | bytes 307208 | tf_op jit(solution)/shard_map/ppermute | solution.py:419
  22.0 5.2 %collective-permute-start.8 = (bf16[400,128]{1,0:T(8,128)(2,1)S(1)}, bf16[400,128]{1,0:T(8,128)(2,1)S(1)}, u32[]{:S(2)}, u32[]{:S(2)}) collective-permute-start(bf16[400,128]{1,0:T(8,128)(2,1)S(1)} %get-tuple-element.25), channel_id=1, source_target_pairs={{0,1},{1,0},{2,3},{3,2},{4,5},{5,4},{6,7},{7,6},{8,9},{9,8},{10,11... | collective-permute-start | bytes 307208 | tf_op jit(solution)/shard_map/ppermute | solution.py:419

commit v9 on v8

--- a/solution.py
+++ b/solution.py
@@ -51,7 +51,7 @@
     return table
 
 
-def fit_tables(coef_count):
+def fit_table(coef_count):
     scales = np.where(np.arange(coef_count)[:, None] == 0, 1.0, 2.0) / STEPS
     fit = (basis_table(coef_count, STEPS) * scales).astype(np.float32)
     whole = np.zeros((GROUP * coef_count, GROUP * STEPS), np.float32)
@@ -59,7 +59,7 @@
         whole[g * coef_count : (g + 1) * coef_count, g * STEPS : (g + 1) * STEPS] = fit
     high = whole.astype(ml_dtypes.bfloat16)
     low = (whole - high.astype(np.float32)).astype(ml_dtypes.bfloat16)
-    return high, low
+    return np.concatenate([high, high, low], axis=1)
 
 
 TOGETHER = 8
@@ -248,24 +248,32 @@
     pitch = peers * span
     block_rows = weights.shape[2]
     for turn in range(0, weights.shape[0], UNROLL):
-        sums = []
-        for t in range(turn, turn + UNROLL, 2):
-            both = []
-            for u in (t, t + 1):
-                fraction = frac[0, u]
-                start = tiles[0, u]
-                earlier = hist[pl.ds(start, STEPS), :]
-                later = hist[pl.ds(start + 1, STEPS), :]
-                both.append(
-                    ((1.0 - fraction) * later + fraction * earlier).astype(jnp.bfloat16)
-                )
-            product = lax.dot_general(
-                jnp.concatenate(both, axis=0),
-                weights[t : t + 2].reshape(2 * block_rows, block_rows),
-                (((1,), (1,)), ((), ())),
-                preferred_element_type=jnp.float32,
-            )
-            sums += [product[:STEPS, :block_rows], product[STEPS:, block_rows:]]
+        rows = []
+        for t in range(turn, turn + UNROLL):
+            fraction = frac[0, t]
+            start = tiles[0, t]
+            earlier = hist[pl.ds(start, STEPS), :]
+            later = hist[pl.ds(start + 1, STEPS), :]
+            rows.append(((1.0 - fraction) * later + fraction * earlier).astype(jnp.bfloat16))
+        none = jnp.zeros((2 * STEPS, block_rows), jnp.bfloat16)
+        left = jnp.concatenate([*rows[:2], none], axis=0)
+        right = jnp.concatenate([none, *rows[2:]], axis=0)
+        product = lax.dot_general(
+            jnp.concatenate([left, right], axis=1),
+            jnp.concatenate(
+                [
+                    weights[t : t + 2].reshape(2 * block_rows, block_rows)
+                    for t in (turn, turn + 2)
+                ],
+                axis=1,
+            ),
+            (((1,), (1,)), ((), ())),
+            preferred_element_type=jnp.float32,
+        )
+        sums = [
+            product[i * STEPS : (i + 1) * STEPS, i % 2 * block_rows : (i % 2 + 1) * block_rows]
+            for i in range(UNROLL)
+        ]
         for t in range(turn, turn + UNROLL):
             first = tiles[1, t]
             for g in range(STEPS // TOGETHER):
@@ -284,7 +292,7 @@
 def window_kernel(*refs, peers, own_blocks, peer_targets, coef_count):
     shares = dict(zip([*range(2, peers), 1, 0], refs))
     (
-        ready_ref, high_ref, low_ref, coefs_hbm, state_hbm, samples, rates, coefs, state, sems,
+        ready_ref, fit_ref, coefs_hbm, state_hbm, samples, rates, coefs, state, sems,
     ) = refs[peers:]
     block_rows = ready_ref.shape[1]
     width = TOGETHER * peer_targets
@@ -348,8 +356,7 @@
     copies = [pltpu.make_async_copy(state, state_hbm, sems.at[0])]
     copies[0].start()
 
-    high = high_ref[...]
-    low = low_ref[...]
+    fit = fit_ref[...]
     for g in range(0, own_blocks // GROUP, 2):
         part = jnp.concatenate(
             [
@@ -366,10 +373,9 @@
         )
         part_high = part.astype(jnp.bfloat16)
         part_low = (part - part_high.astype(jnp.float32)).astype(jnp.bfloat16)
-        fitted = (
-            jnp.dot(high, part_high, preferred_element_type=jnp.float32)
-            + jnp.dot(high, part_low, preferred_element_type=jnp.float32)
-            + jnp.dot(low, part_high, preferred_element_type=jnp.float32)
+        fitted = jnp.dot(
+            fit, jnp.concatenate([part_high, part_low, part_high], axis=0),
+            preferred_element_type=jnp.float32,
         ).astype(jnp.bfloat16)
         for i in range(2):
             coefs[(g + i) * GROUP : (g + i + 1) * GROUP] = fitted[
@@ -453,7 +459,7 @@
             pltpu.VMEM((tile_count, block_rows, block_rows), jnp.bfloat16),
             pltpu.VMEM((4 * own_blocks + STEPS, block_rows), jnp.float32),
             pltpu.VMEM((slot_count * LENGTH, block_rows), jnp.float32),
-            pltpu.VMEM((8, 128), jnp.int32),
+            pltpu.VMEM((2, 128), jnp.int32),
             pltpu.VMEM((1, tile_count), jnp.float32),
             pltpu.VMEM((peers, HEAD, 128), jnp.bfloat16),
         ],
@@ -507,7 +513,7 @@
         in_specs=[vmem_spec] * (5 + wide_peers),
         out_specs=[vmem_spec] * peers,
         scratch_shapes=[
-            SMEM((8, 128), jnp.int32),
+            SMEM((2, 128), jnp.int32),
             SMEM((1, tile_count), jnp.float32),
             VMEM((slot_count * LENGTH, block_rows), jnp.float32),
             VMEM((peers * peer_targets * STEPS, block_rows), jnp.float32),
@@ -519,7 +525,6 @@
     order = [*range(2, peers), 1, 0]
     arrived = [swap(shares[r], "narrow", r) if r else shares[r] for r in order]
 
-    high, low = fit_tables(coef_count)
     new_coefs, final_state = pl.pallas_call(
         functools.partial(
             window_kernel,
@@ -529,7 +534,7 @@
             jax.ShapeDtypeStruct(fresh_coefs.shape, jnp.bfloat16),
             jax.ShapeDtypeStruct(state.shape, jnp.float32),
         ],
-        in_specs=[vmem_spec] * (peers + 3),
+        in_specs=[vmem_spec] * (peers + 2),
         out_specs=[hbm_spec] * 2,
         scratch_shapes=[
             VMEM((own_blocks * PITCH, block_rows), jnp.float32),
@@ -540,7 +545,7 @@
         ],
         compiler_params=params(),
         name="window_steps",
-    )(*arrived, ready, high, low)
+    )(*arrived, ready, jnp.asarray(fit_table(coef_count)))
     return new_coefs, final_state
 
 

time: 29.1 us -> 28.9 us (level)
  transfers between devices with their start and end apart: 9 -> 9, of which waited for: 4 -> 3; matrix products, arithmetic and copies ran while one was open for 0% -> 0% of each run, Pallas kernels for 11% -> 11%
where the time goes in v9:
time: 28.9 us; the launch traced here: 28.7 us
  starting transfers between devices  12.3 us (43%)
  Pallas kernels  8.08 us (28%)
  waiting for transfers between devices  7.58 us (26%)
  between operations  0.69 us (2%)
    ppermute x9, starting transfers between devices, swap(): lax.ppermute(x, axis, [(i, i ^ r) for i in range(lax.axis_size(axis))])  12.3 us
    ppermute x9, waiting for transfers between devices, swap(): lax.ppermute(x, axis, [(i, i ^ r) for i in range(lax.axis_size(axis))])  7.58 us
    pallas_call x1, Pallas kernels, local(): pl.pallas_call(functools.partial(tract_kernel, wide_peers=wide_peers, pee...  2.66 us
    pallas_call x1, Pallas kernels, local(): pl.pallas_call(functools.partial(prepare_kernel, peers=peers, own_blocks=...  2.21 us
    pallas_call x1, Pallas kernels, local(): pl.pallas_call(functools.partial(window_kernel, peers=peers, own_blocks=o...  1.64 us
    pallas_call x1, Pallas kernels, local(): pl.pallas_call(fresh_kernel, out_shape=pltpu.VMEM(fresh_coefs.shape, jnp....  0.96 us
    pallas_call x1, Pallas kernels, local(): pl.pallas_call(functools.partial(pick_kernel, capacity=capacity, peers=wi...  0.62 us
  transfers between devices with their start and end apart: 9, of which 3 were waited for; matrix products, arithmetic and copies ran while one was open for 0% of the time, Pallas kernels for 11%

profile of v9, /device:TPU:0, one launch (start us, length us, event | category | flops | bytes accessed | tf_op | source)
XLA Modules:
  0.0 28.7 jit_solution(12143114069550774914)
XLA Ops:
  0.6 4.1 %collective-permute-start.2 = (s32[2,4]{1,0:T(2,128)}, s32[2,4]{1,0:T(2,128)S(1)}, u32[]{:S(2)}, u32[]{:S(2)}) collective-permute-start(s32[2,4]{1,0:T(2,128)} %bitcast.15), channel_id=1, source_target_pairs={{0,8},{4,12},{8,0},{12,4},{1,9},{5,13},{9,1},{13,5},{2,10},{6,14},... | collective-permute-start | bytes 104 | tf_op jit(solution)/shard_map/ppermute | solution.py:425
  4.7 1.3 %collective-permute-start.1 = (s32[2,4]{1,0:T(2,128)}, s32[2,4]{1,0:T(2,128)S(1)}, u32[]{:S(2)}, u32[]{:S(2)}) collective-permute-start(s32[2,4]{1,0:T(2,128)} %bitcast.16), channel_id=1, source_target_pairs={{0,12},{4,8},{8,4},{12,0},{1,13},{5,9},{9,5},{13,1},{2,14},{6,10},... | collective-permute-start | bytes 104 | tf_op jit(solution)/shard_map/ppermute | solution.py:425
  6.1 0.2 collective-permute-start
  6.3 1.0 %fresh_near.1.fresh_ref.refs_3_ = bf16[32,32,128]{2,1,0:T(8,128)(2,1)S(1)} custom-call(bf16[32,32,128]{2,1,0:T(8,128)(2,1)} %fresh_hbm.1), custom_call_target="tpu_custom_call" | custom-call | tf_op jit(solution)/shard_map/fresh_near/pallas_call | solution.py:444
  7.3 0.0 collective-permute-done.2.refs_2_
  7.3 3.0 %collective-permute-done.1.refs_1_ = s32[2,4]{1,0:T(2,128)S(1)} collective-permute-done((s32[2,4]{1,0:T(2,128)}, s32[2,4]{1,0:T(2,128)S(1)}, u32[]{:S(2)}, u32[]{:S(2)}) %collective-permute-start.1) | collective-permute-done | bytes 64 | tf_op jit(solution)/shard_map/ppermute | solution.py:425
  10.3 0.0 collective-permute-done.refs_0_
  10.3 0.6 %pick_blocks.1 = (bf16[2,32,128]{2,1,0:T(8,128)(2,1)S(1)}, bf16[2,32,128]{2,1,0:T(8,128)(2,1)S(1)}, bf16[2,32,128]{2,1,0:T(8,128)(2,1)S(1)}) custom-call(s32[2,4]{1,0:T(2,128)S(1)} %collective-permute-done.refs_0_, s32[2,4]{1,0:T(2,128)S(1)} %collective-permute-done.1.refs_1_, s32[2,4]{1,0:T(2,128)S(1)} %collective-permute-done.2.refs_2_, ...), custom_call_target="tpu_custom_call" | custom-call | tf_op jit(solution)/shard_map/pick_blocks/pallas_call | solution.py:492
  10.9 2.1 %collective-permute-start.3 = (bf16[2,32,128]{2,1,0:T(8,128)(2,1)S(1)}, bf16[2,32,128]{2,1,0:T(8,128)(2,1)S(1)}, u32[]{:S(2)}, u32[]{:S(2)}) collective-permute-start(bf16[2,32,128]{2,1,0:T(8,128)(2,1)S(1)} %get-tuple-element.20), channel_id=1, source_target_pairs={{0,12},{4,8},{8,4},{12,0},{1,13},{5,9},{9,5},{13,1},{2,14},{6,10},... | collective-permute-start | bytes 49160 | tf_op jit(solution)/shard_map/ppermute | solution.py:425
  13.0 0.0 collective-permute-start.4
  13.0 2.4 %collective-permute-start.5 = (bf16[2,32,128]{2,1,0:T(8,128)(2,1)S(1)}, bf16[2,32,128]{2,1,0:T(8,128)(2,1)S(1)}, u32[]{:S(2)}, u32[]{:S(2)}) collective-permute-start(bf16[2,32,128]{2,1,0:T(8,128)(2,1)S(1)} %get-tuple-element.22), channel_id=1, source_target_pairs={{0,4},{4,0},{8,12},{12,8},{1,5},{5,1},{9,13},{13,9},{2,6},{6,2},{1... | collective-permute-start | bytes 49160 | tf_op jit(solution)/shard_map/ppermute | solution.py:425
  15.4 0.0 copy-start
  15.4 2.2 %prepare.1 = (bf16[96,128,128]{2,1,0:T(8,128)(2,1)S(1)}, f32[160,128]{1,0:T(8,128)S(1)}, f32[768,128]{1,0:T(8,128)S(1)}, s32[2,128]{1,0:T(2,128)S(1)}, f32[1,96]...) custom-call(bf16[32,32,128]{2,1,0:T(8,128)(2,1)S(1)} %fresh_near.1.fresh_ref.refs_3_, s32[2,4]{1,0:T(2,128)} %bitcast.18, ...), custom_call_target="tpu_custom_call" | custom-call | tf_op jit(solution)/shard_map/prepare/pallas_call | solution.py:453
  17.6 0.0 collective-permute-done.3.refs_0_
  17.6 0.0 collective-permute-done.4.refs_1_
  17.7 0.0 collective-permute-done.5.refs_2_
  17.7 2.7 %tract_tiles.1 = (bf16[400,128]{1,0:T(8,128)(2,1)S(1)}, bf16[400,128]{1,0:T(8,128)(2,1)S(1)}, bf16[400,128]{1,0:T(8,128)(2,1)S(1)}, bf16[400,128]{1,0:T(8,128)(2,1)S(1)}) custom-call(f32[1,96]{1,0:T(1,128)S(1)} %get-tuple-element.15.fracs_ref, s32[2,128]{1,0:T(2,128)S(1)} %get-tuple-element.16.tiles_ref, bf16[96,96]{1,0:T(8,128)(2,1)} %constant.6.clone.table_hbm.table_ref, ...), custom_call_target="tpu_custom_call" | custom-call | tf_op jit(solution)/shard_map/tract_tiles/pallas_call | solution.py:507
  20.3 1.6 %collective-permute-start.6 = (bf16[400,128]{1,0:T(8,128)(2,1)S(1)}, bf16[400,128]{1,0:T(8,128)(2,1)S(1)}, u32[]{:S(2)}, u32[]{:S(2)}) collective-permute-start(bf16[400,128]{1,0:T(8,128)(2,1)S(1)} %get-tuple-element.23), channel_id=1, source_target_pairs={{0,2},{1,3},{2,0},{3,1},{4,6},{5,7},{6,4},{7,5},{8,10},{9,11},{10,... | collective-permute-start | bytes 307208 | tf_op jit(solution)/shard_map/ppermute | solution.py:425
  21.9 0.0 collective-permute-start.7
  21.9 0.6 %collective-permute-start.8 = (bf16[400,128]{1,0:T(8,128)(2,1)S(1)}, bf16[400,128]{1,0:T(8,128)(2,1)S(1)}, u32[]{:S(2)}, u32[]{:S(2)}) collective-permute-start(bf16[400,128]{1,0:T(8,128)(2,1)S(1)} %get-tuple-element.25), channel_id=1, source_target_pairs={{0,1},{1,0},{2,3},{3,2},{4,5},{5,4},{6,7},{7,6},{8,9},{9,8},{10,11... | collective-permute-start | bytes 307208 | tf_op jit(solution)/shard_map/ppermute | solution.py:425
  22.5 2.7 %collective-permute-done.6.refs_0_ = bf16[400,128]{1,0:T(8,128)(2,1)S(1)} collective-permute-done((bf16[400,128]{1,0:T(8,128)(2,1)S(1)}, bf16[400,128]{1,0:T(8,128)(2,1)S(1)}, u32[]{:S(2)}, u32[]{:S(2)}) %collective-permute-start.6) | collective-permute-done | bytes 102432 | tf_op jit(solution)/shard_map/ppermute | solution.py:425
  25.3 1.8 %collective-permute-done.7.refs_1_ = bf16[400,128]{1,0:T(8,128)(2,1)S(1)} collective-permute-done((bf16[400,128]{1,0:T(8,128)(2,1)S(1)}, bf16[400,128]{1,0:T(8,128)(2,1)S(1)}, u32[]{:S(2)}, u32[]{:S(2)}) %collective-permute-start.7) | collective-permute-done | bytes 102432 | tf_op jit(solution)/shard_map/ppermute | solution.py:425
  27.0 0.0 collective-permute-done.8.refs_2_
  27.1 0.0 copy-done
  27.1 1.6 %window_steps.1 = (bf16[32,32,128]{2,1,0:T(8,128)(2,1)}, f32[2,4096]{1,0:T(2,128)}) custom-call(bf16[400,128]{1,0:T(8,128)(2,1)S(1)} %collective-permute-done.6.refs_0_, bf16[400,128]{1,0:T(8,128)(2,1)S(1)} %collective-permute-done.7.refs_1_, bf16[400,128]{1,0:T(8,128)(2,1)S(1)} %collective-permute-done.8.refs_2_, ...), custom_call_target="tpu_custom_call" | custom-call | tf_op jit(solution)/shard_map/window_steps/pallas_call | solution.py:528
Async XLA Ops:
  0.6 6.7 %collective-permute-start.2 = (s32[2,4]{1,0:T(2,128)}, s32[2,4]{1,0:T(2,128)S(1)}, u32[]{:S(2)}, u32[]{:S(2)}) collective-permute-start(s32[2,4]{1,0:T(2,128)} %bitcast.15), channel_id=1, source_target_pairs={{0,8},{4,12},{8,0},{12,4},{1,9},{5,13},{9,1},{13,5},{2,10},{6,14},... | collective-permute-start | bytes 104 | tf_op jit(solution)/shard_map/ppermute | solution.py:425
  4.7 5.6 %collective-permute-start.1 = (s32[2,4]{1,0:T(2,128)}, s32[2,4]{1,0:T(2,128)S(1)}, u32[]{:S(2)}, u32[]{:S(2)}) collective-permute-start(s32[2,4]{1,0:T(2,128)} %bitcast.16), channel_id=1, source_target_pairs={{0,12},{4,8},{8,4},{12,0},{1,13},{5,9},{9,5},{13,1},{2,14},{6,10},... | collective-permute-start | bytes 104 | tf_op jit(solution)/shard_map/ppermute | solution.py:425
  6.1 4.2 %collective-permute-start = (s32[2,4]{1,0:T(2,128)}, s32[2,4]{1,0:T(2,128)S(1)}, u32[]{:S(2)}, u32[]{:S(2)}) collective-permute-start(s32[2,4]{1,0:T(2,128)} %bitcast.17), channel_id=1, source_target_pairs={{0,4},{4,0},{8,12},{12,8},{1,5},{5,1},{9,13},{13,9},{2,6},{6,2},{1... | collective-permute-start | bytes 104 | tf_op jit(solution)/shard_map/ppermute | solution.py:425
  10.9 6.7 %collective-permute-start.3 = (bf16[2,32,128]{2,1,0:T(8,128)(2,1)S(1)}, bf16[2,32,128]{2,1,0:T(8,128)(2,1)S(1)}, u32[]{:S(2)}, u32[]{:S(2)}) collective-permute-start(bf16[2,32,128]{2,1,0:T(8,128)(2,1)S(1)} %get-tuple-element.20), channel_id=1, source_target_pairs={{0,12},{4,8},{8,4},{12,0},{1,13},{5,9},{9,5},{13,1},{2,14},{6,10},... | collective-permute-start | bytes 49160 | tf_op jit(solution)/shard_map/ppermute | solution.py:425
  13.0 4.6 %collective-permute-start.4 = (bf16[2,32,128]{2,1,0:T(8,128)(2,1)S(1)}, bf16[2,32,128]{2,1,0:T(8,128)(2,1)S(1)}, u32[]{:S(2)}, u32[]{:S(2)}) collective-permute-start(bf16[2,32,128]{2,1,0:T(8,128)(2,1)S(1)} %get-tuple-element.21), channel_id=1, source_target_pairs={{0,8},{4,12},{8,0},{12,4},{1,9},{5,13},{9,1},{13,5},{2,10},{6,14},... | collective-permute-start | bytes 49160 | tf_op jit(solution)/shard_map/ppermute | solution.py:425
  13.0 4.6 %collective-permute-start.5 = (bf16[2,32,128]{2,1,0:T(8,128)(2,1)S(1)}, bf16[2,32,128]{2,1,0:T(8,128)(2,1)S(1)}, u32[]{:S(2)}, u32[]{:S(2)}) collective-permute-start(bf16[2,32,128]{2,1,0:T(8,128)(2,1)S(1)} %get-tuple-element.22), channel_id=1, source_target_pairs={{0,4},{4,0},{8,12},{12,8},{1,5},{5,1},{9,13},{13,9},{2,6},{6,2},{1... | collective-permute-start | bytes 49160 | tf_op jit(solution)/shard_map/ppermute | solution.py:425
  15.4 11.7 %copy-start = (bf16[128,384]{1,0:T(8,128)(2,1)S(1)}, bf16[128,384]{1,0:T(8,128)(2,1)}, u32[]{:S(2)}) copy-start(bf16[128,384]{1,0:T(8,128)(2,1)} %constant.8.clone.refs_5_) | copy-start | bytes 294916
  20.3 4.9 %collective-permute-start.6 = (bf16[400,128]{1,0:T(8,128)(2,1)S(1)}, bf16[400,128]{1,0:T(8,128)(2,1)S(1)}, u32[]{:S(2)}, u32[]{:S(2)}) collective-permute-start(bf16[400,128]{1,0:T(8,128)(2,1)S(1)} %get-tuple-element.23), channel_id=1, source_target_pairs={{0,2},{1,3},{2,0},{3,1},{4,6},{5,7},{6,4},{7,5},{8,10},{9,11},{10,... | collective-permute-start | bytes 307208 | tf_op jit(solution)/shard_map/ppermute | solution.py:425
  21.9 5.2 %collective-permute-start.7 = (bf16[400,128]{1,0:T(8,128)(2,1)S(1)}, bf16[400,128]{1,0:T(8,128)(2,1)S(1)}, u32[]{:S(2)}, u32[]{:S(2)}) collective-permute-start(bf16[400,128]{1,0:T(8,128)(2,1)S(1)} %get-tuple-element.24), channel_id=1, source_target_pairs={{0,3},{1,2},{2,1},{3,0},{4,7},{5,6},{6,5},{7,4},{8,11},{9,10},{10,... | collective-permute-start | bytes 307208 | tf_op jit(solution)/shard_map/ppermute | solution.py:425
  21.9 5.2 %collective-permute-start.8 = (bf16[400,128]{1,0:T(8,128)(2,1)S(1)}, bf16[400,128]{1,0:T(8,128)(2,1)S(1)}, u32[]{:S(2)}, u32[]{:S(2)}) collective-permute-start(bf16[400,128]{1,0:T(8,128)(2,1)S(1)} %get-tuple-element.25), channel_id=1, source_target_pairs={{0,1},{1,0},{2,3},{3,2},{4,5},{5,4},{6,7},{7,6},{8,9},{9,8},{10,11... | collective-permute-start | bytes 307208 | tf_op jit(solution)/shard_map/ppermute | solution.py:425

commit v10 on v9

--- a/solution.py
+++ b/solution.py
@@ -79,8 +79,8 @@
 
 def prepare_kernel(
     fresh_ref, reads_hbm, state_hbm, lesion_hbm, stim_hbm, wave_hbm, slot_hbm, target_hbm,
-    delay_hbm, lanes_hbm, table_hbm, older_hbm, frac_hbm, weights_hbm,
-    weights_out, ready_out, hist_out, tiles_out, fracs_out, head_out,
+    delay_hbm, lanes_hbm, table_hbm, older_hbm, frac_hbm,
+    ready_out, hist_out, tiles_out, fracs_out, head_out,
     reads, state, lesion, stim, wave, slot, target, delay, lanes, table, older, sems,
     *, peers, own_blocks, peer_targets, capacity,
 ):
@@ -93,14 +93,6 @@
     copies = [
         pltpu.make_async_copy(source, into, sems.at[i]) for i, (source, into) in enumerate(pairs)
     ]
-    part = weights_hbm.shape[0] // CHUNKS
-    for i in range(CHUNKS):
-        rows = pl.ds(i * part, part)
-        copies.append(
-            pltpu.make_async_copy(
-                weights_hbm.at[rows], weights_out.at[rows], sems.at[len(pairs) + i]
-            )
-        )
     for copy in copies:
         copy.start()
     for copy in copies[1:5]:
@@ -197,10 +189,18 @@
         copy.wait()
 
 
-def fresh_kernel(fresh_hbm, fresh_out, sem):
-    copy = pltpu.make_async_copy(fresh_hbm, fresh_out, sem)
-    copy.start()
-    copy.wait()
+def near_kernel(fresh_hbm, weights_hbm, fresh_out, weights_out, sems):
+    copies = [pltpu.make_async_copy(fresh_hbm, fresh_out, sems.at[CHUNKS])]
+    part = weights_hbm.shape[0] // CHUNKS
+    for i in range(CHUNKS):
+        rows = pl.ds(i * part, part)
+        copies.append(
+            pltpu.make_async_copy(weights_hbm.at[rows], weights_out.at[rows], sems.at[i])
+        )
+    for copy in copies:
+        copy.start()
+    for copy in copies:
+        copy.wait()
 
 
 def pick_kernel(*refs, capacity, peers, ways):
@@ -441,34 +441,36 @@
         VMEM((slot_count, HSEG, coef_count, block_rows), jnp.bfloat16),
     ]
     table = far(jnp.asarray(expand_table(coef_count)))
-    fresh = pl.pallas_call(
-        fresh_kernel,
-        out_shape=pltpu.VMEM(fresh_coefs.shape, jnp.bfloat16),
-        in_specs=[hbm_spec],
-        out_specs=vmem_spec,
-        scratch_shapes=[pltpu.SemaphoreType.DMA],
+    fresh, weights = pl.pallas_call(
+        near_kernel,
+        out_shape=[
+            pltpu.VMEM(fresh_coefs.shape, jnp.bfloat16),
+            pltpu.VMEM((tile_count, block_rows, block_rows), jnp.bfloat16),
+        ],
+        in_specs=[hbm_spec] * 2,
+        out_specs=[vmem_spec] * 2,
+        scratch_shapes=[pltpu.SemaphoreType.DMA((CHUNKS + 1,))],
         compiler_params=params(),
-        name="fresh_near",
-    )(far(fresh_coefs))
-    weights, ready, hist, tiles, fracs, heads = pl.pallas_call(
+        name="near",
+    )(far(fresh_coefs), far(tract_weights.reshape(tile_count, block_rows, block_rows)))
+    ready, hist, tiles, fracs, heads = pl.pallas_call(
         functools.partial(
             prepare_kernel,
             peers=peers, own_blocks=own_blocks, peer_targets=peer_targets, capacity=capacity,
         ),
         out_shape=[
-            pltpu.VMEM((tile_count, block_rows, block_rows), jnp.bfloat16),
             pltpu.VMEM((4 * own_blocks + STEPS, block_rows), jnp.float32),
             pltpu.VMEM((slot_count * LENGTH, block_rows), jnp.float32),
             pltpu.VMEM((2, 128), jnp.int32),
             pltpu.VMEM((1, tile_count), jnp.float32),
             pltpu.VMEM((peers, HEAD, 128), jnp.bfloat16),
         ],
-        in_specs=[vmem_spec] + [hbm_spec] * 13,
-        out_specs=[vmem_spec] * 6,
+        in_specs=[vmem_spec] + [hbm_spec] * 12,
+        out_specs=[vmem_spec] * 5,
         scratch_shapes=[
             SMEM((capacity, wide_peers), jnp.int32),
             *vmem_inputs,
-            pltpu.SemaphoreType.DMA((12 + CHUNKS,)),
+            pltpu.SemaphoreType.DMA((12,)),
         ],
         compiler_params=params(),
         name="prepare",
@@ -486,7 +488,6 @@
         table,
         far(older_coefs.reshape(slot_count, HSEG, coef_count, block_rows)),
         far(tract_frac.reshape(1, tile_count)),
-        far(tract_weights.reshape(tile_count, block_rows, block_rows)),
     )
 
     picked = pl.pallas_call(

time: 28.9 us -> 28.9 us (level)
  Pallas kernels: 8.08 us -> 8.61 us
  waiting for transfers between devices: 7.58 us -> 7.06 us
    pallas_call x1, Pallas kernels: 0.96 us -> 2.01 us  [local(): pl.pallas_call(near_kernel, out_shape=[pltpu.VMEM(fresh_coefs.shape, jnp....]
    ppermute x9, waiting for transfers between devices: 7.58 us -> 7.06 us  [swap(): lax.ppermute(x, axis, [(i, i ^ r) for i in range(lax.axis_size(axis))])]
    pallas_call x1, Pallas kernels: 2.21 us -> 1.69 us  [local(): pl.pallas_call(functools.partial(prepare_kernel, peers=peers, own_blocks=...]
  transfers between devices with their start and end apart: 9 -> 9, of which waited for: 3 -> 4; matrix products, arithmetic and copies ran while one was open for 0% -> 0% of each run, Pallas kernels for 11% -> 13%
where the time goes in v10:
time: 28.9 us; the launch traced here: 28.7 us
  starting transfers between devices  12.3 us (43%)
  Pallas kernels  8.61 us (30%)
  waiting for transfers between devices  7.06 us (24%)
  between operations  0.69 us (2%)
    ppermute x9, starting transfers between devices, swap(): lax.ppermute(x, axis, [(i, i ^ r) for i in range(lax.axis_size(axis))])  12.3 us
    ppermute x9, waiting for transfers between devices, swap(): lax.ppermute(x, axis, [(i, i ^ r) for i in range(lax.axis_size(axis))])  7.06 us
    pallas_call x1, Pallas kernels, local(): pl.pallas_call(functools.partial(tract_kernel, wide_peers=wide_peers, pee...  2.65 us
    pallas_call x1, Pallas kernels, local(): pl.pallas_call(near_kernel, out_shape=[pltpu.VMEM(fresh_coefs.shape, jnp....  2.01 us
    pallas_call x1, Pallas kernels, local(): pl.pallas_call(functools.partial(prepare_kernel, peers=peers, own_blocks=...  1.69 us
    pallas_call x1, Pallas kernels, local(): pl.pallas_call(functools.partial(window_kernel, peers=peers, own_blocks=o...  1.64 us
    pallas_call x1, Pallas kernels, local(): pl.pallas_call(functools.partial(pick_kernel, capacity=capacity, peers=wi...  0.62 us
  transfers between devices with their start and end apart: 9, of which 4 were waited for; matrix products, arithmetic and copies ran while one was open for 0% of the time, Pallas kernels for 13%

profile of v10, /device:TPU:0, one launch (start us, length us, event | category | flops | bytes accessed | tf_op | source)
XLA Modules:
  0.0 28.7 jit_solution(15866076372708229511)
XLA Ops:
  0.6 4.1 %collective-permute-start.2 = (s32[2,4]{1,0:T(2,128)}, s32[2,4]{1,0:T(2,128)S(1)}, u32[]{:S(2)}, u32[]{:S(2)}) collective-permute-start(s32[2,4]{1,0:T(2,128)} %bitcast.15), channel_id=1, source_target_pairs={{0,8},{4,12},{8,0},{12,4},{1,9},{5,13},{9,1},{13,5},{2,10},{6,14},... | collective-permute-start | bytes 104 | tf_op jit(solution)/shard_map/ppermute | solution.py:425
  4.7 1.3 %collective-permute-start.1 = (s32[2,4]{1,0:T(2,128)}, s32[2,4]{1,0:T(2,128)S(1)}, u32[]{:S(2)}, u32[]{:S(2)}) collective-permute-start(s32[2,4]{1,0:T(2,128)} %bitcast.16), channel_id=1, source_target_pairs={{0,12},{4,8},{8,4},{12,0},{1,13},{5,9},{9,5},{13,1},{2,14},{6,10},... | collective-permute-start | bytes 104 | tf_op jit(solution)/shard_map/ppermute | solution.py:425
  6.1 0.2 collective-permute-start
  6.3 0.0 copy-start
  6.3 2.0 %near.1 = (bf16[32,32,128]{2,1,0:T(8,128)(2,1)S(1)}, bf16[96,128,128]{2,1,0:T(8,128)(2,1)S(1)}) custom-call(bf16[32,32,128]{2,1,0:T(8,128)(2,1)} %fresh_hbm.1, bf16[96,128,128]{2,1,0:T(8,128)(2,1)} %bitcast.12), custom_call_target="tpu_custom_call" | custom-call | tf_op jit(solution)/shard_map/near/pallas_call | solution.py:444
  8.3 0.0 collective-permute-done.2.refs_2_
  8.3 2.0 %collective-permute-done.1.refs_1_ = s32[2,4]{1,0:T(2,128)S(1)} collective-permute-done((s32[2,4]{1,0:T(2,128)}, s32[2,4]{1,0:T(2,128)S(1)}, u32[]{:S(2)}, u32[]{:S(2)}) %collective-permute-start.1) | collective-permute-done | bytes 64 | tf_op jit(solution)/shard_map/ppermute | solution.py:425
  10.3 0.0 collective-permute-done.refs_0_
  10.3 0.6 %pick_blocks.1 = (bf16[2,32,128]{2,1,0:T(8,128)(2,1)S(1)}, bf16[2,32,128]{2,1,0:T(8,128)(2,1)S(1)}, bf16[2,32,128]{2,1,0:T(8,128)(2,1)S(1)}) custom-call(s32[2,4]{1,0:T(2,128)S(1)} %collective-permute-done.refs_0_, s32[2,4]{1,0:T(2,128)S(1)} %collective-permute-done.1.refs_1_, s32[2,4]{1,0:T(2,128)S(1)} %collective-permute-done.2.refs_2_, ...), custom_call_target="tpu_custom_call" | custom-call | tf_op jit(solution)/shard_map/pick_blocks/pallas_call | solution.py:493
  10.9 2.1 %collective-permute-start.3 = (bf16[2,32,128]{2,1,0:T(8,128)(2,1)S(1)}, bf16[2,32,128]{2,1,0:T(8,128)(2,1)S(1)}, u32[]{:S(2)}, u32[]{:S(2)}) collective-permute-start(bf16[2,32,128]{2,1,0:T(8,128)(2,1)S(1)} %get-tuple-element.22), channel_id=1, source_target_pairs={{0,12},{4,8},{8,4},{12,0},{1,13},{5,9},{9,5},{13,1},{2,14},{6,10},... | collective-permute-start | bytes 49160 | tf_op jit(solution)/shard_map/ppermute | solution.py:425
  13.0 0.0 collective-permute-start.4
  13.0 2.4 %collective-permute-start.5 = (bf16[2,32,128]{2,1,0:T(8,128)(2,1)S(1)}, bf16[2,32,128]{2,1,0:T(8,128)(2,1)S(1)}, u32[]{:S(2)}, u32[]{:S(2)}) collective-permute-start(bf16[2,32,128]{2,1,0:T(8,128)(2,1)S(1)} %get-tuple-element.24), channel_id=1, source_target_pairs={{0,4},{4,0},{8,12},{12,8},{1,5},{5,1},{9,13},{13,9},{2,6},{6,2},{1... | collective-permute-start | bytes 49160 | tf_op jit(solution)/shard_map/ppermute | solution.py:425
  15.4 1.7 %prepare.1 = (f32[160,128]{1,0:T(8,128)S(1)}, f32[768,128]{1,0:T(8,128)S(1)}, s32[2,128]{1,0:T(2,128)S(1)}, f32[1,96]{1,0:T(1,128)S(1)}, bf16[4,16,128]{2,1,0:T(8,128)(2,1)S(1)}) custom-call(bf16[32,32,128]{2,1,0:T(8,128)(2,1)S(1)} %get-tuple-element.16.fresh_ref.refs_3_, s32[2,4]{1,0:T(2,128)} %bitcast.18, f32[2,4096]{1,0:T(2,128)} %state_hbm.1, ...), custom_call_target="tpu_custom_call" | custom-call | tf_op jit(solution)/shard_map/prepare/pallas_call | solution.py:456
  17.1 0.0 collective-permute-done.3.refs_0_
  17.1 0.6 %collective-permute-done.4.refs_1_ = bf16[2,32,128]{2,1,0:T(8,128)(2,1)S(1)} collective-permute-done((bf16[2,32,128]{2,1,0:T(8,128)(2,1)S(1)}, bf16[2,32,128]{2,1,0:T(8,128)(2,1)S(1)}, u32[]{:S(2)}, u32[]{:S(2)}) %collective-permute-start.4) | collective-permute-done | bytes 16416 | tf_op jit(solution)/shard_map/ppermute | solution.py:425
  17.7 0.0 collective-permute-done.5.refs_2_
  17.7 2.7 %tract_tiles.1 = (bf16[400,128]{1,0:T(8,128)(2,1)S(1)}, bf16[400,128]{1,0:T(8,128)(2,1)S(1)}, bf16[400,128]{1,0:T(8,128)(2,1)S(1)}, bf16[400,128]{1,0:T(8,128)(2,1)S(1)}) custom-call(f32[1,96]{1,0:T(1,128)S(1)} %get-tuple-element.17.fracs_ref, s32[2,128]{1,0:T(2,128)S(1)} %get-tuple-element.18.tiles_ref, bf16[96,96]{1,0:T(8,128)(2,1)} %constant.6.clone.table_hbm.table_ref, ...), custom_call_target="tpu_custom_call" | custom-call | tf_op jit(solution)/shard_map/tract_tiles/pallas_call | solution.py:508
  20.3 1.6 %collective-permute-start.6 = (bf16[400,128]{1,0:T(8,128)(2,1)S(1)}, bf16[400,128]{1,0:T(8,128)(2,1)S(1)}, u32[]{:S(2)}, u32[]{:S(2)}) collective-permute-start(bf16[400,128]{1,0:T(8,128)(2,1)S(1)} %get-tuple-element.25), channel_id=1, source_target_pairs={{0,2},{1,3},{2,0},{3,1},{4,6},{5,7},{6,4},{7,5},{8,10},{9,11},{10,... | collective-permute-start | bytes 307208 | tf_op jit(solution)/shard_map/ppermute | solution.py:425
  21.9 0.0 collective-permute-start.7
  21.9 0.6 %collective-permute-start.8 = (bf16[400,128]{1,0:T(8,128)(2,1)S(1)}, bf16[400,128]{1,0:T(8,128)(2,1)S(1)}, u32[]{:S(2)}, u32[]{:S(2)}) collective-permute-start(bf16[400,128]{1,0:T(8,128)(2,1)S(1)} %get-tuple-element.27), channel_id=1, source_target_pairs={{0,1},{1,0},{2,3},{3,2},{4,5},{5,4},{6,7},{7,6},{8,9},{9,8},{10,11... | collective-permute-start | bytes 307208 | tf_op jit(solution)/shard_map/ppermute | solution.py:425
  22.5 2.7 %collective-permute-done.6.refs_0_ = bf16[400,128]{1,0:T(8,128)(2,1)S(1)} collective-permute-done((bf16[400,128]{1,0:T(8,128)(2,1)S(1)}, bf16[400,128]{1,0:T(8,128)(2,1)S(1)}, u32[]{:S(2)}, u32[]{:S(2)}) %collective-permute-start.6) | collective-permute-done | bytes 102432 | tf_op jit(solution)/shard_map/ppermute | solution.py:425
  25.2 1.8 %collective-permute-done.7.refs_1_ = bf16[400,128]{1,0:T(8,128)(2,1)S(1)} collective-permute-done((bf16[400,128]{1,0:T(8,128)(2,1)S(1)}, bf16[400,128]{1,0:T(8,128)(2,1)S(1)}, u32[]{:S(2)}, u32[]{:S(2)}) %collective-permute-start.7) | collective-permute-done | bytes 102432 | tf_op jit(solution)/shard_map/ppermute | solution.py:425
  27.0 0.0 collective-permute-done.8.refs_2_
  27.1 0.0 copy-done
  27.1 1.6 %window_steps.1 = (bf16[32,32,128]{2,1,0:T(8,128)(2,1)}, f32[2,4096]{1,0:T(2,128)}) custom-call(bf16[400,128]{1,0:T(8,128)(2,1)S(1)} %collective-permute-done.6.refs_0_, bf16[400,128]{1,0:T(8,128)(2,1)S(1)} %collective-permute-done.7.refs_1_, bf16[400,128]{1,0:T(8,128)(2,1)S(1)} %collective-permute-done.8.refs_2_, ...), custom_call_target="tpu_custom_call" | custom-call | tf_op jit(solution)/shard_map/window_steps/pallas_call | solution.py:529
Async XLA Ops:
  0.6 7.7 %collective-permute-start.2 = (s32[2,4]{1,0:T(2,128)}, s32[2,4]{1,0:T(2,128)S(1)}, u32[]{:S(2)}, u32[]{:S(2)}) collective-permute-start(s32[2,4]{1,0:T(2,128)} %bitcast.15), channel_id=1, source_target_pairs={{0,8},{4,12},{8,0},{12,4},{1,9},{5,13},{9,1},{13,5},{2,10},{6,14},... | collective-permute-start | bytes 104 | tf_op jit(solution)/shard_map/ppermute | solution.py:425
  4.7 5.6 %collective-permute-start.1 = (s32[2,4]{1,0:T(2,128)}, s32[2,4]{1,0:T(2,128)S(1)}, u32[]{:S(2)}, u32[]{:S(2)}) collective-permute-start(s32[2,4]{1,0:T(2,128)} %bitcast.16), channel_id=1, source_target_pairs={{0,12},{4,8},{8,4},{12,0},{1,13},{5,9},{9,5},{13,1},{2,14},{6,10},... | collective-permute-start | bytes 104 | tf_op jit(solution)/shard_map/ppermute | solution.py:425
  6.1 4.2 %collective-permute-start = (s32[2,4]{1,0:T(2,128)}, s32[2,4]{1,0:T(2,128)S(1)}, u32[]{:S(2)}, u32[]{:S(2)}) collective-permute-start(s32[2,4]{1,0:T(2,128)} %bitcast.17), channel_id=1, source_target_pairs={{0,4},{4,0},{8,12},{12,8},{1,5},{5,1},{9,13},{13,9},{2,6},{6,2},{1... | collective-permute-start | bytes 104 | tf_op jit(solution)/shard_map/ppermute | solution.py:425
  6.3 20.7 %copy-start = (bf16[128,384]{1,0:T(8,128)(2,1)S(1)}, bf16[128,384]{1,0:T(8,128)(2,1)}, u32[]{:S(2)}) copy-start(bf16[128,384]{1,0:T(8,128)(2,1)} %constant.8.clone.refs_5_) | copy-start | bytes 294916
  10.9 6.2 %collective-permute-start.3 = (bf16[2,32,128]{2,1,0:T(8,128)(2,1)S(1)}, bf16[2,32,128]{2,1,0:T(8,128)(2,1)S(1)}, u32[]{:S(2)}, u32[]{:S(2)}) collective-permute-start(bf16[2,32,128]{2,1,0:T(8,128)(2,1)S(1)} %get-tuple-element.22), channel_id=1, source_target_pairs={{0,12},{4,8},{8,4},{12,0},{1,13},{5,9},{9,5},{13,1},{2,14},{6,10},... | collective-permute-start | bytes 49160 | tf_op jit(solution)/shard_map/ppermute | solution.py:425
  13.0 4.6 %collective-permute-start.4 = (bf16[2,32,128]{2,1,0:T(8,128)(2,1)S(1)}, bf16[2,32,128]{2,1,0:T(8,128)(2,1)S(1)}, u32[]{:S(2)}, u32[]{:S(2)}) collective-permute-start(bf16[2,32,128]{2,1,0:T(8,128)(2,1)S(1)} %get-tuple-element.23), channel_id=1, source_target_pairs={{0,8},{4,12},{8,0},{12,4},{1,9},{5,13},{9,1},{13,5},{2,10},{6,14},... | collective-permute-start | bytes 49160 | tf_op jit(solution)/shard_map/ppermute | solution.py:425
  13.0 4.6 %collective-permute-start.5 = (bf16[2,32,128]{2,1,0:T(8,128)(2,1)S(1)}, bf16[2,32,128]{2,1,0:T(8,128)(2,1)S(1)}, u32[]{:S(2)}, u32[]{:S(2)}) collective-permute-start(bf16[2,32,128]{2,1,0:T(8,128)(2,1)S(1)} %get-tuple-element.24), channel_id=1, source_target_pairs={{0,4},{4,0},{8,12},{12,8},{1,5},{5,1},{9,13},{13,9},{2,6},{6,2},{1... | collective-permute-start | bytes 49160 | tf_op jit(solution)/shard_map/ppermute | solution.py:425
  20.3 4.9 %collective-permute-start.6 = (bf16[400,128]{1,0:T(8,128)(2,1)S(1)}, bf16[400,128]{1,0:T(8,128)(2,1)S(1)}, u32[]{:S(2)}, u32[]{:S(2)}) collective-permute-start(bf16[400,128]{1,0:T(8,128)(2,1)S(1)} %get-tuple-element.25), channel_id=1, source_target_pairs={{0,2},{1,3},{2,0},{3,1},{4,6},{5,7},{6,4},{7,5},{8,10},{9,11},{10,... | collective-permute-start | bytes 307208 | tf_op jit(solution)/shard_map/ppermute | solution.py:425
  21.9 5.2 %collective-permute-start.7 = (bf16[400,128]{1,0:T(8,128)(2,1)S(1)}, bf16[400,128]{1,0:T(8,128)(2,1)S(1)}, u32[]{:S(2)}, u32[]{:S(2)}) collective-permute-start(bf16[400,128]{1,0:T(8,128)(2,1)S(1)} %get-tuple-element.26), channel_id=1, source_target_pairs={{0,3},{1,2},{2,1},{3,0},{4,7},{5,6},{6,5},{7,4},{8,11},{9,10},{10,... | collective-permute-start | bytes 307208 | tf_op jit(solution)/shard_map/ppermute | solution.py:425
  21.9 5.2 %collective-permute-start.8 = (bf16[400,128]{1,0:T(8,128)(2,1)S(1)}, bf16[400,128]{1,0:T(8,128)(2,1)S(1)}, u32[]{:S(2)}, u32[]{:S(2)}) collective-permute-start(bf16[400,128]{1,0:T(8,128)(2,1)S(1)} %get-tuple-element.27), channel_id=1, source_target_pairs={{0,1},{1,0},{2,3},{3,2},{4,5},{5,4},{6,7},{7,6},{8,9},{9,8},{10,11... | collective-permute-start | bytes 307208 | tf_op jit(solution)/shard_map/ppermute | solution.py:425

commit v11 on v10

--- a/solution.py
+++ b/solution.py
@@ -81,21 +81,21 @@
     fresh_ref, reads_hbm, state_hbm, lesion_hbm, stim_hbm, wave_hbm, slot_hbm, target_hbm,
     delay_hbm, lanes_hbm, table_hbm, older_hbm, frac_hbm,
     ready_out, hist_out, tiles_out, fracs_out, head_out,
-    reads, state, lesion, stim, wave, slot, target, delay, lanes, table, older, sems,
+    reads, state, lesion, stim, wave, slot, target, delay, frac, lanes, table, older, sems,
     *, peers, own_blocks, peer_targets, capacity,
 ):
     pairs = [
         (reads_hbm, reads), (target_hbm, target), (slot_hbm, slot),
         (delay_hbm, delay), (lanes_hbm, lanes), (table_hbm, table), (older_hbm, older),
         (state_hbm, state), (lesion_hbm, lesion), (stim_hbm, stim), (wave_hbm, wave),
-        (frac_hbm, fracs_out),
+        (frac_hbm, frac),
     ]
     copies = [
         pltpu.make_async_copy(source, into, sems.at[i]) for i, (source, into) in enumerate(pairs)
     ]
     for copy in copies:
         copy.start()
-    for copy in copies[1:5]:
+    for copy in (*copies[1:5], copies[11]):
         copy.wait()
     place = lax.axis_index("narrow")
     owner = lax.axis_index("wide")
@@ -135,8 +135,29 @@
     across = jnp.zeros((1, tile_count), jnp.int32)
     for p in range(1, peers):
         across = across + jnp.where(target[...] >= p * own_blocks, 1, 0)
-    tiles_out[0:1, :tile_count] = slot[...] * LENGTH + (LENGTH - 1) - delay[...]
-    tiles_out[1:2, :tile_count] = (across * peer_targets + ranks.astype(jnp.int32)) * TOGETHER
+    key_row = ((peers - 1) - (across ^ place)).astype(jnp.float32)
+    shape = (tile_count, tile_count)
+    down = lax.broadcasted_iota(jnp.int32, shape, 0)
+    along = lax.broadcasted_iota(jnp.int32, shape, 1)
+    key = jnp.sum(jnp.where(down == along, key_row, 0.0), axis=1, keepdims=True)
+    ahead = (key_row < key) | ((key_row == key) & (along < down))
+    position = jnp.sum(jnp.where(ahead, 1.0, 0.0), axis=1, keepdims=True)
+    lane = lax.broadcasted_iota(jnp.int32, (tile_count, 128), 1).astype(jnp.float32)
+    chosen = jnp.where(position == lane, 1.0, 0.0)
+    starts = (slot[...] * LENGTH + (LENGTH - 1) - delay[...]).astype(jnp.float32)
+    index = lax.broadcasted_iota(jnp.int32, (1, tile_count), 1).astype(jnp.float32)
+    firsts = (key_row * float(peer_targets) + ranks) * float(TOGETHER)
+    facts = jnp.concatenate(
+        [index, starts, firsts, frac[...], jnp.zeros((4, tile_count), jnp.float32)], axis=0
+    )
+    ordered = jnp.dot(
+        facts, chosen, precision=lax.Precision.HIGHEST, preferred_element_type=jnp.float32
+    )
+    fracs_out[...] = ordered[3:4, :]
+    tiles_out[0:3, :] = (ordered[0:3, :] + 0.5).astype(jnp.int32)
+    tiles_out[3:4, :] = jnp.sum(
+        jnp.where(key < lane, 1.0, 0.0), axis=0, keepdims=True
+    ).astype(jnp.int32)
 
     for copy in copies[5:7]:
         copy.wait()
@@ -185,8 +206,6 @@
     diagonal = lax.broadcasted_iota(jnp.int32, shape, 0) == lax.broadcasted_iota(jnp.int32, shape, 1)
     column = jnp.sum(jnp.where(diagonal, wave[...], 0.0), axis=1, keepdims=True)
     ready_out[4 * own_blocks :, :] = jnp.broadcast_to(column, (STEPS, block_rows))
-    for copy in copies[11:]:
-        copy.wait()
 
 
 def near_kernel(fresh_hbm, weights_hbm, fresh_out, weights_out, sems):
@@ -218,13 +237,55 @@
             outs[r - 1][c] = fresh[jnp.maximum(asked[i, c, place], 0)]
 
 
-def tract_kernel(
+def add_tiles(tiles, frac, hist, weights, total, pitch, items):
+    block_rows = weights.shape[2]
+    rows = []
+    for t, _ in items:
+        fraction = frac[0, t]
+        start = tiles[1, t]
+        earlier = hist[pl.ds(start, STEPS), :]
+        later = hist[pl.ds(start + 1, STEPS), :]
+        rows.append(((1.0 - fraction) * later + fraction * earlier).astype(jnp.bfloat16))
+    tile = [weights[tiles[0, t]] for t, _ in items]
+    none = jnp.zeros((2 * STEPS, block_rows), jnp.bfloat16)
+    product = lax.dot_general(
+        jnp.concatenate(
+            [
+                jnp.concatenate([*rows[:2], none], axis=0),
+                jnp.concatenate([none, *rows[2:]], axis=0),
+            ],
+            axis=1,
+        ),
+        jnp.concatenate(
+            [jnp.concatenate(tile[:2], axis=0), jnp.concatenate(tile[2:], axis=0)], axis=1
+        ),
+        (((1,), (1,)), ((), ())),
+        preferred_element_type=jnp.float32,
+    )
+    for i, (_, first) in enumerate(items):
+        left = i % 2 * block_rows
+        for g in range(STEPS // TOGETHER):
+            where = pl.ds(pl.multiple_of(first + g * pitch, 8), TOGETHER)
+            top = i * STEPS + g * TOGETHER
+            total[where, :] += product[top : top + TOGETHER, left : left + block_rows]
+
+
+def write_share(pieces, total, head, first, span, pitch):
+    groups = STEPS // TOGETHER // len(pieces)
+    for i, piece in enumerate(pieces):
+        for g in range(groups):
+            top = (i * groups + g) * pitch + first
+            piece[g * span : (g + 1) * span, :] = total[top : top + span, :].astype(jnp.bfloat16)
+    pieces[-1][groups * span :, :] = head
+
+
+def far_kernel(
     fracs_ref, tiles_ref, table_ref, head_ref, weights, hist_ref, *refs,
-    wide_peers, peers, capacity, peer_targets,
+    wide_peers, peers, capacity, peer_targets, fixed,
 ):
     news = refs[: wide_peers - 1]
-    outs = refs[wide_peers - 1 : wide_peers - 1 + peers]
-    tiles, frac, hist, total, sems = refs[wide_peers - 1 + peers :]
+    outs = refs[wide_peers - 1 : wide_peers + peers - 3]
+    hist, total, tiles, frac, sems = refs[wide_peers + peers - 3 :]
     place = lax.axis_index("narrow")
     owner = lax.axis_index("wide")
     copies = [
@@ -245,62 +306,67 @@
         copy.wait()
 
     span = peer_targets * TOGETHER
-    pitch = peers * span
-    block_rows = weights.shape[2]
-    for turn in range(0, weights.shape[0], UNROLL):
-        rows = []
-        for t in range(turn, turn + UNROLL):
-            fraction = frac[0, t]
-            start = tiles[0, t]
-            earlier = hist[pl.ds(start, STEPS), :]
-            later = hist[pl.ds(start + 1, STEPS), :]
-            rows.append(((1.0 - fraction) * later + fraction * earlier).astype(jnp.bfloat16))
-        none = jnp.zeros((2 * STEPS, block_rows), jnp.bfloat16)
-        left = jnp.concatenate([*rows[:2], none], axis=0)
-        right = jnp.concatenate([none, *rows[2:]], axis=0)
-        product = lax.dot_general(
-            jnp.concatenate([left, right], axis=1),
-            jnp.concatenate(
-                [
-                    weights[t : t + 2].reshape(2 * block_rows, block_rows)
-                    for t in (turn, turn + 2)
-                ],
-                axis=1,
-            ),
-            (((1,), (1,)), ((), ())),
-            preferred_element_type=jnp.float32,
-        )
-        sums = [
-            product[i * STEPS : (i + 1) * STEPS, i % 2 * block_rows : (i % 2 + 1) * block_rows]
-            for i in range(UNROLL)
+    spare = peers * span
+    pitch = spare + TOGETHER
+    for t in range(0, fixed, UNROLL):
+        items = [(u, tiles[2, u]) for u in range(t, t + UNROLL)]
+        add_tiles(tiles, frac, hist, weights, total, pitch, items)
+    far_count = tiles[3, peers - 2]
+
+    @pl.loop(0, lax.div(jnp.maximum(far_count - fixed, 0) + (UNROLL - 1), UNROLL))
+    def _(turn):
+        places = [fixed + turn * UNROLL + u for u in range(UNROLL)]
+        items = [(t, jnp.where(t < far_count, tiles[2, t], spare)) for t in places]
+        add_tiles(tiles, frac, hist, weights, total, pitch, items)
+
+    for part, out in enumerate(outs):
+        write_share([out], total, head_ref[place ^ (peers - 1 - part)], part * span, span, pitch)
+
+
+def near_tiles_kernel(
+    fracs_ref, tiles_ref, head_ref, weights, hist, total_ref, *refs,
+    peers, peer_targets, fixed,
+):
+    *pair, own, tiles, frac, total, sems = refs
+    place = lax.axis_index("narrow")
+    copies = [
+        pltpu.make_async_copy(tiles_ref, tiles, sems.at[0]),
+        pltpu.make_async_copy(fracs_ref, frac, sems.at[1]),
+    ]
+    for copy in copies:
+        copy.start()
+    total[...] = total_ref[...]
+    for copy in copies:
+        copy.wait()
+    span = peer_targets * TOGETHER
+    spare = peers * span
+    pitch = spare + TOGETHER
+    far_count = tiles[3, peers - 2]
+    for t in range(fixed, weights.shape[0], UNROLL):
+        items = [
+            (u, jnp.where(u < far_count, spare, tiles[2, u])) for u in range(t, t + UNROLL)
         ]
-        for t in range(turn, turn + UNROLL):
-            first = tiles[1, t]
-            for g in range(STEPS // TOGETHER):
-                rows = pl.ds(pl.multiple_of(first + g * pitch, 8), TOGETHER)
-                total[rows, :] += sums[t - turn][g * TOGETHER : (g + 1) * TOGETHER]
-
-    for r in range(peers):
-        for g in range(STEPS // TOGETHER):
-            first = pl.multiple_of(g * pitch + (place ^ r) * span, 8)
-            outs[r][g * span : (g + 1) * span, :] = total[pl.ds(first, span), :].astype(
-                jnp.bfloat16
-            )
-        outs[r][peer_targets * STEPS :, :] = head_ref[place ^ r]
+        add_tiles(tiles, frac, hist, weights, total, pitch, items)
+    write_share(pair, total, head_ref[place ^ 1], (peers - 2) * span, span, pitch)
+    write_share([own], total, head_ref[place], (peers - 1) * span, span, pitch)
+
+
+def share_rows(pieces, group, width):
+    groups = STEPS // TOGETHER // len(pieces)
+    first = group % groups * width
+    return pieces[group // groups][first : first + width, :]
 
 
 def window_kernel(*refs, peers, own_blocks, peer_targets, coef_count):
-    shares = dict(zip([*range(2, peers), 1, 0], refs))
+    shares = {r: (ref,) for r, ref in zip(range(2, peers), refs)}
+    shares |= {1: refs[peers - 2 : peers], 0: (refs[peers],)}
     (
         ready_ref, fit_ref, coefs_hbm, state_hbm, samples, rates, coefs, state, sems,
-    ) = refs[peers:]
+    ) = refs[peers + 1 :]
     block_rows = ready_ref.shape[1]
     width = TOGETHER * peer_targets
-    span = peer_targets * STEPS
-
-    head = shares[0][span:, :].astype(jnp.float32)
-    for r in range(1, peers):
-        head = head + shares[r][span:, :].astype(jnp.float32)
+
+    head = sum(shares[r][-1][-HEAD:, :].astype(jnp.float32) for r in range(peers))
     row = lax.broadcasted_iota(jnp.int32, (TOGETHER * own_blocks, 128), 0).astype(jnp.float32) + 1.0
     columns = peers * width
     scatter = jnp.concatenate(
@@ -322,7 +388,7 @@
         arrived = jnp.concatenate(
             [
                 jnp.concatenate(
-                    [shares[r][g * width : (g + 1) * width, :] for r in range(peers)], axis=0
+                    [share_rows(shares[r], g, width) for r in range(peers)], axis=0
                 )
                 for g in (pair, pair + 1)
             ],
@@ -436,6 +502,7 @@
         VMEM((1, tile_count), jnp.int32),
         VMEM((1, tile_count), jnp.int32),
         VMEM((1, tile_count), jnp.int32),
+        VMEM((1, tile_count), jnp.float32),
         VMEM((3, HEAD, 128), jnp.float32),
         VMEM((LENGTH, SEGS * coef_count), jnp.bfloat16),
         VMEM((slot_count, HSEG, coef_count, block_rows), jnp.bfloat16),
@@ -461,8 +528,8 @@
         out_shape=[
             pltpu.VMEM((4 * own_blocks + STEPS, block_rows), jnp.float32),
             pltpu.VMEM((slot_count * LENGTH, block_rows), jnp.float32),
-            pltpu.VMEM((2, 128), jnp.int32),
-            pltpu.VMEM((1, tile_count), jnp.float32),
+            pltpu.VMEM((4, 128), jnp.int32),
+            pltpu.VMEM((1, 128), jnp.float32),
             pltpu.VMEM((peers, HEAD, 128), jnp.bfloat16),
         ],
         in_specs=[vmem_spec] + [hbm_spec] * 12,
@@ -505,26 +572,40 @@
     )(*asked, fresh)
     news = [swap(picked[r - 1], "wide", r) for r in range(wide_peers - 1, 0, -1)]
 
-    shares = pl.pallas_call(
+    fixed = tile_count * (peers - 2) // peers + 2 * UNROLL
+    fixed = min(tile_count, -(-fixed // UNROLL) * UNROLL)
+    share = pltpu.VMEM((share_rows, block_rows), jnp.bfloat16)
+    total = pltpu.VMEM(((peers * peer_targets + 1) * STEPS, block_rows), jnp.float32)
+    scalars = [SMEM((4, 128), jnp.int32), SMEM((1, 128), jnp.float32)]
+    *shares, hist, sums = pl.pallas_call(
         functools.partial(
-            tract_kernel,
+            far_kernel,
             wide_peers=wide_peers, peers=peers, capacity=capacity, peer_targets=peer_targets,
+            fixed=fixed,
         ),
-        out_shape=[pltpu.VMEM((share_rows, block_rows), jnp.bfloat16)] * peers,
+        out_shape=[share] * (peers - 2) + [pltpu.VMEM(hist.shape, jnp.float32), total],
         in_specs=[vmem_spec] * (5 + wide_peers),
         out_specs=[vmem_spec] * peers,
-        scratch_shapes=[
-            SMEM((2, 128), jnp.int32),
-            SMEM((1, tile_count), jnp.float32),
-            VMEM((slot_count * LENGTH, block_rows), jnp.float32),
-            VMEM((peers * peer_targets * STEPS, block_rows), jnp.float32),
-            pltpu.SemaphoreType.DMA((2,)),
-        ],
+        scratch_shapes=[*scalars, pltpu.SemaphoreType.DMA((2,))],
         compiler_params=params(),
-        name="tract_tiles",
+        name="far_tiles",
     )(fracs, tiles, table, heads, weights, hist, *news)
-    order = [*range(2, peers), 1, 0]
-    arrived = [swap(shares[r], "narrow", r) if r else shares[r] for r in order]
+    sent = {r: swap(shares[peers - 1 - r], "narrow", r) for r in range(2, peers)}
+
+    half = peer_targets * STEPS // 2
+    pieces = [
+        pltpu.VMEM((rows, block_rows), jnp.bfloat16) for rows in (half, share_rows - half)
+    ]
+    *pair, own = pl.pallas_call(
+        functools.partial(near_tiles_kernel, peers=peers, peer_targets=peer_targets, fixed=fixed),
+        out_shape=[*pieces, share],
+        in_specs=[vmem_spec] * 6,
+        out_specs=[vmem_spec] * 3,
+        scratch_shapes=[*scalars, VMEM(total.shape, jnp.float32), pltpu.SemaphoreType.DMA((2,))],
+        compiler_params=params(),
+        name="near_tiles",
+    )(fracs, tiles, heads, weights, hist, sums)
+    arrived = [sent[r] for r in range(2, peers)] + [swap(x, "narrow", 1) for x in pair] + [own]
 
     new_coefs, final_state = pl.pallas_call(
         functools.partial(
@@ -535,7 +616,7 @@
             jax.ShapeDtypeStruct(fresh_coefs.shape, jnp.bfloat16),
             jax.ShapeDtypeStruct(state.shape, jnp.float32),
         ],
-        in_specs=[vmem_spec] * (peers + 2),
+        in_specs=[vmem_spec] * (peers + 3),
         out_specs=[hbm_spec] * 2,
         scratch_shapes=[
             VMEM((own_blocks * PITCH, block_rows), jnp.float32),

time: 28.9 us -> 28.4 us (0.983)
  waiting for transfers between devices: 7.06 us -> 5.47 us
  Pallas kernels: 8.61 us -> 9.56 us
    ppermute x9 -> x10, waiting for transfers between devices: 7.06 us -> 5.47 us  [swap(): lax.ppermute(x, axis, [(i, i ^ r) for i in range(lax.axis_size(axis))])]
    pallas_call x1 -> x2, Pallas kernels: 2.65 us -> 3.39 us  [the longest x1 2.17 us: local(): pl.pallas_call(functools.partial(far_kernel, wide_peers=wide_peers, peers...]
    ppermute x9 -> x10, starting transfers between devices: 12.3 us -> 12.5 us  [swap(): lax.ppermute(x, axis, [(i, i ^ r) for i in range(lax.axis_size(axis))])]
  transfers between devices with their start and end apart: 9 -> 10, of which waited for: 4 -> 5; matrix products, arithmetic and copies ran while one was open for 0% -> 0% of each run, Pallas kernels for 13% -> 18%
where the time goes in v11:
time: 28.4 us; the launch traced here: 28.2 us
  starting transfers between devices  12.5 us (44%)
  Pallas kernels  9.56 us (34%)
  waiting for transfers between devices  5.47 us (19%)
  between operations  0.7 us (2%)
    ppermute x10, starting transfers between devices, swap(): lax.ppermute(x, axis, [(i, i ^ r) for i in range(lax.axis_size(axis))])  12.5 us
    ppermute x10, waiting for transfers between devices, swap(): lax.ppermute(x, axis, [(i, i ^ r) for i in range(lax.axis_size(axis))])  5.47 us
    pallas_call x1, Pallas kernels, local(): pl.pallas_call(functools.partial(far_kernel, wide_peers=wide_peers, peers...  2.17 us
    pallas_call x1, Pallas kernels, local(): pl.pallas_call(near_kernel, out_shape=[pltpu.VMEM(fresh_coefs.shape, jnp....  1.98 us
    pallas_call x1, Pallas kernels, local(): pl.pallas_call(functools.partial(prepare_kernel, peers=peers, own_blocks=...  1.94 us
    pallas_call x1, Pallas kernels, local(): pl.pallas_call(functools.partial(window_kernel, peers=peers, own_blocks=o...  1.64 us
    pallas_call x1, Pallas kernels, local(): pl.pallas_call(functools.partial(near_tiles_kernel, peers=peers, peer_tar...  1.22 us
    pallas_call x1, Pallas kernels, local(): pl.pallas_call(functools.partial(pick_kernel, capacity=capacity, peers=wi...  0.62 us
  transfers between devices with their start and end apart: 10, of which 5 were waited for; matrix products, arithmetic and copies ran while one was open for 0% of the time, Pallas kernels for 18%

profile of v11, /device:TPU:0, one launch (start us, length us, event | category | flops | bytes accessed | tf_op | source)
XLA Modules:
  0.0 28.2 jit_solution(6935833009056084876)
XLA Ops:
  0.6 4.1 %collective-permute-start.2 = (s32[2,4]{1,0:T(2,128)}, s32[2,4]{1,0:T(2,128)S(1)}, u32[]{:S(2)}, u32[]{:S(2)}) collective-permute-start(s32[2,4]{1,0:T(2,128)} %bitcast.15), channel_id=1, source_target_pairs={{0,8},{4,12},{8,0},{12,4},{1,9},{5,13},{9,1},{13,5},{2,10},{6,14},... | collective-permute-start | bytes 104 | tf_op jit(solution)/shard_map/ppermute | solution.py:491
  4.7 1.3 %collective-permute-start.1 = (s32[2,4]{1,0:T(2,128)}, s32[2,4]{1,0:T(2,128)S(1)}, u32[]{:S(2)}, u32[]{:S(2)}) collective-permute-start(s32[2,4]{1,0:T(2,128)} %bitcast.16), channel_id=1, source_target_pairs={{0,12},{4,8},{8,4},{12,0},{1,13},{5,9},{9,5},{13,1},{2,14},{6,10},... | collective-permute-start | bytes 104 | tf_op jit(solution)/shard_map/ppermute | solution.py:491
  6.1 0.2 collective-permute-start
  6.3 2.0 %near.1 = (bf16[32,32,128]{2,1,0:T(8,128)(2,1)S(1)}, bf16[96,128,128]{2,1,0:T(8,128)(2,1)S(1)}) custom-call(bf16[32,32,128]{2,1,0:T(8,128)(2,1)} %fresh_hbm.1, bf16[96,128,128]{2,1,0:T(8,128)(2,1)} %bitcast.12), custom_call_target="tpu_custom_call" | custom-call | tf_op jit(solution)/shard_map/near/pallas_call | solution.py:511
  8.3 0.0 collective-permute-done.2.refs_2_
  8.3 2.0 %collective-permute-done.1.refs_1_ = s32[2,4]{1,0:T(2,128)S(1)} collective-permute-done((s32[2,4]{1,0:T(2,128)}, s32[2,4]{1,0:T(2,128)S(1)}, u32[]{:S(2)}, u32[]{:S(2)}) %collective-permute-start.1) | collective-permute-done | bytes 64 | tf_op jit(solution)/shard_map/ppermute | solution.py:491
  10.3 0.0 collective-permute-done.refs_0_
  10.3 0.6 %pick_blocks.1 = (bf16[2,32,128]{2,1,0:T(8,128)(2,1)S(1)}, bf16[2,32,128]{2,1,0:T(8,128)(2,1)S(1)}, bf16[2,32,128]{2,1,0:T(8,128)(2,1)S(1)}) custom-call(s32[2,4]{1,0:T(2,128)S(1)} %collective-permute-done.refs_0_, s32[2,4]{1,0:T(2,128)S(1)} %collective-permute-done.1.refs_1_, s32[2,4]{1,0:T(2,128)S(1)} %collective-permute-done.2.refs_2_, ...), custom_call_target="tpu_custom_call" | custom-call | tf_op jit(solution)/shard_map/pick_blocks/pallas_call | solution.py:560
  10.9 2.1 %collective-permute-start.3 = (bf16[2,32,128]{2,1,0:T(8,128)(2,1)S(1)}, bf16[2,32,128]{2,1,0:T(8,128)(2,1)S(1)}, u32[]{:S(2)}, u32[]{:S(2)}) collective-permute-start(bf16[2,32,128]{2,1,0:T(8,128)(2,1)S(1)} %get-tuple-element.25), channel_id=1, source_target_pairs={{0,12},{4,8},{8,4},{12,0},{1,13},{5,9},{9,5},{13,1},{2,14},{6,10},... | collective-permute-start | bytes 49160 | tf_op jit(solution)/shard_map/ppermute | solution.py:491
  13.0 0.0 collective-permute-start.4
  13.0 2.4 %collective-permute-start.5 = (bf16[2,32,128]{2,1,0:T(8,128)(2,1)S(1)}, bf16[2,32,128]{2,1,0:T(8,128)(2,1)S(1)}, u32[]{:S(2)}, u32[]{:S(2)}) collective-permute-start(bf16[2,32,128]{2,1,0:T(8,128)(2,1)S(1)} %get-tuple-element.27), channel_id=1, source_target_pairs={{0,4},{4,0},{8,12},{12,8},{1,5},{5,1},{9,13},{13,9},{2,6},{6,2},{1... | collective-permute-start | bytes 49160 | tf_op jit(solution)/shard_map/ppermute | solution.py:491
  15.4 1.9 %prepare.1 = (f32[160,128]{1,0:T(8,128)S(1)}, f32[768,128]{1,0:T(8,128)S(1)}, s32[4,128]{1,0:T(4,128)S(1)}, f32[1,128]{1,0:T(1,128)S(1)}, bf16[4,16,128]{2,1,0:T(8,128)(2,1)S(1)}) custom-call(bf16[32,32,128]{2,1,0:T(8,128)(2,1)S(1)} %get-tuple-element.19.fresh_ref.refs_3_, s32[2,4]{1,0:T(2,128)} %bitcast.18, f32[2,4096]{1,0:T(2,128)} %state_hbm.1, ...), custom_call_target="tpu_custom_call" | custom-call | tf_op jit(solution)/shard_map/prepare/pallas_call | solution.py:523
  17.3 0.0 collective-permute-done.3.refs_0_
  17.3 0.3 %collective-permute-done.4.refs_1_ = bf16[2,32,128]{2,1,0:T(8,128)(2,1)S(1)} collective-permute-done((bf16[2,32,128]{2,1,0:T(8,128)(2,1)S(1)}, bf16[2,32,128]{2,1,0:T(8,128)(2,1)S(1)}, u32[]{:S(2)}, u32[]{:S(2)}) %collective-permute-start.4) | collective-permute-done | bytes 16416 | tf_op jit(solution)/shard_map/ppermute | solution.py:491
  17.7 0.0 collective-permute-done.5.refs_2_
  17.7 0.0 copy-start
  17.7 2.2 %far_tiles.1 = (bf16[400,128]{1,0:T(8,128)(2,1)S(1)}, bf16[400,128]{1,0:T(8,128)(2,1)S(1)}, f32[768,128]{1,0:T(8,128)S(1)}, f32[1568,128]{1,0:T(8,128)S(1)}) custom-call(f32[1,128]{1,0:T(1,128)S(1)} %get-tuple-element.20.fracs_ref, s32[4,128]{1,0:T(4,128)S(1)} %get-tuple-element.21.tiles_ref, bf16[96,96]{1,0:T(8,128)(2,1)} %constant.6.clone.table_hbm.table_ref, ...), custom_call_target="tpu_custom_call" | custom-call | tf_op jit(solution)/shard_map/far_tiles/pallas_call | solution.py:580
  19.9 1.6 %collective-permute-start.6 = (bf16[400,128]{1,0:T(8,128)(2,1)S(1)}, bf16[400,128]{1,0:T(8,128)(2,1)S(1)}, u32[]{:S(2)}, u32[]{:S(2)}) collective-permute-start(bf16[400,128]{1,0:T(8,128)(2,1)S(1)} %get-tuple-element.28), channel_id=1, source_target_pairs={{0,2},{1,3},{2,0},{3,1},{4,6},{5,7},{6,4},{7,5},{8,10},{9,11},{10,... | collective-permute-start | bytes 307208 | tf_op jit(solution)/shard_map/ppermute | solution.py:491
  21.4 0.0 collective-permute-start.7
  21.4 1.2 %near_tiles.1 = (bf16[192,128]{1,0:T(8,128)(2,1)S(1)}, bf16[208,128]{1,0:T(8,128)(2,1)S(1)}, bf16[400,128]{1,0:T(8,128)(2,1)S(1)}) custom-call(f32[1,128]{1,0:T(1,128)S(1)} %get-tuple-element.20.fracs_ref, s32[4,128]{1,0:T(4,128)S(1)} %get-tuple-element.21.tiles_ref, bf16[4,16,128]{2,1,0:T(8,128)(2,1)S(1)} %get-tuple-element.22.head_ref, ...), custom_call_target="tpu_custom_call" | custom-call | tf_op jit(solution)/shard_map/near_tiles/pallas_call | solution.py:599
  22.6 0.7 %collective-permute-start.9 = (bf16[208,128]{1,0:T(8,128)(2,1)S(1)}, bf16[208,128]{1,0:T(8,128)(2,1)S(1)}, u32[]{:S(2)}, u32[]{:S(2)}) collective-permute-start(bf16[208,128]{1,0:T(8,128)(2,1)S(1)} %get-tuple-element.33), channel_id=1, source_target_pairs={{0,1},{1,0},{2,3},{3,2},{4,5},{5,4},{6,7},{7,6},{8,9},{9,8},{10,11... | collective-permute-start | bytes 159752 | tf_op jit(solution)/shard_map/ppermute | solution.py:491
  23.3 0.1 collective-permute-start.8
  23.4 1.2 %collective-permute-done.8.refs_2_ = bf16[192,128]{1,0:T(8,128)(2,1)S(1)} collective-permute-done((bf16[192,128]{1,0:T(8,128)(2,1)S(1)}, bf16[192,128]{1,0:T(8,128)(2,1)S(1)}, u32[]{:S(2)}, u32[]{:S(2)}) %collective-permute-start.8) | collective-permute-done | bytes 49184 | tf_op jit(solution)/shard_map/ppermute | solution.py:491
  24.6 0.0 collective-permute-done.9.refs_3_
  24.6 0.2 collective-permute-done.6.refs_0_
  24.8 1.8 %collective-permute-done.7.refs_1_ = bf16[400,128]{1,0:T(8,128)(2,1)S(1)} collective-permute-done((bf16[400,128]{1,0:T(8,128)(2,1)S(1)}, bf16[400,128]{1,0:T(8,128)(2,1)S(1)}, u32[]{:S(2)}, u32[]{:S(2)}) %collective-permute-start.7) | collective-permute-done | bytes 102432 | tf_op jit(solution)/shard_map/ppermute | solution.py:491
  26.6 0.0 copy-done
  26.6 1.6 %window_steps.1 = (bf16[32,32,128]{2,1,0:T(8,128)(2,1)}, f32[2,4096]{1,0:T(2,128)}) custom-call(bf16[400,128]{1,0:T(8,128)(2,1)S(1)} %collective-permute-done.6.refs_0_, bf16[400,128]{1,0:T(8,128)(2,1)S(1)} %collective-permute-done.7.refs_1_, bf16[192,128]{1,0:T(8,128)(2,1)S(1)} %collective-permute-done.8.refs_2_, ...), custom_call_target="tpu_custom_call" | custom-call | tf_op jit(solution)/shard_map/window_steps/pallas_call | solution.py:610
Async XLA Ops:
  0.6 7.7 %collective-permute-start.2 = (s32[2,4]{1,0:T(2,128)}, s32[2,4]{1,0:T(2,128)S(1)}, u32[]{:S(2)}, u32[]{:S(2)}) collective-permute-start(s32[2,4]{1,0:T(2,128)} %bitcast.15), channel_id=1, source_target_pairs={{0,8},{4,12},{8,0},{12,4},{1,9},{5,13},{9,1},{13,5},{2,10},{6,14},... | collective-permute-start | bytes 104 | tf_op jit(solution)/shard_map/ppermute | solution.py:491
  4.7 5.6 %collective-permute-start.1 = (s32[2,4]{1,0:T(2,128)}, s32[2,4]{1,0:T(2,128)S(1)}, u32[]{:S(2)}, u32[]{:S(2)}) collective-permute-start(s32[2,4]{1,0:T(2,128)} %bitcast.16), channel_id=1, source_target_pairs={{0,12},{4,8},{8,4},{12,0},{1,13},{5,9},{9,5},{13,1},{2,14},{6,10},... | collective-permute-start | bytes 104 | tf_op jit(solution)/shard_map/ppermute | solution.py:491
  6.1 4.2 %collective-permute-start = (s32[2,4]{1,0:T(2,128)}, s32[2,4]{1,0:T(2,128)S(1)}, u32[]{:S(2)}, u32[]{:S(2)}) collective-permute-start(s32[2,4]{1,0:T(2,128)} %bitcast.17), channel_id=1, source_target_pairs={{0,4},{4,0},{8,12},{12,8},{1,5},{5,1},{9,13},{13,9},{2,6},{6,2},{1... | collective-permute-start | bytes 104 | tf_op jit(solution)/shard_map/ppermute | solution.py:491
  10.9 6.4 %collective-permute-start.3 = (bf16[2,32,128]{2,1,0:T(8,128)(2,1)S(1)}, bf16[2,32,128]{2,1,0:T(8,128)(2,1)S(1)}, u32[]{:S(2)}, u32[]{:S(2)}) collective-permute-start(bf16[2,32,128]{2,1,0:T(8,128)(2,1)S(1)} %get-tuple-element.25), channel_id=1, source_target_pairs={{0,12},{4,8},{8,4},{12,0},{1,13},{5,9},{9,5},{13,1},{2,14},{6,10},... | collective-permute-start | bytes 49160 | tf_op jit(solution)/shard_map/ppermute | solution.py:491
  13.0 4.6 %collective-permute-start.4 = (bf16[2,32,128]{2,1,0:T(8,128)(2,1)S(1)}, bf16[2,32,128]{2,1,0:T(8,128)(2,1)S(1)}, u32[]{:S(2)}, u32[]{:S(2)}) collective-permute-start(bf16[2,32,128]{2,1,0:T(8,128)(2,1)S(1)} %get-tuple-element.26), channel_id=1, source_target_pairs={{0,8},{4,12},{8,0},{12,4},{1,9},{5,13},{9,1},{13,5},{2,10},{6,14},... | collective-permute-start | bytes 49160 | tf_op jit(solution)/shard_map/ppermute | solution.py:491
  13.0 4.6 %collective-permute-start.5 = (bf16[2,32,128]{2,1,0:T(8,128)(2,1)S(1)}, bf16[2,32,128]{2,1,0:T(8,128)(2,1)S(1)}, u32[]{:S(2)}, u32[]{:S(2)}) collective-permute-start(bf16[2,32,128]{2,1,0:T(8,128)(2,1)S(1)} %get-tuple-element.27), channel_id=1, source_target_pairs={{0,4},{4,0},{8,12},{12,8},{1,5},{5,1},{9,13},{13,9},{2,6},{6,2},{1... | collective-permute-start | bytes 49160 | tf_op jit(solution)/shard_map/ppermute | solution.py:491
  17.7 8.9 %copy-start = (bf16[128,384]{1,0:T(8,128)(2,1)S(1)}, bf16[128,384]{1,0:T(8,128)(2,1)}, u32[]{:S(2)}) copy-start(bf16[128,384]{1,0:T(8,128)(2,1)} %constant.8.clone.refs_6_) | copy-start | bytes 294916
  19.9 4.9 %collective-permute-start.6 = (bf16[400,128]{1,0:T(8,128)(2,1)S(1)}, bf16[400,128]{1,0:T(8,128)(2,1)S(1)}, u32[]{:S(2)}, u32[]{:S(2)}) collective-permute-start(bf16[400,128]{1,0:T(8,128)(2,1)S(1)} %get-tuple-element.28), channel_id=1, source_target_pairs={{0,2},{1,3},{2,0},{3,1},{4,6},{5,7},{6,4},{7,5},{8,10},{9,11},{10,... | collective-permute-start | bytes 307208 | tf_op jit(solution)/shard_map/ppermute | solution.py:491
  21.4 5.2 %collective-permute-start.7 = (bf16[400,128]{1,0:T(8,128)(2,1)S(1)}, bf16[400,128]{1,0:T(8,128)(2,1)S(1)}, u32[]{:S(2)}, u32[]{:S(2)}) collective-permute-start(bf16[400,128]{1,0:T(8,128)(2,1)S(1)} %get-tuple-element.29), channel_id=1, source_target_pairs={{0,3},{1,2},{2,1},{3,0},{4,7},{5,6},{6,5},{7,4},{8,11},{9,10},{10,... | collective-permute-start | bytes 307208 | tf_op jit(solution)/shard_map/ppermute | solution.py:491
  22.6 1.9 %collective-permute-start.9 = (bf16[208,128]{1,0:T(8,128)(2,1)S(1)}, bf16[208,128]{1,0:T(8,128)(2,1)S(1)}, u32[]{:S(2)}, u32[]{:S(2)}) collective-permute-start(bf16[208,128]{1,0:T(8,128)(2,1)S(1)} %get-tuple-element.33), channel_id=1, source_target_pairs={{0,1},{1,0},{2,3},{3,2},{4,5},{5,4},{6,7},{7,6},{8,9},{9,8},{10,11... | collective-permute-start | bytes 159752 | tf_op jit(solution)/shard_map/ppermute | solution.py:491
  23.3 1.2 %collective-permute-start.8 = (bf16[192,128]{1,0:T(8,128)(2,1)S(1)}, bf16[192,128]{1,0:T(8,128)(2,1)S(1)}, u32[]{:S(2)}, u32[]{:S(2)}) collective-permute-start(bf16[192,128]{1,0:T(8,128)(2,1)S(1)} %get-tuple-element.32), channel_id=1, source_target_pairs={{0,1},{1,0},{2,3},{3,2},{4,5},{5,4},{6,7},{7,6},{8,9},{9,8},{10,11... | collective-permute-start | bytes 147464 | tf_op jit(solution)/shard_map/ppermute | solution.py:491

commit v12 on v11

--- a/solution.py
+++ b/solution.py
@@ -80,8 +80,8 @@
 def prepare_kernel(
     fresh_ref, reads_hbm, state_hbm, lesion_hbm, stim_hbm, wave_hbm, slot_hbm, target_hbm,
     delay_hbm, lanes_hbm, table_hbm, older_hbm, frac_hbm,
-    ready_out, hist_out, tiles_out, fracs_out, head_out,
-    reads, state, lesion, stim, wave, slot, target, delay, frac, lanes, table, older, sems,
+    ready_out, hist_out, tiles_out, fracs_out, head_out, table,
+    reads, state, lesion, stim, wave, slot, target, delay, frac, lanes, older, sems,
     *, peers, own_blocks, peer_targets, capacity,
 ):
     pairs = [
@@ -122,7 +122,7 @@
         rank = jnp.dot(below, held[part].astype(jnp.bfloat16), preferred_element_type=jnp.float32)
         ranks = ranks + jnp.sum(hits[part] * rank[:, :tile_count], axis=0, keepdims=True)
         rank = jnp.where(held[part] > 0.5, rank, -1.0)
-        source = (place ^ p).astype(jnp.float32)
+        source = ((peers - 1) - (place ^ p)).astype(jnp.float32)
         rows = []
         for h in range(head_rows):
             match = rank == lanes[0, h : h + 1, :]
@@ -296,12 +296,19 @@
         copy.start()
     total[...] = jnp.zeros_like(total)
     hist[...] = hist_ref[...]
-    for i, block in enumerate(news):
-        table = table_ref[:STEPS, : block.shape[1]]
-        for c in range(capacity):
+    came = [(i, c) for i in range(len(news)) for c in range(capacity)]
+    coef_count = news[0].shape[1]
+    for first in range(0, len(came), SEGS):
+        some = came[first : first + SEGS]
+        values = jnp.dot(
+            table_ref[: len(some) * STEPS, : len(some) * coef_count],
+            jnp.concatenate([news[i][c] for i, c in some], axis=0),
+            preferred_element_type=jnp.float32,
+        )
+        for place_here, (i, c) in enumerate(some):
             slot = (owner ^ (wide_peers - 1 - i)) * capacity + c
             rows = pl.ds(pl.multiple_of(slot * LENGTH + HSEG * STEPS, 8), STEPS)
-            hist[rows, :] = jnp.dot(table, block[c], preferred_element_type=jnp.float32)
+            hist[rows, :] = values[place_here * STEPS : (place_here + 1) * STEPS]
     for copy in copies:
         copy.wait()
 
@@ -357,52 +364,80 @@
     return pieces[group // groups][first : first + width, :]
 
 
-def window_kernel(*refs, peers, own_blocks, peer_targets, coef_count):
-    shares = {r: (ref,) for r, ref in zip(range(2, peers), refs)}
-    shares |= {1: refs[peers - 2 : peers], 0: (refs[peers],)}
-    (
-        ready_ref, fit_ref, coefs_hbm, state_hbm, samples, rates, coefs, state, sems,
-    ) = refs[peers + 1 :]
+def one_hot(head, rows, columns):
+    row = lax.broadcasted_iota(jnp.int32, (rows, 128), 0).astype(jnp.float32) + 1.0
+    parts = [
+        jnp.where(row == head[h : h + 1, :], 1.0, 0.0).astype(jnp.bfloat16)
+        for h in range(pl.cdiv(columns, 128))
+    ]
+    return jnp.concatenate(parts, axis=1)[:, :columns]
+
+
+def two_groups(shares, pair, width):
+    return jnp.concatenate(
+        [
+            jnp.concatenate([share_rows(share, g, width) for share in shares], axis=0)
+            for g in (pair, pair + 1)
+        ],
+        axis=1,
+    )
+
+
+def forcing_kernel(*refs, peers, own_blocks, peer_targets):
+    shares = {r: (ref,) for r, ref in zip(range(2, peers - 1), refs)}
+    shares |= {1: refs[peers - 3 : peers - 1], 0: (refs[peers - 1],)}
+    ready_ref, out_ref = refs[peers:]
     block_rows = ready_ref.shape[1]
     width = TOGETHER * peer_targets
-
-    head = sum(shares[r][-1][-HEAD:, :].astype(jnp.float32) for r in range(peers))
-    row = lax.broadcasted_iota(jnp.int32, (TOGETHER * own_blocks, 128), 0).astype(jnp.float32) + 1.0
-    columns = peers * width
-    scatter = jnp.concatenate(
-        [
-            jnp.where(row == head[h : h + 1, :], 1.0, 0.0).astype(jnp.bfloat16)
-            for h in range(pl.cdiv(columns, 128))
-        ],
-        axis=1,
-    )[:, :columns]
-
-    excite, inhibit, gain, counts = [
-        ready_ref[i * own_blocks : (i + 1) * own_blocks, :] for i in range(4)
-    ]
-    a = excite_excite / 2
-    gain = 0.5 * gain
-    counts = 0.5 * counts
-    carried = a * excite
+    head = sum(share[-1][-HEAD:, :].astype(jnp.float32) for share in shares.values())
+    scatter = one_hot(head, TOGETHER * own_blocks, peers * width)
+    stack = [shares[r] for r in (peers - 2, *range(peers - 2, -1, -1))]
+    gain, counts = [
+        0.5 * ready_ref[i * own_blocks : (i + 1) * own_blocks, :] for i in (2, 3)
+    ]
     for pair in range(0, STEPS // TOGETHER, 2):
-        arrived = jnp.concatenate(
-            [
-                jnp.concatenate(
-                    [share_rows(shares[r], g, width) for r in range(peers)], axis=0
-                )
-                for g in (pair, pair + 1)
-            ],
-            axis=1,
-        )
-        inflow = jnp.dot(scatter, arrived, preferred_element_type=jnp.float32)
+        inflow = jnp.dot(
+            scatter, two_groups(stack, pair, width), preferred_element_type=jnp.float32
+        )
         for jj in range(2 * TOGETHER):
             j = pair * TOGETHER + jj
             wave = ready_ref[4 * own_blocks + j : 4 * own_blocks + j + 1, :]
             first = jj % TOGETHER * own_blocks
             left = jj // TOGETHER * block_rows
-            half_forcing = gain * inflow[
+            out_ref[j * own_blocks : (j + 1) * own_blocks, :] = gain * inflow[
                 first : first + own_blocks, left : left + block_rows
             ] + (wave * counts - excite_offset / 2)
+
+
+def window_kernel(
+    share_ref, forcing_ref, ready_ref, fit_ref, coefs_hbm, state_hbm,
+    samples, rates, coefs, state, sems,
+    *, own_blocks, peer_targets, coef_count,
+):
+    block_rows = ready_ref.shape[1]
+    width = TOGETHER * peer_targets
+    scatter = one_hot(
+        share_ref[-HEAD:, :].astype(jnp.float32), TOGETHER * own_blocks, width
+    )
+
+    excite, inhibit, gain = [
+        ready_ref[i * own_blocks : (i + 1) * own_blocks, :] for i in range(3)
+    ]
+    a = excite_excite / 2
+    gain = 0.5 * gain
+    carried = a * excite
+    for pair in range(0, STEPS // TOGETHER, 2):
+        inflow = jnp.dot(
+            scatter, two_groups([(share_ref,)], pair, width), preferred_element_type=jnp.float32
+        )
+        for jj in range(2 * TOGETHER):
+            j = pair * TOGETHER + jj
+            first = jj % TOGETHER * own_blocks
+            left = jj // TOGETHER * block_rows
+            half_forcing = (
+                forcing_ref[j * own_blocks : (j + 1) * own_blocks, :]
+                + gain * inflow[first : first + own_blocks, left : left + block_rows]
+            )
             inhibit_drive = (inhibit_inhibit / 2) * inhibit + inhibit_offset / 2
             excite_turn = jnp.tanh(carried + (half_forcing - (inhibit_excite / 2) * inhibit))
             inhibit_turn = jnp.tanh((excite_inhibit / 2 / a) * carried - inhibit_drive)
@@ -504,10 +539,8 @@
         VMEM((1, tile_count), jnp.int32),
         VMEM((1, tile_count), jnp.float32),
         VMEM((3, HEAD, 128), jnp.float32),
-        VMEM((LENGTH, SEGS * coef_count), jnp.bfloat16),
         VMEM((slot_count, HSEG, coef_count, block_rows), jnp.bfloat16),
     ]
-    table = far(jnp.asarray(expand_table(coef_count)))
     fresh, weights = pl.pallas_call(
         near_kernel,
         out_shape=[
@@ -520,7 +553,7 @@
         compiler_params=params(),
         name="near",
     )(far(fresh_coefs), far(tract_weights.reshape(tile_count, block_rows, block_rows)))
-    ready, hist, tiles, fracs, heads = pl.pallas_call(
+    ready, hist, tiles, fracs, heads, table = pl.pallas_call(
         functools.partial(
             prepare_kernel,
             peers=peers, own_blocks=own_blocks, peer_targets=peer_targets, capacity=capacity,
@@ -531,9 +564,10 @@
             pltpu.VMEM((4, 128), jnp.int32),
             pltpu.VMEM((1, 128), jnp.float32),
             pltpu.VMEM((peers, HEAD, 128), jnp.bfloat16),
+            pltpu.VMEM((LENGTH, SEGS * coef_count), jnp.bfloat16),
         ],
         in_specs=[vmem_spec] + [hbm_spec] * 12,
-        out_specs=[vmem_spec] * 5,
+        out_specs=[vmem_spec] * 6,
         scratch_shapes=[
             SMEM((capacity, wide_peers), jnp.int32),
             *vmem_inputs,
@@ -552,7 +586,7 @@
         far(tract_target.reshape(1, tile_count)),
         far(tract_delay.reshape(1, tile_count)),
         far(jnp.asarray(lane_tables(peers, peer_targets, own_blocks))),
-        table,
+        far(jnp.asarray(expand_table(coef_count))),
         far(older_coefs.reshape(slot_count, HSEG, coef_count, block_rows)),
         far(tract_frac.reshape(1, tile_count)),
     )
@@ -605,18 +639,28 @@
         compiler_params=params(),
         name="near_tiles",
     )(fracs, tiles, heads, weights, hist, sums)
-    arrived = [sent[r] for r in range(2, peers)] + [swap(x, "narrow", 1) for x in pair] + [own]
+    pair = [swap(x, "narrow", 1) for x in pair]
+    forcing = pl.pallas_call(
+        functools.partial(
+            forcing_kernel, peers=peers, own_blocks=own_blocks, peer_targets=peer_targets
+        ),
+        out_shape=pltpu.VMEM((STEPS * own_blocks, block_rows), jnp.float32),
+        in_specs=[vmem_spec] * (peers + 1),
+        out_specs=vmem_spec,
+        compiler_params=params(),
+        name="forcing",
+    )(*[sent[r] for r in range(2, peers - 1)], *pair, own, ready)
 
     new_coefs, final_state = pl.pallas_call(
         functools.partial(
             window_kernel,
-            peers=peers, own_blocks=own_blocks, peer_targets=peer_targets, coef_count=coef_count,
+            own_blocks=own_blocks, peer_targets=peer_targets, coef_count=coef_count,
         ),
         out_shape=[
             jax.ShapeDtypeStruct(fresh_coefs.shape, jnp.bfloat16),
             jax.ShapeDtypeStruct(state.shape, jnp.float32),
         ],
-        in_specs=[vmem_spec] * (peers + 3),
+        in_specs=[vmem_spec] * 4,
         out_specs=[hbm_spec] * 2,
         scratch_shapes=[
             VMEM((own_blocks * PITCH, block_rows), jnp.float32),
@@ -627,7 +671,7 @@
         ],
         compiler_params=params(),
         name="window_steps",
-    )(*arrived, ready, jnp.asarray(fit_table(coef_count)))
+    )(sent[peers - 1], forcing, ready, jnp.asarray(fit_table(coef_count)))
     return new_coefs, final_state
 
 

time: 28.4 us -> 27.5 us (0.968)
  Pallas kernels: 9.56 us -> 9 us
  waiting for transfers between devices: 5.47 us -> 5.15 us
    pallas_call x1, Pallas kernels: 2.17 us -> 1.41 us  [local(): pl.pallas_call(functools.partial(far_kernel, wide_peers=wide_peers, peers...]
    ppermute x10, waiting for transfers between devices: 5.47 us -> 5.15 us  [swap(): lax.ppermute(x, axis, [(i, i ^ r) for i in range(lax.axis_size(axis))])]
    pallas_call x1 -> x2, Pallas kernels: 1.64 us -> 1.83 us  [the longest x1 1.53 us: local(): pl.pallas_call(functools.partial(window_kernel, own_blocks=own_blocks, pe...]
  transfers between devices with their start and end apart: 10 -> 10, of which waited for: 5 -> 5; matrix products, arithmetic and copies ran while one was open for 0% -> 0% of each run, Pallas kernels for 18% -> 20%
where the time goes in v12:
time: 27.5 us; the launch traced here: 27.4 us
  starting transfers between devices  12.5 us (45%)
  Pallas kernels  9 us (33%)
  waiting for transfers between devices  5.15 us (19%)
  between operations  0.71 us (3%)
    ppermute x10, starting transfers between devices, swap(): lax.ppermute(x, axis, [(i, i ^ r) for i in range(lax.axis_size(axis))])  12.5 us
    ppermute x10, waiting for transfers between devices, swap(): lax.ppermute(x, axis, [(i, i ^ r) for i in range(lax.axis_size(axis))])  5.15 us
    pallas_call x1, Pallas kernels, local(): pl.pallas_call(near_kernel, out_shape=[pltpu.VMEM(fresh_coefs.shape, jnp....  1.98 us
    pallas_call x1, Pallas kernels, local(): pl.pallas_call(functools.partial(prepare_kernel, peers=peers, own_blocks=...  1.94 us
    pallas_call x1, Pallas kernels, local(): pl.pallas_call(functools.partial(window_kernel, own_blocks=own_blocks, pe...  1.53 us
    pallas_call x1, Pallas kernels, local(): pl.pallas_call(functools.partial(far_kernel, wide_peers=wide_peers, peers...  1.41 us
    pallas_call x1, Pallas kernels, local(): pl.pallas_call(functools.partial(near_tiles_kernel, peers=peers, peer_tar...  1.22 us
    pallas_call x1, Pallas kernels, local(): pl.pallas_call(functools.partial(pick_kernel, capacity=capacity, peers=wi...  0.62 us
  transfers between devices with their start and end apart: 10, of which 5 were waited for; matrix products, arithmetic and copies ran while one was open for 0% of the time, Pallas kernels for 20%

profile of v12, /device:TPU:0, one launch (start us, length us, event | category | flops | bytes accessed | tf_op | source)
XLA Modules:
  0.0 27.4 jit_solution(2203442089256755857)
XLA Ops:
  0.6 4.1 %collective-permute-start.2 = (s32[2,4]{1,0:T(2,128)}, s32[2,4]{1,0:T(2,128)S(1)}, u32[]{:S(2)}, u32[]{:S(2)}) collective-permute-start(s32[2,4]{1,0:T(2,128)} %bitcast.15), channel_id=1, source_target_pairs={{0,8},{4,12},{8,0},{12,4},{1,9},{5,13},{9,1},{13,5},{2,10},{6,14},... | collective-permute-start | bytes 104 | tf_op jit(solution)/shard_map/ppermute | solution.py:526
  4.7 1.3 %collective-permute-start.1 = (s32[2,4]{1,0:T(2,128)}, s32[2,4]{1,0:T(2,128)S(1)}, u32[]{:S(2)}, u32[]{:S(2)}) collective-permute-start(s32[2,4]{1,0:T(2,128)} %bitcast.16), channel_id=1, source_target_pairs={{0,12},{4,8},{8,4},{12,0},{1,13},{5,9},{9,5},{13,1},{2,14},{6,10},... | collective-permute-start | bytes 104 | tf_op jit(solution)/shard_map/ppermute | solution.py:526
  6.1 0.2 collective-permute-start
  6.3 2.0 %near.1 = (bf16[32,32,128]{2,1,0:T(8,128)(2,1)S(1)}, bf16[96,128,128]{2,1,0:T(8,128)(2,1)S(1)}) custom-call(bf16[32,32,128]{2,1,0:T(8,128)(2,1)} %fresh_hbm.1, bf16[96,128,128]{2,1,0:T(8,128)(2,1)} %bitcast.12), custom_call_target="tpu_custom_call" | custom-call | tf_op jit(solution)/shard_map/near/pallas_call | solution.py:544
  8.3 0.0 collective-permute-done.2.refs_2_
  8.3 2.0 %collective-permute-done.1.refs_1_ = s32[2,4]{1,0:T(2,128)S(1)} collective-permute-done((s32[2,4]{1,0:T(2,128)}, s32[2,4]{1,0:T(2,128)S(1)}, u32[]{:S(2)}, u32[]{:S(2)}) %collective-permute-start.1) | collective-permute-done | bytes 64 | tf_op jit(solution)/shard_map/ppermute | solution.py:526
  10.3 0.0 collective-permute-done.refs_0_
  10.3 0.6 %pick_blocks.1 = (bf16[2,32,128]{2,1,0:T(8,128)(2,1)S(1)}, bf16[2,32,128]{2,1,0:T(8,128)(2,1)S(1)}, bf16[2,32,128]{2,1,0:T(8,128)(2,1)S(1)}) custom-call(s32[2,4]{1,0:T(2,128)S(1)} %collective-permute-done.refs_0_, s32[2,4]{1,0:T(2,128)S(1)} %collective-permute-done.1.refs_1_, s32[2,4]{1,0:T(2,128)S(1)} %collective-permute-done.2.refs_2_, ...), custom_call_target="tpu_custom_call" | custom-call | tf_op jit(solution)/shard_map/pick_blocks/pallas_call | solution.py:594
  10.9 2.1 %collective-permute-start.3 = (bf16[2,32,128]{2,1,0:T(8,128)(2,1)S(1)}, bf16[2,32,128]{2,1,0:T(8,128)(2,1)S(1)}, u32[]{:S(2)}, u32[]{:S(2)}) collective-permute-start(bf16[2,32,128]{2,1,0:T(8,128)(2,1)S(1)} %get-tuple-element.27), channel_id=1, source_target_pairs={{0,12},{4,8},{8,4},{12,0},{1,13},{5,9},{9,5},{13,1},{2,14},{6,10},... | collective-permute-start | bytes 49160 | tf_op jit(solution)/shard_map/ppermute | solution.py:526
  13.0 0.0 collective-permute-start.4
  13.0 2.4 %collective-permute-start.5 = (bf16[2,32,128]{2,1,0:T(8,128)(2,1)S(1)}, bf16[2,32,128]{2,1,0:T(8,128)(2,1)S(1)}, u32[]{:S(2)}, u32[]{:S(2)}) collective-permute-start(bf16[2,32,128]{2,1,0:T(8,128)(2,1)S(1)} %get-tuple-element.29), channel_id=1, source_target_pairs={{0,4},{4,0},{8,12},{12,8},{1,5},{5,1},{9,13},{13,9},{2,6},{6,2},{1... | collective-permute-start | bytes 49160 | tf_op jit(solution)/shard_map/ppermute | solution.py:526
  15.4 1.9 %prepare.1 = (f32[160,128]{1,0:T(8,128)S(1)}, f32[768,128]{1,0:T(8,128)S(1)}, s32[4,128]{1,0:T(4,128)S(1)}, f32[1,128]{1,0:T(1,128)S(1)}, bf16[4,16,128]{2,1,0:T(8,128)(2,1)S(1)}, /*index=5*/bf16[96,96]{1,0:T(8,128)(2,1)S(1)}) custom-call(bf16[32,32,128]{2,1,0:T(8,128)(2,1)S(1)} %get-tuple-element.20.fresh_ref.refs_3_, s32[2,4]{1,0:T(2,128)} %bitcast.18, ...), custom_call_target="tpu_custom_call" | custom-call | tf_op jit(solution)/shard_map/prepare/pallas_call | solution.py:556
  17.3 0.0 collective-permute-done.3.refs_0_
  17.3 0.3 %collective-permute-done.4.refs_1_ = bf16[2,32,128]{2,1,0:T(8,128)(2,1)S(1)} collective-permute-done((bf16[2,32,128]{2,1,0:T(8,128)(2,1)S(1)}, bf16[2,32,128]{2,1,0:T(8,128)(2,1)S(1)}, u32[]{:S(2)}, u32[]{:S(2)}) %collective-permute-start.4) | collective-permute-done | bytes 16416 | tf_op jit(solution)/shard_map/ppermute | solution.py:526
  17.7 0.0 collective-permute-done.5.refs_2_
  17.7 1.4 %far_tiles.1 = (bf16[400,128]{1,0:T(8,128)(2,1)S(1)}, bf16[400,128]{1,0:T(8,128)(2,1)S(1)}, f32[768,128]{1,0:T(8,128)S(1)}, f32[1568,128]{1,0:T(8,128)S(1)}) custom-call(f32[1,128]{1,0:T(1,128)S(1)} %get-tuple-element.21.fracs_ref, s32[4,128]{1,0:T(4,128)S(1)} %get-tuple-element.22.tiles_ref, bf16[96,96]{1,0:T(8,128)(2,1)S(1)} %get-tuple-element.23.table_ref, ...), custom_call_target="tpu_custom_call" | custom-call | tf_op jit(solution)/shard_map/far_tiles/pallas_call | solution.py:614
  19.1 0.0 copy-start
  19.1 1.6 %collective-permute-start.7 = (bf16[400,128]{1,0:T(8,128)(2,1)S(1)}, bf16[400,128]{1,0:T(8,128)(2,1)S(1)}, u32[]{:S(2)}, u32[]{:S(2)}) collective-permute-start(bf16[400,128]{1,0:T(8,128)(2,1)S(1)} %get-tuple-element.31), channel_id=1, source_target_pairs={{0,2},{1,3},{2,0},{3,1},{4,6},{5,7},{6,4},{7,5},{8,10},{9,11},{10,... | collective-permute-start | bytes 307208 | tf_op jit(solution)/shard_map/ppermute | solution.py:526
  20.7 0.0 collective-permute-start.6
  20.7 1.2 %near_tiles.1 = (bf16[192,128]{1,0:T(8,128)(2,1)S(1)}, bf16[208,128]{1,0:T(8,128)(2,1)S(1)}, bf16[400,128]{1,0:T(8,128)(2,1)S(1)}) custom-call(f32[1,128]{1,0:T(1,128)S(1)} %get-tuple-element.21.fracs_ref, s32[4,128]{1,0:T(4,128)S(1)} %get-tuple-element.22.tiles_ref, bf16[4,16,128]{2,1,0:T(8,128)(2,1)S(1)} %get-tuple-element.24.head_ref, ...), custom_call_target="tpu_custom_call" | custom-call | tf_op jit(solution)/shard_map/near_tiles/pallas_call | solution.py:633
  21.9 0.7 %collective-permute-start.9 = (bf16[208,128]{1,0:T(8,128)(2,1)S(1)}, bf16[208,128]{1,0:T(8,128)(2,1)S(1)}, u32[]{:S(2)}, u32[]{:S(2)}) collective-permute-start(bf16[208,128]{1,0:T(8,128)(2,1)S(1)} %get-tuple-element.35), channel_id=1, source_target_pairs={{0,1},{1,0},{2,3},{3,2},{4,5},{5,4},{6,7},{7,6},{8,9},{9,8},{10,11... | collective-permute-start | bytes 159752 | tf_op jit(solution)/shard_map/ppermute | solution.py:526
  22.6 0.1 collective-permute-start.8
  22.7 1.2 %collective-permute-done.8.refs_1_ = bf16[192,128]{1,0:T(8,128)(2,1)S(1)} collective-permute-done((bf16[192,128]{1,0:T(8,128)(2,1)S(1)}, bf16[192,128]{1,0:T(8,128)(2,1)S(1)}, u32[]{:S(2)}, u32[]{:S(2)}) %collective-permute-start.8) | collective-permute-done | bytes 49184 | tf_op jit(solution)/shard_map/ppermute | solution.py:526
  23.8 0.0 collective-permute-done.9.refs_2_
  23.8 0.2 collective-permute-done.7.refs_0_
  24.0 0.3 %forcing.1.forcing_ref = f32[1024,128]{1,0:T(8,128)S(1)} custom-call(bf16[400,128]{1,0:T(8,128)(2,1)S(1)} %collective-permute-done.7.refs_0_, bf16[192,128]{1,0:T(8,128)(2,1)S(1)} %collective-permute-done.8.refs_1_, bf16[208,128]{1,0:T(8,128)(2,1)S(1)} %collective-permute-done.9.refs_2_, bf16[400,128]{1,0:T(8,128)(2,1)S(1)} %get-tuple-element.36.refs_3_, ...), custom_call_target="tpu_custom_call" | custom-call | tf_op jit(solution)/shard_map/forcing/pallas_call | solution.py:643
  24.3 1.5 %collective-permute-done.6.share_ref = bf16[400,128]{1,0:T(8,128)(2,1)S(1)} collective-permute-done((bf16[400,128]{1,0:T(8,128)(2,1)S(1)}, bf16[400,128]{1,0:T(8,128)(2,1)S(1)}, u32[]{:S(2)}, u32[]{:S(2)}) %collective-permute-start.6) | collective-permute-done | bytes 102432 | tf_op jit(solution)/shard_map/ppermute | solution.py:526
  25.8 0.0 copy-done
  25.8 1.5 %window_steps.1 = (bf16[32,32,128]{2,1,0:T(8,128)(2,1)}, f32[2,4096]{1,0:T(2,128)}) custom-call(bf16[400,128]{1,0:T(8,128)(2,1)S(1)} %collective-permute-done.6.share_ref, f32[1024,128]{1,0:T(8,128)S(1)} %forcing.1.forcing_ref, f32[160,128]{1,0:T(8,128)S(1)} %get-tuple-element.37.refs_4_.ready_ref, bf16[128,384]{1,0:T(8,128)(2,1)S(1)} %copy-done), custom_call_target="tpu_custom_call" | custom-call | tf_op jit(solution)/shard_map/window_steps/pallas_call | solution.py:654
Async XLA Ops:
  0.6 7.7 %collective-permute-start.2 = (s32[2,4]{1,0:T(2,128)}, s32[2,4]{1,0:T(2,128)S(1)}, u32[]{:S(2)}, u32[]{:S(2)}) collective-permute-start(s32[2,4]{1,0:T(2,128)} %bitcast.15), channel_id=1, source_target_pairs={{0,8},{4,12},{8,0},{12,4},{1,9},{5,13},{9,1},{13,5},{2,10},{6,14},... | collective-permute-start | bytes 104 | tf_op jit(solution)/shard_map/ppermute | solution.py:526
  4.7 5.6 %collective-permute-start.1 = (s32[2,4]{1,0:T(2,128)}, s32[2,4]{1,0:T(2,128)S(1)}, u32[]{:S(2)}, u32[]{:S(2)}) collective-permute-start(s32[2,4]{1,0:T(2,128)} %bitcast.16), channel_id=1, source_target_pairs={{0,12},{4,8},{8,4},{12,0},{1,13},{5,9},{9,5},{13,1},{2,14},{6,10},... | collective-permute-start | bytes 104 | tf_op jit(solution)/shard_map/ppermute | solution.py:526
  6.1 4.2 %collective-permute-start = (s32[2,4]{1,0:T(2,128)}, s32[2,4]{1,0:T(2,128)S(1)}, u32[]{:S(2)}, u32[]{:S(2)}) collective-permute-start(s32[2,4]{1,0:T(2,128)} %bitcast.17), channel_id=1, source_target_pairs={{0,4},{4,0},{8,12},{12,8},{1,5},{5,1},{9,13},{13,9},{2,6},{6,2},{1... | collective-permute-start | bytes 104 | tf_op jit(solution)/shard_map/ppermute | solution.py:526
  10.9 6.4 %collective-permute-start.3 = (bf16[2,32,128]{2,1,0:T(8,128)(2,1)S(1)}, bf16[2,32,128]{2,1,0:T(8,128)(2,1)S(1)}, u32[]{:S(2)}, u32[]{:S(2)}) collective-permute-start(bf16[2,32,128]{2,1,0:T(8,128)(2,1)S(1)} %get-tuple-element.27), channel_id=1, source_target_pairs={{0,12},{4,8},{8,4},{12,0},{1,13},{5,9},{9,5},{13,1},{2,14},{6,10},... | collective-permute-start | bytes 49160 | tf_op jit(solution)/shard_map/ppermute | solution.py:526
  13.0 4.6 %collective-permute-start.4 = (bf16[2,32,128]{2,1,0:T(8,128)(2,1)S(1)}, bf16[2,32,128]{2,1,0:T(8,128)(2,1)S(1)}, u32[]{:S(2)}, u32[]{:S(2)}) collective-permute-start(bf16[2,32,128]{2,1,0:T(8,128)(2,1)S(1)} %get-tuple-element.28), channel_id=1, source_target_pairs={{0,8},{4,12},{8,0},{12,4},{1,9},{5,13},{9,1},{13,5},{2,10},{6,14},... | collective-permute-start | bytes 49160 | tf_op jit(solution)/shard_map/ppermute | solution.py:526
  13.0 4.6 %collective-permute-start.5 = (bf16[2,32,128]{2,1,0:T(8,128)(2,1)S(1)}, bf16[2,32,128]{2,1,0:T(8,128)(2,1)S(1)}, u32[]{:S(2)}, u32[]{:S(2)}) collective-permute-start(bf16[2,32,128]{2,1,0:T(8,128)(2,1)S(1)} %get-tuple-element.29), channel_id=1, source_target_pairs={{0,4},{4,0},{8,12},{12,8},{1,5},{5,1},{9,13},{13,9},{2,6},{6,2},{1... | collective-permute-start | bytes 49160 | tf_op jit(solution)/shard_map/ppermute | solution.py:526
  19.1 6.7 %copy-start = (bf16[128,384]{1,0:T(8,128)(2,1)S(1)}, bf16[128,384]{1,0:T(8,128)(2,1)}, u32[]{:S(2)}) copy-start(bf16[128,384]{1,0:T(8,128)(2,1)} %constant.8.clone.fit_ref) | copy-start | bytes 294916
  19.1 4.9 %collective-permute-start.7 = (bf16[400,128]{1,0:T(8,128)(2,1)S(1)}, bf16[400,128]{1,0:T(8,128)(2,1)S(1)}, u32[]{:S(2)}, u32[]{:S(2)}) collective-permute-start(bf16[400,128]{1,0:T(8,128)(2,1)S(1)} %get-tuple-element.31), channel_id=1, source_target_pairs={{0,2},{1,3},{2,0},{3,1},{4,6},{5,7},{6,4},{7,5},{8,10},{9,11},{10,... | collective-permute-start | bytes 307208 | tf_op jit(solution)/shard_map/ppermute | solution.py:526
  20.7 5.2 %collective-permute-start.6 = (bf16[400,128]{1,0:T(8,128)(2,1)S(1)}, bf16[400,128]{1,0:T(8,128)(2,1)S(1)}, u32[]{:S(2)}, u32[]{:S(2)}) collective-permute-start(bf16[400,128]{1,0:T(8,128)(2,1)S(1)} %get-tuple-element.30), channel_id=1, source_target_pairs={{0,3},{1,2},{2,1},{3,0},{4,7},{5,6},{6,5},{7,4},{8,11},{9,10},{10,... | collective-permute-start | bytes 307208 | tf_op jit(solution)/shard_map/ppermute | solution.py:526
  21.9 1.9 %collective-permute-start.9 = (bf16[208,128]{1,0:T(8,128)(2,1)S(1)}, bf16[208,128]{1,0:T(8,128)(2,1)S(1)}, u32[]{:S(2)}, u32[]{:S(2)}) collective-permute-start(bf16[208,128]{1,0:T(8,128)(2,1)S(1)} %get-tuple-element.35), channel_id=1, source_target_pairs={{0,1},{1,0},{2,3},{3,2},{4,5},{5,4},{6,7},{7,6},{8,9},{9,8},{10,11... | collective-permute-start | bytes 159752 | tf_op jit(solution)/shard_map/ppermute | solution.py:526
  22.6 1.2 %collective-permute-start.8 = (bf16[192,128]{1,0:T(8,128)(2,1)S(1)}, bf16[192,128]{1,0:T(8,128)(2,1)S(1)}, u32[]{:S(2)}, u32[]{:S(2)}) collective-permute-start(bf16[192,128]{1,0:T(8,128)(2,1)S(1)} %get-tuple-element.34), channel_id=1, source_target_pairs={{0,1},{1,0},{2,3},{3,2},{4,5},{5,4},{6,7},{7,6},{8,9},{9,8},{10,11... | collective-permute-start | bytes 147464 | tf_op jit(solution)/shard_map/ppermute | solution.py:526

commit v13 on v12

--- a/solution.py
+++ b/solution.py
@@ -16,7 +16,7 @@
 LENGTH = SEGS * STEPS
 GROUP = 4
 HEAD = 16
-PITCH = STEPS + 1
+PITCH = STEPS // 2 + 1
 CHUNKS = 8
 UNROLL = 4
 
@@ -54,12 +54,18 @@
 def fit_table(coef_count):
     scales = np.where(np.arange(coef_count)[:, None] == 0, 1.0, 2.0) / STEPS
     fit = (basis_table(coef_count, STEPS) * scales).astype(np.float32)
-    whole = np.zeros((GROUP * coef_count, GROUP * STEPS), np.float32)
-    for g in range(GROUP):
-        whole[g * coef_count : (g + 1) * coef_count, g * STEPS : (g + 1) * STEPS] = fit
-    high = whole.astype(ml_dtypes.bfloat16)
-    low = (whole - high.astype(np.float32)).astype(ml_dtypes.bfloat16)
-    return np.concatenate([high, high, low], axis=1)
+    half = STEPS // 2
+    tables = []
+    for i in range(2):
+        whole = np.zeros((GROUP * coef_count, GROUP * half), np.float32)
+        for g in range(GROUP):
+            whole[g * coef_count : (g + 1) * coef_count, g * half : (g + 1) * half] = fit[
+                :, i * half : (i + 1) * half
+            ]
+        high = whole.astype(ml_dtypes.bfloat16)
+        low = (whole - high.astype(np.float32)).astype(ml_dtypes.bfloat16)
+        tables.append(np.concatenate([high, high, low], axis=1))
+    return np.stack(tables)
 
 
 TOGETHER = 8
@@ -222,8 +228,8 @@
         copy.wait()
 
 
-def pick_kernel(*refs, capacity, peers, ways):
-    tables = refs[: peers - 1]
+def pick_kernel(*refs, capacity, peers):
+    tables = refs[: peers - 1][::-1]
     fresh = refs[peers - 1]
     outs = refs[peers : 2 * peers - 1]
     asked, sems = refs[2 * peers - 1 :]
@@ -231,10 +237,17 @@
     copies = [pltpu.make_async_copy(tables[r], asked.at[r], sems.at[r]) for r in range(peers - 1)]
     for copy in copies:
         copy.start()
-    for i, r in enumerate(ways):
-        copies[i].wait()
+
+    def ring_place(i):
+        return jnp.where(i % 2 == 1, (i + 1) // 2, (peers - i // 2) % peers)
+
+    for copy in copies:
+        copy.wait()
+    for distance in range(1, peers):
+        way = (ring_place(place) - ring_place(place ^ distance) + peers) % peers
         for c in range(capacity):
-            outs[r - 1][c] = fresh[jnp.maximum(asked[i, c, place], 0)]
+            block = jnp.maximum(asked[way - 1, c, place], 0)
+            outs[distance - 1][c] = fresh[block]
 
 
 def add_tiles(tiles, frac, hist, weights, total, pitch, items):
@@ -411,9 +424,10 @@
 
 def window_kernel(
     share_ref, forcing_ref, ready_ref, fit_ref, coefs_hbm, state_hbm,
-    samples, rates, coefs, state, sems,
+    early, late, rates, coefs, state, sems,
     *, own_blocks, peer_targets, coef_count,
 ):
+    samples = (early, late)
     block_rows = ready_ref.shape[1]
     width = TOGETHER * peer_targets
     scatter = one_hot(
@@ -426,6 +440,34 @@
     a = excite_excite / 2
     gain = 0.5 * gain
     carried = a * excite
+
+    def fit_half(values, fit):
+        products = []
+        for g in range(0, own_blocks // GROUP, 2):
+            part = jnp.concatenate(
+                [
+                    jnp.concatenate(
+                        [
+                            values[b * PITCH : b * PITCH + STEPS // 2, :]
+                            for b in range((g + i) * GROUP, (g + i + 1) * GROUP)
+                        ],
+                        axis=0,
+                    )
+                    for i in range(2)
+                ],
+                axis=1,
+            )
+            high = part.astype(jnp.bfloat16)
+            low = (part - high.astype(jnp.float32)).astype(jnp.bfloat16)
+            products.append(
+                jnp.dot(
+                    fit, jnp.concatenate([high, low, high], axis=0),
+                    preferred_element_type=jnp.float32,
+                )
+            )
+        return products
+
+    fitted = [None, None]
     for pair in range(0, STEPS // TOGETHER, 2):
         inflow = jnp.dot(
             scatter, two_groups([(share_ref,)], pair, width), preferred_element_type=jnp.float32
@@ -447,7 +489,8 @@
             inhibit = ((1 - inhibit_rate) * inhibit + inhibit_rate / 2) + (
                 inhibit_rate / 2
             ) * inhibit_turn
-            samples[pl.ds(j, own_blocks, stride=PITCH), :] = carried * (1 / a)
+            samples[pair // 2][pl.ds(jj, own_blocks, stride=PITCH), :] = carried * (1 / a)
+        fitted[pair // 2] = fit_half(samples[pair // 2], fit_ref[pair // 2])
     rates[0] = carried * (1 / a)
     rates[1] = inhibit
     for b in range(own_blocks):
@@ -457,29 +500,10 @@
     copies = [pltpu.make_async_copy(state, state_hbm, sems.at[0])]
     copies[0].start()
 
-    fit = fit_ref[...]
     for g in range(0, own_blocks // GROUP, 2):
-        part = jnp.concatenate(
-            [
-                jnp.concatenate(
-                    [
-                        samples[b * PITCH : b * PITCH + STEPS, :]
-                        for b in range((g + i) * GROUP, (g + i + 1) * GROUP)
-                    ],
-                    axis=0,
-                )
-                for i in range(2)
-            ],
-            axis=1,
-        )
-        part_high = part.astype(jnp.bfloat16)
-        part_low = (part - part_high.astype(jnp.float32)).astype(jnp.bfloat16)
-        fitted = jnp.dot(
-            fit, jnp.concatenate([part_high, part_low, part_high], axis=0),
-            preferred_element_type=jnp.float32,
-        ).astype(jnp.bfloat16)
+        both = (fitted[0][g // 2] + fitted[1][g // 2]).astype(jnp.bfloat16)
         for i in range(2):
-            coefs[(g + i) * GROUP : (g + i + 1) * GROUP] = fitted[
+            coefs[(g + i) * GROUP : (g + i + 1) * GROUP] = both[
                 :, i * block_rows : (i + 1) * block_rows
             ].reshape(GROUP, coef_count, block_rows)
         where = pl.ds(g * GROUP, 2 * GROUP)
@@ -526,8 +550,13 @@
         return lax.ppermute(x, axis, [(i, i ^ r) for i in range(lax.axis_size(axis))])
 
     reads = read_blocks.reshape(wide_peers, capacity).T
-    ways = [1, *range(wide_peers - 1, 1, -1)]
-    asked = [swap(reads, "wide", r) for r in ways]
+    ring = [0, *range(1, wide_peers, 2), *reversed(range(2, wide_peers, 2))]
+    asked = [
+        lax.ppermute(
+            reads, "wide", [(ring[k], ring[(k + r) % wide_peers]) for k in range(wide_peers)]
+        )
+        for r in range(1, wide_peers)
+    ]
 
     vmem_inputs = [
         VMEM(state.shape, jnp.float32),
@@ -592,7 +621,7 @@
     )
 
     picked = pl.pallas_call(
-        functools.partial(pick_kernel, capacity=capacity, peers=wide_peers, ways=ways),
+        functools.partial(pick_kernel, capacity=capacity, peers=wide_peers),
         out_shape=[pltpu.VMEM((capacity, coef_count, block_rows), jnp.bfloat16)]
         * (wide_peers - 1),
         in_specs=[vmem_spec] * wide_peers,
@@ -603,7 +632,7 @@
         ],
         compiler_params=params(),
         name="pick_blocks",
-    )(*asked, fresh)
+    )(*asked[::-1], fresh)
     news = [swap(picked[r - 1], "wide", r) for r in range(wide_peers - 1, 0, -1)]
 
     fixed = tile_count * (peers - 2) // peers + 2 * UNROLL
@@ -664,6 +693,7 @@
         out_specs=[hbm_spec] * 2,
         scratch_shapes=[
             VMEM((own_blocks * PITCH, block_rows), jnp.float32),
+            VMEM((own_blocks * PITCH, block_rows), jnp.float32),
             VMEM((2, own_blocks, block_rows), jnp.float32),
             VMEM(fresh_coefs.shape, jnp.bfloat16),
             VMEM(state.shape, jnp.float32),

time: 27.5 us -> 27 us (0.982)
  waiting for transfers between devices: 5.15 us -> 3.18 us
  starting transfers between devices: 12.5 us -> 13.9 us
    ppermute x0 -> x3, starting transfers between devices: none -> 7.13 us  [local(): lax.ppermute(reads, 'wide', [(ring[k], ring[(k + r) % wide_peers]) for k...]
    ppermute x10 -> x7, starting transfers between devices: 12.5 us -> 6.8 us  [swap(): lax.ppermute(x, axis, [(i, i ^ r) for i in range(lax.axis_size(axis))])]
    ppermute x10 -> x7, waiting for transfers between devices: 5.15 us -> 2.98 us  [swap(): lax.ppermute(x, axis, [(i, i ^ r) for i in range(lax.axis_size(axis))])]
where the time goes in v13:
time: 27 us; the launch traced here: 26.9 us
  starting transfers between devices  13.9 us (51%)
  Pallas kernels  9.04 us (33%)
  waiting for transfers between devices  3.18 us (12%)
  between operations  0.72 us (3%)
    ppermute x3, starting transfers between devices, local(): lax.ppermute(reads, 'wide', [(ring[k], ring[(k + r) % wide_peers]) for k...  7.13 us
    ppermute x7, starting transfers between devices, swap(): lax.ppermute(x, axis, [(i, i ^ r) for i in range(lax.axis_size(axis))])  6.8 us
    ppermute x7, waiting for transfers between devices, swap(): lax.ppermute(x, axis, [(i, i ^ r) for i in range(lax.axis_size(axis))])  2.98 us
    pallas_call x1, Pallas kernels, local(): pl.pallas_call(near_kernel, out_shape=[pltpu.VMEM(fresh_coefs.shape, jnp....  1.98 us
    pallas_call x1, Pallas kernels, local(): pl.pallas_call(functools.partial(prepare_kernel, peers=peers, own_blocks=...  1.94 us
    pallas_call x1, Pallas kernels, local(): pl.pallas_call(functools.partial(window_kernel, own_blocks=own_blocks, pe...  1.52 us
    pallas_call x1, Pallas kernels, local(): pl.pallas_call(functools.partial(far_kernel, wide_peers=wide_peers, peers...  1.4 us
    pallas_call x1, Pallas kernels, local(): pl.pallas_call(functools.partial(near_tiles_kernel, peers=peers, peer_tar...  1.22 us
  transfers between devices with their start and end apart: 10, of which 5 were waited for; matrix products, arithmetic and copies ran while one was open for 0% of the time, Pallas kernels for 20%

profile of v13, /device:TPU:0, one launch (start us, length us, event | category | flops | bytes accessed | tf_op | source)
XLA Modules:
  0.0 26.9 jit_solution(8533612913235278973)
XLA Ops:
  0.6 3.1 %collective-permute-start.2 = (s32[2,4]{1,0:T(2,128)}, s32[2,4]{1,0:T(2,128)S(1)}, u32[]{:S(2)}, u32[]{:S(2)}) collective-permute-start(s32[2,4]{1,0:T(2,128)} %bitcast.15), channel_id=1, source_target_pairs={{0,4},{4,12},{12,8},{8,0},{1,5},{5,13},{13,9},{9,1},{2,6},{6,14},{... | collective-permute-start | bytes 104 | tf_op jit(solution)/shard_map/ppermute | solution.py:555
  3.7 2.5 %collective-permute-start.1 = (s32[2,4]{1,0:T(2,128)}, s32[2,4]{1,0:T(2,128)S(1)}, u32[]{:S(2)}, u32[]{:S(2)}) collective-permute-start(s32[2,4]{1,0:T(2,128)} %bitcast.16), channel_id=1, source_target_pairs={{0,12},{4,8},{12,0},{8,4},{1,13},{5,9},{13,1},{9,5},{2,14},{6,10},... | collective-permute-start | bytes 104 | tf_op jit(solution)/shard_map/ppermute | solution.py:555
  6.2 1.6 %collective-permute-start = (s32[2,4]{1,0:T(2,128)}, s32[2,4]{1,0:T(2,128)S(1)}, u32[]{:S(2)}, u32[]{:S(2)}) collective-permute-start(s32[2,4]{1,0:T(2,128)} %bitcast.17), channel_id=1, source_target_pairs={{0,8},{4,0},{12,4},{8,12},{1,9},{5,1},{13,5},{9,13},{2,10},{6,2},{... | collective-permute-start | bytes 104 | tf_op jit(solution)/shard_map/ppermute | solution.py:555
  7.8 2.0 %near.1 = (bf16[32,32,128]{2,1,0:T(8,128)(2,1)S(1)}, bf16[96,128,128]{2,1,0:T(8,128)(2,1)S(1)}) custom-call(bf16[32,32,128]{2,1,0:T(8,128)(2,1)} %fresh_hbm.1, bf16[96,128,128]{2,1,0:T(8,128)(2,1)} %bitcast.12), custom_call_target="tpu_custom_call" | custom-call | tf_op jit(solution)/shard_map/near/pallas_call | solution.py:573
  9.7 0.0 collective-permute-done.2.refs_2_
  9.8 0.0 collective-permute-done.1.refs_1_
  9.8 0.2 collective-permute-done.refs_0_
  10.0 0.7 %pick_blocks.1 = (bf16[2,32,128]{2,1,0:T(8,128)(2,1)S(1)}, bf16[2,32,128]{2,1,0:T(8,128)(2,1)S(1)}, bf16[2,32,128]{2,1,0:T(8,128)(2,1)S(1)}) custom-call(s32[2,4]{1,0:T(2,128)S(1)} %collective-permute-done.refs_0_, s32[2,4]{1,0:T(2,128)S(1)} %collective-permute-done.1.refs_1_, s32[2,4]{1,0:T(2,128)S(1)} %collective-permute-done.2.refs_2_, ...), custom_call_target="tpu_custom_call" | custom-call | tf_op jit(solution)/shard_map/pick_blocks/pallas_call | solution.py:623
  10.7 1.9 %collective-permute-start.3 = (bf16[2,32,128]{2,1,0:T(8,128)(2,1)S(1)}, bf16[2,32,128]{2,1,0:T(8,128)(2,1)S(1)}, u32[]{:S(2)}, u32[]{:S(2)}) collective-permute-start(bf16[2,32,128]{2,1,0:T(8,128)(2,1)S(1)} %get-tuple-element.27), channel_id=1, source_target_pairs={{0,12},{4,8},{8,4},{12,0},{1,13},{5,9},{9,5},{13,1},{2,14},{6,10},... | collective-permute-start | bytes 49160 | tf_op jit(solution)/shard_map/ppermute | solution.py:550
  12.5 0.8 %collective-permute-start.4 = (bf16[2,32,128]{2,1,0:T(8,128)(2,1)S(1)}, bf16[2,32,128]{2,1,0:T(8,128)(2,1)S(1)}, u32[]{:S(2)}, u32[]{:S(2)}) collective-permute-start(bf16[2,32,128]{2,1,0:T(8,128)(2,1)S(1)} %get-tuple-element.28), channel_id=1, source_target_pairs={{0,8},{4,12},{8,0},{12,4},{1,9},{5,13},{9,1},{13,5},{2,10},{6,14},... | collective-permute-start | bytes 49160 | tf_op jit(solution)/shard_map/ppermute | solution.py:550
  13.3 1.8 %collective-permute-start.5 = (bf16[2,32,128]{2,1,0:T(8,128)(2,1)S(1)}, bf16[2,32,128]{2,1,0:T(8,128)(2,1)S(1)}, u32[]{:S(2)}, u32[]{:S(2)}) collective-permute-start(bf16[2,32,128]{2,1,0:T(8,128)(2,1)S(1)} %get-tuple-element.29), channel_id=1, source_target_pairs={{0,4},{4,0},{8,12},{12,8},{1,5},{5,1},{9,13},{13,9},{2,6},{6,2},{1... | collective-permute-start | bytes 49160 | tf_op jit(solution)/shard_map/ppermute | solution.py:550
  15.1 1.9 %prepare.1 = (f32[160,128]{1,0:T(8,128)S(1)}, f32[768,128]{1,0:T(8,128)S(1)}, s32[4,128]{1,0:T(4,128)S(1)}, f32[1,128]{1,0:T(1,128)S(1)}, bf16[4,16,128]{2,1,0:T(8,128)(2,1)S(1)}, /*index=5*/bf16[96,96]{1,0:T(8,128)(2,1)S(1)}) custom-call(bf16[32,32,128]{2,1,0:T(8,128)(2,1)S(1)} %get-tuple-element.20.fresh_ref.refs_3_, s32[2,4]{1,0:T(2,128)} %bitcast.18, ...), custom_call_target="tpu_custom_call" | custom-call | tf_op jit(solution)/shard_map/prepare/pallas_call | solution.py:585
  17.1 0.0 collective-permute-done.3.refs_0_
  17.1 0.1 collective-permute-done.4.refs_1_
  17.2 0.0 collective-permute-done.5.refs_2_
  17.2 1.4 %far_tiles.1 = (bf16[400,128]{1,0:T(8,128)(2,1)S(1)}, bf16[400,128]{1,0:T(8,128)(2,1)S(1)}, f32[768,128]{1,0:T(8,128)S(1)}, f32[1568,128]{1,0:T(8,128)S(1)}) custom-call(f32[1,128]{1,0:T(1,128)S(1)} %get-tuple-element.21.fracs_ref, s32[4,128]{1,0:T(4,128)S(1)} %get-tuple-element.22.tiles_ref, bf16[96,96]{1,0:T(8,128)(2,1)S(1)} %get-tuple-element.23.table_ref, ...), custom_call_target="tpu_custom_call" | custom-call | tf_op jit(solution)/shard_map/far_tiles/pallas_call | solution.py:643
  18.6 0.0 copy-start
  18.6 1.6 %collective-permute-start.7 = (bf16[400,128]{1,0:T(8,128)(2,1)S(1)}, bf16[400,128]{1,0:T(8,128)(2,1)S(1)}, u32[]{:S(2)}, u32[]{:S(2)}) collective-permute-start(bf16[400,128]{1,0:T(8,128)(2,1)S(1)} %get-tuple-element.31), channel_id=1, source_target_pairs={{0,2},{1,3},{2,0},{3,1},{4,6},{5,7},{6,4},{7,5},{8,10},{9,11},{10,... | collective-permute-start | bytes 307208 | tf_op jit(solution)/shard_map/ppermute | solution.py:550
  20.2 0.0 collective-permute-start.6
  20.2 1.2 %near_tiles.1 = (bf16[192,128]{1,0:T(8,128)(2,1)S(1)}, bf16[208,128]{1,0:T(8,128)(2,1)S(1)}, bf16[400,128]{1,0:T(8,128)(2,1)S(1)}) custom-call(f32[1,128]{1,0:T(1,128)S(1)} %get-tuple-element.21.fracs_ref, s32[4,128]{1,0:T(4,128)S(1)} %get-tuple-element.22.tiles_ref, bf16[4,16,128]{2,1,0:T(8,128)(2,1)S(1)} %get-tuple-element.24.head_ref, ...), custom_call_target="tpu_custom_call" | custom-call | tf_op jit(solution)/shard_map/near_tiles/pallas_call | solution.py:662
  21.4 0.7 %collective-permute-start.9 = (bf16[208,128]{1,0:T(8,128)(2,1)S(1)}, bf16[208,128]{1,0:T(8,128)(2,1)S(1)}, u32[]{:S(2)}, u32[]{:S(2)}) collective-permute-start(bf16[208,128]{1,0:T(8,128)(2,1)S(1)} %get-tuple-element.35), channel_id=1, source_target_pairs={{0,1},{1,0},{2,3},{3,2},{4,5},{5,4},{6,7},{7,6},{8,9},{9,8},{10,11... | collective-permute-start | bytes 159752 | tf_op jit(solution)/shard_map/ppermute | solution.py:550
  22.1 0.1 collective-permute-start.8
  22.2 1.2 %collective-permute-done.8.refs_1_ = bf16[192,128]{1,0:T(8,128)(2,1)S(1)} collective-permute-done((bf16[192,128]{1,0:T(8,128)(2,1)S(1)}, bf16[192,128]{1,0:T(8,128)(2,1)S(1)}, u32[]{:S(2)}, u32[]{:S(2)}) %collective-permute-start.8) | collective-permute-done | bytes 49184 | tf_op jit(solution)/shard_map/ppermute | solution.py:550
  23.3 0.0 collective-permute-done.9.refs_2_
  23.3 0.2 collective-permute-done.7.refs_0_
  23.5 0.3 %forcing.1.forcing_ref = f32[1024,128]{1,0:T(8,128)S(1)} custom-call(bf16[400,128]{1,0:T(8,128)(2,1)S(1)} %collective-permute-done.7.refs_0_, bf16[192,128]{1,0:T(8,128)(2,1)S(1)} %collective-permute-done.8.refs_1_, bf16[208,128]{1,0:T(8,128)(2,1)S(1)} %collective-permute-done.9.refs_2_, bf16[400,128]{1,0:T(8,128)(2,1)S(1)} %get-tuple-element.36.refs_3_, ...), custom_call_target="tpu_custom_call" | custom-call | tf_op jit(solution)/shard_map/forcing/pallas_call | solution.py:672
  23.8 1.5 %collective-permute-done.6.share_ref = bf16[400,128]{1,0:T(8,128)(2,1)S(1)} collective-permute-done((bf16[400,128]{1,0:T(8,128)(2,1)S(1)}, bf16[400,128]{1,0:T(8,128)(2,1)S(1)}, u32[]{:S(2)}, u32[]{:S(2)}) %collective-permute-start.6) | collective-permute-done | bytes 102432 | tf_op jit(solution)/shard_map/ppermute | solution.py:550
  25.3 0.0 copy-done
  25.4 1.5 %window_steps.1 = (bf16[32,32,128]{2,1,0:T(8,128)(2,1)}, f32[2,4096]{1,0:T(2,128)}) custom-call(bf16[400,128]{1,0:T(8,128)(2,1)S(1)} %collective-permute-done.6.share_ref, f32[1024,128]{1,0:T(8,128)S(1)} %forcing.1.forcing_ref, f32[160,128]{1,0:T(8,128)S(1)} %get-tuple-element.37.refs_4_.ready_ref, bf16[2,128,192]{2,1,0:T(8,128)(2,1)S(1)} %copy-done), custom_call_target="tpu_custom_call" | custom-call | tf_op jit(solution)/shard_map/window_steps/pallas_call | solution.py:683
Async XLA Ops:
  0.6 9.1 %collective-permute-start.2 = (s32[2,4]{1,0:T(2,128)}, s32[2,4]{1,0:T(2,128)S(1)}, u32[]{:S(2)}, u32[]{:S(2)}) collective-permute-start(s32[2,4]{1,0:T(2,128)} %bitcast.15), channel_id=1, source_target_pairs={{0,4},{4,12},{12,8},{8,0},{1,5},{5,13},{13,9},{9,1},{2,6},{6,14},{... | collective-permute-start | bytes 104 | tf_op jit(solution)/shard_map/ppermute | solution.py:555
  3.7 6.1 %collective-permute-start.1 = (s32[2,4]{1,0:T(2,128)}, s32[2,4]{1,0:T(2,128)S(1)}, u32[]{:S(2)}, u32[]{:S(2)}) collective-permute-start(s32[2,4]{1,0:T(2,128)} %bitcast.16), channel_id=1, source_target_pairs={{0,12},{4,8},{12,0},{8,4},{1,13},{5,9},{13,1},{9,5},{2,14},{6,10},... | collective-permute-start | bytes 104 | tf_op jit(solution)/shard_map/ppermute | solution.py:555
  6.2 3.8 %collective-permute-start = (s32[2,4]{1,0:T(2,128)}, s32[2,4]{1,0:T(2,128)S(1)}, u32[]{:S(2)}, u32[]{:S(2)}) collective-permute-start(s32[2,4]{1,0:T(2,128)} %bitcast.17), channel_id=1, source_target_pairs={{0,8},{4,0},{12,4},{8,12},{1,9},{5,1},{13,5},{9,13},{2,10},{6,2},{... | collective-permute-start | bytes 104 | tf_op jit(solution)/shard_map/ppermute | solution.py:555
  10.7 6.4 %collective-permute-start.3 = (bf16[2,32,128]{2,1,0:T(8,128)(2,1)S(1)}, bf16[2,32,128]{2,1,0:T(8,128)(2,1)S(1)}, u32[]{:S(2)}, u32[]{:S(2)}) collective-permute-start(bf16[2,32,128]{2,1,0:T(8,128)(2,1)S(1)} %get-tuple-element.27), channel_id=1, source_target_pairs={{0,12},{4,8},{8,4},{12,0},{1,13},{5,9},{9,5},{13,1},{2,14},{6,10},... | collective-permute-start | bytes 49160 | tf_op jit(solution)/shard_map/ppermute | solution.py:550
  12.5 4.7 %collective-permute-start.4 = (bf16[2,32,128]{2,1,0:T(8,128)(2,1)S(1)}, bf16[2,32,128]{2,1,0:T(8,128)(2,1)S(1)}, u32[]{:S(2)}, u32[]{:S(2)}) collective-permute-start(bf16[2,32,128]{2,1,0:T(8,128)(2,1)S(1)} %get-tuple-element.28), channel_id=1, source_target_pairs={{0,8},{4,12},{8,0},{12,4},{1,9},{5,13},{9,1},{13,5},{2,10},{6,14},... | collective-permute-start | bytes 49160 | tf_op jit(solution)/shard_map/ppermute | solution.py:550
  13.3 3.9 %collective-permute-start.5 = (bf16[2,32,128]{2,1,0:T(8,128)(2,1)S(1)}, bf16[2,32,128]{2,1,0:T(8,128)(2,1)S(1)}, u32[]{:S(2)}, u32[]{:S(2)}) collective-permute-start(bf16[2,32,128]{2,1,0:T(8,128)(2,1)S(1)} %get-tuple-element.29), channel_id=1, source_target_pairs={{0,4},{4,0},{8,12},{12,8},{1,5},{5,1},{9,13},{13,9},{2,6},{6,2},{1... | collective-permute-start | bytes 49160 | tf_op jit(solution)/shard_map/ppermute | solution.py:550
  18.6 6.8 %copy-start = (bf16[2,128,192]{2,1,0:T(8,128)(2,1)S(1)}, bf16[2,128,192]{2,1,0:T(8,128)(2,1)}, u32[]{:S(2)}) copy-start(bf16[2,128,192]{2,1,0:T(8,128)(2,1)} %constant.8.clone.fit_ref) | copy-start | bytes 294916
  18.6 4.9 %collective-permute-start.7 = (bf16[400,128]{1,0:T(8,128)(2,1)S(1)}, bf16[400,128]{1,0:T(8,128)(2,1)S(1)}, u32[]{:S(2)}, u32[]{:S(2)}) collective-permute-start(bf16[400,128]{1,0:T(8,128)(2,1)S(1)} %get-tuple-element.31), channel_id=1, source_target_pairs={{0,2},{1,3},{2,0},{3,1},{4,6},{5,7},{6,4},{7,5},{8,10},{9,11},{10,... | collective-permute-start | bytes 307208 | tf_op jit(solution)/shard_map/ppermute | solution.py:550
  20.2 5.2 %collective-permute-start.6 = (bf16[400,128]{1,0:T(8,128)(2,1)S(1)}, bf16[400,128]{1,0:T(8,128)(2,1)S(1)}, u32[]{:S(2)}, u32[]{:S(2)}) collective-permute-start(bf16[400,128]{1,0:T(8,128)(2,1)S(1)} %get-tuple-element.30), channel_id=1, source_target_pairs={{0,3},{1,2},{2,1},{3,0},{4,7},{5,6},{6,5},{7,4},{8,11},{9,10},{10,... | collective-permute-start | bytes 307208 | tf_op jit(solution)/shard_map/ppermute | solution.py:550
  21.4 1.9 %collective-permute-start.9 = (bf16[208,128]{1,0:T(8,128)(2,1)S(1)}, bf16[208,128]{1,0:T(8,128)(2,1)S(1)}, u32[]{:S(2)}, u32[]{:S(2)}) collective-permute-start(bf16[208,128]{1,0:T(8,128)(2,1)S(1)} %get-tuple-element.35), channel_id=1, source_target_pairs={{0,1},{1,0},{2,3},{3,2},{4,5},{5,4},{6,7},{7,6},{8,9},{9,8},{10,11... | collective-permute-start | bytes 159752 | tf_op jit(solution)/shard_map/ppermute | solution.py:550
  22.1 1.2 %collective-permute-start.8 = (bf16[192,128]{1,0:T(8,128)(2,1)S(1)}, bf16[192,128]{1,0:T(8,128)(2,1)S(1)}, u32[]{:S(2)}, u32[]{:S(2)}) collective-permute-start(bf16[192,128]{1,0:T(8,128)(2,1)S(1)} %get-tuple-element.34), channel_id=1, source_target_pairs={{0,1},{1,0},{2,3},{3,2},{4,5},{5,4},{6,7},{7,6},{8,9},{9,8},{10,11... | collective-permute-start | bytes 147464 | tf_op jit(solution)/shard_map/ppermute | solution.py:550

commit v14 on v13

--- a/solution.py
+++ b/solution.py
@@ -228,26 +228,60 @@
         copy.wait()
 
 
-def pick_kernel(*refs, capacity, peers):
-    tables = refs[: peers - 1][::-1]
-    fresh = refs[peers - 1]
-    outs = refs[peers : 2 * peers - 1]
-    asked, sems = refs[2 * peers - 1 :]
+def wide_plans(count):
+    if count == 4:
+        requests = [
+            [(2, 1), (3, 0)],
+            [(0, 1), (2, 0)],
+            [(0, 2), (1, 0), (2, 3), (3, 1)],
+            [(0, 3), (1, 2)],
+            [(1, 3), (3, 2)],
+        ]
+        blocks = [
+            [(2, 0)],
+            [(1, 0), (3, 1)],
+            [(0, 3), (1, 2), (2, 1), (3, 0)],
+            [(0, 1), (1, 3), (3, 2)],
+            [(0, 2), (2, 3)],
+        ]
+        return requests, blocks
+    whole = [[(i, i ^ r) for i in range(count)] for r in range(1, count)]
+    return whole, whole
+
+
+def ways(plan, pairs):
+    return [next((k for k, part in enumerate(plan) if pair in part), None) for pair in pairs]
+
+
+def by_place(place, values):
+    known = [v for v in values if v is not None]
+    result = known[0]
+    for i, value in enumerate(values):
+        if value is not None and value != known[0]:
+            result = jnp.where(place == i, value, result)
+    return result
+
+
+def pick_kernel(*refs, capacity, requests, blocks):
+    tables = refs[: len(requests)][::-1]
+    fresh = refs[len(requests)]
+    outs = refs[len(requests) + 1 : len(requests) + 1 + len(blocks)]
+    asked, sems = refs[len(requests) + 1 + len(blocks) :]
     place = lax.axis_index("wide")
-    copies = [pltpu.make_async_copy(tables[r], asked.at[r], sems.at[r]) for r in range(peers - 1)]
+    count = lax.axis_size("wide")
+    copies = [
+        pltpu.make_async_copy(table, asked.at[k], sems.at[k]) for k, table in enumerate(tables)
+    ]
     for copy in copies:
         copy.start()
-
-    def ring_place(i):
-        return jnp.where(i % 2 == 1, (i + 1) // 2, (peers - i // 2) % peers)
-
     for copy in copies:
         copy.wait()
-    for distance in range(1, peers):
-        way = (ring_place(place) - ring_place(place ^ distance) + peers) % peers
+    for out, part in zip(outs, blocks):
+        target = dict(part)
+        way = by_place(place, ways(requests, [(target.get(i), i) for i in range(count)]))
         for c in range(capacity):
-            block = jnp.maximum(asked[way - 1, c, place], 0)
-            outs[distance - 1][c] = fresh[block]
+            block = jnp.clip(asked[way, c, place], 0, fresh.shape[0] - 1)
+            out[c] = fresh[block]
 
 
 def add_tiles(tiles, frac, hist, weights, total, pitch, items):
@@ -294,11 +328,11 @@
 
 def far_kernel(
     fracs_ref, tiles_ref, table_ref, head_ref, weights, hist_ref, *refs,
-    wide_peers, peers, capacity, peer_targets, fixed,
+    blocks, wide_peers, peers, capacity, peer_targets, fixed,
 ):
-    news = refs[: wide_peers - 1]
-    outs = refs[wide_peers - 1 : wide_peers + peers - 3]
-    hist, total, tiles, frac, sems = refs[wide_peers + peers - 3 :]
+    news = refs[: len(blocks)]
+    outs = refs[len(blocks) : len(blocks) + peers - 2]
+    hist, total, tiles, frac, sems = refs[len(blocks) + peers - 2 :]
     place = lax.axis_index("narrow")
     owner = lax.axis_index("wide")
     copies = [
@@ -309,17 +343,25 @@
         copy.start()
     total[...] = jnp.zeros_like(total)
     hist[...] = hist_ref[...]
-    came = [(i, c) for i in range(len(news)) for c in range(capacity)]
+    came = []
+    for r in range(1, wide_peers):
+        possible = ways(blocks, [(i ^ r, i) for i in range(wide_peers)])
+        way = by_place(owner, possible)
+        for c in range(capacity):
+            block = news[possible[0]][c]
+            for k in sorted(set(possible) - {possible[0]}):
+                block = jnp.where(way == k, news[k][c], block)
+            came.append((r, c, block))
     coef_count = news[0].shape[1]
     for first in range(0, len(came), SEGS):
         some = came[first : first + SEGS]
         values = jnp.dot(
             table_ref[: len(some) * STEPS, : len(some) * coef_count],
-            jnp.concatenate([news[i][c] for i, c in some], axis=0),
+            jnp.concatenate([block for _, _, block in some], axis=0),
             preferred_element_type=jnp.float32,
         )
-        for place_here, (i, c) in enumerate(some):
-            slot = (owner ^ (wide_peers - 1 - i)) * capacity + c
+        for place_here, (r, c, _) in enumerate(some):
+            slot = (owner ^ r) * capacity + c
             rows = pl.ds(pl.multiple_of(slot * LENGTH + HSEG * STEPS, 8), STEPS)
             hist[rows, :] = values[place_here * STEPS : (place_here + 1) * STEPS]
     for copy in copies:
@@ -550,13 +592,8 @@
         return lax.ppermute(x, axis, [(i, i ^ r) for i in range(lax.axis_size(axis))])
 
     reads = read_blocks.reshape(wide_peers, capacity).T
-    ring = [0, *range(1, wide_peers, 2), *reversed(range(2, wide_peers, 2))]
-    asked = [
-        lax.ppermute(
-            reads, "wide", [(ring[k], ring[(k + r) % wide_peers]) for k in range(wide_peers)]
-        )
-        for r in range(1, wide_peers)
-    ]
+    requests, blocks = wide_plans(wide_peers)
+    asked = [lax.ppermute(reads, "wide", part) for part in requests]
 
     vmem_inputs = [
         VMEM(state.shape, jnp.float32),
@@ -621,19 +658,20 @@
     )
 
     picked = pl.pallas_call(
-        functools.partial(pick_kernel, capacity=capacity, peers=wide_peers),
-        out_shape=[pltpu.VMEM((capacity, coef_count, block_rows), jnp.bfloat16)]
-        * (wide_peers - 1),
-        in_specs=[vmem_spec] * wide_peers,
-        out_specs=[vmem_spec] * (wide_peers - 1),
+        functools.partial(
+            pick_kernel, capacity=capacity, requests=requests, blocks=blocks
+        ),
+        out_shape=[pltpu.VMEM((capacity, coef_count, block_rows), jnp.bfloat16)] * len(blocks),
+        in_specs=[vmem_spec] * (len(requests) + 1),
+        out_specs=[vmem_spec] * len(blocks),
         scratch_shapes=[
-            SMEM((wide_peers - 1, capacity, wide_peers), jnp.int32),
-            pltpu.SemaphoreType.DMA((wide_peers - 1,)),
+            SMEM((len(requests), capacity, wide_peers), jnp.int32),
+            pltpu.SemaphoreType.DMA((len(requests),)),
         ],
         compiler_params=params(),
         name="pick_blocks",
     )(*asked[::-1], fresh)
-    news = [swap(picked[r - 1], "wide", r) for r in range(wide_peers - 1, 0, -1)]
+    news = [lax.ppermute(x, "wide", part) for x, part in zip(picked, blocks)]
 
     fixed = tile_count * (peers - 2) // peers + 2 * UNROLL
     fixed = min(tile_count, -(-fixed // UNROLL) * UNROLL)
@@ -643,11 +681,11 @@
     *shares, hist, sums = pl.pallas_call(
         functools.partial(
             far_kernel,
-            wide_peers=wide_peers, peers=peers, capacity=capacity, peer_targets=peer_targets,
+            blocks=blocks, wide_peers=wide_peers, peers=peers, capacity=capacity, peer_targets=peer_targets,
             fixed=fixed,
         ),
         out_shape=[share] * (peers - 2) + [pltpu.VMEM(hist.shape, jnp.float32), total],
-        in_specs=[vmem_spec] * (5 + wide_peers),
+        in_specs=[vmem_spec] * (6 + len(blocks)),
         out_specs=[vmem_spec] * peers,
         scratch_shapes=[*scalars, pltpu.SemaphoreType.DMA((2,))],
         compiler_params=params(),

time: 27 us -> 36 us (1.33)
  starting transfers between devices: 13.9 us -> 22.9 us
    ppermute x3 -> x10, starting transfers between devices: 7.13 us -> 20.5 us  [the longest x5 10.6 us: local(): asked = [lax.ppermute(reads, 'wide', part) for part in requests]]
    ppermute x7 -> x4, starting transfers between devices: 6.8 us -> 2.36 us  [swap(): lax.ppermute(x, axis, [(i, i ^ r) for i in range(lax.axis_size(axis))])]
    ppermute x7 -> x4, waiting for transfers between devices: 2.98 us -> 2.85 us  [swap(): lax.ppermute(x, axis, [(i, i ^ r) for i in range(lax.axis_size(axis))])]
  transfers between devices with their start and end apart: 10 -> 14, of which waited for: 5 -> 3; matrix products, arithmetic and copies ran while one was open for 0% -> 0% of each run, Pallas kernels for 20% -> 15%
where the time goes in v14:
time: 36 us; the launch traced here: 35.7 us
  starting transfers between devices  22.9 us (64%)
  Pallas kernels  9.08 us (25%)
  waiting for transfers between devices  2.87 us (8%)
  between operations  0.83 us (2%)
    ppermute x5, starting transfers between devices, local(): asked = [lax.ppermute(reads, 'wide', part) for part in requests]  10.6 us
    ppermute x5, starting transfers between devices, local(): news = [lax.ppermute(x, 'wide', part) for x, part in zip(picked, blocks)]  9.94 us
    ppermute x4, waiting for transfers between devices, swap(): lax.ppermute(x, axis, [(i, i ^ r) for i in range(lax.axis_size(axis))])  2.85 us
    ppermute x4, starting transfers between devices, swap(): lax.ppermute(x, axis, [(i, i ^ r) for i in range(lax.axis_size(axis))])  2.36 us
    pallas_call x1, Pallas kernels, local(): pl.pallas_call(near_kernel, out_shape=[pltpu.VMEM(fresh_coefs.shape, jnp....  1.98 us
    pallas_call x1, Pallas kernels, local(): pl.pallas_call(functools.partial(prepare_kernel, peers=peers, own_blocks=...  1.95 us
    pallas_call x1, Pallas kernels, local(): pl.pallas_call(functools.partial(window_kernel, own_blocks=own_blocks, pe...  1.51 us
    pallas_call x1, Pallas kernels, local(): pl.pallas_call(functools.partial(far_kernel, blocks=blocks, wide_peers=wi...  1.42 us
  transfers between devices with their start and end apart: 14, of which 3 were waited for; matrix products, arithmetic and copies ran while one was open for 0% of the time, Pallas kernels for 15%

profile of v14, /device:TPU:0, one launch (start us, length us, event | category | flops | bytes accessed | tf_op | source)
XLA Modules:
  0.0 35.7 jit_solution(6437988939868401046)
XLA Ops:
  0.6 1.3 %collective-permute-start.4 = (s32[2,4]{1,0:T(2,128)}, s32[2,4]{1,0:T(2,128)S(1)}, u32[]{:S(2)}, u32[]{:S(2)}) collective-permute-start(s32[2,4]{1,0:T(2,128)} %bitcast.15), channel_id=1, source_target_pairs={{8,4},{12,0},{9,5},{13,1},{10,6},{14,2},{11,7},{15,3},{24,20},{28,... | collective-permute-start | bytes 104 | tf_op jit(solution)/shard_map/ppermute | solution.py:596
  1.9 4.9 %collective-permute-start.3 = (s32[2,4]{1,0:T(2,128)}, s32[2,4]{1,0:T(2,128)S(1)}, u32[]{:S(2)}, u32[]{:S(2)}) collective-permute-start(s32[2,4]{1,0:T(2,128)} %bitcast.16), channel_id=1, source_target_pairs={{0,4},{8,0},{1,5},{9,1},{2,6},{10,2},{3,7},{11,3},{16,20},{24,16},... | collective-permute-start | bytes 104 | tf_op jit(solution)/shard_map/ppermute | solution.py:596
  6.9 1.5 %collective-permute-start.2 = (s32[2,4]{1,0:T(2,128)}, s32[2,4]{1,0:T(2,128)S(1)}, u32[]{:S(2)}, u32[]{:S(2)}) collective-permute-start(s32[2,4]{1,0:T(2,128)} %bitcast.17), channel_id=1, source_target_pairs={{0,8},{4,0},{8,12},{12,4},{1,9},{5,1},{9,13},{13,5},{2,10},{6,2},{... | collective-permute-start | bytes 104 | tf_op jit(solution)/shard_map/ppermute | solution.py:596
  8.4 2.2 %collective-permute-start.1 = (s32[2,4]{1,0:T(2,128)}, s32[2,4]{1,0:T(2,128)S(1)}, u32[]{:S(2)}, u32[]{:S(2)}) collective-permute-start(s32[2,4]{1,0:T(2,128)} %bitcast.18), channel_id=1, source_target_pairs={{0,12},{4,8},{1,13},{5,9},{2,14},{6,10},{3,15},{7,11},{16,28},{20,... | collective-permute-start | bytes 104 | tf_op jit(solution)/shard_map/ppermute | solution.py:596
  10.6 0.7 %collective-permute-start = (s32[2,4]{1,0:T(2,128)}, s32[2,4]{1,0:T(2,128)S(1)}, u32[]{:S(2)}, u32[]{:S(2)}) collective-permute-start(s32[2,4]{1,0:T(2,128)} %bitcast.19), channel_id=1, source_target_pairs={{4,12},{12,8},{5,13},{13,9},{6,14},{14,10},{7,15},{15,11},{20,28},... | collective-permute-start | bytes 104 | tf_op jit(solution)/shard_map/ppermute | solution.py:596
  11.2 2.0 %near.1 = (bf16[32,32,128]{2,1,0:T(8,128)(2,1)S(1)}, bf16[96,128,128]{2,1,0:T(8,128)(2,1)S(1)}) custom-call(bf16[32,32,128]{2,1,0:T(8,128)(2,1)} %fresh_hbm.1, bf16[96,128,128]{2,1,0:T(8,128)(2,1)} %bitcast.12), custom_call_target="tpu_custom_call" | custom-call | tf_op jit(solution)/shard_map/near/pallas_call | solution.py:610
  13.2 0.0 collective-permute-done.4.refs_4_
  13.2 0.0 collective-permute-done.3.refs_3_
  13.3 0.0 collective-permute-done.2.refs_2_
  13.3 0.0 collective-permute-done.1.refs_1_
  13.3 0.0 collective-permute-done.refs_0_
  13.3 0.7 %pick_blocks.1 = (bf16[2,32,128]{2,1,0:T(8,128)(2,1)S(1)}, bf16[2,32,128]{2,1,0:T(8,128)(2,1)S(1)}, bf16[2,32,128]{2,1,0:T(8,128)(2,1)S(1)}, bf16[2,32,128]{2,1,0:T(8,128)(2,1)S(1)}, bf16[2,32,128]{2,1,0:T(8,128)(2,1)S(1)}) custom-call(s32[2,4]{1,0:T(2,128)S(1)} %collective-permute-done.refs_0_, s32[2,4]{1,0:T(2,128)S(1)} %collective-permute-done.1.refs_1_, ...), custom_call_target="tpu_custom_call" | custom-call | tf_op jit(solution)/shard_map/pick_blocks/pallas_call | solution.py:660
  14.0 1.3 %collective-permute-start.5 = (bf16[2,32,128]{2,1,0:T(8,128)(2,1)S(1)}, bf16[2,32,128]{2,1,0:T(8,128)(2,1)S(1)}, u32[]{:S(2)}, u32[]{:S(2)}) collective-permute-start(bf16[2,32,128]{2,1,0:T(8,128)(2,1)S(1)} %get-tuple-element.29), channel_id=1, source_target_pairs={{8,0},{9,1},{10,2},{11,3},{24,16},{25,17},{26,18},{27,19}} | collective-permute-start | bytes 49160 | tf_op jit(solution)/shard_map/ppermute | solution.py:674
  15.3 1.3 %collective-permute-start.6 = (bf16[2,32,128]{2,1,0:T(8,128)(2,1)S(1)}, bf16[2,32,128]{2,1,0:T(8,128)(2,1)S(1)}, u32[]{:S(2)}, u32[]{:S(2)}) collective-permute-start(bf16[2,32,128]{2,1,0:T(8,128)(2,1)S(1)} %get-tuple-element.30), channel_id=1, source_target_pairs={{4,0},{12,4},{5,1},{13,5},{6,2},{14,6},{7,3},{15,7},{20,16},{28,20... | collective-permute-start | bytes 49160 | tf_op jit(solution)/shard_map/ppermute | solution.py:674
  16.6 3.6 %collective-permute-start.7 = (bf16[2,32,128]{2,1,0:T(8,128)(2,1)S(1)}, bf16[2,32,128]{2,1,0:T(8,128)(2,1)S(1)}, u32[]{:S(2)}, u32[]{:S(2)}) collective-permute-start(bf16[2,32,128]{2,1,0:T(8,128)(2,1)S(1)} %get-tuple-element.31), channel_id=1, source_target_pairs={{0,12},{4,8},{8,4},{12,0},{1,13},{5,9},{9,5},{13,1},{2,14},{6,10},... | collective-permute-start | bytes 49160 | tf_op jit(solution)/shard_map/ppermute | solution.py:674
  20.2 1.8 %collective-permute-start.8 = (bf16[2,32,128]{2,1,0:T(8,128)(2,1)S(1)}, bf16[2,32,128]{2,1,0:T(8,128)(2,1)S(1)}, u32[]{:S(2)}, u32[]{:S(2)}) collective-permute-start(bf16[2,32,128]{2,1,0:T(8,128)(2,1)S(1)} %get-tuple-element.32), channel_id=1, source_target_pairs={{0,4},{4,12},{12,8},{1,5},{5,13},{13,9},{2,6},{6,14},{14,10},{3,7}... | collective-permute-start | bytes 49160 | tf_op jit(solution)/shard_map/ppermute | solution.py:674
  22.0 1.9 %collective-permute-start.9 = (bf16[2,32,128]{2,1,0:T(8,128)(2,1)S(1)}, bf16[2,32,128]{2,1,0:T(8,128)(2,1)S(1)}, u32[]{:S(2)}, u32[]{:S(2)}) collective-permute-start(bf16[2,32,128]{2,1,0:T(8,128)(2,1)S(1)} %get-tuple-element.33), channel_id=1, source_target_pairs={{0,8},{8,12},{1,9},{9,13},{2,10},{10,14},{3,11},{11,15},{16,24},{2... | collective-permute-start | bytes 49160 | tf_op jit(solution)/shard_map/ppermute | solution.py:674
  24.0 2.0 %prepare.1 = (f32[160,128]{1,0:T(8,128)S(1)}, f32[768,128]{1,0:T(8,128)S(1)}, s32[4,128]{1,0:T(4,128)S(1)}, f32[1,128]{1,0:T(1,128)S(1)}, bf16[4,16,128]{2,1,0:T(8,128)(2,1)S(1)}, /*index=5*/bf16[96,96]{1,0:T(8,128)(2,1)S(1)}) custom-call(bf16[32,32,128]{2,1,0:T(8,128)(2,1)S(1)} %get-tuple-element.22.fresh_ref.refs_5_, s32[2,4]{1,0:T(2,128)} %bitcast.20, ...), custom_call_target="tpu_custom_call" | custom-call | tf_op jit(solution)/shard_map/prepare/pallas_call | solution.py:622
  25.9 0.0 collective-permute-done.5.refs_0_
  25.9 0.0 collective-permute-done.6.refs_1_
  25.9 0.0 collective-permute-done.7.refs_2_
  25.9 0.0 collective-permute-done.8.refs_3_
  26.0 0.0 collective-permute-done.9.refs_4_
  26.0 1.4 %far_tiles.1 = (bf16[400,128]{1,0:T(8,128)(2,1)S(1)}, bf16[400,128]{1,0:T(8,128)(2,1)S(1)}, f32[768,128]{1,0:T(8,128)S(1)}, f32[1568,128]{1,0:T(8,128)S(1)}) custom-call(f32[1,128]{1,0:T(1,128)S(1)} %get-tuple-element.23.fracs_ref, s32[4,128]{1,0:T(4,128)S(1)} %get-tuple-element.24.tiles_ref, bf16[96,96]{1,0:T(8,128)(2,1)S(1)} %get-tuple-element.25.table_ref, ...), custom_call_target="tpu_custom_call" | custom-call | tf_op jit(solution)/shard_map/far_tiles/pallas_call | solution.py:681
  27.4 0.0 copy-start
  27.4 1.6 %collective-permute-start.11 = (bf16[400,128]{1,0:T(8,128)(2,1)S(1)}, bf16[400,128]{1,0:T(8,128)(2,1)S(1)}, u32[]{:S(2)}, u32[]{:S(2)}) collective-permute-start(bf16[400,128]{1,0:T(8,128)(2,1)S(1)} %get-tuple-element.35), channel_id=1, source_target_pairs={{0,2},{1,3},{2,0},{3,1},{4,6},{5,7},{6,4},{7,5},{8,10},{9,11},{10,... | collective-permute-start | bytes 307208 | tf_op jit(solution)/shard_map/ppermute | solution.py:592
  29.0 0.0 collective-permute-start.10
  29.0 1.2 %near_tiles.1 = (bf16[192,128]{1,0:T(8,128)(2,1)S(1)}, bf16[208,128]{1,0:T(8,128)(2,1)S(1)}, bf16[400,128]{1,0:T(8,128)(2,1)S(1)}) custom-call(f32[1,128]{1,0:T(1,128)S(1)} %get-tuple-element.23.fracs_ref, s32[4,128]{1,0:T(4,128)S(1)} %get-tuple-element.24.tiles_ref, bf16[4,16,128]{2,1,0:T(8,128)(2,1)S(1)} %get-tuple-element.26.head_ref, ...), custom_call_target="tpu_custom_call" | custom-call | tf_op jit(solution)/shard_map/near_tiles/pallas_call | solution.py:700
  30.2 0.7 %collective-permute-start.13 = (bf16[208,128]{1,0:T(8,128)(2,1)S(1)}, bf16[208,128]{1,0:T(8,128)(2,1)S(1)}, u32[]{:S(2)}, u32[]{:S(2)}) collective-permute-start(bf16[208,128]{1,0:T(8,128)(2,1)S(1)} %get-tuple-element.39), channel_id=1, source_target_pairs={{0,1},{1,0},{2,3},{3,2},{4,5},{5,4},{6,7},{7,6},{8,9},{9,8},{10,11... | collective-permute-start | bytes 159752 | tf_op jit(solution)/shard_map/ppermute | solution.py:592
  30.9 0.1 collective-permute-start.12
  31.0 1.2 %collective-permute-done.12.refs_1_ = bf16[192,128]{1,0:T(8,128)(2,1)S(1)} collective-permute-done((bf16[192,128]{1,0:T(8,128)(2,1)S(1)}, bf16[192,128]{1,0:T(8,128)(2,1)S(1)}, u32[]{:S(2)}, u32[]{:S(2)}) %collective-permute-start.12) | collective-permute-done | bytes 49184 | tf_op jit(solution)/shard_map/ppermute | solution.py:592
  32.1 0.0 collective-permute-done.13.refs_2_
  32.1 0.2 collective-permute-done.11.refs_0_
  32.3 0.3 forcing.1.forcing_ref
  32.6 1.5 %collective-permute-done.10.share_ref = bf16[400,128]{1,0:T(8,128)(2,1)S(1)} collective-permute-done((bf16[400,128]{1,0:T(8,128)(2,1)S(1)}, bf16[400,128]{1,0:T(8,128)(2,1)S(1)}, u32[]{:S(2)}, u32[]{:S(2)}) %collective-permute-start.10) | collective-permute-done | bytes 102432 | tf_op jit(solution)/shard_map/ppermute | solution.py:592
  34.2 0.0 copy-done
  34.2 1.5 %window_steps.1 = (bf16[32,32,128]{2,1,0:T(8,128)(2,1)}, f32[2,4096]{1,0:T(2,128)}) custom-call(bf16[400,128]{1,0:T(8,128)(2,1)S(1)} %collective-permute-done.10.share_ref, f32[1024,128]{1,0:T(8,128)S(1)} %forcing.1.forcing_ref, f32[160,128]{1,0:T(8,128)S(1)} %get-tuple-element.41.refs_4_.ready_ref, bf16[2,128,192]{2,1,0:T(8,128)(2,1)S(1)} %copy-done), custom_call_target="tpu_custom_call" | custom-call | tf_op jit(solution)/shard_map/window_steps/pallas_call | solution.py:721
Async XLA Ops:
  0.6 12.6 %collective-permute-start.4 = (s32[2,4]{1,0:T(2,128)}, s32[2,4]{1,0:T(2,128)S(1)}, u32[]{:S(2)}, u32[]{:S(2)}) collective-permute-start(s32[2,4]{1,0:T(2,128)} %bitcast.15), channel_id=1, source_target_pairs={{8,4},{12,0},{9,5},{13,1},{10,6},{14,2},{11,7},{15,3},{24,20},{28,... | collective-permute-start | bytes 104 | tf_op jit(solution)/shard_map/ppermute | solution.py:596
  1.9 11.3 %collective-permute-start.3 = (s32[2,4]{1,0:T(2,128)}, s32[2,4]{1,0:T(2,128)S(1)}, u32[]{:S(2)}, u32[]{:S(2)}) collective-permute-start(s32[2,4]{1,0:T(2,128)} %bitcast.16), channel_id=1, source_target_pairs={{0,4},{8,0},{1,5},{9,1},{2,6},{10,2},{3,7},{11,3},{16,20},{24,16},... | collective-permute-start | bytes 104 | tf_op jit(solution)/shard_map/ppermute | solution.py:596
  6.9 6.4 %collective-permute-start.2 = (s32[2,4]{1,0:T(2,128)}, s32[2,4]{1,0:T(2,128)S(1)}, u32[]{:S(2)}, u32[]{:S(2)}) collective-permute-start(s32[2,4]{1,0:T(2,128)} %bitcast.17), channel_id=1, source_target_pairs={{0,8},{4,0},{8,12},{12,4},{1,9},{5,1},{9,13},{13,5},{2,10},{6,2},{... | collective-permute-start | bytes 104 | tf_op jit(solution)/shard_map/ppermute | solution.py:596
  8.4 4.9 %collective-permute-start.1 = (s32[2,4]{1,0:T(2,128)}, s32[2,4]{1,0:T(2,128)S(1)}, u32[]{:S(2)}, u32[]{:S(2)}) collective-permute-start(s32[2,4]{1,0:T(2,128)} %bitcast.18), channel_id=1, source_target_pairs={{0,12},{4,8},{1,13},{5,9},{2,14},{6,10},{3,15},{7,11},{16,28},{20,... | collective-permute-start | bytes 104 | tf_op jit(solution)/shard_map/ppermute | solution.py:596
  10.6 2.7 %collective-permute-start = (s32[2,4]{1,0:T(2,128)}, s32[2,4]{1,0:T(2,128)S(1)}, u32[]{:S(2)}, u32[]{:S(2)}) collective-permute-start(s32[2,4]{1,0:T(2,128)} %bitcast.19), channel_id=1, source_target_pairs={{4,12},{12,8},{5,13},{13,9},{6,14},{14,10},{7,15},{15,11},{20,28},... | collective-permute-start | bytes 104 | tf_op jit(solution)/shard_map/ppermute | solution.py:596
  14.0 11.9 %collective-permute-start.5 = (bf16[2,32,128]{2,1,0:T(8,128)(2,1)S(1)}, bf16[2,32,128]{2,1,0:T(8,128)(2,1)S(1)}, u32[]{:S(2)}, u32[]{:S(2)}) collective-permute-start(bf16[2,32,128]{2,1,0:T(8,128)(2,1)S(1)} %get-tuple-element.29), channel_id=1, source_target_pairs={{8,0},{9,1},{10,2},{11,3},{24,16},{25,17},{26,18},{27,19}} | collective-permute-start | bytes 49160 | tf_op jit(solution)/shard_map/ppermute | solution.py:674
  15.3 10.6 %collective-permute-start.6 = (bf16[2,32,128]{2,1,0:T(8,128)(2,1)S(1)}, bf16[2,32,128]{2,1,0:T(8,128)(2,1)S(1)}, u32[]{:S(2)}, u32[]{:S(2)}) collective-permute-start(bf16[2,32,128]{2,1,0:T(8,128)(2,1)S(1)} %get-tuple-element.30), channel_id=1, source_target_pairs={{4,0},{12,4},{5,1},{13,5},{6,2},{14,6},{7,3},{15,7},{20,16},{28,20... | collective-permute-start | bytes 49160 | tf_op jit(solution)/shard_map/ppermute | solution.py:674
  16.6 9.4 %collective-permute-start.7 = (bf16[2,32,128]{2,1,0:T(8,128)(2,1)S(1)}, bf16[2,32,128]{2,1,0:T(8,128)(2,1)S(1)}, u32[]{:S(2)}, u32[]{:S(2)}) collective-permute-start(bf16[2,32,128]{2,1,0:T(8,128)(2,1)S(1)} %get-tuple-element.31), channel_id=1, source_target_pairs={{0,12},{4,8},{8,4},{12,0},{1,13},{5,9},{9,5},{13,1},{2,14},{6,10},... | collective-permute-start | bytes 49160 | tf_op jit(solution)/shard_map/ppermute | solution.py:674
  20.2 5.8 %collective-permute-start.8 = (bf16[2,32,128]{2,1,0:T(8,128)(2,1)S(1)}, bf16[2,32,128]{2,1,0:T(8,128)(2,1)S(1)}, u32[]{:S(2)}, u32[]{:S(2)}) collective-permute-start(bf16[2,32,128]{2,1,0:T(8,128)(2,1)S(1)} %get-tuple-element.32), channel_id=1, source_target_pairs={{0,4},{4,12},{12,8},{1,5},{5,13},{13,9},{2,6},{6,14},{14,10},{3,7}... | collective-permute-start | bytes 49160 | tf_op jit(solution)/shard_map/ppermute | solution.py:674
  22.0 3.9 %collective-permute-start.9 = (bf16[2,32,128]{2,1,0:T(8,128)(2,1)S(1)}, bf16[2,32,128]{2,1,0:T(8,128)(2,1)S(1)}, u32[]{:S(2)}, u32[]{:S(2)}) collective-permute-start(bf16[2,32,128]{2,1,0:T(8,128)(2,1)S(1)} %get-tuple-element.33), channel_id=1, source_target_pairs={{0,8},{8,12},{1,9},{9,13},{2,10},{10,14},{3,11},{11,15},{16,24},{2... | collective-permute-start | bytes 49160 | tf_op jit(solution)/shard_map/ppermute | solution.py:674
  27.4 6.8 %copy-start = (bf16[2,128,192]{2,1,0:T(8,128)(2,1)S(1)}, bf16[2,128,192]{2,1,0:T(8,128)(2,1)}, u32[]{:S(2)}) copy-start(bf16[2,128,192]{2,1,0:T(8,128)(2,1)} %constant.8.clone.fit_ref) | copy-start | bytes 294916
  27.4 4.9 %collective-permute-start.11 = (bf16[400,128]{1,0:T(8,128)(2,1)S(1)}, bf16[400,128]{1,0:T(8,128)(2,1)S(1)}, u32[]{:S(2)}, u32[]{:S(2)}) collective-permute-start(bf16[400,128]{1,0:T(8,128)(2,1)S(1)} %get-tuple-element.35), channel_id=1, source_target_pairs={{0,2},{1,3},{2,0},{3,1},{4,6},{5,7},{6,4},{7,5},{8,10},{9,11},{10,... | collective-permute-start | bytes 307208 | tf_op jit(solution)/shard_map/ppermute | solution.py:592
  29.0 5.2 %collective-permute-start.10 = (bf16[400,128]{1,0:T(8,128)(2,1)S(1)}, bf16[400,128]{1,0:T(8,128)(2,1)S(1)}, u32[]{:S(2)}, u32[]{:S(2)}) collective-permute-start(bf16[400,128]{1,0:T(8,128)(2,1)S(1)} %get-tuple-element.34), channel_id=1, source_target_pairs={{0,3},{1,2},{2,1},{3,0},{4,7},{5,6},{6,5},{7,4},{8,11},{9,10},{10,... | collective-permute-start | bytes 307208 | tf_op jit(solution)/shard_map/ppermute | solution.py:592
  30.2 1.9 %collective-permute-start.13 = (bf16[208,128]{1,0:T(8,128)(2,1)S(1)}, bf16[208,128]{1,0:T(8,128)(2,1)S(1)}, u32[]{:S(2)}, u32[]{:S(2)}) collective-permute-start(bf16[208,128]{1,0:T(8,128)(2,1)S(1)} %get-tuple-element.39), channel_id=1, source_target_pairs={{0,1},{1,0},{2,3},{3,2},{4,5},{5,4},{6,7},{7,6},{8,9},{9,8},{10,11... | collective-permute-start | bytes 159752 | tf_op jit(solution)/shard_map/ppermute | solution.py:592
  30.9 1.2 %collective-permute-start.12 = (bf16[192,128]{1,0:T(8,128)(2,1)S(1)}, bf16[192,128]{1,0:T(8,128)(2,1)S(1)}, u32[]{:S(2)}, u32[]{:S(2)}) collective-permute-start(bf16[192,128]{1,0:T(8,128)(2,1)S(1)} %get-tuple-element.38), channel_id=1, source_target_pairs={{0,1},{1,0},{2,3},{3,2},{4,5},{5,4},{6,7},{7,6},{8,9},{9,8},{10,11... | collective-permute-start | bytes 147464 | tf_op jit(solution)/shard_map/ppermute | solution.py:592

commit v15 on v13

--- a/solution.py
+++ b/solution.py
@@ -16,6 +16,7 @@
 LENGTH = SEGS * STEPS
 GROUP = 4
 HEAD = 16
+LAST = 2
 PITCH = STEPS // 2 + 1
 CHUNKS = 8
 UNROLL = 4
@@ -128,7 +129,10 @@
         rank = jnp.dot(below, held[part].astype(jnp.bfloat16), preferred_element_type=jnp.float32)
         ranks = ranks + jnp.sum(hits[part] * rank[:, :tile_count], axis=0, keepdims=True)
         rank = jnp.where(held[part] > 0.5, rank, -1.0)
-        source = ((peers - 1) - (place ^ p)).astype(jnp.float32)
+        source = place ^ p
+        source = jnp.where(
+            source == LAST, 0, (peers - 1) - source + jnp.where(source > LAST, 1, 0)
+        ).astype(jnp.float32)
         rows = []
         for h in range(head_rows):
             match = rank == lanes[0, h : h + 1, :]
@@ -228,6 +232,10 @@
         copy.wait()
 
 
+def folded_ring(count):
+    return [0, *range(1, count, 2), *reversed(range(2, count, 2))]
+
+
 def pick_kernel(*refs, capacity, peers):
     tables = refs[: peers - 1][::-1]
     fresh = refs[peers - 1]
@@ -238,13 +246,15 @@
     for copy in copies:
         copy.start()
 
-    def ring_place(i):
-        return jnp.where(i % 2 == 1, (i + 1) // 2, (peers - i // 2) % peers)
-
     for copy in copies:
         copy.wait()
+    ring = folded_ring(peers)
     for distance in range(1, peers):
-        way = (ring_place(place) - ring_place(place ^ distance) + peers) % peers
+        turns = [(ring.index(i) - ring.index(i ^ distance)) % peers for i in range(peers)]
+        way = turns[0]
+        for i in range(1, peers):
+            if turns[i] != turns[0]:
+                way = jnp.where(place == i, turns[i], way)
         for c in range(capacity):
             block = jnp.maximum(asked[way - 1, c, place], 0)
             outs[distance - 1][c] = fresh[block]
@@ -397,14 +407,14 @@
 
 
 def forcing_kernel(*refs, peers, own_blocks, peer_targets):
-    shares = {r: (ref,) for r, ref in zip(range(2, peers - 1), refs)}
+    shares = {r: (ref,) for r, ref in zip(range(LAST + 1, peers), refs)}
     shares |= {1: refs[peers - 3 : peers - 1], 0: (refs[peers - 1],)}
     ready_ref, out_ref = refs[peers:]
     block_rows = ready_ref.shape[1]
     width = TOGETHER * peer_targets
     head = sum(share[-1][-HEAD:, :].astype(jnp.float32) for share in shares.values())
     scatter = one_hot(head, TOGETHER * own_blocks, peers * width)
-    stack = [shares[r] for r in (peers - 2, *range(peers - 2, -1, -1))]
+    stack = [shares[r] for r in (0, *range(peers - 1, LAST, -1), *range(LAST - 1, -1, -1))]
     gain, counts = [
         0.5 * ready_ref[i * own_blocks : (i + 1) * own_blocks, :] for i in (2, 3)
     ]
@@ -550,7 +560,7 @@
         return lax.ppermute(x, axis, [(i, i ^ r) for i in range(lax.axis_size(axis))])
 
     reads = read_blocks.reshape(wide_peers, capacity).T
-    ring = [0, *range(1, wide_peers, 2), *reversed(range(2, wide_peers, 2))]
+    ring = folded_ring(wide_peers)
     asked = [
         lax.ppermute(
             reads, "wide", [(ring[k], ring[(k + r) % wide_peers]) for k in range(wide_peers)]
@@ -678,7 +688,7 @@
         out_specs=vmem_spec,
         compiler_params=params(),
         name="forcing",
-    )(*[sent[r] for r in range(2, peers - 1)], *pair, own, ready)
+    )(*[sent[r] for r in range(LAST + 1, peers)], *pair, own, ready)
 
     new_coefs, final_state = pl.pallas_call(
         functools.partial(
@@ -701,7 +711,7 @@
         ],
         compiler_params=params(),
         name="window_steps",
-    )(sent[peers - 1], forcing, ready, jnp.asarray(fit_table(coef_count)))
+    )(sent[LAST], forcing, ready, jnp.asarray(fit_table(coef_count)))
     return new_coefs, final_state
 
 

time: 27 us -> 27.7 us (1.026)
  waiting for transfers between devices: 3.18 us -> 4.02 us
    ppermute x7, waiting for transfers between devices: 2.98 us -> 3.82 us  [swap(): lax.ppermute(x, axis, [(i, i ^ r) for i in range(lax.axis_size(axis))])]
where the time goes in v15:
time: 27.7 us; the launch traced here: 27.5 us
  starting transfers between devices  13.8 us (50%)
  Pallas kernels  8.99 us (32%)
  waiting for transfers between devices  4.02 us (15%)
  between operations  0.73 us (3%)
    ppermute x3, starting transfers between devices, local(): lax.ppermute(reads, 'wide', [(ring[k], ring[(k + r) % wide_peers]) for k...  7.13 us
    ppermute x7, starting transfers between devices, swap(): lax.ppermute(x, axis, [(i, i ^ r) for i in range(lax.axis_size(axis))])  6.65 us
    ppermute x7, waiting for transfers between devices, swap(): lax.ppermute(x, axis, [(i, i ^ r) for i in range(lax.axis_size(axis))])  3.82 us
    pallas_call x1, Pallas kernels, local(): pl.pallas_call(near_kernel, out_shape=[pltpu.VMEM(fresh_coefs.shape, jnp....  1.98 us
    pallas_call x1, Pallas kernels, local(): pl.pallas_call(functools.partial(prepare_kernel, peers=peers, own_blocks=...  1.94 us
    pallas_call x1, Pallas kernels, local(): pl.pallas_call(functools.partial(window_kernel, own_blocks=own_blocks, pe...  1.52 us
    pallas_call x1, Pallas kernels, local(): pl.pallas_call(functools.partial(far_kernel, wide_peers=wide_peers, peers...  1.41 us
    pallas_call x1, Pallas kernels, local(): pl.pallas_call(functools.partial(near_tiles_kernel, peers=peers, peer_tar...  1.22 us
  transfers between devices with their start and end apart: 10, of which 5 were waited for; matrix products, arithmetic and copies ran while one was open for 0% of the time, Pallas kernels for 20%

profile of v15, /device:TPU:0, one launch (start us, length us, event | category | flops | bytes accessed | tf_op | source)
XLA Modules:
  0.0 27.5 jit_solution(7779516440305128574)
XLA Ops:
  0.6 3.1 %collective-permute-start.2 = (s32[2,4]{1,0:T(2,128)}, s32[2,4]{1,0:T(2,128)S(1)}, u32[]{:S(2)}, u32[]{:S(2)}) collective-permute-start(s32[2,4]{1,0:T(2,128)} %bitcast.15), channel_id=1, source_target_pairs={{0,4},{4,12},{12,8},{8,0},{1,5},{5,13},{13,9},{9,1},{2,6},{6,14},{... | collective-permute-start | bytes 104 | tf_op jit(solution)/shard_map/ppermute | solution.py:565
  3.7 2.5 %collective-permute-start.1 = (s32[2,4]{1,0:T(2,128)}, s32[2,4]{1,0:T(2,128)S(1)}, u32[]{:S(2)}, u32[]{:S(2)}) collective-permute-start(s32[2,4]{1,0:T(2,128)} %bitcast.16), channel_id=1, source_target_pairs={{0,12},{4,8},{12,0},{8,4},{1,13},{5,9},{13,1},{9,5},{2,14},{6,10},... | collective-permute-start | bytes 104 | tf_op jit(solution)/shard_map/ppermute | solution.py:565
  6.2 1.6 %collective-permute-start = (s32[2,4]{1,0:T(2,128)}, s32[2,4]{1,0:T(2,128)S(1)}, u32[]{:S(2)}, u32[]{:S(2)}) collective-permute-start(s32[2,4]{1,0:T(2,128)} %bitcast.17), channel_id=1, source_target_pairs={{0,8},{4,0},{12,4},{8,12},{1,9},{5,1},{13,5},{9,13},{2,10},{6,2},{... | collective-permute-start | bytes 104 | tf_op jit(solution)/shard_map/ppermute | solution.py:565
  7.8 2.0 %near.1 = (bf16[32,32,128]{2,1,0:T(8,128)(2,1)S(1)}, bf16[96,128,128]{2,1,0:T(8,128)(2,1)S(1)}) custom-call(bf16[32,32,128]{2,1,0:T(8,128)(2,1)} %fresh_hbm.1, bf16[96,128,128]{2,1,0:T(8,128)(2,1)} %bitcast.12), custom_call_target="tpu_custom_call" | custom-call | tf_op jit(solution)/shard_map/near/pallas_call | solution.py:583
  9.7 0.0 collective-permute-done.2.refs_2_
  9.8 0.0 collective-permute-done.1.refs_1_
  9.8 0.2 collective-permute-done.refs_0_
  10.0 0.6 %pick_blocks.1 = (bf16[2,32,128]{2,1,0:T(8,128)(2,1)S(1)}, bf16[2,32,128]{2,1,0:T(8,128)(2,1)S(1)}, bf16[2,32,128]{2,1,0:T(8,128)(2,1)S(1)}) custom-call(s32[2,4]{1,0:T(2,128)S(1)} %collective-permute-done.refs_0_, s32[2,4]{1,0:T(2,128)S(1)} %collective-permute-done.1.refs_1_, s32[2,4]{1,0:T(2,128)S(1)} %collective-permute-done.2.refs_2_, ...), custom_call_target="tpu_custom_call" | custom-call | tf_op jit(solution)/shard_map/pick_blocks/pallas_call | solution.py:633
  10.6 1.9 %collective-permute-start.3 = (bf16[2,32,128]{2,1,0:T(8,128)(2,1)S(1)}, bf16[2,32,128]{2,1,0:T(8,128)(2,1)S(1)}, u32[]{:S(2)}, u32[]{:S(2)}) collective-permute-start(bf16[2,32,128]{2,1,0:T(8,128)(2,1)S(1)} %get-tuple-element.27), channel_id=1, source_target_pairs={{0,12},{4,8},{8,4},{12,0},{1,13},{5,9},{9,5},{13,1},{2,14},{6,10},... | collective-permute-start | bytes 49160 | tf_op jit(solution)/shard_map/ppermute | solution.py:560
  12.5 0.8 %collective-permute-start.4 = (bf16[2,32,128]{2,1,0:T(8,128)(2,1)S(1)}, bf16[2,32,128]{2,1,0:T(8,128)(2,1)S(1)}, u32[]{:S(2)}, u32[]{:S(2)}) collective-permute-start(bf16[2,32,128]{2,1,0:T(8,128)(2,1)S(1)} %get-tuple-element.28), channel_id=1, source_target_pairs={{0,8},{4,12},{8,0},{12,4},{1,9},{5,13},{9,1},{13,5},{2,10},{6,14},... | collective-permute-start | bytes 49160 | tf_op jit(solution)/shard_map/ppermute | solution.py:560
  13.2 1.8 %collective-permute-start.5 = (bf16[2,32,128]{2,1,0:T(8,128)(2,1)S(1)}, bf16[2,32,128]{2,1,0:T(8,128)(2,1)S(1)}, u32[]{:S(2)}, u32[]{:S(2)}) collective-permute-start(bf16[2,32,128]{2,1,0:T(8,128)(2,1)S(1)} %get-tuple-element.29), channel_id=1, source_target_pairs={{0,4},{4,0},{8,12},{12,8},{1,5},{5,1},{9,13},{13,9},{2,6},{6,2},{1... | collective-permute-start | bytes 49160 | tf_op jit(solution)/shard_map/ppermute | solution.py:560
  15.0 1.9 %prepare.1 = (f32[160,128]{1,0:T(8,128)S(1)}, f32[768,128]{1,0:T(8,128)S(1)}, s32[4,128]{1,0:T(4,128)S(1)}, f32[1,128]{1,0:T(1,128)S(1)}, bf16[4,16,128]{2,1,0:T(8,128)(2,1)S(1)}, /*index=5*/bf16[96,96]{1,0:T(8,128)(2,1)S(1)}) custom-call(bf16[32,32,128]{2,1,0:T(8,128)(2,1)S(1)} %get-tuple-element.20.fresh_ref.refs_3_, s32[2,4]{1,0:T(2,128)} %bitcast.18, ...), custom_call_target="tpu_custom_call" | custom-call | tf_op jit(solution)/shard_map/prepare/pallas_call | solution.py:595
  17.0 0.0 collective-permute-done.3.refs_0_
  17.0 0.1 collective-permute-done.4.refs_1_
  17.1 0.0 collective-permute-done.5.refs_2_
  17.1 1.4 %far_tiles.1 = (bf16[400,128]{1,0:T(8,128)(2,1)S(1)}, bf16[400,128]{1,0:T(8,128)(2,1)S(1)}, f32[768,128]{1,0:T(8,128)S(1)}, f32[1568,128]{1,0:T(8,128)S(1)}) custom-call(f32[1,128]{1,0:T(1,128)S(1)} %get-tuple-element.21.fracs_ref, s32[4,128]{1,0:T(4,128)S(1)} %get-tuple-element.22.tiles_ref, bf16[96,96]{1,0:T(8,128)(2,1)S(1)} %get-tuple-element.23.table_ref, ...), custom_call_target="tpu_custom_call" | custom-call | tf_op jit(solution)/shard_map/far_tiles/pallas_call | solution.py:653
  18.5 0.0 copy-start
  18.6 0.1 collective-permute-start.7
  18.6 1.6 %collective-permute-start.6 = (bf16[400,128]{1,0:T(8,128)(2,1)S(1)}, bf16[400,128]{1,0:T(8,128)(2,1)S(1)}, u32[]{:S(2)}, u32[]{:S(2)}) collective-permute-start(bf16[400,128]{1,0:T(8,128)(2,1)S(1)} %get-tuple-element.30), channel_id=1, source_target_pairs={{0,2},{1,3},{2,0},{3,1},{4,6},{5,7},{6,4},{7,5},{8,10},{9,11},{10,... | collective-permute-start | bytes 307208 | tf_op jit(solution)/shard_map/ppermute | solution.py:560
  20.2 1.2 %near_tiles.1 = (bf16[192,128]{1,0:T(8,128)(2,1)S(1)}, bf16[208,128]{1,0:T(8,128)(2,1)S(1)}, bf16[400,128]{1,0:T(8,128)(2,1)S(1)}) custom-call(f32[1,128]{1,0:T(1,128)S(1)} %get-tuple-element.21.fracs_ref, s32[4,128]{1,0:T(4,128)S(1)} %get-tuple-element.22.tiles_ref, bf16[4,16,128]{2,1,0:T(8,128)(2,1)S(1)} %get-tuple-element.24.head_ref, ...), custom_call_target="tpu_custom_call" | custom-call | tf_op jit(solution)/shard_map/near_tiles/pallas_call | solution.py:672
  21.4 0.4 %collective-permute-start.9 = (bf16[208,128]{1,0:T(8,128)(2,1)S(1)}, bf16[208,128]{1,0:T(8,128)(2,1)S(1)}, u32[]{:S(2)}, u32[]{:S(2)}) collective-permute-start(bf16[208,128]{1,0:T(8,128)(2,1)S(1)} %get-tuple-element.35), channel_id=1, source_target_pairs={{0,1},{1,0},{2,3},{3,2},{4,5},{5,4},{6,7},{7,6},{8,9},{9,8},{10,11... | collective-permute-start | bytes 159752 | tf_op jit(solution)/shard_map/ppermute | solution.py:560
  21.8 0.2 collective-permute-start.8
  22.0 1.0 %collective-permute-done.8.refs_1_ = bf16[192,128]{1,0:T(8,128)(2,1)S(1)} collective-permute-done((bf16[192,128]{1,0:T(8,128)(2,1)S(1)}, bf16[192,128]{1,0:T(8,128)(2,1)S(1)}, u32[]{:S(2)}, u32[]{:S(2)}) %collective-permute-start.8) | collective-permute-done | bytes 49184 | tf_op jit(solution)/shard_map/ppermute | solution.py:560
  23.0 0.0 collective-permute-done.9.refs_2_
  23.0 0.7 %collective-permute-done.7.refs_0_ = bf16[400,128]{1,0:T(8,128)(2,1)S(1)} collective-permute-done((bf16[400,128]{1,0:T(8,128)(2,1)S(1)}, bf16[400,128]{1,0:T(8,128)(2,1)S(1)}, u32[]{:S(2)}, u32[]{:S(2)}) %collective-permute-start.7) | collective-permute-done | bytes 102432 | tf_op jit(solution)/shard_map/ppermute | solution.py:560
  23.8 0.3 %forcing.1.forcing_ref = f32[1024,128]{1,0:T(8,128)S(1)} custom-call(bf16[400,128]{1,0:T(8,128)(2,1)S(1)} %collective-permute-done.7.refs_0_, bf16[192,128]{1,0:T(8,128)(2,1)S(1)} %collective-permute-done.8.refs_1_, bf16[208,128]{1,0:T(8,128)(2,1)S(1)} %collective-permute-done.9.refs_2_, bf16[400,128]{1,0:T(8,128)(2,1)S(1)} %get-tuple-element.36.refs_3_, ...), custom_call_target="tpu_custom_call" | custom-call | tf_op jit(solution)/shard_map/forcing/pallas_call | solution.py:682
  24.1 1.9 %collective-permute-done.6.share_ref = bf16[400,128]{1,0:T(8,128)(2,1)S(1)} collective-permute-done((bf16[400,128]{1,0:T(8,128)(2,1)S(1)}, bf16[400,128]{1,0:T(8,128)(2,1)S(1)}, u32[]{:S(2)}, u32[]{:S(2)}) %collective-permute-start.6) | collective-permute-done | bytes 102432 | tf_op jit(solution)/shard_map/ppermute | solution.py:560
  26.0 0.0 copy-done
  26.0 1.5 %window_steps.1 = (bf16[32,32,128]{2,1,0:T(8,128)(2,1)}, f32[2,4096]{1,0:T(2,128)}) custom-call(bf16[400,128]{1,0:T(8,128)(2,1)S(1)} %collective-permute-done.6.share_ref, f32[1024,128]{1,0:T(8,128)S(1)} %forcing.1.forcing_ref, f32[160,128]{1,0:T(8,128)S(1)} %get-tuple-element.37.refs_4_.ready_ref, bf16[2,128,192]{2,1,0:T(8,128)(2,1)S(1)} %copy-done), custom_call_target="tpu_custom_call" | custom-call | tf_op jit(solution)/shard_map/window_steps/pallas_call | solution.py:693
Async XLA Ops:
  0.6 9.1 %collective-permute-start.2 = (s32[2,4]{1,0:T(2,128)}, s32[2,4]{1,0:T(2,128)S(1)}, u32[]{:S(2)}, u32[]{:S(2)}) collective-permute-start(s32[2,4]{1,0:T(2,128)} %bitcast.15), channel_id=1, source_target_pairs={{0,4},{4,12},{12,8},{8,0},{1,5},{5,13},{13,9},{9,1},{2,6},{6,14},{... | collective-permute-start | bytes 104 | tf_op jit(solution)/shard_map/ppermute | solution.py:565
  3.7 6.1 %collective-permute-start.1 = (s32[2,4]{1,0:T(2,128)}, s32[2,4]{1,0:T(2,128)S(1)}, u32[]{:S(2)}, u32[]{:S(2)}) collective-permute-start(s32[2,4]{1,0:T(2,128)} %bitcast.16), channel_id=1, source_target_pairs={{0,12},{4,8},{12,0},{8,4},{1,13},{5,9},{13,1},{9,5},{2,14},{6,10},... | collective-permute-start | bytes 104 | tf_op jit(solution)/shard_map/ppermute | solution.py:565
  6.2 3.8 %collective-permute-start = (s32[2,4]{1,0:T(2,128)}, s32[2,4]{1,0:T(2,128)S(1)}, u32[]{:S(2)}, u32[]{:S(2)}) collective-permute-start(s32[2,4]{1,0:T(2,128)} %bitcast.17), channel_id=1, source_target_pairs={{0,8},{4,0},{12,4},{8,12},{1,9},{5,1},{13,5},{9,13},{2,10},{6,2},{... | collective-permute-start | bytes 104 | tf_op jit(solution)/shard_map/ppermute | solution.py:565
  10.6 6.4 %collective-permute-start.3 = (bf16[2,32,128]{2,1,0:T(8,128)(2,1)S(1)}, bf16[2,32,128]{2,1,0:T(8,128)(2,1)S(1)}, u32[]{:S(2)}, u32[]{:S(2)}) collective-permute-start(bf16[2,32,128]{2,1,0:T(8,128)(2,1)S(1)} %get-tuple-element.27), channel_id=1, source_target_pairs={{0,12},{4,8},{8,4},{12,0},{1,13},{5,9},{9,5},{13,1},{2,14},{6,10},... | collective-permute-start | bytes 49160 | tf_op jit(solution)/shard_map/ppermute | solution.py:560
  12.5 4.7 %collective-permute-start.4 = (bf16[2,32,128]{2,1,0:T(8,128)(2,1)S(1)}, bf16[2,32,128]{2,1,0:T(8,128)(2,1)S(1)}, u32[]{:S(2)}, u32[]{:S(2)}) collective-permute-start(bf16[2,32,128]{2,1,0:T(8,128)(2,1)S(1)} %get-tuple-element.28), channel_id=1, source_target_pairs={{0,8},{4,12},{8,0},{12,4},{1,9},{5,13},{9,1},{13,5},{2,10},{6,14},... | collective-permute-start | bytes 49160 | tf_op jit(solution)/shard_map/ppermute | solution.py:560
  13.2 3.9 %collective-permute-start.5 = (bf16[2,32,128]{2,1,0:T(8,128)(2,1)S(1)}, bf16[2,32,128]{2,1,0:T(8,128)(2,1)S(1)}, u32[]{:S(2)}, u32[]{:S(2)}) collective-permute-start(bf16[2,32,128]{2,1,0:T(8,128)(2,1)S(1)} %get-tuple-element.29), channel_id=1, source_target_pairs={{0,4},{4,0},{8,12},{12,8},{1,5},{5,1},{9,13},{13,9},{2,6},{6,2},{1... | collective-permute-start | bytes 49160 | tf_op jit(solution)/shard_map/ppermute | solution.py:560
  18.5 7.5 %copy-start = (bf16[2,128,192]{2,1,0:T(8,128)(2,1)S(1)}, bf16[2,128,192]{2,1,0:T(8,128)(2,1)}, u32[]{:S(2)}) copy-start(bf16[2,128,192]{2,1,0:T(8,128)(2,1)} %constant.8.clone.fit_ref) | copy-start | bytes 294916
  18.6 5.2 %collective-permute-start.7 = (bf16[400,128]{1,0:T(8,128)(2,1)S(1)}, bf16[400,128]{1,0:T(8,128)(2,1)S(1)}, u32[]{:S(2)}, u32[]{:S(2)}) collective-permute-start(bf16[400,128]{1,0:T(8,128)(2,1)S(1)} %get-tuple-element.31), channel_id=1, source_target_pairs={{0,3},{1,2},{2,1},{3,0},{4,7},{5,6},{6,5},{7,4},{8,11},{9,10},{10,... | collective-permute-start | bytes 307208 | tf_op jit(solution)/shard_map/ppermute | solution.py:560
  18.6 7.4 %collective-permute-start.6 = (bf16[400,128]{1,0:T(8,128)(2,1)S(1)}, bf16[400,128]{1,0:T(8,128)(2,1)S(1)}, u32[]{:S(2)}, u32[]{:S(2)}) collective-permute-start(bf16[400,128]{1,0:T(8,128)(2,1)S(1)} %get-tuple-element.30), channel_id=1, source_target_pairs={{0,2},{1,3},{2,0},{3,1},{4,6},{5,7},{6,4},{7,5},{8,10},{9,11},{10,... | collective-permute-start | bytes 307208 | tf_op jit(solution)/shard_map/ppermute | solution.py:560
  21.4 1.6 %collective-permute-start.9 = (bf16[208,128]{1,0:T(8,128)(2,1)S(1)}, bf16[208,128]{1,0:T(8,128)(2,1)S(1)}, u32[]{:S(2)}, u32[]{:S(2)}) collective-permute-start(bf16[208,128]{1,0:T(8,128)(2,1)S(1)} %get-tuple-element.35), channel_id=1, source_target_pairs={{0,1},{1,0},{2,3},{3,2},{4,5},{5,4},{6,7},{7,6},{8,9},{9,8},{10,11... | collective-permute-start | bytes 159752 | tf_op jit(solution)/shard_map/ppermute | solution.py:560
  21.8 1.2 %collective-permute-start.8 = (bf16[192,128]{1,0:T(8,128)(2,1)S(1)}, bf16[192,128]{1,0:T(8,128)(2,1)S(1)}, u32[]{:S(2)}, u32[]{:S(2)}) collective-permute-start(bf16[192,128]{1,0:T(8,128)(2,1)S(1)} %get-tuple-element.34), channel_id=1, source_target_pairs={{0,1},{1,0},{2,3},{3,2},{4,5},{5,4},{6,7},{7,6},{8,9},{9,8},{10,11... | collective-permute-start | bytes 147464 | tf_op jit(solution)/shard_map/ppermute | solution.py:560

commit v16 on v15

--- a/solution.py
+++ b/solution.py
@@ -16,7 +16,6 @@
 LENGTH = SEGS * STEPS
 GROUP = 4
 HEAD = 16
-LAST = 2
 PITCH = STEPS // 2 + 1
 CHUNKS = 8
 UNROLL = 4
@@ -54,7 +53,7 @@
 
 def fit_table(coef_count):
     scales = np.where(np.arange(coef_count)[:, None] == 0, 1.0, 2.0) / STEPS
-    fit = (basis_table(coef_count, STEPS) * scales).astype(np.float32)
+    fit = (basis_table(coef_count, STEPS) * scales / (excite_excite / 2)).astype(np.float32)
     half = STEPS // 2
     tables = []
     for i in range(2):
@@ -129,10 +128,7 @@
         rank = jnp.dot(below, held[part].astype(jnp.bfloat16), preferred_element_type=jnp.float32)
         ranks = ranks + jnp.sum(hits[part] * rank[:, :tile_count], axis=0, keepdims=True)
         rank = jnp.where(held[part] > 0.5, rank, -1.0)
-        source = place ^ p
-        source = jnp.where(
-            source == LAST, 0, (peers - 1) - source + jnp.where(source > LAST, 1, 0)
-        ).astype(jnp.float32)
+        source = ((peers - 1) - (place ^ p)).astype(jnp.float32)
         rows = []
         for h in range(head_rows):
             match = rank == lanes[0, h : h + 1, :]
@@ -407,14 +403,14 @@
 
 
 def forcing_kernel(*refs, peers, own_blocks, peer_targets):
-    shares = {r: (ref,) for r, ref in zip(range(LAST + 1, peers), refs)}
+    shares = {r: (ref,) for r, ref in zip(range(2, peers - 1), refs)}
     shares |= {1: refs[peers - 3 : peers - 1], 0: (refs[peers - 1],)}
     ready_ref, out_ref = refs[peers:]
     block_rows = ready_ref.shape[1]
     width = TOGETHER * peer_targets
     head = sum(share[-1][-HEAD:, :].astype(jnp.float32) for share in shares.values())
     scatter = one_hot(head, TOGETHER * own_blocks, peers * width)
-    stack = [shares[r] for r in (0, *range(peers - 1, LAST, -1), *range(LAST - 1, -1, -1))]
+    stack = [shares[r] for r in (0, *range(peers - 2, -1, -1))]
     gain, counts = [
         0.5 * ready_ref[i * own_blocks : (i + 1) * own_blocks, :] for i in (2, 3)
     ]
@@ -499,7 +495,7 @@
             inhibit = ((1 - inhibit_rate) * inhibit + inhibit_rate / 2) + (
                 inhibit_rate / 2
             ) * inhibit_turn
-            samples[pair // 2][pl.ds(jj, own_blocks, stride=PITCH), :] = carried * (1 / a)
+            samples[pair // 2][pl.ds(jj, own_blocks, stride=PITCH), :] = carried
         fitted[pair // 2] = fit_half(samples[pair // 2], fit_ref[pair // 2])
     rates[0] = carried * (1 / a)
     rates[1] = inhibit
@@ -688,7 +684,7 @@
         out_specs=vmem_spec,
         compiler_params=params(),
         name="forcing",
-    )(*[sent[r] for r in range(LAST + 1, peers)], *pair, own, ready)
+    )(*[sent[r] for r in range(2, peers - 1)], *pair, own, ready)
 
     new_coefs, final_state = pl.pallas_call(
         functools.partial(
@@ -711,7 +707,7 @@
         ],
         compiler_params=params(),
         name="window_steps",
-    )(sent[LAST], forcing, ready, jnp.asarray(fit_table(coef_count)))
+    )(sent[peers - 1], forcing, ready, jnp.asarray(fit_table(coef_count)))
     return new_coefs, final_state
 
 

time: 27.7 us -> 27 us (0.975)
  waiting for transfers between devices: 4.02 us -> 3.17 us
    ppermute x7, waiting for transfers between devices: 3.82 us -> 2.97 us  [swap(): lax.ppermute(x, axis, [(i, i ^ r) for i in range(lax.axis_size(axis))])]
where the time goes in v16:
time: 27 us; the launch traced here: 26.8 us
  starting transfers between devices  13.9 us (51%)
  Pallas kernels  8.98 us (33%)
  waiting for transfers between devices  3.17 us (12%)
  between operations  0.72 us (3%)
    ppermute x3, starting transfers between devices, local(): lax.ppermute(reads, 'wide', [(ring[k], ring[(k + r) % wide_peers]) for k...  7.13 us
    ppermute x7, starting transfers between devices, swap(): lax.ppermute(x, axis, [(i, i ^ r) for i in range(lax.axis_size(axis))])  6.8 us
    ppermute x7, waiting for transfers between devices, swap(): lax.ppermute(x, axis, [(i, i ^ r) for i in range(lax.axis_size(axis))])  2.97 us
    pallas_call x1, Pallas kernels, local(): pl.pallas_call(near_kernel, out_shape=[pltpu.VMEM(fresh_coefs.shape, jnp....  1.98 us
    pallas_call x1, Pallas kernels, local(): pl.pallas_call(functools.partial(prepare_kernel, peers=peers, own_blocks=...  1.94 us
    pallas_call x1, Pallas kernels, local(): pl.pallas_call(functools.partial(window_kernel, own_blocks=own_blocks, pe...  1.51 us
    pallas_call x1, Pallas kernels, local(): pl.pallas_call(functools.partial(far_kernel, wide_peers=wide_peers, peers...  1.41 us
    pallas_call x1, Pallas kernels, local(): pl.pallas_call(functools.partial(near_tiles_kernel, peers=peers, peer_tar...  1.22 us
  transfers between devices with their start and end apart: 10, of which 5 were waited for; matrix products, arithmetic and copies ran while one was open for 0% of the time, Pallas kernels for 20%

profile of v16, /device:TPU:0, one launch (start us, length us, event | category | flops | bytes accessed | tf_op | source)
XLA Modules:
  0.0 26.8 jit_solution(5906317172641885040)
XLA Ops:
  0.6 3.1 %collective-permute-start.2 = (s32[2,4]{1,0:T(2,128)}, s32[2,4]{1,0:T(2,128)S(1)}, u32[]{:S(2)}, u32[]{:S(2)}) collective-permute-start(s32[2,4]{1,0:T(2,128)} %bitcast.15), channel_id=1, source_target_pairs={{0,4},{4,12},{12,8},{8,0},{1,5},{5,13},{13,9},{9,1},{2,6},{6,14},{... | collective-permute-start | bytes 104 | tf_op jit(solution)/shard_map/ppermute | solution.py:561
  3.7 2.5 %collective-permute-start.1 = (s32[2,4]{1,0:T(2,128)}, s32[2,4]{1,0:T(2,128)S(1)}, u32[]{:S(2)}, u32[]{:S(2)}) collective-permute-start(s32[2,4]{1,0:T(2,128)} %bitcast.16), channel_id=1, source_target_pairs={{0,12},{4,8},{12,0},{8,4},{1,13},{5,9},{13,1},{9,5},{2,14},{6,10},... | collective-permute-start | bytes 104 | tf_op jit(solution)/shard_map/ppermute | solution.py:561
  6.2 1.6 %collective-permute-start = (s32[2,4]{1,0:T(2,128)}, s32[2,4]{1,0:T(2,128)S(1)}, u32[]{:S(2)}, u32[]{:S(2)}) collective-permute-start(s32[2,4]{1,0:T(2,128)} %bitcast.17), channel_id=1, source_target_pairs={{0,8},{4,0},{12,4},{8,12},{1,9},{5,1},{13,5},{9,13},{2,10},{6,2},{... | collective-permute-start | bytes 104 | tf_op jit(solution)/shard_map/ppermute | solution.py:561
  7.8 2.0 %near.1 = (bf16[32,32,128]{2,1,0:T(8,128)(2,1)S(1)}, bf16[96,128,128]{2,1,0:T(8,128)(2,1)S(1)}) custom-call(bf16[32,32,128]{2,1,0:T(8,128)(2,1)} %fresh_hbm.1, bf16[96,128,128]{2,1,0:T(8,128)(2,1)} %bitcast.12), custom_call_target="tpu_custom_call" | custom-call | tf_op jit(solution)/shard_map/near/pallas_call | solution.py:579
  9.7 0.0 collective-permute-done.2.refs_2_
  9.8 0.0 collective-permute-done.1.refs_1_
  9.8 0.2 collective-permute-done.refs_0_
  10.0 0.6 %pick_blocks.1 = (bf16[2,32,128]{2,1,0:T(8,128)(2,1)S(1)}, bf16[2,32,128]{2,1,0:T(8,128)(2,1)S(1)}, bf16[2,32,128]{2,1,0:T(8,128)(2,1)S(1)}) custom-call(s32[2,4]{1,0:T(2,128)S(1)} %collective-permute-done.refs_0_, s32[2,4]{1,0:T(2,128)S(1)} %collective-permute-done.1.refs_1_, s32[2,4]{1,0:T(2,128)S(1)} %collective-permute-done.2.refs_2_, ...), custom_call_target="tpu_custom_call" | custom-call | tf_op jit(solution)/shard_map/pick_blocks/pallas_call | solution.py:629
  10.6 1.9 %collective-permute-start.3 = (bf16[2,32,128]{2,1,0:T(8,128)(2,1)S(1)}, bf16[2,32,128]{2,1,0:T(8,128)(2,1)S(1)}, u32[]{:S(2)}, u32[]{:S(2)}) collective-permute-start(bf16[2,32,128]{2,1,0:T(8,128)(2,1)S(1)} %get-tuple-element.27), channel_id=1, source_target_pairs={{0,12},{4,8},{8,4},{12,0},{1,13},{5,9},{9,5},{13,1},{2,14},{6,10},... | collective-permute-start | bytes 49160 | tf_op jit(solution)/shard_map/ppermute | solution.py:556
  12.5 0.8 %collective-permute-start.4 = (bf16[2,32,128]{2,1,0:T(8,128)(2,1)S(1)}, bf16[2,32,128]{2,1,0:T(8,128)(2,1)S(1)}, u32[]{:S(2)}, u32[]{:S(2)}) collective-permute-start(bf16[2,32,128]{2,1,0:T(8,128)(2,1)S(1)} %get-tuple-element.28), channel_id=1, source_target_pairs={{0,8},{4,12},{8,0},{12,4},{1,9},{5,13},{9,1},{13,5},{2,10},{6,14},... | collective-permute-start | bytes 49160 | tf_op jit(solution)/shard_map/ppermute | solution.py:556
  13.2 1.8 %collective-permute-start.5 = (bf16[2,32,128]{2,1,0:T(8,128)(2,1)S(1)}, bf16[2,32,128]{2,1,0:T(8,128)(2,1)S(1)}, u32[]{:S(2)}, u32[]{:S(2)}) collective-permute-start(bf16[2,32,128]{2,1,0:T(8,128)(2,1)S(1)} %get-tuple-element.29), channel_id=1, source_target_pairs={{0,4},{4,0},{8,12},{12,8},{1,5},{5,1},{9,13},{13,9},{2,6},{6,2},{1... | collective-permute-start | bytes 49160 | tf_op jit(solution)/shard_map/ppermute | solution.py:556
  15.0 1.9 %prepare.1 = (f32[160,128]{1,0:T(8,128)S(1)}, f32[768,128]{1,0:T(8,128)S(1)}, s32[4,128]{1,0:T(4,128)S(1)}, f32[1,128]{1,0:T(1,128)S(1)}, bf16[4,16,128]{2,1,0:T(8,128)(2,1)S(1)}, /*index=5*/bf16[96,96]{1,0:T(8,128)(2,1)S(1)}) custom-call(bf16[32,32,128]{2,1,0:T(8,128)(2,1)S(1)} %get-tuple-element.20.fresh_ref.refs_3_, s32[2,4]{1,0:T(2,128)} %bitcast.18, ...), custom_call_target="tpu_custom_call" | custom-call | tf_op jit(solution)/shard_map/prepare/pallas_call | solution.py:591
  17.0 0.0 collective-permute-done.3.refs_0_
  17.0 0.1 collective-permute-done.4.refs_1_
  17.1 0.0 collective-permute-done.5.refs_2_
  17.1 1.4 %far_tiles.1 = (bf16[400,128]{1,0:T(8,128)(2,1)S(1)}, bf16[400,128]{1,0:T(8,128)(2,1)S(1)}, f32[768,128]{1,0:T(8,128)S(1)}, f32[1568,128]{1,0:T(8,128)S(1)}) custom-call(f32[1,128]{1,0:T(1,128)S(1)} %get-tuple-element.21.fracs_ref, s32[4,128]{1,0:T(4,128)S(1)} %get-tuple-element.22.tiles_ref, bf16[96,96]{1,0:T(8,128)(2,1)S(1)} %get-tuple-element.23.table_ref, ...), custom_call_target="tpu_custom_call" | custom-call | tf_op jit(solution)/shard_map/far_tiles/pallas_call | solution.py:649
  18.5 0.0 copy-start
  18.6 1.6 %collective-permute-start.7 = (bf16[400,128]{1,0:T(8,128)(2,1)S(1)}, bf16[400,128]{1,0:T(8,128)(2,1)S(1)}, u32[]{:S(2)}, u32[]{:S(2)}) collective-permute-start(bf16[400,128]{1,0:T(8,128)(2,1)S(1)} %get-tuple-element.31), channel_id=1, source_target_pairs={{0,2},{1,3},{2,0},{3,1},{4,6},{5,7},{6,4},{7,5},{8,10},{9,11},{10,... | collective-permute-start | bytes 307208 | tf_op jit(solution)/shard_map/ppermute | solution.py:556
  20.1 0.0 collective-permute-start.6
  20.1 1.2 %near_tiles.1 = (bf16[192,128]{1,0:T(8,128)(2,1)S(1)}, bf16[208,128]{1,0:T(8,128)(2,1)S(1)}, bf16[400,128]{1,0:T(8,128)(2,1)S(1)}) custom-call(f32[1,128]{1,0:T(1,128)S(1)} %get-tuple-element.21.fracs_ref, s32[4,128]{1,0:T(4,128)S(1)} %get-tuple-element.22.tiles_ref, bf16[4,16,128]{2,1,0:T(8,128)(2,1)S(1)} %get-tuple-element.24.head_ref, ...), custom_call_target="tpu_custom_call" | custom-call | tf_op jit(solution)/shard_map/near_tiles/pallas_call | solution.py:668
  21.3 0.7 %collective-permute-start.9 = (bf16[208,128]{1,0:T(8,128)(2,1)S(1)}, bf16[208,128]{1,0:T(8,128)(2,1)S(1)}, u32[]{:S(2)}, u32[]{:S(2)}) collective-permute-start(bf16[208,128]{1,0:T(8,128)(2,1)S(1)} %get-tuple-element.35), channel_id=1, source_target_pairs={{0,1},{1,0},{2,3},{3,2},{4,5},{5,4},{6,7},{7,6},{8,9},{9,8},{10,11... | collective-permute-start | bytes 159752 | tf_op jit(solution)/shard_map/ppermute | solution.py:556
  22.1 0.1 collective-permute-start.8
  22.1 1.2 %collective-permute-done.8.refs_1_ = bf16[192,128]{1,0:T(8,128)(2,1)S(1)} collective-permute-done((bf16[192,128]{1,0:T(8,128)(2,1)S(1)}, bf16[192,128]{1,0:T(8,128)(2,1)S(1)}, u32[]{:S(2)}, u32[]{:S(2)}) %collective-permute-start.8) | collective-permute-done | bytes 49184 | tf_op jit(solution)/shard_map/ppermute | solution.py:556
  23.3 0.0 collective-permute-done.9.refs_2_
  23.3 0.2 collective-permute-done.7.refs_0_
  23.5 0.3 %forcing.1.forcing_ref = f32[1024,128]{1,0:T(8,128)S(1)} custom-call(bf16[400,128]{1,0:T(8,128)(2,1)S(1)} %collective-permute-done.7.refs_0_, bf16[192,128]{1,0:T(8,128)(2,1)S(1)} %collective-permute-done.8.refs_1_, bf16[208,128]{1,0:T(8,128)(2,1)S(1)} %collective-permute-done.9.refs_2_, bf16[400,128]{1,0:T(8,128)(2,1)S(1)} %get-tuple-element.36.refs_3_, ...), custom_call_target="tpu_custom_call" | custom-call | tf_op jit(solution)/shard_map/forcing/pallas_call | solution.py:678
  23.8 1.5 %collective-permute-done.6.share_ref = bf16[400,128]{1,0:T(8,128)(2,1)S(1)} collective-permute-done((bf16[400,128]{1,0:T(8,128)(2,1)S(1)}, bf16[400,128]{1,0:T(8,128)(2,1)S(1)}, u32[]{:S(2)}, u32[]{:S(2)}) %collective-permute-start.6) | collective-permute-done | bytes 102432 | tf_op jit(solution)/shard_map/ppermute | solution.py:556
  25.3 0.0 copy-done
  25.3 1.5 %window_steps.1 = (bf16[32,32,128]{2,1,0:T(8,128)(2,1)}, f32[2,4096]{1,0:T(2,128)}) custom-call(bf16[400,128]{1,0:T(8,128)(2,1)S(1)} %collective-permute-done.6.share_ref, f32[1024,128]{1,0:T(8,128)S(1)} %forcing.1.forcing_ref, f32[160,128]{1,0:T(8,128)S(1)} %get-tuple-element.37.refs_4_.ready_ref, bf16[2,128,192]{2,1,0:T(8,128)(2,1)S(1)} %copy-done), custom_call_target="tpu_custom_call" | custom-call | tf_op jit(solution)/shard_map/window_steps/pallas_call | solution.py:689
Async XLA Ops:
  0.6 9.1 %collective-permute-start.2 = (s32[2,4]{1,0:T(2,128)}, s32[2,4]{1,0:T(2,128)S(1)}, u32[]{:S(2)}, u32[]{:S(2)}) collective-permute-start(s32[2,4]{1,0:T(2,128)} %bitcast.15), channel_id=1, source_target_pairs={{0,4},{4,12},{12,8},{8,0},{1,5},{5,13},{13,9},{9,1},{2,6},{6,14},{... | collective-permute-start | bytes 104 | tf_op jit(solution)/shard_map/ppermute | solution.py:561
  3.7 6.1 %collective-permute-start.1 = (s32[2,4]{1,0:T(2,128)}, s32[2,4]{1,0:T(2,128)S(1)}, u32[]{:S(2)}, u32[]{:S(2)}) collective-permute-start(s32[2,4]{1,0:T(2,128)} %bitcast.16), channel_id=1, source_target_pairs={{0,12},{4,8},{12,0},{8,4},{1,13},{5,9},{13,1},{9,5},{2,14},{6,10},... | collective-permute-start | bytes 104 | tf_op jit(solution)/shard_map/ppermute | solution.py:561
  6.2 3.8 %collective-permute-start = (s32[2,4]{1,0:T(2,128)}, s32[2,4]{1,0:T(2,128)S(1)}, u32[]{:S(2)}, u32[]{:S(2)}) collective-permute-start(s32[2,4]{1,0:T(2,128)} %bitcast.17), channel_id=1, source_target_pairs={{0,8},{4,0},{12,4},{8,12},{1,9},{5,1},{13,5},{9,13},{2,10},{6,2},{... | collective-permute-start | bytes 104 | tf_op jit(solution)/shard_map/ppermute | solution.py:561
  10.6 6.4 %collective-permute-start.3 = (bf16[2,32,128]{2,1,0:T(8,128)(2,1)S(1)}, bf16[2,32,128]{2,1,0:T(8,128)(2,1)S(1)}, u32[]{:S(2)}, u32[]{:S(2)}) collective-permute-start(bf16[2,32,128]{2,1,0:T(8,128)(2,1)S(1)} %get-tuple-element.27), channel_id=1, source_target_pairs={{0,12},{4,8},{8,4},{12,0},{1,13},{5,9},{9,5},{13,1},{2,14},{6,10},... | collective-permute-start | bytes 49160 | tf_op jit(solution)/shard_map/ppermute | solution.py:556
  12.5 4.7 %collective-permute-start.4 = (bf16[2,32,128]{2,1,0:T(8,128)(2,1)S(1)}, bf16[2,32,128]{2,1,0:T(8,128)(2,1)S(1)}, u32[]{:S(2)}, u32[]{:S(2)}) collective-permute-start(bf16[2,32,128]{2,1,0:T(8,128)(2,1)S(1)} %get-tuple-element.28), channel_id=1, source_target_pairs={{0,8},{4,12},{8,0},{12,4},{1,9},{5,13},{9,1},{13,5},{2,10},{6,14},... | collective-permute-start | bytes 49160 | tf_op jit(solution)/shard_map/ppermute | solution.py:556
  13.2 3.9 %collective-permute-start.5 = (bf16[2,32,128]{2,1,0:T(8,128)(2,1)S(1)}, bf16[2,32,128]{2,1,0:T(8,128)(2,1)S(1)}, u32[]{:S(2)}, u32[]{:S(2)}) collective-permute-start(bf16[2,32,128]{2,1,0:T(8,128)(2,1)S(1)} %get-tuple-element.29), channel_id=1, source_target_pairs={{0,4},{4,0},{8,12},{12,8},{1,5},{5,1},{9,13},{13,9},{2,6},{6,2},{1... | collective-permute-start | bytes 49160 | tf_op jit(solution)/shard_map/ppermute | solution.py:556
  18.5 6.7 %copy-start = (bf16[2,128,192]{2,1,0:T(8,128)(2,1)S(1)}, bf16[2,128,192]{2,1,0:T(8,128)(2,1)}, u32[]{:S(2)}) copy-start(bf16[2,128,192]{2,1,0:T(8,128)(2,1)} %constant.8.clone.fit_ref) | copy-start | bytes 294916
  18.6 4.9 %collective-permute-start.7 = (bf16[400,128]{1,0:T(8,128)(2,1)S(1)}, bf16[400,128]{1,0:T(8,128)(2,1)S(1)}, u32[]{:S(2)}, u32[]{:S(2)}) collective-permute-start(bf16[400,128]{1,0:T(8,128)(2,1)S(1)} %get-tuple-element.31), channel_id=1, source_target_pairs={{0,2},{1,3},{2,0},{3,1},{4,6},{5,7},{6,4},{7,5},{8,10},{9,11},{10,... | collective-permute-start | bytes 307208 | tf_op jit(solution)/shard_map/ppermute | solution.py:556
  20.1 5.2 %collective-permute-start.6 = (bf16[400,128]{1,0:T(8,128)(2,1)S(1)}, bf16[400,128]{1,0:T(8,128)(2,1)S(1)}, u32[]{:S(2)}, u32[]{:S(2)}) collective-permute-start(bf16[400,128]{1,0:T(8,128)(2,1)S(1)} %get-tuple-element.30), channel_id=1, source_target_pairs={{0,3},{1,2},{2,1},{3,0},{4,7},{5,6},{6,5},{7,4},{8,11},{9,10},{10,... | collective-permute-start | bytes 307208 | tf_op jit(solution)/shard_map/ppermute | solution.py:556
  21.3 1.9 %collective-permute-start.9 = (bf16[208,128]{1,0:T(8,128)(2,1)S(1)}, bf16[208,128]{1,0:T(8,128)(2,1)S(1)}, u32[]{:S(2)}, u32[]{:S(2)}) collective-permute-start(bf16[208,128]{1,0:T(8,128)(2,1)S(1)} %get-tuple-element.35), channel_id=1, source_target_pairs={{0,1},{1,0},{2,3},{3,2},{4,5},{5,4},{6,7},{7,6},{8,9},{9,8},{10,11... | collective-permute-start | bytes 159752 | tf_op jit(solution)/shard_map/ppermute | solution.py:556
  22.1 1.2 %collective-permute-start.8 = (bf16[192,128]{1,0:T(8,128)(2,1)S(1)}, bf16[192,128]{1,0:T(8,128)(2,1)S(1)}, u32[]{:S(2)}, u32[]{:S(2)}) collective-permute-start(bf16[192,128]{1,0:T(8,128)(2,1)S(1)} %get-tuple-element.34), channel_id=1, source_target_pairs={{0,1},{1,0},{2,3},{3,2},{4,5},{5,4},{6,7},{7,6},{8,9},{9,8},{10,11... | collective-permute-start | bytes 147464 | tf_op jit(solution)/shard_map/ppermute | solution.py:556

commit v17 on v16

--- a/solution.py
+++ b/solution.py
@@ -152,7 +152,7 @@
     chosen = jnp.where(position == lane, 1.0, 0.0)
     starts = (slot[...] * LENGTH + (LENGTH - 1) - delay[...]).astype(jnp.float32)
     index = lax.broadcasted_iota(jnp.int32, (1, tile_count), 1).astype(jnp.float32)
-    firsts = (key_row * float(peer_targets) + ranks) * float(TOGETHER)
+    firsts = key_row * float(peer_targets) + ranks
     facts = jnp.concatenate(
         [index, starts, firsts, frac[...], jnp.zeros((4, tile_count), jnp.float32)], axis=0
     )
@@ -160,10 +160,10 @@
         facts, chosen, precision=lax.Precision.HIGHEST, preferred_element_type=jnp.float32
     )
     fracs_out[...] = ordered[3:4, :]
-    tiles_out[0:3, :] = (ordered[0:3, :] + 0.5).astype(jnp.int32)
-    tiles_out[3:4, :] = jnp.sum(
-        jnp.where(key < lane, 1.0, 0.0), axis=0, keepdims=True
-    ).astype(jnp.int32)
+    ints = (ordered + 0.5).astype(jnp.int32)
+    packed = ints[1:2, :] * (1 << 16) + ints[0:1, :] * (1 << 8) + ints[2:3, :]
+    before = jnp.sum(jnp.where(key < lane - float(tile_count), 1.0, 0.0), axis=0, keepdims=True)
+    tiles_out[...] = jnp.where(lane[0:1, :] < tile_count, packed, before.astype(jnp.int32))
 
     for copy in copies[5:7]:
         copy.wait()
@@ -256,16 +256,20 @@
             outs[distance - 1][c] = fresh[block]
 
 
+def row_of(tiles, t):
+    return (tiles[0, t] & 255) * TOGETHER
+
+
 def add_tiles(tiles, frac, hist, weights, total, pitch, items):
     block_rows = weights.shape[2]
     rows = []
     for t, _ in items:
         fraction = frac[0, t]
-        start = tiles[1, t]
+        start = lax.shift_right_logical(tiles[0, t], 16)
         earlier = hist[pl.ds(start, STEPS), :]
         later = hist[pl.ds(start + 1, STEPS), :]
         rows.append(((1.0 - fraction) * later + fraction * earlier).astype(jnp.bfloat16))
-    tile = [weights[tiles[0, t]] for t, _ in items]
+    tile = [weights[lax.shift_right_logical(tiles[0, t], 8) & 255] for t, _ in items]
     none = jnp.zeros((2 * STEPS, block_rows), jnp.bfloat16)
     product = lax.dot_general(
         jnp.concatenate(
@@ -335,14 +339,14 @@
     spare = peers * span
     pitch = spare + TOGETHER
     for t in range(0, fixed, UNROLL):
-        items = [(u, tiles[2, u]) for u in range(t, t + UNROLL)]
+        items = [(u, row_of(tiles, u)) for u in range(t, t + UNROLL)]
         add_tiles(tiles, frac, hist, weights, total, pitch, items)
-    far_count = tiles[3, peers - 2]
+    far_count = tiles[0, weights.shape[0] + peers - 2]
 
     @pl.loop(0, lax.div(jnp.maximum(far_count - fixed, 0) + (UNROLL - 1), UNROLL))
     def _(turn):
         places = [fixed + turn * UNROLL + u for u in range(UNROLL)]
-        items = [(t, jnp.where(t < far_count, tiles[2, t], spare)) for t in places]
+        items = [(t, jnp.where(t < far_count, row_of(tiles, t), spare)) for t in places]
         add_tiles(tiles, frac, hist, weights, total, pitch, items)
 
     for part, out in enumerate(outs):
@@ -367,10 +371,10 @@
     span = peer_targets * TOGETHER
     spare = peers * span
     pitch = spare + TOGETHER
-    far_count = tiles[3, peers - 2]
+    far_count = tiles[0, weights.shape[0] + peers - 2]
     for t in range(fixed, weights.shape[0], UNROLL):
         items = [
-            (u, jnp.where(u < far_count, spare, tiles[2, u])) for u in range(t, t + UNROLL)
+            (u, jnp.where(u < far_count, spare, row_of(tiles, u))) for u in range(t, t + UNROLL)
         ]
         add_tiles(tiles, frac, hist, weights, total, pitch, items)
     write_share(pair, total, head_ref[place ^ 1], (peers - 2) * span, span, pitch)
@@ -596,7 +600,7 @@
         out_shape=[
             pltpu.VMEM((4 * own_blocks + STEPS, block_rows), jnp.float32),
             pltpu.VMEM((slot_count * LENGTH, block_rows), jnp.float32),
-            pltpu.VMEM((4, 128), jnp.int32),
+            pltpu.VMEM((1, 128), jnp.int32),
             pltpu.VMEM((1, 128), jnp.float32),
             pltpu.VMEM((peers, HEAD, 128), jnp.bfloat16),
             pltpu.VMEM((LENGTH, SEGS * coef_count), jnp.bfloat16),
@@ -645,7 +649,7 @@
     fixed = min(tile_count, -(-fixed // UNROLL) * UNROLL)
     share = pltpu.VMEM((share_rows, block_rows), jnp.bfloat16)
     total = pltpu.VMEM(((peers * peer_targets + 1) * STEPS, block_rows), jnp.float32)
-    scalars = [SMEM((4, 128), jnp.int32), SMEM((1, 128), jnp.float32)]
+    scalars = [SMEM((1, 128), jnp.int32), SMEM((1, 128), jnp.float32)]
     *shares, hist, sums = pl.pallas_call(
         functools.partial(
             far_kernel,
@@ -698,8 +702,8 @@
         in_specs=[vmem_spec] * 4,
         out_specs=[hbm_spec] * 2,
         scratch_shapes=[
-            VMEM((own_blocks * PITCH, block_rows), jnp.float32),
-            VMEM((own_blocks * PITCH, block_rows), jnp.float32),
+            VMEM(((own_blocks + 1) * PITCH, block_rows), jnp.float32),
+            VMEM(((own_blocks + 1) * PITCH, block_rows), jnp.float32),
             VMEM((2, own_blocks, block_rows), jnp.float32),
             VMEM(fresh_coefs.shape, jnp.bfloat16),
             VMEM(state.shape, jnp.float32),

time: 27 us -> 26.9 us (level)
  no operation moved by 1% of the time
where the time goes in v17:
time: 26.9 us; the launch traced here: 26.8 us
  starting transfers between devices  13.9 us (52%)
  Pallas kernels  8.93 us (33%)
  waiting for transfers between devices  3.2 us (12%)
  between operations  0.72 us (3%)
    ppermute x3, starting transfers between devices, local(): lax.ppermute(reads, 'wide', [(ring[k], ring[(k + r) % wide_peers]) for k...  7.13 us
    ppermute x7, starting transfers between devices, swap(): lax.ppermute(x, axis, [(i, i ^ r) for i in range(lax.axis_size(axis))])  6.8 us
    ppermute x7, waiting for transfers between devices, swap(): lax.ppermute(x, axis, [(i, i ^ r) for i in range(lax.axis_size(axis))])  3 us
    pallas_call x1, Pallas kernels, local(): pl.pallas_call(near_kernel, out_shape=[pltpu.VMEM(fresh_coefs.shape, jnp....  1.98 us
    pallas_call x1, Pallas kernels, local(): pl.pallas_call(functools.partial(prepare_kernel, peers=peers, own_blocks=...  1.94 us
    pallas_call x1, Pallas kernels, local(): pl.pallas_call(functools.partial(window_kernel, own_blocks=own_blocks, pe...  1.51 us
    pallas_call x1, Pallas kernels, local(): pl.pallas_call(functools.partial(far_kernel, wide_peers=wide_peers, peers...  1.37 us
    pallas_call x1, Pallas kernels, local(): pl.pallas_call(functools.partial(near_tiles_kernel, peers=peers, peer_tar...  1.2 us
  transfers between devices with their start and end apart: 10, of which 5 were waited for; matrix products, arithmetic and copies ran while one was open for 0% of the time, Pallas kernels for 20%

profile of v17, /device:TPU:0, one launch (start us, length us, event | category | flops | bytes accessed | tf_op | source)
XLA Modules:
  0.0 26.8 jit_solution(2717975487472457848)
XLA Ops:
  0.6 3.1 %collective-permute-start.2 = (s32[2,4]{1,0:T(2,128)}, s32[2,4]{1,0:T(2,128)S(1)}, u32[]{:S(2)}, u32[]{:S(2)}) collective-permute-start(s32[2,4]{1,0:T(2,128)} %bitcast.15), channel_id=1, source_target_pairs={{0,4},{4,12},{12,8},{8,0},{1,5},{5,13},{13,9},{9,1},{2,6},{6,14},{... | collective-permute-start | bytes 104 | tf_op jit(solution)/shard_map/ppermute | solution.py:565
  3.7 2.5 %collective-permute-start.1 = (s32[2,4]{1,0:T(2,128)}, s32[2,4]{1,0:T(2,128)S(1)}, u32[]{:S(2)}, u32[]{:S(2)}) collective-permute-start(s32[2,4]{1,0:T(2,128)} %bitcast.16), channel_id=1, source_target_pairs={{0,12},{4,8},{12,0},{8,4},{1,13},{5,9},{13,1},{9,5},{2,14},{6,10},... | collective-permute-start | bytes 104 | tf_op jit(solution)/shard_map/ppermute | solution.py:565
  6.2 1.6 %collective-permute-start = (s32[2,4]{1,0:T(2,128)}, s32[2,4]{1,0:T(2,128)S(1)}, u32[]{:S(2)}, u32[]{:S(2)}) collective-permute-start(s32[2,4]{1,0:T(2,128)} %bitcast.17), channel_id=1, source_target_pairs={{0,8},{4,0},{12,4},{8,12},{1,9},{5,1},{13,5},{9,13},{2,10},{6,2},{... | collective-permute-start | bytes 104 | tf_op jit(solution)/shard_map/ppermute | solution.py:565
  7.8 2.0 %near.1 = (bf16[32,32,128]{2,1,0:T(8,128)(2,1)S(1)}, bf16[96,128,128]{2,1,0:T(8,128)(2,1)S(1)}) custom-call(bf16[32,32,128]{2,1,0:T(8,128)(2,1)} %fresh_hbm.1, bf16[96,128,128]{2,1,0:T(8,128)(2,1)} %bitcast.12), custom_call_target="tpu_custom_call" | custom-call | tf_op jit(solution)/shard_map/near/pallas_call | solution.py:583
  9.7 0.0 collective-permute-done.2.refs_2_
  9.8 0.0 collective-permute-done.1.refs_1_
  9.8 0.2 collective-permute-done.refs_0_
  10.0 0.6 %pick_blocks.1 = (bf16[2,32,128]{2,1,0:T(8,128)(2,1)S(1)}, bf16[2,32,128]{2,1,0:T(8,128)(2,1)S(1)}, bf16[2,32,128]{2,1,0:T(8,128)(2,1)S(1)}) custom-call(s32[2,4]{1,0:T(2,128)S(1)} %collective-permute-done.refs_0_, s32[2,4]{1,0:T(2,128)S(1)} %collective-permute-done.1.refs_1_, s32[2,4]{1,0:T(2,128)S(1)} %collective-permute-done.2.refs_2_, ...), custom_call_target="tpu_custom_call" | custom-call | tf_op jit(solution)/shard_map/pick_blocks/pallas_call | solution.py:633
  10.6 1.9 %collective-permute-start.3 = (bf16[2,32,128]{2,1,0:T(8,128)(2,1)S(1)}, bf16[2,32,128]{2,1,0:T(8,128)(2,1)S(1)}, u32[]{:S(2)}, u32[]{:S(2)}) collective-permute-start(bf16[2,32,128]{2,1,0:T(8,128)(2,1)S(1)} %get-tuple-element.27), channel_id=1, source_target_pairs={{0,12},{4,8},{8,4},{12,0},{1,13},{5,9},{9,5},{13,1},{2,14},{6,10},... | collective-permute-start | bytes 49160 | tf_op jit(solution)/shard_map/ppermute | solution.py:560
  12.5 0.8 %collective-permute-start.4 = (bf16[2,32,128]{2,1,0:T(8,128)(2,1)S(1)}, bf16[2,32,128]{2,1,0:T(8,128)(2,1)S(1)}, u32[]{:S(2)}, u32[]{:S(2)}) collective-permute-start(bf16[2,32,128]{2,1,0:T(8,128)(2,1)S(1)} %get-tuple-element.28), channel_id=1, source_target_pairs={{0,8},{4,12},{8,0},{12,4},{1,9},{5,13},{9,1},{13,5},{2,10},{6,14},... | collective-permute-start | bytes 49160 | tf_op jit(solution)/shard_map/ppermute | solution.py:560
  13.2 1.8 %collective-permute-start.5 = (bf16[2,32,128]{2,1,0:T(8,128)(2,1)S(1)}, bf16[2,32,128]{2,1,0:T(8,128)(2,1)S(1)}, u32[]{:S(2)}, u32[]{:S(2)}) collective-permute-start(bf16[2,32,128]{2,1,0:T(8,128)(2,1)S(1)} %get-tuple-element.29), channel_id=1, source_target_pairs={{0,4},{4,0},{8,12},{12,8},{1,5},{5,1},{9,13},{13,9},{2,6},{6,2},{1... | collective-permute-start | bytes 49160 | tf_op jit(solution)/shard_map/ppermute | solution.py:560
  15.0 1.9 %prepare.1 = (f32[160,128]{1,0:T(8,128)S(1)}, f32[768,128]{1,0:T(8,128)S(1)}, s32[1,128]{1,0:T(1,128)S(1)}, f32[1,128]{1,0:T(1,128)S(1)}, bf16[4,16,128]{2,1,0:T(8,128)(2,1)S(1)}, /*index=5*/bf16[96,96]{1,0:T(8,128)(2,1)S(1)}) custom-call(bf16[32,32,128]{2,1,0:T(8,128)(2,1)S(1)} %get-tuple-element.20.fresh_ref.refs_3_, s32[2,4]{1,0:T(2,128)} %bitcast.18, ...), custom_call_target="tpu_custom_call" | custom-call | tf_op jit(solution)/shard_map/prepare/pallas_call | solution.py:595
  17.0 0.0 collective-permute-done.3.refs_0_
  17.0 0.1 collective-permute-done.4.refs_1_
  17.1 0.0 collective-permute-done.5.refs_2_
  17.1 1.4 %far_tiles.1 = (bf16[400,128]{1,0:T(8,128)(2,1)S(1)}, bf16[400,128]{1,0:T(8,128)(2,1)S(1)}, f32[768,128]{1,0:T(8,128)S(1)}, f32[1568,128]{1,0:T(8,128)S(1)}) custom-call(f32[1,128]{1,0:T(1,128)S(1)} %get-tuple-element.21.fracs_ref, s32[1,128]{1,0:T(1,128)S(1)} %get-tuple-element.22.tiles_ref, bf16[96,96]{1,0:T(8,128)(2,1)S(1)} %get-tuple-element.23.table_ref, ...), custom_call_target="tpu_custom_call" | custom-call | tf_op jit(solution)/shard_map/far_tiles/pallas_call | solution.py:653
  18.5 0.0 copy-start
  18.5 1.6 %collective-permute-start.7 = (bf16[400,128]{1,0:T(8,128)(2,1)S(1)}, bf16[400,128]{1,0:T(8,128)(2,1)S(1)}, u32[]{:S(2)}, u32[]{:S(2)}) collective-permute-start(bf16[400,128]{1,0:T(8,128)(2,1)S(1)} %get-tuple-element.31), channel_id=1, source_target_pairs={{0,2},{1,3},{2,0},{3,1},{4,6},{5,7},{6,4},{7,5},{8,10},{9,11},{10,... | collective-permute-start | bytes 307208 | tf_op jit(solution)/shard_map/ppermute | solution.py:560
  20.1 0.0 collective-permute-start.6
  20.1 1.2 %near_tiles.1 = (bf16[192,128]{1,0:T(8,128)(2,1)S(1)}, bf16[208,128]{1,0:T(8,128)(2,1)S(1)}, bf16[400,128]{1,0:T(8,128)(2,1)S(1)}) custom-call(f32[1,128]{1,0:T(1,128)S(1)} %get-tuple-element.21.fracs_ref, s32[1,128]{1,0:T(1,128)S(1)} %get-tuple-element.22.tiles_ref, bf16[4,16,128]{2,1,0:T(8,128)(2,1)S(1)} %get-tuple-element.24.head_ref, ...), custom_call_target="tpu_custom_call" | custom-call | tf_op jit(solution)/shard_map/near_tiles/pallas_call | solution.py:672
  21.3 0.7 %collective-permute-start.9 = (bf16[208,128]{1,0:T(8,128)(2,1)S(1)}, bf16[208,128]{1,0:T(8,128)(2,1)S(1)}, u32[]{:S(2)}, u32[]{:S(2)}) collective-permute-start(bf16[208,128]{1,0:T(8,128)(2,1)S(1)} %get-tuple-element.35), channel_id=1, source_target_pairs={{0,1},{1,0},{2,3},{3,2},{4,5},{5,4},{6,7},{7,6},{8,9},{9,8},{10,11... | collective-permute-start | bytes 159752 | tf_op jit(solution)/shard_map/ppermute | solution.py:560
  22.0 0.1 collective-permute-start.8
  22.1 1.2 %collective-permute-done.8.refs_1_ = bf16[192,128]{1,0:T(8,128)(2,1)S(1)} collective-permute-done((bf16[192,128]{1,0:T(8,128)(2,1)S(1)}, bf16[192,128]{1,0:T(8,128)(2,1)S(1)}, u32[]{:S(2)}, u32[]{:S(2)}) %collective-permute-start.8) | collective-permute-done | bytes 49184 | tf_op jit(solution)/shard_map/ppermute | solution.py:560
  23.2 0.0 collective-permute-done.9.refs_2_
  23.2 0.2 collective-permute-done.7.refs_0_
  23.4 0.3 %forcing.1.forcing_ref = f32[1024,128]{1,0:T(8,128)S(1)} custom-call(bf16[400,128]{1,0:T(8,128)(2,1)S(1)} %collective-permute-done.7.refs_0_, bf16[192,128]{1,0:T(8,128)(2,1)S(1)} %collective-permute-done.8.refs_1_, bf16[208,128]{1,0:T(8,128)(2,1)S(1)} %collective-permute-done.9.refs_2_, bf16[400,128]{1,0:T(8,128)(2,1)S(1)} %get-tuple-element.36.refs_3_, ...), custom_call_target="tpu_custom_call" | custom-call | tf_op jit(solution)/shard_map/forcing/pallas_call | solution.py:682
  23.7 1.5 %collective-permute-done.6.share_ref = bf16[400,128]{1,0:T(8,128)(2,1)S(1)} collective-permute-done((bf16[400,128]{1,0:T(8,128)(2,1)S(1)}, bf16[400,128]{1,0:T(8,128)(2,1)S(1)}, u32[]{:S(2)}, u32[]{:S(2)}) %collective-permute-start.6) | collective-permute-done | bytes 102432 | tf_op jit(solution)/shard_map/ppermute | solution.py:560
  25.3 0.0 copy-done
  25.3 1.5 %window_steps.1 = (bf16[32,32,128]{2,1,0:T(8,128)(2,1)}, f32[2,4096]{1,0:T(2,128)}) custom-call(bf16[400,128]{1,0:T(8,128)(2,1)S(1)} %collective-permute-done.6.share_ref, f32[1024,128]{1,0:T(8,128)S(1)} %forcing.1.forcing_ref, f32[160,128]{1,0:T(8,128)S(1)} %get-tuple-element.37.refs_4_.ready_ref, bf16[2,128,192]{2,1,0:T(8,128)(2,1)S(1)} %copy-done), custom_call_target="tpu_custom_call" | custom-call | tf_op jit(solution)/shard_map/window_steps/pallas_call | solution.py:693
Async XLA Ops:
  0.6 9.1 %collective-permute-start.2 = (s32[2,4]{1,0:T(2,128)}, s32[2,4]{1,0:T(2,128)S(1)}, u32[]{:S(2)}, u32[]{:S(2)}) collective-permute-start(s32[2,4]{1,0:T(2,128)} %bitcast.15), channel_id=1, source_target_pairs={{0,4},{4,12},{12,8},{8,0},{1,5},{5,13},{13,9},{9,1},{2,6},{6,14},{... | collective-permute-start | bytes 104 | tf_op jit(solution)/shard_map/ppermute | solution.py:565
  3.7 6.1 %collective-permute-start.1 = (s32[2,4]{1,0:T(2,128)}, s32[2,4]{1,0:T(2,128)S(1)}, u32[]{:S(2)}, u32[]{:S(2)}) collective-permute-start(s32[2,4]{1,0:T(2,128)} %bitcast.16), channel_id=1, source_target_pairs={{0,12},{4,8},{12,0},{8,4},{1,13},{5,9},{13,1},{9,5},{2,14},{6,10},... | collective-permute-start | bytes 104 | tf_op jit(solution)/shard_map/ppermute | solution.py:565
  6.2 3.8 %collective-permute-start = (s32[2,4]{1,0:T(2,128)}, s32[2,4]{1,0:T(2,128)S(1)}, u32[]{:S(2)}, u32[]{:S(2)}) collective-permute-start(s32[2,4]{1,0:T(2,128)} %bitcast.17), channel_id=1, source_target_pairs={{0,8},{4,0},{12,4},{8,12},{1,9},{5,1},{13,5},{9,13},{2,10},{6,2},{... | collective-permute-start | bytes 104 | tf_op jit(solution)/shard_map/ppermute | solution.py:565
  10.6 6.4 %collective-permute-start.3 = (bf16[2,32,128]{2,1,0:T(8,128)(2,1)S(1)}, bf16[2,32,128]{2,1,0:T(8,128)(2,1)S(1)}, u32[]{:S(2)}, u32[]{:S(2)}) collective-permute-start(bf16[2,32,128]{2,1,0:T(8,128)(2,1)S(1)} %get-tuple-element.27), channel_id=1, source_target_pairs={{0,12},{4,8},{8,4},{12,0},{1,13},{5,9},{9,5},{13,1},{2,14},{6,10},... | collective-permute-start | bytes 49160 | tf_op jit(solution)/shard_map/ppermute | solution.py:560
  12.5 4.7 %collective-permute-start.4 = (bf16[2,32,128]{2,1,0:T(8,128)(2,1)S(1)}, bf16[2,32,128]{2,1,0:T(8,128)(2,1)S(1)}, u32[]{:S(2)}, u32[]{:S(2)}) collective-permute-start(bf16[2,32,128]{2,1,0:T(8,128)(2,1)S(1)} %get-tuple-element.28), channel_id=1, source_target_pairs={{0,8},{4,12},{8,0},{12,4},{1,9},{5,13},{9,1},{13,5},{2,10},{6,14},... | collective-permute-start | bytes 49160 | tf_op jit(solution)/shard_map/ppermute | solution.py:560
  13.2 3.9 %collective-permute-start.5 = (bf16[2,32,128]{2,1,0:T(8,128)(2,1)S(1)}, bf16[2,32,128]{2,1,0:T(8,128)(2,1)S(1)}, u32[]{:S(2)}, u32[]{:S(2)}) collective-permute-start(bf16[2,32,128]{2,1,0:T(8,128)(2,1)S(1)} %get-tuple-element.29), channel_id=1, source_target_pairs={{0,4},{4,0},{8,12},{12,8},{1,5},{5,1},{9,13},{13,9},{2,6},{6,2},{1... | collective-permute-start | bytes 49160 | tf_op jit(solution)/shard_map/ppermute | solution.py:560
  18.5 6.8 %copy-start = (bf16[2,128,192]{2,1,0:T(8,128)(2,1)S(1)}, bf16[2,128,192]{2,1,0:T(8,128)(2,1)}, u32[]{:S(2)}) copy-start(bf16[2,128,192]{2,1,0:T(8,128)(2,1)} %constant.8.clone.fit_ref) | copy-start | bytes 294916
  18.5 4.9 %collective-permute-start.7 = (bf16[400,128]{1,0:T(8,128)(2,1)S(1)}, bf16[400,128]{1,0:T(8,128)(2,1)S(1)}, u32[]{:S(2)}, u32[]{:S(2)}) collective-permute-start(bf16[400,128]{1,0:T(8,128)(2,1)S(1)} %get-tuple-element.31), channel_id=1, source_target_pairs={{0,2},{1,3},{2,0},{3,1},{4,6},{5,7},{6,4},{7,5},{8,10},{9,11},{10,... | collective-permute-start | bytes 307208 | tf_op jit(solution)/shard_map/ppermute | solution.py:560
  20.1 5.2 %collective-permute-start.6 = (bf16[400,128]{1,0:T(8,128)(2,1)S(1)}, bf16[400,128]{1,0:T(8,128)(2,1)S(1)}, u32[]{:S(2)}, u32[]{:S(2)}) collective-permute-start(bf16[400,128]{1,0:T(8,128)(2,1)S(1)} %get-tuple-element.30), channel_id=1, source_target_pairs={{0,3},{1,2},{2,1},{3,0},{4,7},{5,6},{6,5},{7,4},{8,11},{9,10},{10,... | collective-permute-start | bytes 307208 | tf_op jit(solution)/shard_map/ppermute | solution.py:560
  21.3 1.9 %collective-permute-start.9 = (bf16[208,128]{1,0:T(8,128)(2,1)S(1)}, bf16[208,128]{1,0:T(8,128)(2,1)S(1)}, u32[]{:S(2)}, u32[]{:S(2)}) collective-permute-start(bf16[208,128]{1,0:T(8,128)(2,1)S(1)} %get-tuple-element.35), channel_id=1, source_target_pairs={{0,1},{1,0},{2,3},{3,2},{4,5},{5,4},{6,7},{7,6},{8,9},{9,8},{10,11... | collective-permute-start | bytes 159752 | tf_op jit(solution)/shard_map/ppermute | solution.py:560
  22.0 1.2 %collective-permute-start.8 = (bf16[192,128]{1,0:T(8,128)(2,1)S(1)}, bf16[192,128]{1,0:T(8,128)(2,1)S(1)}, u32[]{:S(2)}, u32[]{:S(2)}) collective-permute-start(bf16[192,128]{1,0:T(8,128)(2,1)S(1)} %get-tuple-element.34), channel_id=1, source_target_pairs={{0,1},{1,0},{2,3},{3,2},{4,5},{5,4},{6,7},{7,6},{8,9},{9,8},{10,11... | collective-permute-start | bytes 147464 | tf_op jit(solution)/shard_map/ppermute | solution.py:560
